TPU v7x, 256 devices: a whole 4x4x8 slice. The times are simulated.
256 devices in a mesh: row: 16 (over x, y), col: 16 (over z, core).
Axes of the slice: x: 4, y: 4, z: 8, core: 2. Of those that a mesh axis runs over, the one named last changes fastest.
Arguments:
- tokens: bfloat16 [512, 16384], P('col', 'row'), may hold values from -6 to 6
- weight: bfloat16 [16384, 53248], P('row', 'col')
- down_adapter: float32 [16384, 16], P('row'), may hold values from -0.046875 to 0.046875
- up_adapter: float32 [16, 53248], P(None, 'col'), may hold values from -0.75 to 0.75
- magnitude: float32 [53248], P('col'), may hold values from 0.5 to 2
- out_cotangent: bfloat16 [512, 53248], P('row', 'col')
Outputs:
- output: bfloat16 [512, 53248], P('row', 'col')
- grad_tokens: bfloat16 [512, 16384], P('col', 'row')
- grad_magnitude: float32 [53248], P('col')
- up_gradient: float32 [16, 53248], P(None, 'col')
- down_gradient: float32 [16384, 16], P('row')
All inputs are finite; a program needn't handle non-finite values.
Results may differ from a plain program's by a relative error of at most 0.0058.
Values may be sent and summed in bfloat16 or wider, within the bound.
No kernel may reach another device: no remote copies, remote signals or barrier semaphores. Data moves between devices by JAX's collectives and lax.ppermute only.
A program may use at most 128 MiB of HBM per device.

v0:
```python
import jax
import jax.numpy as jnp
from jax import lax
from jax.sharding import PartitionSpec as P

adapter_scale = 2.0
epsilon = 1e-06
highest = lax.Precision.HIGHEST


def on_device(tokens, weight, down_adapter, up_adapter, magnitude, out_cotangent):
    merged = weight.astype(jnp.float32) + adapter_scale * jnp.dot(
        down_adapter, up_adapter, precision=highest
    )
    merged_low = merged.astype(jnp.bfloat16)
    square_sums = jnp.sum(merged * merged, axis=0)
    norm_squares = lax.psum(square_sums, "row")
    column_norm = jnp.sqrt(norm_squares + epsilon)
    factor = magnitude / column_norm
    gathered = lax.all_gather(tokens, "col", axis=0, tiled=True)
    adapter_part = jnp.dot(gathered.astype(jnp.float32), down_adapter, precision=highest)
    adapter_proj = lax.psum(adapter_part, "row")
    cotangent = out_cotangent.astype(jnp.float32)
    part_rows = gathered
    out_full = lax.psum_scatter(
        jnp.dot(part_rows, merged_low, preferred_element_type=jnp.float32) * factor,
        "row",
        scatter_dimension=0,
        tiled=True,
    )
    magnitude_part = jnp.sum(cotangent * out_full, axis=0) / magnitude
    output = out_full.astype(jnp.bfloat16)
    grad_rows = (cotangent * factor).astype(jnp.bfloat16)
    grad_full = lax.all_gather(grad_rows, "row", axis=0, tiled=True)
    part_rows = grad_full
    grad_tokens = lax.psum_scatter(
        lax.dot_general(
            part_rows, merged_low, (((1,), (1,)), ((), ())), preferred_element_type=jnp.float32
        ),
        "col",
        scatter_dimension=0,
        tiled=True,
    ).astype(jnp.bfloat16)
    grad_float = grad_full.astype(jnp.float32)
    low_part = lax.dot_general(grad_float, up_adapter, (((1,), (1,)), ((), ())), precision=highest)
    low_rank = lax.psum(low_part, "col")
    grad_magnitude = lax.psum(magnitude_part, "row")
    up_gradient = adapter_scale * lax.dot_general(
        adapter_proj, grad_float, (((0,), (0,)), ((), ())), precision=highest
    )
    down_gradient = adapter_scale * lax.dot_general(
        gathered.astype(jnp.float32), low_rank, (((0,), (0,)), ((), ())), precision=highest
    )
    return (output, grad_tokens, grad_magnitude, up_gradient, down_gradient)


def solution(mesh):
    return jax.shard_map(
        on_device,
        mesh=mesh,
        in_specs=(
            P("col", "row"),
            P("row", "col"),
            P("row", None),
            P(None, "col"),
            P("col"),
            P("row", "col"),
        ),
        out_specs=(P("row", "col"), P("col", "row"), P("col"), P(None, "col"), P("row", None)),
        check_vma=False,
    )
```

profile of v0, /device:TPU:8, one launch (start us, length us, event | category | flops | bytes accessed | tf_op | source)
XLA Modules:
  0.0 401.9 jit_solution(5958858901072714557)
XLA Ops:
  7.2 0.0 copy-start
  7.2 0.0 all-gather.3.cloned.1.call-start
  7.2 0.7 all-gather.3.cloned.1.call-update
  7.9 0.0 copy-start.5
  7.9 0.0 reduce-scatter.7.cloned.1.call-start
  8.0 0.1 copy-done
  8.1 16.2 %multiply_reduce_fusion = (f32[3328]{0:T(1024)S(1)}, bf16[1024,3328]{1,0:T(8,128)(2,1)}) fusion(f32[1024,16]{0,1:T(8,128)} %param.8, f32[16,3328]{1,0:T(8,128)S(1)} %copy-done, bf16[1024,3328]{1,0:T(8,128)(2,1)} %param.7), kind=kOutput, calls=%fused_computation | convolution fusion | flops 674755328 | bytes 13923328 | tf_op jit(solution)/shard_map/dot_general | solution.py:12
  24.3 69.4 %psum.28 = f32[3328]{0:T(1024)S(1)} all-reduce(f32[3328]{0:T(1024)S(1)} %get-tuple-element.24), channel_id=1, replica_groups=mesh['row'=16,'col'=16] {'row'}, use_global_device_ids=true, to_apply=%region_1.0 | all-reduce | flops 3328 | bytes 26624 | tf_op jit(solution)/shard_map/psum | solution.py:17
  93.8 0.0 copy-done.5
  93.8 0.0 all-gather.3.cloned.1.call-done
  93.8 10.3 %multiply_bitcast_fusion = f32[512,3328]{0,1:T(8,128)} fusion(bf16[512,1024]{1,0:T(8,128)(2,1)} %all-gather.3.cloned.1.call-done, f32[3328]{0:T(1024)S(1)} %rsqrt_multiply_fusion, bf16[1024,3328]{1,0:T(8,128)(2,1)} %get-tuple-element.25), kind=kOutput, calls=%fused_computation.2 | convolution fusion | flops 3491364864 | bytes 14693376 | tf_op jit(solution)/shard_map/dot_general | solution.py:26
  104.1 7.7 %copy.18 = f32[512,3328]{1,0:T(8,128)} copy(f32[512,3328]{0,1:T(8,128)} %multiply_bitcast_fusion) | data formatting | bytes 13631488
  111.8 0.0 copy-start.3
  111.8 0.0 reduce-scatter.7.cloned.1.call-update
  111.8 0.0 all-gather.5.cloned.1.call-start
  111.9 89.9 %reduce-scatter.7.cloned.1.call-done = f32[32,3328]{1,0:T(8,128)} async-done(((f32[512,3328]{1,0:T(8,128)}), f32[32,3328]{1,0:T(8,128)}) %reduce-scatter.7.cloned.1.call-update) | async-done | bytes 426000 | tf_op jit(solution)/shard_map/reduce_scatter | solution.py:25
  201.8 0.0 copy-done.3
  201.8 1.8 fusion.5
  203.6 0.0 all-gather.5.cloned.1.call-update
  203.6 0.0 copy-start.1
  203.6 0.0 copy-start.4
  203.6 0.0 copy-start.2
  203.6 0.2 reduce-scatter.5.cloned.1.call-start
  203.8 54.0 %all-gather.5.cloned.1.call-done = bf16[512,3328]{1,0:T(8,128)(2,1)} async-done(((bf16[32,3328]{1,0:T(8,128)(2,1)}), bf16[512,3328]{1,0:T(8,128)(2,1)}) %all-gather.5.cloned.1.call-update) | async-done | bytes 3407888 | tf_op jit(solution)/shard_map/all_gather | solution.py:34
  257.9 9.0 %fusion = f32[512,1024]{1,0:T(8,128)} fusion(bf16[512,3328]{1,0:T(8,128)(2,1)} %all-gather.5.cloned.1.call-done, bf16[1024,3328]{1,0:T(8,128)(2,1)} %get-tuple-element.25), kind=kOutput, calls=%fused_computation.4 | convolution fusion | flops 3489660928 | bytes 12320768 | tf_op jit(solution)/shard_map/dot_general | solution.py:37
  266.9 0.0 reduce-scatter.5.cloned.1.call-update
  266.9 0.0 copy-done.1
  266.9 0.0 copy-done.4
  266.9 0.9 fusion.6
  267.8 0.0 copy-done.2
  267.9 0.4 copy.19
  268.3 1.0 copy.17
  269.3 68.6 %all-reduce = (f32[3328]{0:T(1024)}, f32[512,16]{0,1:T(8,128)S(1)}) all-reduce(f32[3328]{0:T(1024)S(1)} %div.7, f32[512,16]{0,1:T(8,128)S(1)} %fusion.6), channel_id=1, replica_groups=mesh['row'=16,'col'=16] {'row'}, use_global_device_ids=true, to_apply=%region_5.0 | all-reduce | flops 11520 | bytes 92160 | tf_op jit(solution)/shard_map/psum | solution.py:47
  337.8 4.7 %fusion.7 = f32[512,16]{0,1:T(8,128)S(1)} fusion(bf16[512,3328]{1,0:T(8,128)(2,1)} %all-gather.5.cloned.1.call-done, f32[16,3328]{1,0:T(8,128)S(1)} %copy-done), kind=kOutput, calls=%fused_computation.15 | convolution fusion | flops 327155712 | bytes 3653632 | tf_op jit(solution)/shard_map/dot_general | solution.py:45
  342.5 46.1 %psum.31 = f32[512,16]{0,1:T(8,128)S(1)} all-reduce(f32[512,16]{0,1:T(8,128)S(1)} %fusion.7), channel_id=1, replica_groups=mesh['row'=16,'col'=16] {'col'}, use_global_device_ids=true, to_apply=%region_7.0 | all-reduce | flops 8192 | bytes 65536 | tf_op jit(solution)/shard_map/psum | solution.py:46
  388.6 1.2 fusion.3
  389.7 4.1 %convolution_multiply_fusion = f32[16,3328]{1,0:T(8,128)} fusion(f32[512,16]{0,1:T(8,128)S(1)} %get-tuple-element.21, bf16[512,3328]{1,0:T(8,128)(2,1)} %all-gather.5.cloned.1.call-done), kind=kOutput, calls=%fused_computation.3 | convolution fusion | flops 327208960 | bytes 3653632 | tf_op jit(solution)/shard_map/dot_general | solution.py:48
  393.8 0.0 reduce-scatter.5.cloned.1.call-done
  393.8 1.5 convert_element_type.26
  (2 shorter events, 0.0 us)
Async XLA Ops:
  7.2 0.9 copy-start
  7.2 86.6 %all-gather.3.cloned.1.call-start = ((), (), s32[]{:S(2)}) async-start(), calls=%async_computation.2 | async-start | bytes 1114112 | tf_op jit(solution)/shard_map/all_gather | solution.py:20
  7.9 85.9 %copy-start.5 = (f32[3328]{0:T(1024)S(1)}, f32[3328]{0:T(1024)}, u32[]{:S(2)}) copy-start(f32[3328]{0:T(1024)} %param.10) | copy-start | bytes 39940
  7.9 193.9 %reduce-scatter.7.cloned.1.call-start = ((), (), s32[]{:S(2)}) async-start(), calls=%async_computation.5 | async-start | bytes 7241728 | tf_op jit(solution)/shard_map/reduce_scatter | solution.py:25
  111.8 90.0 %copy-start.3 = (bf16[32,3328]{1,0:T(8,128)(2,1)S(1)}, bf16[32,3328]{1,0:T(8,128)(2,1)}, u32[]{:S(2)}) copy-start(bf16[32,3328]{1,0:T(8,128)(2,1)} %param.11) | copy-start | bytes 638980
  111.8 146.0 %all-gather.5.cloned.1.call-start = ((), (), s32[]{:S(2)}) async-start(), calls=%async_computation.3 | async-start | bytes 3620864 | tf_op jit(solution)/shard_map/all_gather | solution.py:34
  203.6 63.3 %copy-start.1 = (bf16[512,1024]{1,0:T(8,128)(2,1)S(1)}, bf16[512,1024]{1,0:T(8,128)(2,1)}, u32[]{:S(2)}) copy-start(bf16[512,1024]{1,0:T(8,128)(2,1)} %all-gather.3.cloned.1.call-done) | copy-start | bytes 3145732
  203.6 63.3 %copy-start.4 = (f32[1024,16]{0,1:T(8,128)S(1)}, f32[1024,16]{0,1:T(8,128)}, u32[]{:S(2)}) copy-start(f32[1024,16]{0,1:T(8,128)} %param.8) | copy-start | bytes 196612
  203.6 64.2 %copy-start.2 = (f32[32,3328]{1,0:T(8,128)S(1)}, f32[32,3328]{1,0:T(8,128)}, u32[]{:S(2)}) copy-start(f32[32,3328]{1,0:T(8,128)} %reduce-scatter.7.cloned.1.call-done) | copy-start | bytes 1277956
  203.6 190.2 %reduce-scatter.5.cloned.1.call-start = ((), (), s32[]{:S(2)}) async-start(), calls=%async_computation.4 | async-start | bytes 2228224 | tf_op jit(solution)/shard_map/reduce_scatter | solution.py:36
Sparse Core Ops, SparseCore 0:
  9.8 41.4 all-gather.2
  112.0 89.7 reduce-scatter.6
  205.2 52.6 all-gather.4
  267.0 59.1 reduce-scatter.4
where the time goes:
time: 406 us; the launch traced here: 402 us
  blocking collectives  184 us (45%)
  waiting for transfers between devices  145 us (36%)
  matrix products  46.4 us (11%)
  between operations  13.9 us (3%)
  local copies, waits for them, and re-layouts  9.22 us (2%)
    reduce_scatter x1, waiting for transfers between devices, on_device(): lax.psum_scatter(jnp.dot(part_rows, merged_low, preferred_element_type=jn...  89.9 us
    psum x1, blocking collectives, on_device(): norm_squares = lax.psum(square_sums, 'row')  69.4 us
    psum x1, blocking collectives, on_device(): grad_magnitude = lax.psum(magnitude_part, 'row')  68.6 us
    all_gather x1, waiting for transfers between devices, on_device(): grad_full = lax.all_gather(grad_rows, 'row', axis=0, tiled=True)  54 us
    psum x1, blocking collectives, on_device(): low_rank = lax.psum(low_part, 'col')  46.1 us
    dot_general x1, matrix products, on_device(): jnp.dot(down_adapter, up_adapter, precision=highest)  16.2 us
    dot_general x1, matrix products, on_device(): jnp.dot(part_rows, merged_low, preferred_element_type=jnp.float32) * factor  10.3 us
    unnamed x15, local copies, waits for them, and re-layouts  9.22 us
  transfers between devices with their start and end apart: 4, of which 2 were waited for; matrix products, arithmetic and copies ran while one was open for 7% of the time, Pallas kernels for 0%

commit v1 on v0

v1 whole, which is shorter than its diff:
```python
import jax
import jax.numpy as jnp
from jax import lax
from jax.experimental import pallas as pl
from jax.experimental.pallas import tpu as pltpu
from jax.sharding import Mesh
from jax.sharding import PartitionSpec as P

adapter_scale = 2.0
epsilon = 1e-06
bf16 = jnp.bfloat16
f32 = jnp.float32
ROW = ("x", "y")
COL = ("z", "c")
TILE = 256
VMEM = 56 * 1024 * 1024


def pieces(value):
    high = value.astype(bf16)
    rest = value - high.astype(f32)
    mid = rest.astype(bf16)
    low = (rest - mid.astype(f32)).astype(bf16)
    return high, mid, low


def dot(left, right, left_dim, right_dim):
    return lax.dot_general(
        left, right, (((left_dim,), (right_dim,)), ((), ())), preferred_element_type=f32
    )


def params(semantics=("arbitrary",)):
    return pltpu.CompilerParams(dimension_semantics=semantics, vmem_limit_bytes=VMEM)


def merge_kernel(down_ref, up_ref, weight_ref, merged_ref, sums_ref, up_cat, totals):
    step = pl.program_id(0)
    rows, width = weight_ref.shape

    @pl.when(step == 0)
    def _():
        totals[...] = jnp.zeros_like(totals)
        for start in range(0, width, TILE):
            cols = slice(start, start + TILE)
            u1, u2, u3 = pieces(up_ref[:, cols])
            up_cat[:, cols] = jnp.concatenate([u1, u2, u1, u3, u1, u2], axis=0)

    d1, d2, d3 = pieces(down_ref[...] * adapter_scale)
    down_cat = jnp.concatenate([d1, d1, d2, d1, d3, d2], axis=0)
    for start in range(0, width, TILE):
        cols = slice(start, start + TILE)
        merged = weight_ref[:, cols].astype(f32) + dot(down_cat, up_cat[:, cols], 0, 0)
        merged_ref[:, cols] = merged.astype(bf16)
        totals[:, cols] += jnp.sum((merged * merged).reshape(rows // 8, 8, TILE), axis=0)

    @pl.when(step == pl.num_programs(0) - 1)
    def _():
        sums_ref[...] = jnp.sum(totals[...], axis=0, keepdims=True)


def merge(down_t, up, weight):
    depth, width = weight.shape
    rows = 256
    return pl.pallas_call(
        merge_kernel,
        grid=(depth // rows,),
        in_specs=[
            pl.BlockSpec((16, rows), lambda i: (0, i)),
            pl.BlockSpec((16, width), lambda i: (0, 0)),
            pl.BlockSpec((rows, width), lambda i: (i, 0)),
        ],
        out_specs=[
            pl.BlockSpec((rows, width), lambda i: (i, 0)),
            pl.BlockSpec((1, width), lambda i: (0, 0)),
        ],
        out_shape=[
            jax.ShapeDtypeStruct((depth, width), bf16),
            jax.ShapeDtypeStruct((1, width), f32),
        ],
        scratch_shapes=[pltpu.VMEM((96, width), bf16), pltpu.VMEM((8, width), f32)],
        compiler_params=params(),
        cost_estimate=pl.CostEstimate(
            flops=12 * depth * width, bytes_accessed=4 * depth * width, transcendentals=0
        ),
        name="merge",
    )(down_t, up, weight)


def forward_kernel(core_ref, own_ref, other_ref, down_ref, merged_ref, part_ref, tokens_ref, adapter_ref):
    core = core_ref[0]
    blocks = own_ref.shape[0]
    depth = own_ref.shape[2]

    @pl.when(pl.program_id(0) == 0)
    def _():
        d1, d2, d3 = pieces(down_ref[...])
        down_cat = jnp.concatenate([d1, d2, d3], axis=0)
        for source, parity in ((own_ref, core), (other_ref, 1 - core)):
            proj = dot(source[...].reshape(-1, depth), down_cat, 1, 1)
            proj = proj[:, :16] + proj[:, 16:32] + proj[:, 32:48]
            for z in range(blocks):
                tokens_ref[2 * z + parity] = source[z]
                adapter_ref[2 * z + parity] = proj[32 * z : 32 * z + 32]

    for source, parity in ((own_ref, core), (other_ref, 1 - core)):
        out = dot(source[...].reshape(-1, depth), merged_ref[...], 1, 0).astype(bf16)
        for z in range(blocks):
            part_ref[2 * z + parity] = out[32 * z : 32 * z + 32]


def forward(core, own, other, down_t, merged_low):
    blocks, size, depth = own.shape
    width = merged_low.shape[1]
    whole = lambda i, c: (0, 0, 0)
    return pl.pallas_call(
        forward_kernel,
        grid_spec=pltpu.PrefetchScalarGridSpec(
            num_scalar_prefetch=1,
            grid=(width // TILE,),
            in_specs=[
                pl.BlockSpec((blocks, size, depth), whole),
                pl.BlockSpec((blocks, size, depth), whole),
                pl.BlockSpec((16, depth), lambda i, c: (0, 0)),
                pl.BlockSpec((depth, TILE), lambda i, c: (0, i)),
            ],
            out_specs=[
                pl.BlockSpec((2 * blocks, size, TILE), lambda i, c: (0, 0, i)),
                pl.BlockSpec((2 * blocks, size, depth), whole),
                pl.BlockSpec((2 * blocks, size, 16), whole),
            ],
        ),
        out_shape=[
            jax.ShapeDtypeStruct((2 * blocks, size, width), bf16),
            jax.ShapeDtypeStruct((2 * blocks, size, depth), bf16),
            jax.ShapeDtypeStruct((2 * blocks, size, 16), f32),
        ],
        compiler_params=params(),
        cost_estimate=pl.CostEstimate(
            flops=2 * 512 * depth * width, bytes_accessed=12 * 1024 * 1024, transcendentals=0
        ),
        name="forward",
    )(core, own, other, down_t, merged_low)


def backward_kernel(
    core_ref, cot_ref, part_ref, factor_ref, up_ref, merged_ref,
    own_ref, other_ref, low_ref, mag_ref, total, low_total,
):
    core = core_ref[0]
    step = pl.program_id(0)

    @pl.when(step == 0)
    def _():
        total[...] = jnp.zeros_like(total)
        low_total[...] = jnp.zeros_like(low_total)

    cot = cot_ref[...].astype(f32)
    mag_ref[...] = jnp.sum(cot * part_ref[...].astype(f32), axis=0, keepdims=True)
    grad = (cot * factor_ref[...]).astype(bf16)
    total[...] += dot(grad, merged_ref[...], 1, 1)
    u1, u2, u3 = pieces(up_ref[...])
    low_total[...] += dot(grad, jnp.concatenate([u1, u2, u3], axis=0), 1, 1)

    @pl.when(step == pl.num_programs(0) - 1)
    def _():
        low_ref[...] = low_total[:, :16] + low_total[:, 16:32] + low_total[:, 32:48]
        for z in range(8):
            own = pl.ds(pl.multiple_of((2 * z + core) * 32, 32), 32)
            other = pl.ds(pl.multiple_of((2 * z + 1 - core) * 32, 32), 32)
            own_ref[z] = total[own, :]
            other_ref[z] = total[other, :].astype(bf16)


def backward(core, cot, part, factor, up, merged_low):
    depth, width = merged_low.shape
    tokens = cot.shape[0]
    return pl.pallas_call(
        backward_kernel,
        grid_spec=pltpu.PrefetchScalarGridSpec(
            num_scalar_prefetch=1,
            grid=(width // TILE,),
            in_specs=[
                pl.BlockSpec((tokens, TILE), lambda i, c: (0, i)),
                pl.BlockSpec((tokens, TILE), lambda i, c: (0, i)),
                pl.BlockSpec((1, TILE), lambda i, c: (0, i)),
                pl.BlockSpec((16, TILE), lambda i, c: (0, i)),
                pl.BlockSpec((depth, TILE), lambda i, c: (0, i)),
            ],
            out_specs=[
                pl.BlockSpec((8, 32, depth), lambda i, c: (0, 0, 0)),
                pl.BlockSpec((8, 32, depth), lambda i, c: (0, 0, 0)),
                pl.BlockSpec((tokens, 16), lambda i, c: (0, 0)),
                pl.BlockSpec((1, TILE), lambda i, c: (0, i)),
            ],
            scratch_shapes=[pltpu.VMEM((tokens, depth), f32), pltpu.VMEM((tokens, 48), f32)],
        ),
        out_shape=[
            jax.ShapeDtypeStruct((8, 32, depth), f32),
            jax.ShapeDtypeStruct((8, 32, depth), bf16),
            jax.ShapeDtypeStruct((tokens, 16), f32),
            jax.ShapeDtypeStruct((1, width), f32),
        ],
        compiler_params=params(),
        cost_estimate=pl.CostEstimate(
            flops=2 * 512 * depth * width, bytes_accessed=16 * 1024 * 1024, transcendentals=0
        ),
        name="backward",
    )(core, cot, part, factor, up, merged_low)


def up_kernel(proj_ref, cot_ref, factor_ref, out_ref):
    a1, a2, a3 = pieces(proj_ref[...] * adapter_scale)
    grad = (cot_ref[...].astype(f32) * factor_ref[...]).astype(bf16)
    out = dot(jnp.concatenate([a1, a2, a3], axis=1), grad, 0, 0)
    out_ref[...] = out[:16] + out[16:32] + out[32:48]


def up_gradient_of(proj, cot, factor):
    tokens, width = cot.shape
    tile = width // 2
    return pl.pallas_call(
        up_kernel,
        grid=(2,),
        in_specs=[
            pl.BlockSpec((tokens, 16), lambda i: (0, 0)),
            pl.BlockSpec((tokens, tile), lambda i: (0, i)),
            pl.BlockSpec((1, tile), lambda i: (0, i)),
        ],
        out_specs=pl.BlockSpec((16, tile), lambda i: (0, i)),
        out_shape=jax.ShapeDtypeStruct((16, width), f32),
        compiler_params=params(),
        cost_estimate=pl.CostEstimate(
            flops=2 * 512 * 256 * width, bytes_accessed=4 * 1024 * 1024, transcendentals=0
        ),
        name="up_gradient",
    )(proj, cot, factor)


def down_kernel(low_ref, tokens_ref, out_ref):
    a1, a2, a3 = pieces(low_ref[...] * adapter_scale)
    out = dot(jnp.concatenate([a1, a2, a3], axis=1), tokens_ref[...], 0, 0)
    out_ref[...] = out[:16] + out[16:32] + out[32:48]


def down_gradient_of(low, tokens):
    return pl.pallas_call(
        down_kernel,
        out_shape=jax.ShapeDtypeStruct((16, tokens.shape[1]), f32),
        compiler_params=pltpu.CompilerParams(vmem_limit_bytes=VMEM),
        cost_estimate=pl.CostEstimate(
            flops=2 * 512 * 256 * 1024, bytes_accessed=1024 * 1024, transcendentals=0
        ),
        name="down_gradient",
    )(low, tokens)


def exchange(blocks, axis):
    return lax.all_to_all(blocks, axis, 0, 0, tiled=False)


def add_up(part, axis):
    return jnp.sum(exchange(jnp.broadcast_to(part[None], (16,) + part.shape), axis), axis=0)


def on_device(tokens, weight, down_adapter, up_adapter, magnitude, out_cotangent):
    core = lax.axis_index("c")
    core_ref = core.astype(jnp.int32).reshape(1)
    swap = [(0, 1), (1, 0)]
    down_t = down_adapter.T
    cot_full = lax.all_gather(out_cotangent, ROW, axis=0, tiled=True)
    own_tokens = exchange(jnp.broadcast_to(tokens[None], (8,) + tokens.shape), "z")
    other_tokens = lax.ppermute(own_tokens, "c", swap)
    merged_low, square_sums = merge(down_t, up_adapter, weight)
    norm_squares = add_up(square_sums.reshape(26, 128), ROW).reshape(1, -1)
    column_norm = jnp.sqrt(norm_squares + epsilon)
    factor = magnitude.reshape(1, -1) / column_norm
    part, tokens_full, adapter_part = forward(core_ref, own_tokens, other_tokens, down_t, merged_low)
    out_parts = exchange(part, ROW)
    output = (jnp.sum(out_parts.astype(f32), axis=0) * factor).astype(bf16)
    own_grad, other_grad, low_part, magnitude_part = backward(
        core_ref, cot_full, part.reshape(512, -1), factor, up_adapter, merged_low
    )
    pair = (own_grad + lax.ppermute(other_grad, "c", swap).astype(f32)).astype(bf16)
    grad_tokens = jnp.sum(exchange(pair, "z").astype(f32), axis=0).astype(bf16)
    low_rank = add_up(low_part.reshape(64, 128), COL).reshape(512, 16)
    small = jnp.concatenate([magnitude_part.reshape(26, 128), adapter_part.reshape(64, 128)], axis=0)
    small = add_up(small, ROW)
    grad_magnitude = small[:26].reshape(-1) / column_norm.reshape(-1)
    adapter_proj = small[26:].reshape(512, 16)
    up_gradient = up_gradient_of(adapter_proj, cot_full, factor)
    down_gradient = down_gradient_of(low_rank, tokens_full.reshape(512, -1)).T
    return (output, grad_tokens, grad_magnitude, up_gradient, down_gradient)


def solution(mesh):
    split = Mesh(mesh.devices.reshape(4, 4, 8, 2), ROW + COL)
    return jax.shard_map(
        on_device,
        mesh=split,
        in_specs=(P(COL, ROW), P(ROW, COL), P(ROW, None), P(None, COL), P(COL), P(ROW, COL)),
        out_specs=(P(ROW, COL), P(COL, ROW), P(COL), P(None, COL), P(ROW, None)),
        check_vma=False,
    )
```

time: 406 us -> 196 us (0.48)
  blocking collectives: 184 us -> 25.8 us
  waiting for transfers between devices: 145 us -> 59.1 us
  matrix products: 46.4 us -> 0 us
  Pallas kernels: 0 us -> 41.1 us
  starting transfers between devices: 0.34 us -> 33.6 us
  other arithmetic: 3.32 us -> 8.98 us
    psum x3 -> x0, blocking collectives: 184 us -> none  [the longest x1 69.4 us: on_device(): norm_squares = lax.psum(square_sums, 'row')]
    reduce_scatter x2 -> x0, waiting for transfers between devices: 89.9 us -> none  [the longest x1 89.9 us: on_device(): lax.psum_scatter(jnp.dot(part_rows, merged_low, preferred_element_type=jn...]
    all_to_all x0 -> x5, waiting for transfers between devices: none -> 57.8 us  [exchange(): return lax.all_to_all(blocks, axis, 0, 0, tiled=False)]
    all_gather x2 -> x1, waiting for transfers between devices: 54.1 us -> 0.02 us  [on_device(): cot_full = lax.all_gather(out_cotangent, ROW, axis=0, tiled=True)]
    dot_general x7 -> x0, matrix products: 46.4 us -> none  [the longest x1 16.2 us: on_device(): jnp.dot(down_adapter, up_adapter, precision=highest)]
    pallas_call x0 -> x5, Pallas kernels: none -> 41.1 us  [the longest x1 14.6 us: backward(): pl.pallas_call(backward_kernel, grid_spec=pltpu.PrefetchScalarGridSpec(nu...]
    all_to_all x0 -> x5, starting transfers between devices: none -> 33.3 us  [exchange(): return lax.all_to_all(blocks, axis, 0, 0, tiled=False)]
    all_to_all x0 -> x1, blocking collectives: none -> 25.8 us  [exchange(): return lax.all_to_all(blocks, axis, 0, 0, tiled=False)]
  transfers between devices with their start and end apart: 4 -> 8, of which waited for: 2 -> 5; matrix products, arithmetic and copies ran while one was open for 7% -> 7% of each run, Pallas kernels for 0% -> 21%
where the time goes in v1:
time: 196 us; the launch traced here: 192 us
  waiting for transfers between devices  59.1 us (30%)
  Pallas kernels  41.1 us (21%)
  starting transfers between devices  33.6 us (17%)
  blocking collectives  25.8 us (13%)
  between operations  14.2 us (7%)
  local copies, waits for them, and re-layouts  9.35 us (5%)
  other arithmetic  8.98 us (5%)
    all_to_all x5, waiting for transfers between devices, exchange(): return lax.all_to_all(blocks, axis, 0, 0, tiled=False)  57.8 us
    all_to_all x5, starting transfers between devices, exchange(): return lax.all_to_all(blocks, axis, 0, 0, tiled=False)  33.3 us
    all_to_all x1, blocking collectives, exchange(): return lax.all_to_all(blocks, axis, 0, 0, tiled=False)  25.8 us
    pallas_call x1, Pallas kernels, backward(): pl.pallas_call(backward_kernel, grid_spec=pltpu.PrefetchScalarGridSpec(nu...  14.6 us
    pallas_call x1, Pallas kernels, forward(): pl.pallas_call(forward_kernel, grid_spec=pltpu.PrefetchScalarGridSpec(num...  13 us
    pallas_call x1, Pallas kernels, merge(): pl.pallas_call(merge_kernel, grid=(depth // rows,), in_specs=[pl.BlockSpe...  7.9 us
  transfers between devices with their start and end apart: 8, of which 5 were waited for; matrix products, arithmetic and copies ran while one was open for 7% of the time, Pallas kernels for 21%

profile of v1, /device:TPU:8, one launch (start us, length us, event | category | flops | bytes accessed | tf_op | source)
XLA Modules:
  0.0 192.1 jit_solution(3158552673979163839)
XLA Ops:
  7.2 0.0 all-gather.2.cloned.1.call-start
  7.2 0.7 all-gather.2.cloned.1.call-update
  7.9 0.9 broadcast_in_dim.12
  8.8 25.8 %all_to_all.30.own_ref = bf16[8,32,1024]{2,1,0:T(8,128)(2,1)S(1)} all-to-all(bf16[8,32,1024]{2,1,0:T(8,128)(2,1)S(1)} %broadcast_in_dim.12), channel_id=1, replica_groups=mesh['x'=4,'y'=4,'z'=8,'c'=2] {'z'}, dimensions={0} | all-to-all | bytes 1048576 | tf_op jit(solution)/shard_map/all_to_all | solution.py:259
  34.6 0.0 collective-permute-start
  34.6 7.9 %merge.1 = (bf16[1024,3328]{1,0:T(8,128)(2,1)}, f32[1,3328]{1,0:T(1,128)}) custom-call(f32[16,1024]{1,0:T(8,128)} %bitcast.16, f32[16,3328]{1,0:T(8,128)} %up_ref.3, bf16[1024,3328]{1,0:T(8,128)(2,1)} %weight_ref.1), custom_call_target="tpu_custom_call" | custom-call | flops 40894464 | bytes 13631488 | tf_op jit(solution)/shard_map/merge/pallas_call | solution.py:65
  42.5 0.0 copy-done.3
  42.5 0.7 reduce.1
  43.2 0.7 broadcast_in_dim.28
  43.9 7.4 %all-to-all-start.2 = ((f32[16,26,128]{2,1,0:T(8,128)}), f32[16,26,128]{2,1,0:T(8,128)S(1)}, u32[]{:S(2)}, u32[]{:S(2)}) async-start(f32[16,26,128]{2,1,0:T(8,128)} %broadcast_in_dim.28), calls=%async_computation.2 | async-start | bytes 524288 | tf_op jit(solution)/shard_map/all_to_all | solution.py:259
  51.3 0.0 collective-permute-done.other_ref
  51.3 0.8 copy-done.5
  52.1 13.0 %forward.1 = (bf16[16,32,3328]{2,1,0:T(8,128)(2,1)}, bf16[16,32,1024]{2,1,0:T(8,128)(2,1)}, f32[16,32,16]{2,1,0:T(8,128)}) custom-call(s32[1]{0:T(128)} %bitcast.core_ref, bf16[8,32,1024]{2,1,0:T(8,128)(2,1)} %copy-done.3, bf16[8,32,1024]{2,1,0:T(8,128)(2,1)} %copy-done.5, f32[16,1024]{1,0:T(8,128)} %bitcast.17, bf16[1024,3328]{1,0:T(8,128)(2,1)} %get-tuple-element.14.merged_ref), custom_call_target="tpu_custom_call" | custom-call | flops 3489660928 | bytes 12582912 | tf_op jit(solution)/shard_map/forward/pallas_call | solution.py:116
  65.2 0.0 all-to-all-done.2
  65.2 0.0 copy-start.4
  65.2 0.7 copy-done.2
  65.9 7.2 %all-to-all-start.1 = ((bf16[16,32,3328]{2,1,0:T(8,128)(2,1)}), bf16[16,32,3328]{2,1,0:T(8,128)(2,1)S(1)}, u32[]{:S(2)}, u32[]{:S(2)}) async-start(bf16[16,32,3328]{2,1,0:T(8,128)(2,1)} %get-tuple-element.15), calls=%async_computation.1 | async-start | bytes 6815744 | tf_op jit(solution)/shard_map/all_to_all | solution.py:259
  73.1 1.0 reduce_sum.49
  74.1 0.6 div.9.factor_ref
  74.7 1.1 reshape.54
  75.8 0.0 all-gather.2.cloned.1.call-done.cot_ref
  75.8 14.6 %backward.1 = (f32[8,32,1024]{2,1,0:T(8,128)}, bf16[8,32,1024]{2,1,0:T(8,128)(2,1)}, f32[512,16]{1,0:T(8,128)}, f32[1,3328]{1,0:T(1,128)}) custom-call(s32[1]{0:T(128)} %bitcast.core_ref, bf16[512,3328]{1,0:T(8,128)(2,1)} %all-gather.2.cloned.1.call-done.cot_ref, bf16[512,3328]{1,0:T(8,128)(2,1)} %bitcast.14, f32[1,3328]{1,0:T(1,128)} %div.9.factor_ref, ...), custom_call_target="tpu_custom_call" | custom-call | flops 3489660928 | bytes 16777216 | tf_op jit(solution)/shard_map/backward/pallas_call | solution.py:178
  90.4 0.7 reduce.2
  91.2 26.2 %all-to-all-done.1 = bf16[16,32,3328]{2,1,0:T(8,128)(2,1)S(1)} async-done(((bf16[16,32,3328]{2,1,0:T(8,128)(2,1)}), bf16[16,32,3328]{2,1,0:T(8,128)(2,1)S(1)}, u32[]{:S(2)}, u32[]{:S(2)}) %all-to-all-start.1) | async-done | bytes 3407904 | tf_op jit(solution)/shard_map/all_to_all | solution.py:259
  117.3 1.0 broadcast_in_dim.29
  118.3 10.3 %all-to-all-start.4 = ((f32[16,90,128]{2,1,0:T(8,128)}), f32[16,90,128]{2,1,0:T(8,128)}, u32[]{:S(2)}, u32[]{:S(2)}) async-start(f32[16,90,128]{2,1,0:T(8,128)} %broadcast_in_dim.29), calls=%async_computation.4 | async-start | bytes 1572864 | tf_op jit(solution)/shard_map/all_to_all | solution.py:259
  128.6 1.1 broadcast_in_dim.30
  129.7 10.7 %all-to-all-done.4 = f32[16,90,128]{2,1,0:T(8,128)} async-done(((f32[16,90,128]{2,1,0:T(8,128)}), f32[16,90,128]{2,1,0:T(8,128)}, u32[]{:S(2)}, u32[]{:S(2)}) %all-to-all-start.4) | async-done | bytes 737312 | tf_op jit(solution)/shard_map/all_to_all | solution.py:259
  140.4 0.8 broadcast_in_dim.31
  141.2 4.2 %all-to-all-start.5 = ((f32[16,64,128]{2,1,0:T(8,128)}), f32[16,64,128]{2,1,0:T(8,128)}, u32[]{:S(2)}, u32[]{:S(2)}) async-start(f32[16,64,128]{2,1,0:T(8,128)} %broadcast_in_dim.31), calls=%async_computation.5 | async-start | bytes 1048576 | tf_op jit(solution)/shard_map/all_to_all | solution.py:259
  145.5 0.0 copy-start.1
  145.5 0.3 collective-permute-start.1
  145.8 1.3 convert_reduce_fusion
  147.1 0.6 collective-permute-done.1
  147.7 0.0 copy-done.1
  147.7 0.9 add_convert_fusion
  148.6 12.8 %all-to-all-done.5 = f32[16,64,128]{2,1,0:T(8,128)} async-done(((f32[16,64,128]{2,1,0:T(8,128)}), f32[16,64,128]{2,1,0:T(8,128)}, u32[]{:S(2)}, u32[]{:S(2)}) %all-to-all-start.5) | async-done | bytes 524320 | tf_op jit(solution)/shard_map/all_to_all | solution.py:259
  161.4 4.1 %all-to-all-start.3 = ((bf16[8,32,1024]{2,1,0:T(8,128)(2,1)}), bf16[8,32,1024]{2,1,0:T(8,128)(2,1)S(1)}, u32[]{:S(2)}, u32[]{:S(2)}) async-start(bf16[8,32,1024]{2,1,0:T(8,128)(2,1)} %add_convert_fusion), calls=%async_computation.3 | async-start | bytes 1048576 | tf_op jit(solution)/shard_map/all_to_all | solution.py:259
  165.6 0.7 multiply_convert_fusion
  166.3 1.2 reduce_sum.51
  167.5 0.8 reshape.56.proj_ref
  168.3 3.2 %up_gradient.1 = f32[16,3328]{1,0:T(8,128)} custom-call(f32[512,16]{1,0:T(8,128)} %reshape.56.proj_ref, bf16[512,3328]{1,0:T(8,128)(2,1)} %all-gather.2.cloned.1.call-done.cot_ref, f32[1,3328]{1,0:T(1,128)} %div.9.factor_ref), custom_call_target="tpu_custom_call" | custom-call | flops 872415232 | bytes 4194304 | tf_op jit(solution)/shard_map/up_gradient/pallas_call | solution.py:222
  171.5 0.6 fusion
  172.1 1.1 reduce_sum.52
  173.2 0.8 reshape.57.low_ref
  174.1 2.3 %down_gradient.1 = f32[16,1024]{1,0:T(8,128)} custom-call(f32[512,16]{1,0:T(8,128)} %reshape.57.low_ref, bf16[512,1024]{1,0:T(8,128)(2,1)} %bitcast.15), custom_call_target="tpu_custom_call" | custom-call | flops 268435456 | bytes 1048576 | tf_op jit(solution)/shard_map/down_gradient/pallas_call | solution.py:247
  176.4 8.1 %all-to-all-done.3 = bf16[8,32,1024]{2,1,0:T(8,128)(2,1)S(1)} async-done(((bf16[8,32,1024]{2,1,0:T(8,128)(2,1)}), bf16[8,32,1024]{2,1,0:T(8,128)(2,1)S(1)}, u32[]{:S(2)}, u32[]{:S(2)}) %all-to-all-start.3) | async-done | bytes 524320 | tf_op jit(solution)/shard_map/all_to_all | solution.py:259
  184.5 0.7 reduce_sum.50
  (9 shorter events, 0.0 us)
Async XLA Ops:
  7.2 68.7 %all-gather.2.cloned.1.call-start = ((), (), s32[]{:S(2)}) async-start(), calls=%async_computation.6 | async-start | bytes 3620864 | tf_op jit(solution)/shard_map/all_gather | solution.py:271
  34.6 7.9 %copy-start.3 = (bf16[8,32,1024]{2,1,0:T(8,128)(2,1)}, bf16[8,32,1024]{2,1,0:T(8,128)(2,1)S(1)}, u32[]{:S(2)}) copy-start(bf16[8,32,1024]{2,1,0:T(8,128)(2,1)S(1)} %all_to_all.30.own_ref) | copy-start | bytes 1572868
  34.6 16.8 %collective-permute-start = (bf16[8,32,1024]{2,1,0:T(8,128)(2,1)S(1)}, bf16[8,32,1024]{2,1,0:T(8,128)(2,1)S(1)}, u32[]{:S(2)}, u32[]{:S(2)}) collective-permute-start(bf16[8,32,1024]{2,1,0:T(8,128)(2,1)S(1)} %all_to_all.30.own_ref), channel_id=1, source_target_pairs={{0,1},{1,0},{2,3},{3,2},{4,5},{5,4},{6,7},{7,6},{8,9},{9,8},{10,11... | collective-permute-start | bytes 1572872 | tf_op jit(solution)/shard_map/ppermute | solution.py:273
  43.9 21.2 %all-to-all-start.2 = ((f32[16,26,128]{2,1,0:T(8,128)}), f32[16,26,128]{2,1,0:T(8,128)S(1)}, u32[]{:S(2)}, u32[]{:S(2)}) async-start(f32[16,26,128]{2,1,0:T(8,128)} %broadcast_in_dim.28), calls=%async_computation.2 | async-start | bytes 524288 | tf_op jit(solution)/shard_map/all_to_all | solution.py:259
  51.3 0.8 copy-start.5
  65.2 0.7 copy-start.2
  65.2 8.9 %copy-start.4 = (f32[3328]{0:T(1024)S(1)}, f32[3328]{0:T(1024)}, u32[]{:S(2)}) copy-start(f32[3328]{0:T(1024)} %param.10) | copy-start | bytes 39940
  65.9 51.4 %all-to-all-start.1 = ((bf16[16,32,3328]{2,1,0:T(8,128)(2,1)}), bf16[16,32,3328]{2,1,0:T(8,128)(2,1)S(1)}, u32[]{:S(2)}, u32[]{:S(2)}) async-start(bf16[16,32,3328]{2,1,0:T(8,128)(2,1)} %get-tuple-element.15), calls=%async_computation.1 | async-start | bytes 6815744 | tf_op jit(solution)/shard_map/all_to_all | solution.py:259
  118.3 22.1 %all-to-all-start.4 = ((f32[16,90,128]{2,1,0:T(8,128)}), f32[16,90,128]{2,1,0:T(8,128)}, u32[]{:S(2)}, u32[]{:S(2)}) async-start(f32[16,90,128]{2,1,0:T(8,128)} %broadcast_in_dim.29), calls=%async_computation.4 | async-start | bytes 1572864 | tf_op jit(solution)/shard_map/all_to_all | solution.py:259
  141.2 20.2 %all-to-all-start.5 = ((f32[16,64,128]{2,1,0:T(8,128)}), f32[16,64,128]{2,1,0:T(8,128)}, u32[]{:S(2)}, u32[]{:S(2)}) async-start(f32[16,64,128]{2,1,0:T(8,128)} %broadcast_in_dim.31), calls=%async_computation.5 | async-start | bytes 1048576 | tf_op jit(solution)/shard_map/all_to_all | solution.py:259
  145.5 2.2 %copy-start.1 = (f32[8,32,1024]{2,1,0:T(8,128)S(1)}, f32[8,32,1024]{2,1,0:T(8,128)}, u32[]{:S(2)}) copy-start(f32[8,32,1024]{2,1,0:T(8,128)} %get-tuple-element.17) | copy-start | bytes 3145732
  145.5 2.2 %collective-permute-start.1 = (bf16[8,32,1024]{2,1,0:T(8,128)(2,1)}, bf16[8,32,1024]{2,1,0:T(8,128)(2,1)S(1)}, u32[]{:S(2)}, u32[]{:S(2)}) collective-permute-start(bf16[8,32,1024]{2,1,0:T(8,128)(2,1)} %get-tuple-element.18), channel_id=1, source_target_pairs={{0,1},{1,0},{2,3},{3,2},{4,5},{5,4},{6,7},{7,6},{8,9},{9,8},{10,11... | collective-permute-start | bytes 1572872 | tf_op jit(solution)/shard_map/ppermute | solution.py:284
  147.1 18.5 %copy-start = (f32[32,3328]{1,0:T(8,128)S(1)}, f32[32,3328]{1,0:T(8,128)}, u32[]{:S(2)}) copy-start(f32[32,3328]{1,0:T(8,128)} %convert_reduce_fusion) | copy-start | bytes 1277956
  161.4 23.1 %all-to-all-start.3 = ((bf16[8,32,1024]{2,1,0:T(8,128)(2,1)}), bf16[8,32,1024]{2,1,0:T(8,128)(2,1)S(1)}, u32[]{:S(2)}, u32[]{:S(2)}) async-start(bf16[8,32,1024]{2,1,0:T(8,128)(2,1)} %add_convert_fusion), calls=%async_computation.3 | async-start | bytes 1048576 | tf_op jit(solution)/shard_map/all_to_all | solution.py:259
Sparse Core Ops, SparseCore 0:
  10.5 58.6 all-gather.1

commit v2 on v0

v2 whole, which is shorter than its diff:
```python
import jax
import jax.numpy as jnp
from jax import lax
from jax.experimental import pallas as pl
from jax.experimental.pallas import tpu as pltpu
from jax.sharding import Mesh
from jax.sharding import PartitionSpec as P

adapter_scale = 2.0
epsilon = 1e-06
bf16 = jnp.bfloat16
f32 = jnp.float32
ROW = ("x", "y")
COL = ("z", "c")
CHUNK = 512
RANK = 16
MIB = 1024 * 1024
ANY = pl.BlockSpec(memory_space=pl.ANY)
VMEM = pl.BlockSpec(memory_space=pltpu.VMEM)
SMEM = pl.BlockSpec(memory_space=pltpu.SMEM)


def pieces(value):
    high = value.astype(bf16)
    rest = value - high.astype(f32)
    mid = rest.astype(bf16)
    low = (rest - mid.astype(f32)).astype(bf16)
    return high, mid, low


def dot(left, right, left_dim, right_dim):
    return lax.dot_general(
        left, right, (((left_dim,), (right_dim,)), ((), ())), preferred_element_type=f32
    )


def three(left, right, left_dim, right_dim):
    out = dot(jnp.concatenate(pieces(left), axis=0), right, left_dim, right_dim)
    return out[:RANK] + out[RANK : 2 * RANK] + out[2 * RANK :]


def chunks_of(width):
    return [(at, min(CHUNK, width - at)) for at in range(0, width, CHUNK)]


def call(body, flops, moved, limit, **options):
    return pl.pallas_call(
        body,
        compiler_params=pltpu.CompilerParams(vmem_limit_bytes=limit * MIB),
        cost_estimate=pl.CostEstimate(flops=flops, bytes_accessed=moved, transcendentals=0),
        **options,
    )


def merge_kernel(
    down_ref, up_ref, weight_hbm, merged_hbm, sums_ref, weight, merged, up_cat, totals, in_sem, out_sem
):
    depth, width = weight.shape
    rows, tile = 256, 256

    def fetch(j):
        part = pl.ds(j * rows, rows)
        return pltpu.make_async_copy(weight_hbm.at[part], weight.at[part], in_sem.at[j])

    def store(j):
        part = pl.ds(j * rows, rows)
        return pltpu.make_async_copy(merged.at[part], merged_hbm.at[part], out_sem.at[j])

    steps = range(depth // rows)
    for j in steps:
        fetch(j).start()
    totals[...] = jnp.zeros_like(totals)
    for at in range(0, width, tile):
        cols = slice(at, at + tile)
        u1, u2, u3 = pieces(up_ref[:, cols])
        up_cat[:, cols] = jnp.concatenate([u1, u2, u1, u3, u1, u2], axis=0)
    d1, d2, d3 = pieces(down_ref[...] * adapter_scale)
    down_cat = jnp.concatenate([d1, d1, d2, d1, d3, d2], axis=0)
    for j in steps:
        fetch(j).wait()
        part = slice(j * rows, (j + 1) * rows)
        for at in range(0, width, tile):
            cols = slice(at, at + tile)
            value = weight[part, cols].astype(f32) + dot(down_cat[:, part], up_cat[:, cols], 0, 0)
            merged[part, cols] = value.astype(bf16)
            totals[:, cols] += jnp.sum((value * value).reshape(rows // 8, 8, tile), axis=0)
        store(j).start()
    sums_ref[...] = jnp.sum(totals[...], axis=0, keepdims=True)
    for j in steps:
        store(j).wait()


def merge(down_t, up, weight):
    depth, width = weight.shape
    return call(
        merge_kernel,
        12 * depth * width,
        4 * depth * width,
        20,
        in_specs=[VMEM, VMEM, ANY],
        out_specs=[ANY, VMEM],
        out_shape=[
            jax.ShapeDtypeStruct((depth, width), bf16),
            jax.ShapeDtypeStruct((1, width), f32),
        ],
        scratch_shapes=[
            pltpu.VMEM((depth, width), bf16),
            pltpu.VMEM((depth, width), bf16),
            pltpu.VMEM((6 * RANK, width), bf16),
            pltpu.VMEM((8, width), f32),
            pltpu.SemaphoreType.DMA((4,)),
            pltpu.SemaphoreType.DMA((4,)),
        ],
        name="merge",
    )(down_t, up, weight)


def forward_kernel(
    core_ref, own_ref, other_ref, down_ref, sums_ref, merged_hbm,
    part_hbm, tokens_ref, small_ref, merged, part, in_sem, out_sem,
):
    core = core_ref[0]
    depth, width = merged.shape
    chunks = chunks_of(width)

    def fetch(j):
        cols = pl.ds(*chunks[j])
        return pltpu.make_async_copy(merged_hbm.at[:, cols], merged.at[:, cols], in_sem.at[j])

    def store(j):
        cols = pl.ds(*chunks[j])
        return pltpu.make_async_copy(part.at[:, :, cols], part_hbm.at[:, :, cols], out_sem.at[j])

    for j in range(len(chunks)):
        fetch(j).start()
    for z in range(8):
        tokens_ref[2 * z + core] = own_ref[z]
        tokens_ref[2 * z + 1 - core] = other_ref[z]
    tokens = tokens_ref[...].reshape(512, depth)
    small_ref[:RANK, :] = three(down_ref[...], tokens, 1, 1)
    small_ref[RANK:, :] = jnp.zeros((8, CHUNK), f32)
    for j, (at, size) in enumerate(chunks):
        small_ref[RANK + j : RANK + j + 1, :size] = sums_ref[:, at : at + size]
    for j, (at, size) in enumerate(chunks):
        fetch(j).wait()
        cols = slice(at, at + size)
        part[:, :, cols] = dot(tokens, merged[:, cols], 1, 0).astype(bf16).reshape(16, 32, size)
        store(j).start()
    for j in range(len(chunks)):
        store(j).wait()


def forward(core, own, other, down_t, sums, merged_low):
    depth, width = merged_low.shape
    count = len(chunks_of(width))
    return call(
        forward_kernel,
        2 * 512 * depth * width,
        12 * MIB,
        24,
        in_specs=[SMEM, VMEM, VMEM, VMEM, VMEM, ANY],
        out_specs=[ANY, VMEM, VMEM],
        out_shape=[
            jax.ShapeDtypeStruct((16, 32, width), bf16),
            jax.ShapeDtypeStruct((16, 32, depth), bf16),
            jax.ShapeDtypeStruct((RANK + 8, CHUNK), f32),
        ],
        scratch_shapes=[
            pltpu.VMEM((depth, width), bf16),
            pltpu.VMEM((16, 32, width), bf16),
            pltpu.SemaphoreType.DMA((count,)),
            pltpu.SemaphoreType.DMA((count,)),
        ],
        name="forward",
    )(core, own, other, down_t, sums, merged_low)


def pack(low, high_ref):
    high = low.astype(bf16)
    rest = (low - high.astype(f32)).astype(bf16)
    high_ref[:, :CHUNK] = high
    high_ref[:, CHUNK:] = rest
    return high.astype(f32) + rest.astype(f32)


def backward_kernel(
    core_ref, small_ref, magnitude_ref, up_ref, cot_hbm, part_hbm, merged_hbm,
    own_ref, send_ref, low_ref, mag_ref, factor_ref, cot, part, merged, total, sem,
):
    core = core_ref[0]
    width = merged.shape[1]
    chunks = chunks_of(width)

    def fetch(j):
        cols = pl.ds(*chunks[j])
        pairs = ((cot_hbm, cot), (merged_hbm, merged), (part_hbm, part))
        return [
            pltpu.make_async_copy(source.at[:, cols], target.at[:, cols], sem.at[i, j])
            for i, (source, target) in enumerate(pairs)
        ]

    for j in range(len(chunks)):
        for copy in fetch(j):
            copy.start()
    low = jnp.zeros((RANK, CHUNK), f32)
    for j, (at, size) in enumerate(chunks):
        for copy in fetch(j):
            copy.wait()
        cols = slice(at, at + size)
        norm = jnp.sqrt(small_ref[RANK + j : RANK + j + 1, :size] + epsilon)
        factor = magnitude_ref[:, cols] / norm
        factor_ref[:, cols] = factor
        given = cot[:, cols].astype(f32)
        mag_ref[:, cols] = jnp.sum(given * part[:, cols].astype(f32), axis=0, keepdims=True) / norm
        grad = (given * factor).astype(bf16)
        product = dot(grad, merged[:, cols], 1, 1)
        if j == 0:
            total[...] = product
        else:
            total[...] += product
        low += three(up_ref[:, cols], grad, 1, 1)
    low_ref[...] = pack(low, send_ref.at[256:272, :])
    for z in range(8):
        own = pl.ds(pl.multiple_of((2 * z + core) * 32, 32), 32)
        other = pl.ds(pl.multiple_of((2 * z + 1 - core) * 32, 32), 32)
        own_ref[32 * z : 32 * z + 32, :] = total[own, :]
        send_ref[32 * z : 32 * z + 32, :] = total[other, :].astype(bf16)


def backward(core, small, magnitude, up, cot, part, merged_low):
    depth, width = merged_low.shape
    count = len(chunks_of(width))
    return call(
        backward_kernel,
        2 * 512 * depth * width,
        16 * MIB,
        32,
        in_specs=[SMEM, VMEM, VMEM, VMEM, ANY, ANY, ANY],
        out_specs=[VMEM] * 5,
        out_shape=[
            jax.ShapeDtypeStruct((256, depth), f32),
            jax.ShapeDtypeStruct((272, depth), bf16),
            jax.ShapeDtypeStruct((RANK, CHUNK), f32),
            jax.ShapeDtypeStruct((1, width), f32),
            jax.ShapeDtypeStruct((1, width), f32),
        ],
        scratch_shapes=[
            pltpu.VMEM((512, width), bf16),
            pltpu.VMEM((512, width), bf16),
            pltpu.VMEM((depth, width), bf16),
            pltpu.VMEM((512, depth), f32),
            pltpu.SemaphoreType.DMA((3, count)),
        ],
        name="backward",
    )(core, small, magnitude, up, cot, part, merged_low)


def fold_kernel(bit_ref, keep_ref, low_ref, got_ref, keep_out, low_out, send_out):
    bit = bit_ref[0]
    rows = keep_ref.shape[0]
    for i in range(rows // 64):
        kept = pl.ds(pl.multiple_of((2 * i + bit) * 32, 32), 32)
        sent = pl.ds(pl.multiple_of((2 * i + 1 - bit) * 32, 32), 32)
        at = slice(32 * i, 32 * i + 32)
        keep_out[at, :] = keep_ref[kept, :] + got_ref[kept, :].astype(f32)
        send_out[at, :] = (keep_ref[sent, :] + got_ref[sent, :].astype(f32)).astype(bf16)
    got = got_ref[rows : rows + RANK, :].astype(f32)
    low = low_ref[...] + (got[:, :CHUNK] + got[:, CHUNK:])
    low_out[...] = pack(low, send_out.at[rows // 2 : rows // 2 + RANK, :])


def fold(bit, keep, low, got):
    rows, depth = keep.shape
    return call(
        fold_kernel,
        4 * rows * depth,
        12 * rows * depth,
        16,
        in_specs=[SMEM, VMEM, VMEM, VMEM],
        out_specs=[VMEM] * 3,
        out_shape=[
            jax.ShapeDtypeStruct((rows // 2, depth), f32),
            jax.ShapeDtypeStruct((RANK, CHUNK), f32),
            jax.ShapeDtypeStruct((rows // 2 + RANK, depth), bf16),
        ],
        name="fold",
    )(bit, keep, low, got)


def finish_kernel(keep_ref, low_ref, got_ref, tokens_ref, grad_ref, down_ref):
    grad_ref[...] = (keep_ref[...] + got_ref[:32, :].astype(f32)).astype(bf16)
    got = got_ref[32 : 32 + RANK, :].astype(f32)
    low = low_ref[...] + (got[:, :CHUNK] + got[:, CHUNK:])
    down_ref[...] = three(low * adapter_scale, tokens_ref[...], 1, 0)


def finish(keep, low, got, tokens):
    depth = tokens.shape[1]
    return call(
        finish_kernel,
        2 * 512 * 256 * depth,
        2 * MIB,
        16,
        in_specs=[VMEM] * 4,
        out_specs=[VMEM] * 2,
        out_shape=[
            jax.ShapeDtypeStruct((32, depth), bf16),
            jax.ShapeDtypeStruct((RANK, depth), f32),
        ],
        name="finish",
    )(keep, low, got, tokens)


def up_kernel(small_ref, cot_ref, factor_ref, out_ref):
    grad = (cot_ref[...].astype(f32) * factor_ref[...]).astype(bf16)
    out_ref[...] = three(small_ref[:RANK, :] * adapter_scale, grad, 1, 0)


def up_gradient_of(small, cot, factor):
    tokens, width = cot.shape
    tile = width // 2
    return call(
        up_kernel,
        2 * 512 * 256 * width,
        4 * MIB,
        16,
        grid=(2,),
        in_specs=[
            pl.BlockSpec((RANK + 8, CHUNK), lambda i: (0, 0)),
            pl.BlockSpec((tokens, tile), lambda i: (0, i)),
            pl.BlockSpec((1, tile), lambda i: (0, i)),
        ],
        out_specs=pl.BlockSpec((RANK, tile), lambda i: (0, i)),
        out_shape=jax.ShapeDtypeStruct((RANK, width), f32),
        name="up_gradient",
    )(small, cot, factor)


def exchange(blocks, axis):
    return lax.all_to_all(blocks, axis, 0, 0, tiled=False)


def around(value, axis):
    one, two, other = [
        lax.ppermute(value, axis, [(i, (i + k) % 4) for i in range(4)]) for k in (1, 2, 3)
    ]
    return (value + two) + (one + other)


def add_row(value):
    return around(around(value, "x"), "y")


def on_device(tokens, weight, down_adapter, up_adapter, magnitude, out_cotangent):
    core = lax.axis_index("c").astype(jnp.int32).reshape(1)
    z = lax.axis_index("z").astype(jnp.int32)
    swap = [(0, 1), (1, 0)]
    down_t = down_adapter.T
    cot_full = lax.all_gather(out_cotangent, ROW, axis=0, tiled=True)
    own_tokens = exchange(jnp.broadcast_to(tokens[None], (8,) + tokens.shape), "z")
    merged_low, sums = merge(down_t, up_adapter, weight)
    own_tokens, merged_low, sums = lax.optimization_barrier((own_tokens, merged_low, sums))
    other_tokens = lax.ppermute(own_tokens, "c", swap)
    part, tokens_full, small = forward(core, own_tokens, other_tokens, down_t, sums, merged_low)
    out_parts = exchange(part, ROW)
    small = add_row(small)
    keep, send, low, magnitude_part, factor = backward(
        core, small, magnitude.reshape(1, -1), up_adapter, cot_full, part.reshape(512, -1), merged_low
    )
    got = lax.ppermute(send, "c", swap)
    for k in range(3):
        keep, low, send = fold(((z >> k) & 1).reshape(1), keep, low, got)
        got = lax.ppermute(send, "z", [(i, i ^ (1 << k)) for i in range(8)])
    grad_tokens, down_gradient = finish(keep, low, got, tokens_full.reshape(512, -1))
    grad_magnitude = add_row(magnitude_part).reshape(-1)
    up_gradient = up_gradient_of(small, cot_full, factor)
    output = (jnp.sum(out_parts.astype(f32), axis=0) * factor).astype(bf16)
    return (output, grad_tokens, grad_magnitude, up_gradient, down_gradient.T)


def solution(mesh):
    split = Mesh(mesh.devices.reshape(4, 4, 8, 2), ROW + COL)
    return jax.shard_map(
        on_device,
        mesh=split,
        in_specs=(P(COL, ROW), P(ROW, COL), P(ROW, None), P(None, COL), P(COL), P(ROW, COL)),
        out_specs=(P(ROW, COL), P(COL, ROW), P(COL), P(None, COL), P(ROW, None)),
        check_vma=False,
    )
```

time: 406 us -> 189 us (0.47)
  blocking collectives: 184 us -> 0 us
  waiting for transfers between devices: 145 us -> 83.4 us
  matrix products: 46.4 us -> 0 us
  starting transfers between devices: 0.34 us -> 40.9 us
  Pallas kernels: 0 us -> 23.5 us
  local copies, waits for them, and re-layouts: 9.22 us -> 20.2 us
    psum x3 -> x0, blocking collectives: 184 us -> none  [the longest x1 69.4 us: on_device(): norm_squares = lax.psum(square_sums, 'row')]
    reduce_scatter x2 -> x0, waiting for transfers between devices: 89.9 us -> none  [the longest x1 89.9 us: on_device(): lax.psum_scatter(jnp.dot(part_rows, merged_low, preferred_element_type=jn...]
    ppermute x0 -> x17, waiting for transfers between devices: none -> 77.8 us  [the longest x12 60.2 us: around(): lax.ppermute(value, axis, [(i, (i + k) % 4) for i in range(4)])]
    all_gather x2 -> x1, waiting for transfers between devices: 54.1 us -> 0.02 us  [on_device(): cot_full = lax.all_gather(out_cotangent, ROW, axis=0, tiled=True)]
    dot_general x7 -> x0, matrix products: 46.4 us -> none  [the longest x1 16.2 us: on_device(): jnp.dot(down_adapter, up_adapter, precision=highest)]
    ppermute x0 -> x17, starting transfers between devices: none -> 24.9 us  [the longest x12 19 us: around(): lax.ppermute(value, axis, [(i, (i + k) % 4) for i in range(4)])]
    pallas_call x0 -> x8, Pallas kernels: none -> 23.5 us  [the longest x1 7.34 us: backward(): call(backward_kernel, 2 * 512 * depth * width, 16 * MIB, 32, in_specs=[SM...]
    all_to_all x0 -> x2, starting transfers between devices: none -> 16 us  [exchange(): return lax.all_to_all(blocks, axis, 0, 0, tiled=False)]
  transfers between devices with their start and end apart: 4 -> 20, of which waited for: 2 -> 9; matrix products, arithmetic and copies ran while one was open for 7% -> 4% of each run, Pallas kernels for 0% -> 12%
where the time goes in v2:
time: 189 us
  waiting for transfers between devices  83.4 us (44%)
  starting transfers between devices  40.9 us (22%)
  Pallas kernels  23.5 us (12%)
  local copies, waits for them, and re-layouts  20.2 us (11%)
  between operations  14.2 us (8%)
  other arithmetic  6.6 us (3%)
    ppermute x12, waiting for transfers between devices, around(): lax.ppermute(value, axis, [(i, (i + k) % 4) for i in range(4)])  60.2 us
    ppermute x12, starting transfers between devices, around(): lax.ppermute(value, axis, [(i, (i + k) % 4) for i in range(4)])  19 us
    unnamed x30, local copies, waits for them, and re-layouts  18.5 us
    all_to_all x2, starting transfers between devices, exchange(): return lax.all_to_all(blocks, axis, 0, 0, tiled=False)  16 us
    ppermute x3, waiting for transfers between devices, on_device(): got = lax.ppermute(send, 'z', [(i, i ^ 1 << k) for i in range(8)])  15.7 us
    pallas_call x1, Pallas kernels, backward(): call(backward_kernel, 2 * 512 * depth * width, 16 * MIB, 32, in_specs=[SM...  7.34 us
    pallas_call x1, Pallas kernels, forward(): call(forward_kernel, 2 * 512 * depth * width, 12 * MIB, 24, in_specs=[SME...  7.01 us
    ppermute x3, starting transfers between devices, on_device(): got = lax.ppermute(send, 'z', [(i, i ^ 1 << k) for i in range(8)])  5.83 us
  transfers between devices with their start and end apart: 20, of which 9 were waited for; matrix products, arithmetic and copies ran while one was open for 4% of the time, Pallas kernels for 12%

profile of v2, /device:TPU:8, one launch (start us, length us, event | category | flops | bytes accessed | tf_op | source)
XLA Modules:
  0.0 188.8 jit_solution(16965421095751879385)
XLA Ops:
  7.2 0.0 all-gather.2.cloned.1.call-start
  7.2 0.7 all-gather.2.cloned.1.call-update
  7.9 1.7 broadcast_in_dim.2
  9.6 8.5 %all-to-all-start = ((bf16[8,32,1024]{2,1,0:T(8,128)(2,1)}), bf16[8,32,1024]{2,1,0:T(8,128)(2,1)S(1)}, u32[]{:S(2)}, u32[]{:S(2)}) async-start(bf16[8,32,1024]{2,1,0:T(8,128)(2,1)} %broadcast_in_dim.2), calls=%async_computation | async-start | bytes 1048576 | tf_op jit(solution)/shard_map/all_to_all | solution.py:340
  18.1 2.9 %copy-done.2 = bf16[1024,3328]{1,0:T(8,128)(2,1)S(1)} copy-done((bf16[1024,3328]{1,0:T(8,128)(2,1)S(1)}, bf16[1024,3328]{1,0:T(8,128)(2,1)}, u32[]{:S(2)}) %copy-start.2) | copy-done | bytes 6815768
  21.0 0.9 copy-done.10
  21.9 0.8 copy-done.12
  22.8 5.1 %merge.1 = (bf16[1024,3328]{1,0:T(8,128)(2,1)S(1)}, f32[1,3328]{1,0:T(1,128)S(1)}) custom-call(f32[16,1024]{1,0:T(8,128)S(1)} %bitcast.9, f32[16,3328]{1,0:T(8,128)S(1)} %copy-done.10, bf16[1024,3328]{1,0:T(8,128)(2,1)S(1)} %copy-done.2), custom_call_target="tpu_custom_call" | custom-call | flops 40894464 | bytes 13631488 | tf_op jit(solution)/shard_map/merge/pallas_call | solution.py:95
  27.9 2.8 %copy-done.3 = bf16[1024,3328]{1,0:T(8,128)(2,1)} copy-done((bf16[1024,3328]{1,0:T(8,128)(2,1)}, bf16[1024,3328]{1,0:T(8,128)(2,1)S(1)}, u32[]{:S(2)}) %copy-start.3) | copy-done | bytes 6815768
  30.6 4.9 %all-to-all-done.own_ref = bf16[8,32,1024]{2,1,0:T(8,128)(2,1)S(1)} async-done(((bf16[8,32,1024]{2,1,0:T(8,128)(2,1)}), bf16[8,32,1024]{2,1,0:T(8,128)(2,1)S(1)}, u32[]{:S(2)}, u32[]{:S(2)}) %all-to-all-start) | async-done | bytes 524320 | tf_op jit(solution)/shard_map/all_to_all | solution.py:340
  35.6 1.9 %collective-permute-done.other_ref = bf16[8,32,1024]{2,1,0:T(8,128)(2,1)S(1)} collective-permute-done((bf16[8,32,1024]{2,1,0:T(8,128)(2,1)S(1)}, bf16[8,32,1024]{2,1,0:T(8,128)(2,1)S(1)}, u32[]{:S(2)}, u32[]{:S(2)}) %collective-permute-start) | collective-permute-done | bytes 524320 | tf_op jit(solution)/shard_map/ppermute | solution.py:363
  37.5 2.9 %copy-done.4 = bf16[1024,3328]{1,0:T(8,128)(2,1)S(1)} copy-done((bf16[1024,3328]{1,0:T(8,128)(2,1)S(1)}, bf16[1024,3328]{1,0:T(8,128)(2,1)}, u32[]{:S(2)}) %copy-start.4) | copy-done | bytes 6815768
  40.4 7.0 %forward.1 = (bf16[16,32,3328]{2,1,0:T(8,128)(2,1)}, bf16[16,32,1024]{2,1,0:T(8,128)(2,1)S(1)}, f32[24,512]{1,0:T(8,128)S(1)}) custom-call(s32[1]{0:T(128)} %bitcast.core_ref, bf16[8,32,1024]{2,1,0:T(8,128)(2,1)S(1)} %all-to-all-done.own_ref, bf16[8,32,1024]{2,1,0:T(8,128)(2,1)S(1)} %collective-permute-done.other_ref, f32[16,1024]{1,0:T(8,128)S(1)} %bitcast.10, ...), custom_call_target="tpu_custom_call" | custom-call | flops 3489660928 | bytes 12582912 | tf_op jit(solution)/shard_map/forward/pallas_call | solution.py:156
  47.4 1.0 copy-done.6
  48.4 7.5 %all-to-all-start.1 = ((bf16[16,32,3328]{2,1,0:T(8,128)(2,1)}), bf16[16,32,3328]{2,1,0:T(8,128)(2,1)}, u32[]{:S(2)}, u32[]{:S(2)}) async-start(bf16[16,32,3328]{2,1,0:T(8,128)(2,1)} %get-tuple-element.34), calls=%async_computation.1 | async-start | bytes 6815744 | tf_op jit(solution)/shard_map/all_to_all | solution.py:340
  55.9 3.0 %collective-permute-start.1 = (f32[24,512]{1,0:T(8,128)S(1)}, f32[24,512]{1,0:T(8,128)S(1)}, u32[]{:S(2)}, u32[]{:S(2)}) collective-permute-start(f32[24,512]{1,0:T(8,128)S(1)} %get-tuple-element.35), channel_id=1, source_target_pairs={{0,128},{64,192},{128,0},{192,64},{1,129},{65,193},{129,1},{193,65... | collective-permute-start | bytes 147464 | tf_op jit(solution)/shard_map/ppermute | solution.py:345
  58.9 0.6 collective-permute-start.2
  59.5 2.7 %collective-permute-start.3 = (f32[24,512]{1,0:T(8,128)S(1)}, f32[24,512]{1,0:T(8,128)S(1)}, u32[]{:S(2)}, u32[]{:S(2)}) collective-permute-start(f32[24,512]{1,0:T(8,128)S(1)} %get-tuple-element.35), channel_id=1, source_target_pairs={{0,192},{64,0},{128,64},{192,128},{1,193},{65,1},{129,65},{193,129... | collective-permute-start | bytes 147464 | tf_op jit(solution)/shard_map/ppermute | solution.py:345
  62.2 55.3 %collective-permute-done.1 = f32[24,512]{1,0:T(8,128)S(1)} collective-permute-done((f32[24,512]{1,0:T(8,128)S(1)}, f32[24,512]{1,0:T(8,128)S(1)}, u32[]{:S(2)}, u32[]{:S(2)}) %collective-permute-start.1) | collective-permute-done | bytes 49184 | tf_op jit(solution)/shard_map/ppermute | solution.py:345
  117.5 0.8 collective-permute-done.2
  118.3 0.1 collective-permute-start.4
  118.4 0.1 collective-permute-start.5
  118.5 2.0 %collective-permute-start.6 = (f32[24,512]{1,0:T(8,128)S(1)}, f32[24,512]{1,0:T(8,128)S(1)}, u32[]{:S(2)}, u32[]{:S(2)}) collective-permute-start(f32[24,512]{1,0:T(8,128)S(1)} %add_add_fusion.1), channel_id=1, source_target_pairs={{0,48},{16,0},{32,16},{48,32},{1,49},{17,1},{33,17},{49,33},{2,50}... | collective-permute-start | bytes 147464 | tf_op jit(solution)/shard_map/ppermute | solution.py:345
  120.5 3.7 %collective-permute-done.4 = f32[24,512]{1,0:T(8,128)S(1)} collective-permute-done((f32[24,512]{1,0:T(8,128)S(1)}, f32[24,512]{1,0:T(8,128)S(1)}, u32[]{:S(2)}, u32[]{:S(2)}) %collective-permute-start.4) | collective-permute-done | bytes 49184 | tf_op jit(solution)/shard_map/ppermute | solution.py:345
  124.2 0.4 collective-permute-done.6
  124.7 2.0 %copy-done = bf16[512,3328]{1,0:T(8,128)(2,1)S(1)} copy-done((bf16[512,3328]{1,0:T(8,128)(2,1)S(1)}, bf16[512,3328]{1,0:T(8,128)(2,1)}, u32[]{:S(2)}) %copy-start) | copy-done | bytes 3407896
  126.6 2.9 %copy-done.5 = bf16[1024,3328]{1,0:T(8,128)(2,1)S(1)} copy-done((bf16[1024,3328]{1,0:T(8,128)(2,1)S(1)}, bf16[1024,3328]{1,0:T(8,128)(2,1)}, u32[]{:S(2)}) %copy-start.5) | copy-done | bytes 6815768
  129.6 7.3 %backward.1 = (f32[256,1024]{1,0:T(8,128)S(1)}, bf16[272,1024]{1,0:T(8,128)(2,1)}, f32[16,512]{1,0:T(8,128)S(1)}, f32[1,3328]{1,0:T(1,128)S(1)}, f32[1,3328]{1,0:T(1,128)S(1)}) custom-call(s32[1]{0:T(128)} %bitcast.core_ref, f32[24,512]{1,0:T(8,128)S(1)} %add_add_fusion.small_ref, f32[1,3328]{1,0:T(1,128)S(1)} %reshape.36.magnitude_ref, ...), custom_call_target="tpu_custom_call" | custom-call | flops 3489660928 | bytes 16777216 | tf_op jit(solution)/shard_map/backward/pallas_call | solution.py:233
  136.9 1.0 copy-done.8
  137.9 3.4 %convert_reduce_fusion = f32[32,3328]{1,0:T(8,128)} fusion(bf16[16,32,3328]{2,1,0:T(8,128)(2,1)} %all-to-all-done.1), kind=kLoop, calls=%fused_computation | loop fusion | flops 3301376 | bytes 3833856 | tf_op jit(solution)/shard_map/reduce_sum | solution.py:377
  141.3 3.4 %collective-permute-start.11 = (f32[1,3328]{1,0:T(1,128)S(1)}, f32[1,3328]{1,0:T(1,128)S(1)}, u32[]{:S(2)}, u32[]{:S(2)}) collective-permute-start(f32[1,3328]{1,0:T(1,128)S(1)} %get-tuple-element.51), channel_id=1, source_target_pairs={{0,128},{64,192},{128,0},{192,64},{1,129},{65,193},{129,1},{193,65... | collective-permute-start | bytes 39944 | tf_op jit(solution)/shard_map/ppermute | solution.py:345
  144.7 3.2 %collective-permute-start.13 = (f32[1,3328]{1,0:T(1,128)S(1)}, f32[1,3328]{1,0:T(1,128)}, u32[]{:S(2)}, u32[]{:S(2)}) collective-permute-start(f32[1,3328]{1,0:T(1,128)S(1)} %get-tuple-element.51), channel_id=1, source_target_pairs={{0,192},{64,0},{128,64},{192,128},{1,193},{65,1},{129,65},{193,129... | collective-permute-start | bytes 39944 | tf_op jit(solution)/shard_map/ppermute | solution.py:345
  147.9 1.2 copy-done.9
  149.2 1.2 fold.3
  150.4 5.1 %collective-permute-start.8 = (bf16[144,1024]{1,0:T(8,128)(2,1)S(1)}, bf16[144,1024]{1,0:T(8,128)(2,1)S(1)}, u32[]{:S(2)}, u32[]{:S(2)}) collective-permute-start(bf16[144,1024]{1,0:T(8,128)(2,1)S(1)} %get-tuple-element.42), channel_id=1, source_target_pairs={{0,2},{2,0},{4,6},{6,4},{8,10},{10,8},{12,14},{14,12},{1,3},{3,1},... | collective-permute-start | bytes 884744 | tf_op jit(solution)/shard_map/ppermute | solution.py:373
  155.5 1.7 multiply_convert_fusion
  157.2 5.1 %collective-permute-done.8.got_ref = bf16[144,1024]{1,0:T(8,128)(2,1)S(1)} collective-permute-done((bf16[144,1024]{1,0:T(8,128)(2,1)S(1)}, bf16[144,1024]{1,0:T(8,128)(2,1)S(1)}, u32[]{:S(2)}, u32[]{:S(2)}) %collective-permute-start.8) | collective-permute-done | bytes 294944 | tf_op jit(solution)/shard_map/ppermute | solution.py:373
  162.4 0.1 fold.4
  162.4 0.1 collective-permute-start.9
  162.5 0.8 add_add_fusion.2
  163.3 2.0 %collective-permute-start.14 = (f32[1,3328]{1,0:T(1,128)S(1)}, f32[1,3328]{1,0:T(1,128)S(1)}, u32[]{:S(2)}, u32[]{:S(2)}) collective-permute-start(f32[1,3328]{1,0:T(1,128)S(1)} %add_add_fusion.2), channel_id=1, source_target_pairs={{0,32},{16,48},{32,0},{48,16},{1,33},{17,49},{33,1},{49,17},{2,34}... | collective-permute-start | bytes 39944 | tf_op jit(solution)/shard_map/ppermute | solution.py:345
  165.3 2.0 %collective-permute-start.16 = (f32[1,3328]{1,0:T(1,128)S(1)}, f32[1,3328]{1,0:T(1,128)S(1)}, u32[]{:S(2)}, u32[]{:S(2)}) collective-permute-start(f32[1,3328]{1,0:T(1,128)S(1)} %add_add_fusion.2), channel_id=1, source_target_pairs={{0,48},{16,0},{32,16},{48,32},{1,49},{17,1},{33,17},{49,33},{2,50}... | collective-permute-start | bytes 39944 | tf_op jit(solution)/shard_map/ppermute | solution.py:345
  167.3 1.8 up_gradient.1
  169.2 3.0 %collective-permute-done.9.got_ref = bf16[80,1024]{1,0:T(8,128)(2,1)S(1)} collective-permute-done((bf16[80,1024]{1,0:T(8,128)(2,1)S(1)}, bf16[80,1024]{1,0:T(8,128)(2,1)S(1)}, u32[]{:S(2)}, u32[]{:S(2)}) %collective-permute-start.9) | collective-permute-done | bytes 163872 | tf_op jit(solution)/shard_map/ppermute | solution.py:373
  172.2 0.6 collective-permute-start.10
  172.9 0.7 add_reduce_fusion
  173.5 7.5 %collective-permute-done.10.got_ref = bf16[48,1024]{1,0:T(8,128)(2,1)S(1)} collective-permute-done((bf16[48,1024]{1,0:T(8,128)(2,1)S(1)}, bf16[48,1024]{1,0:T(8,128)(2,1)S(1)}, u32[]{:S(2)}, u32[]{:S(2)}) %collective-permute-start.10) | collective-permute-done | bytes 98336 | tf_op jit(solution)/shard_map/ppermute | solution.py:373
  181.0 0.9 finish.1
  (40 shorter events, 0.2 us)
Async XLA Ops:
  7.2 117.5 %all-gather.2.cloned.1.call-start = ((), (), s32[]{:S(2)}) async-start(), calls=%async_computation.2 | async-start | bytes 3620864 | tf_op jit(solution)/shard_map/all_gather | solution.py:359
  9.6 26.0 %all-to-all-start = ((bf16[8,32,1024]{2,1,0:T(8,128)(2,1)}), bf16[8,32,1024]{2,1,0:T(8,128)(2,1)S(1)}, u32[]{:S(2)}, u32[]{:S(2)}) async-start(bf16[8,32,1024]{2,1,0:T(8,128)(2,1)} %broadcast_in_dim.2), calls=%async_computation | async-start | bytes 1048576 | tf_op jit(solution)/shard_map/all_to_all | solution.py:340
  18.1 2.9 %copy-start.2 = (bf16[1024,3328]{1,0:T(8,128)(2,1)S(1)}, bf16[1024,3328]{1,0:T(8,128)(2,1)}, u32[]{:S(2)}) copy-start(bf16[1024,3328]{1,0:T(8,128)(2,1)} %weight_hbm.1) | copy-start | bytes 20447236
  21.0 0.9 copy-start.10
  21.9 0.8 copy-start.12
  22.8 14.7 %copy-start.13 = (f32[1024,16]{0,1:T(8,128)S(1)}, f32[1024,16]{0,1:T(8,128)}, u32[]{:S(2)}) copy-start(f32[1024,16]{0,1:T(8,128)} %param.8) | copy-start | bytes 196612
  27.9 2.8 %copy-start.3 = (bf16[1024,3328]{1,0:T(8,128)(2,1)}, bf16[1024,3328]{1,0:T(8,128)(2,1)S(1)}, u32[]{:S(2)}) copy-start(bf16[1024,3328]{1,0:T(8,128)(2,1)S(1)} %get-tuple-element.33.merged_hbm) | copy-start | bytes 20447236
  35.6 1.9 %collective-permute-start = (bf16[8,32,1024]{2,1,0:T(8,128)(2,1)S(1)}, bf16[8,32,1024]{2,1,0:T(8,128)(2,1)S(1)}, u32[]{:S(2)}, u32[]{:S(2)}) collective-permute-start(bf16[8,32,1024]{2,1,0:T(8,128)(2,1)S(1)} %all-to-all-done.own_ref), channel_id=1, source_target_pairs={{0,1},{1,0},{2,3},{3,2},{4,5},{5,4},{6,7},{7,6},{8,9},{9,8},{10,11... | collective-permute-start | bytes 1572872 | tf_op jit(solution)/shard_map/ppermute | solution.py:363
  37.5 2.9 %copy-start.4 = (bf16[1024,3328]{1,0:T(8,128)(2,1)S(1)}, bf16[1024,3328]{1,0:T(8,128)(2,1)}, u32[]{:S(2)}) copy-start(bf16[1024,3328]{1,0:T(8,128)(2,1)} %copy-done.3) | copy-start | bytes 20447236
  47.4 1.0 copy-start.6
  48.4 72.1 %copy-start.14 = (f32[3328]{0:T(1024)S(1)}, f32[3328]{0:T(1024)}, u32[]{:S(2)}) copy-start(f32[3328]{0:T(1024)} %param.10) | copy-start | bytes 39940
  48.4 76.2 %copy-start.11 = (f32[16,3328]{1,0:T(8,128)S(1)}, f32[16,3328]{1,0:T(8,128)}, u32[]{:S(2)}) copy-start(f32[16,3328]{1,0:T(8,128)} %up_ref.3) | copy-start | bytes 638980
  48.4 89.5 %all-to-all-start.1 = ((bf16[16,32,3328]{2,1,0:T(8,128)(2,1)}), bf16[16,32,3328]{2,1,0:T(8,128)(2,1)}, u32[]{:S(2)}, u32[]{:S(2)}) async-start(bf16[16,32,3328]{2,1,0:T(8,128)(2,1)} %get-tuple-element.34), calls=%async_computation.1 | async-start | bytes 6815744 | tf_op jit(solution)/shard_map/all_to_all | solution.py:340
  55.9 61.5 %collective-permute-start.1 = (f32[24,512]{1,0:T(8,128)S(1)}, f32[24,512]{1,0:T(8,128)S(1)}, u32[]{:S(2)}, u32[]{:S(2)}) collective-permute-start(f32[24,512]{1,0:T(8,128)S(1)} %get-tuple-element.35), channel_id=1, source_target_pairs={{0,128},{64,192},{128,0},{192,64},{1,129},{65,193},{129,1},{193,65... | collective-permute-start | bytes 147464 | tf_op jit(solution)/shard_map/ppermute | solution.py:345
  58.9 59.3 %collective-permute-start.2 = (f32[24,512]{1,0:T(8,128)S(1)}, f32[24,512]{1,0:T(8,128)S(1)}, u32[]{:S(2)}, u32[]{:S(2)}) collective-permute-start(f32[24,512]{1,0:T(8,128)S(1)} %get-tuple-element.35), channel_id=1, source_target_pairs={{0,64},{64,128},{128,192},{192,0},{1,65},{65,129},{129,193},{193,1... | collective-permute-start | bytes 147464 | tf_op jit(solution)/shard_map/ppermute | solution.py:345
  59.5 58.8 %collective-permute-start.3 = (f32[24,512]{1,0:T(8,128)S(1)}, f32[24,512]{1,0:T(8,128)S(1)}, u32[]{:S(2)}, u32[]{:S(2)}) collective-permute-start(f32[24,512]{1,0:T(8,128)S(1)} %get-tuple-element.35), channel_id=1, source_target_pairs={{0,192},{64,0},{128,64},{192,128},{1,193},{65,1},{129,65},{193,129... | collective-permute-start | bytes 147464 | tf_op jit(solution)/shard_map/ppermute | solution.py:345
  118.3 5.9 %collective-permute-start.4 = (f32[24,512]{1,0:T(8,128)S(1)}, f32[24,512]{1,0:T(8,128)S(1)}, u32[]{:S(2)}, u32[]{:S(2)}) collective-permute-start(f32[24,512]{1,0:T(8,128)S(1)} %add_add_fusion.1), channel_id=1, source_target_pairs={{0,32},{16,48},{32,0},{48,16},{1,33},{17,49},{33,1},{49,17},{2,34}... | collective-permute-start | bytes 147464 | tf_op jit(solution)/shard_map/ppermute | solution.py:345
  118.4 5.8 %collective-permute-start.5 = (f32[24,512]{1,0:T(8,128)S(1)}, f32[24,512]{1,0:T(8,128)S(1)}, u32[]{:S(2)}, u32[]{:S(2)}) collective-permute-start(f32[24,512]{1,0:T(8,128)S(1)} %add_add_fusion.1), channel_id=1, source_target_pairs={{0,16},{16,32},{32,48},{48,0},{1,17},{17,33},{33,49},{49,1},{2,18}... | collective-permute-start | bytes 147464 | tf_op jit(solution)/shard_map/ppermute | solution.py:345
  118.5 6.1 %collective-permute-start.6 = (f32[24,512]{1,0:T(8,128)S(1)}, f32[24,512]{1,0:T(8,128)S(1)}, u32[]{:S(2)}, u32[]{:S(2)}) collective-permute-start(f32[24,512]{1,0:T(8,128)S(1)} %add_add_fusion.1), channel_id=1, source_target_pairs={{0,48},{16,0},{32,16},{48,32},{1,49},{17,1},{33,17},{49,33},{2,50}... | collective-permute-start | bytes 147464 | tf_op jit(solution)/shard_map/ppermute | solution.py:345
  124.7 2.0 %copy-start = (bf16[512,3328]{1,0:T(8,128)(2,1)S(1)}, bf16[512,3328]{1,0:T(8,128)(2,1)}, u32[]{:S(2)}) copy-start(bf16[512,3328]{1,0:T(8,128)(2,1)} %all-gather.2.cloned.1.call-done.cot_hbm.cot_ref) | copy-start | bytes 10223620
  126.6 2.9 %copy-start.5 = (bf16[1024,3328]{1,0:T(8,128)(2,1)S(1)}, bf16[1024,3328]{1,0:T(8,128)(2,1)}, u32[]{:S(2)}) copy-start(bf16[1024,3328]{1,0:T(8,128)(2,1)} %copy-done.3) | copy-start | bytes 20447236
  136.9 1.0 copy-start.8
  137.9 10.0 %collective-permute-start.7 = (bf16[272,1024]{1,0:T(8,128)(2,1)}, bf16[272,1024]{1,0:T(8,128)(2,1)}, u32[]{:S(2)}, u32[]{:S(2)}) collective-permute-start(bf16[272,1024]{1,0:T(8,128)(2,1)} %get-tuple-element.39), channel_id=1, source_target_pairs={{0,1},{1,0},{2,3},{3,2},{4,5},{5,4},{6,7},{7,6},{8,9},{9,8},{10,11... | collective-permute-start | bytes 1671176 | tf_op jit(solution)/shard_map/ppermute | solution.py:370
  137.9 29.4 %copy-start.1 = (bf16[512,3328]{1,0:T(8,128)(2,1)S(1)}, bf16[512,3328]{1,0:T(8,128)(2,1)}, u32[]{:S(2)}) copy-start(bf16[512,3328]{1,0:T(8,128)(2,1)} %all-gather.2.cloned.1.call-done.cot_hbm.cot_ref) | copy-start | bytes 10223620
  141.3 21.2 %collective-permute-start.11 = (f32[1,3328]{1,0:T(1,128)S(1)}, f32[1,3328]{1,0:T(1,128)S(1)}, u32[]{:S(2)}, u32[]{:S(2)}) collective-permute-start(f32[1,3328]{1,0:T(1,128)S(1)} %get-tuple-element.51), channel_id=1, source_target_pairs={{0,128},{64,192},{128,0},{192,64},{1,129},{65,193},{129,1},{193,65... | collective-permute-start | bytes 39944 | tf_op jit(solution)/shard_map/ppermute | solution.py:345
  144.6 17.9 %collective-permute-start.12 = (f32[1,3328]{1,0:T(1,128)S(1)}, f32[1,3328]{1,0:T(1,128)}, u32[]{:S(2)}, u32[]{:S(2)}) collective-permute-start(f32[1,3328]{1,0:T(1,128)S(1)} %get-tuple-element.51), channel_id=1, source_target_pairs={{0,64},{64,128},{128,192},{192,0},{1,65},{65,129},{129,193},{193,1... | collective-permute-start | bytes 39944 | tf_op jit(solution)/shard_map/ppermute | solution.py:345
  144.7 17.9 %collective-permute-start.13 = (f32[1,3328]{1,0:T(1,128)S(1)}, f32[1,3328]{1,0:T(1,128)}, u32[]{:S(2)}, u32[]{:S(2)}) collective-permute-start(f32[1,3328]{1,0:T(1,128)S(1)} %get-tuple-element.51), channel_id=1, source_target_pairs={{0,192},{64,0},{128,64},{192,128},{1,193},{65,1},{129,65},{193,129... | collective-permute-start | bytes 39944 | tf_op jit(solution)/shard_map/ppermute | solution.py:345
  147.9 1.2 copy-start.9
  149.2 31.9 %copy-start.7 = (bf16[16,32,1024]{2,1,0:T(8,128)(2,1)S(1)}, bf16[16,32,1024]{2,1,0:T(8,128)(2,1)}, u32[]{:S(2)}) copy-start(bf16[16,32,1024]{2,1,0:T(8,128)(2,1)} %copy-done.6) | copy-start | bytes 3145732
  150.4 12.0 %collective-permute-start.8 = (bf16[144,1024]{1,0:T(8,128)(2,1)S(1)}, bf16[144,1024]{1,0:T(8,128)(2,1)S(1)}, u32[]{:S(2)}, u32[]{:S(2)}) collective-permute-start(bf16[144,1024]{1,0:T(8,128)(2,1)S(1)} %get-tuple-element.42), channel_id=1, source_target_pairs={{0,2},{2,0},{4,6},{6,4},{8,10},{10,8},{12,14},{14,12},{1,3},{3,1},... | collective-permute-start | bytes 884744 | tf_op jit(solution)/shard_map/ppermute | solution.py:373
  162.4 9.8 %collective-permute-start.9 = (bf16[80,1024]{1,0:T(8,128)(2,1)S(1)}, bf16[80,1024]{1,0:T(8,128)(2,1)S(1)}, u32[]{:S(2)}, u32[]{:S(2)}) collective-permute-start(bf16[80,1024]{1,0:T(8,128)(2,1)S(1)} %get-tuple-element.45), channel_id=1, source_target_pairs={{0,4},{2,6},{4,0},{6,2},{8,12},{10,14},{12,8},{14,10},{1,5},{3,7},... | collective-permute-start | bytes 491528 | tf_op jit(solution)/shard_map/ppermute | solution.py:373
  163.3 9.5 %collective-permute-start.14 = (f32[1,3328]{1,0:T(1,128)S(1)}, f32[1,3328]{1,0:T(1,128)S(1)}, u32[]{:S(2)}, u32[]{:S(2)}) collective-permute-start(f32[1,3328]{1,0:T(1,128)S(1)} %add_add_fusion.2), channel_id=1, source_target_pairs={{0,32},{16,48},{32,0},{48,16},{1,33},{17,49},{33,1},{49,17},{2,34}... | collective-permute-start | bytes 39944 | tf_op jit(solution)/shard_map/ppermute | solution.py:345
  165.3 7.5 %collective-permute-start.15 = (f32[1,3328]{1,0:T(1,128)S(1)}, f32[1,3328]{1,0:T(1,128)S(1)}, u32[]{:S(2)}, u32[]{:S(2)}) collective-permute-start(f32[1,3328]{1,0:T(1,128)S(1)} %add_add_fusion.2), channel_id=1, source_target_pairs={{0,16},{16,32},{32,48},{48,0},{1,17},{17,33},{33,49},{49,1},{2,18}... | collective-permute-start | bytes 39944 | tf_op jit(solution)/shard_map/ppermute | solution.py:345
  165.3 7.5 %collective-permute-start.16 = (f32[1,3328]{1,0:T(1,128)S(1)}, f32[1,3328]{1,0:T(1,128)S(1)}, u32[]{:S(2)}, u32[]{:S(2)}) collective-permute-start(f32[1,3328]{1,0:T(1,128)S(1)} %add_add_fusion.2), channel_id=1, source_target_pairs={{0,48},{16,0},{32,16},{48,32},{1,49},{17,1},{33,17},{49,33},{2,50}... | collective-permute-start | bytes 39944 | tf_op jit(solution)/shard_map/ppermute | solution.py:345
  172.2 8.8 %collective-permute-start.10 = (bf16[48,1024]{1,0:T(8,128)(2,1)S(1)}, bf16[48,1024]{1,0:T(8,128)(2,1)S(1)}, u32[]{:S(2)}, u32[]{:S(2)}) collective-permute-start(bf16[48,1024]{1,0:T(8,128)(2,1)S(1)} %get-tuple-element.48), channel_id=1, source_target_pairs={{0,8},{2,10},{4,12},{6,14},{8,0},{10,2},{12,4},{14,6},{1,9},{3,11}... | collective-permute-start | bytes 294920 | tf_op jit(solution)/shard_map/ppermute | solution.py:373
Sparse Core Ops, SparseCore 0:
  10.5 80.7 all-gather.1

commit v3 on v2

v3 whole, which is shorter than its diff:
```python
import jax
import jax.numpy as jnp
from jax import lax
from jax.experimental import pallas as pl
from jax.experimental.pallas import tpu as pltpu
from jax.sharding import Mesh
from jax.sharding import PartitionSpec as P

adapter_scale = 2.0
epsilon = 1e-06
bf16 = jnp.bfloat16
f32 = jnp.float32
ROW = ("x", "y")
COL = ("z", "c")
CHUNK = 512
RANK = 16
EXTRA = 256
MIB = 1024 * 1024
ANY = pl.BlockSpec(memory_space=pl.ANY)
VMEM = pl.BlockSpec(memory_space=pltpu.VMEM)
SMEM = pl.BlockSpec(memory_space=pltpu.SMEM)


def pieces(value):
    high = value.astype(bf16)
    rest = value - high.astype(f32)
    mid = rest.astype(bf16)
    low = (rest - mid.astype(f32)).astype(bf16)
    return high, mid, low


def dot(left, right, left_dim, right_dim):
    return lax.dot_general(
        left, right, (((left_dim,), (right_dim,)), ((), ())), preferred_element_type=f32
    )


def three(left, right, left_dim, right_dim):
    out = dot(jnp.concatenate(pieces(left), axis=0), right, left_dim, right_dim)
    return out[:RANK] + out[RANK : 2 * RANK] + out[2 * RANK :]


def chunks_of(width):
    return [(at, min(CHUNK, width - at)) for at in range(0, width, CHUNK)]


def call(body, flops, moved, limit, **options):
    return pl.pallas_call(
        body,
        compiler_params=pltpu.CompilerParams(vmem_limit_bytes=limit * MIB),
        cost_estimate=pl.CostEstimate(flops=flops, bytes_accessed=moved, transcendentals=0),
        **options,
    )


def begin(source, target, sem):
    copy = pltpu.make_async_copy(source, target, sem)
    copy.start()
    return copy


def merge_kernel(
    down_hbm, up_hbm, weight_hbm, merged_hbm, sums_ref,
    down, up, weight, merged, up_cat, totals, small_sem, in_sem, out_sem,
):
    depth, width = weight.shape
    rows, tile = 256, 256
    steps = [slice(at, at + rows) for at in range(0, depth, rows)]
    first = begin(up_hbm, up, small_sem.at[0]), begin(down_hbm, down, small_sem.at[1])
    fetches = [begin(weight_hbm.at[p], weight.at[p], in_sem.at[j]) for j, p in enumerate(steps)]
    totals[...] = jnp.zeros_like(totals)
    for copy in first:
        copy.wait()
    for at in range(0, width, tile):
        cols = slice(at, at + tile)
        u1, u2, u3 = pieces(up[:, cols])
        up_cat[:, cols] = jnp.concatenate([u1, u2, u1, u3, u1, u2], axis=0)
    d1, d2, d3 = pieces(down[...] * adapter_scale)
    down_cat = jnp.concatenate([d1, d1, d2, d1, d3, d2], axis=0)
    stores = []
    for j, part in enumerate(steps):
        fetches[j].wait()
        for at in range(0, width, tile):
            cols = slice(at, at + tile)
            value = weight[part, cols].astype(f32) + dot(down_cat[:, part], up_cat[:, cols], 0, 0)
            merged[part, cols] = value.astype(bf16)
            totals[:, cols] += jnp.sum((value * value).reshape(rows // 8, 8, tile), axis=0)
        stores.append(begin(merged.at[part], merged_hbm.at[part], out_sem.at[j]))
    sums_ref[...] = jnp.sum(totals[...], axis=0, keepdims=True)
    for copy in stores:
        copy.wait()


def merge(down_t, up, weight):
    depth, width = weight.shape
    return call(
        merge_kernel,
        12 * depth * width,
        4 * depth * width,
        20,
        in_specs=[ANY, ANY, ANY],
        out_specs=[ANY, VMEM],
        out_shape=[
            jax.ShapeDtypeStruct((depth, width), bf16),
            jax.ShapeDtypeStruct((1, width), f32),
        ],
        scratch_shapes=[
            pltpu.VMEM((RANK, depth), f32),
            pltpu.VMEM((RANK, width), f32),
            pltpu.VMEM((depth, width), bf16),
            pltpu.VMEM((depth, width), bf16),
            pltpu.VMEM((6 * RANK, width), bf16),
            pltpu.VMEM((8, width), f32),
            pltpu.SemaphoreType.DMA((2,)),
            pltpu.SemaphoreType.DMA((4,)),
            pltpu.SemaphoreType.DMA((4,)),
        ],
        name="merge",
    )(down_t, up, weight)


def forward_kernel(
    core_ref, own_hbm, other_hbm, down_hbm, sums_ref, merged_hbm,
    part_hbm, tokens_hbm, small_hbm,
    tokens, down, small, merged, part, small_sem, in_sem, out_sem,
):
    core = core_ref[0]
    depth, width = merged.shape
    chunks = chunks_of(width)
    first = (
        begin(own_hbm, tokens.at[:, core], small_sem.at[0]),
        begin(other_hbm, tokens.at[:, 1 - core], small_sem.at[1]),
        begin(down_hbm, down, small_sem.at[2]),
    )
    fetches, stores = [], []
    for j, (at, size) in enumerate(chunks):
        cols = slice(at, at + size)
        fetches.append(begin(merged_hbm.at[:, cols], merged.at[:, cols], in_sem.at[j]))
    for j, (at, size) in enumerate(chunks):
        small[RANK + j : RANK + j + 1, :size] = sums_ref[:, at : at + size]
    at, size = chunks[-1]
    small[RANK + len(chunks) - 1 : RANK + len(chunks), size:] = jnp.zeros((1, CHUNK - size), f32)
    small[RANK + len(chunks) :, :] = jnp.zeros((8 - len(chunks), CHUNK), f32)
    for copy in first:
        copy.wait()
    all_tokens = tokens[...].reshape(512, depth)
    small[:RANK, :] = three(down[...], all_tokens, 1, 1)
    stores.append(begin(small, small_hbm, small_sem.at[0]))
    stores.append(begin(tokens, tokens_hbm, small_sem.at[1]))
    for j, (at, size) in enumerate(chunks):
        fetches[j].wait()
        cols = slice(at, at + size)
        product = dot(all_tokens, merged[:, cols], 1, 0).astype(bf16)
        part[:, :, cols] = product.reshape(16, 32, size)
        stores.append(begin(part.at[:, :, cols], part_hbm.at[:, :, cols], out_sem.at[j]))
    for copy in stores:
        copy.wait()


def forward(core, own, other, down_t, sums, merged_low):
    depth, width = merged_low.shape
    count = len(chunks_of(width))
    return call(
        forward_kernel,
        2 * 512 * depth * width,
        12 * MIB,
        24,
        in_specs=[SMEM, ANY, ANY, ANY, VMEM, ANY],
        out_specs=[ANY, ANY, ANY],
        out_shape=[
            jax.ShapeDtypeStruct((16, 32, width + EXTRA), bf16),
            jax.ShapeDtypeStruct((8, 2, 32, depth), bf16),
            jax.ShapeDtypeStruct((RANK + 8, CHUNK), f32),
        ],
        scratch_shapes=[
            pltpu.VMEM((8, 2, 32, depth), bf16),
            pltpu.VMEM((RANK, depth), f32),
            pltpu.VMEM((RANK + 8, CHUNK), f32),
            pltpu.VMEM((depth, width), bf16),
            pltpu.VMEM((16, 32, width), bf16),
            pltpu.SemaphoreType.DMA((3,)),
            pltpu.SemaphoreType.DMA((count,)),
            pltpu.SemaphoreType.DMA((count,)),
        ],
        name="forward",
    )(core, own, other, down_t, sums, merged_low)


def magnitude_kernel(cot_hbm, part_hbm, out_hbm, cot, part, extra, sem, out_sem):
    width = cot.shape[1]
    chunks = chunks_of(width)
    fetches = []
    for j, (at, size) in enumerate(chunks):
        cols = slice(at, at + size)
        fetches.append(
            (
                begin(cot_hbm.at[:, cols], cot.at[:, cols], sem.at[0, j]),
                begin(part_hbm.at[:, :, cols], part.at[:, :, cols], sem.at[1, j]),
            )
        )
    rows = []
    for j, (at, size) in enumerate(chunks):
        for copy in fetches[j]:
            copy.wait()
        cols = slice(at, at + size)
        product = cot[:, cols].astype(f32) * part[:, :, cols].reshape(512, size).astype(f32)
        total = jnp.sum(product, axis=0, keepdims=True)
        rows += [total[:, k : k + EXTRA] for k in range(0, size, EXTRA)]
    rows += [jnp.zeros((1, EXTRA), f32)] * (16 - len(rows))
    value = jnp.concatenate(rows, axis=0)
    high = value.astype(bf16)
    extra[:16, :] = high
    extra[16:, :] = (value - high.astype(f32)).astype(bf16)
    stores = [
        begin(extra, out_hbm.at[r, :, width : width + EXTRA], out_sem.at[r]) for r in range(16)
    ]
    for copy in stores:
        copy.wait()


def add_magnitude(cot, part):
    tokens, width = cot.shape
    return call(
        magnitude_kernel,
        4 * tokens * width,
        7 * MIB,
        16,
        in_specs=[ANY, ANY],
        out_specs=ANY,
        out_shape=jax.ShapeDtypeStruct(part.shape, bf16),
        scratch_shapes=[
            pltpu.VMEM((tokens, width), bf16),
            pltpu.VMEM((16, 32, width), bf16),
            pltpu.VMEM((32, EXTRA), bf16),
            pltpu.SemaphoreType.DMA((2, len(chunks_of(width)))),
            pltpu.SemaphoreType.DMA((16,)),
        ],
        input_output_aliases={1: 0},
        name="magnitude",
    )(cot, part)


def output_kernel(small_ref, magnitude_ref, parts_hbm, out_hbm, mag_hbm, parts, out, mag, sem, out_sem):
    width = out.shape[1]
    chunks = chunks_of(width)
    tail = begin(parts_hbm.at[:, :, width:], parts.at[:, :, width:], sem.at[len(chunks)])
    fetches, stores = [], []
    for j, (at, size) in enumerate(chunks):
        cols = slice(at, at + size)
        fetches.append(begin(parts_hbm.at[:, :, cols], parts.at[:, :, cols], sem.at[j]))

    def added(cols):
        total = parts[0, :, cols].astype(f32)
        for r in range(1, 16):
            total += parts[r, :, cols].astype(f32)
        return total

    tail.wait()
    extra = added(slice(width, width + EXTRA))
    extra = extra[:16] + extra[16:]
    for j, (at, size) in enumerate(chunks):
        fetches[j].wait()
        cols = slice(at, at + size)
        norm = jnp.sqrt(small_ref[RANK + j : RANK + j + 1, :size] + epsilon)
        out[:, cols] = (added(cols) * (magnitude_ref[:, cols] / norm)).astype(bf16)
        stores.append(begin(out.at[:, cols], out_hbm.at[:, cols], out_sem.at[j]))
        for k in range(0, size, EXTRA):
            row = (at + k) // EXTRA
            mag[:, at + k : at + k + EXTRA] = extra[row : row + 1] / norm[:, k : k + EXTRA]
    stores.append(begin(mag, mag_hbm, out_sem.at[len(chunks)]))
    for copy in stores:
        copy.wait()


def output_of(small, magnitude, parts):
    width = magnitude.shape[1]
    count = len(chunks_of(width)) + 1
    return call(
        output_kernel,
        16 * 32 * width,
        4 * MIB,
        16,
        in_specs=[VMEM, VMEM, ANY],
        out_specs=[ANY, ANY],
        out_shape=[
            jax.ShapeDtypeStruct((32, width), bf16),
            jax.ShapeDtypeStruct((1, width), f32),
        ],
        scratch_shapes=[
            pltpu.VMEM(parts.shape, bf16),
            pltpu.VMEM((32, width), bf16),
            pltpu.VMEM((1, width), f32),
            pltpu.SemaphoreType.DMA((count,)),
            pltpu.SemaphoreType.DMA((count,)),
        ],
        name="output",
    )(small, magnitude, parts)


def pack(low, out):
    high = low.astype(bf16)
    rest = (low - high.astype(f32)).astype(bf16)
    out[:, :CHUNK] = high
    out[:, CHUNK:] = rest
    return high.astype(f32) + rest.astype(f32)


def unpack(got):
    got = got.astype(f32)
    return got[:, :CHUNK] + got[:, CHUNK:]


def backward_kernel(
    core_ref, small_hbm, magnitude_ref, up_hbm, cot_hbm, merged_hbm,
    own_ref, send_hbm, low_ref, small, up, cot, merged, total, send, first_sem, sem,
):
    core = core_ref[0]
    width = merged.shape[1]
    chunks = chunks_of(width)
    first = begin(small_hbm, small, first_sem.at[0]), begin(up_hbm, up, first_sem.at[1])
    fetches = []
    for j, (at, size) in enumerate(chunks):
        cols = slice(at, at + size)
        fetches.append(
            (
                begin(cot_hbm.at[:, cols], cot.at[:, cols], sem.at[0, j]),
                begin(merged_hbm.at[:, cols], merged.at[:, cols], sem.at[1, j]),
            )
        )
    for copy in first:
        copy.wait()
    low = jnp.zeros((RANK, CHUNK), f32)
    for j, (at, size) in enumerate(chunks):
        for copy in fetches[j]:
            copy.wait()
        cols = slice(at, at + size)
        norm = jnp.sqrt(small[RANK + j : RANK + j + 1, :size] + epsilon)
        grad = (cot[:, cols].astype(f32) * (magnitude_ref[:, cols] / norm)).astype(bf16)
        product = dot(grad, merged[:, cols], 1, 1)
        if j == 0:
            total[...] = product
        else:
            total[...] += product
        low += three(up[:, cols], grad, 1, 1)
    low_ref[...] = pack(low, send.at[256:272, :])
    for z in range(8):
        own = pl.ds(pl.multiple_of((2 * z + core) * 32, 32), 32)
        other = pl.ds(pl.multiple_of((2 * z + 1 - core) * 32, 32), 32)
        send[32 * z : 32 * z + 32, :] = total[other, :].astype(bf16)
        own_ref[32 * z : 32 * z + 32, :] = total[own, :]
    copy = begin(send, send_hbm, first_sem.at[0])
    copy.wait()


def backward(core, small, magnitude, up, cot, merged_low):
    depth, width = merged_low.shape
    count = len(chunks_of(width))
    return call(
        backward_kernel,
        2 * 512 * depth * width,
        12 * MIB,
        28,
        in_specs=[SMEM, ANY, VMEM, ANY, ANY, ANY],
        out_specs=[VMEM, ANY, VMEM],
        out_shape=[
            jax.ShapeDtypeStruct((256, depth), f32),
            jax.ShapeDtypeStruct((272, depth), bf16),
            jax.ShapeDtypeStruct((RANK, CHUNK), f32),
        ],
        scratch_shapes=[
            pltpu.VMEM((RANK + 8, CHUNK), f32),
            pltpu.VMEM((RANK, width), f32),
            pltpu.VMEM((512, width), bf16),
            pltpu.VMEM((depth, width), bf16),
            pltpu.VMEM((512, depth), f32),
            pltpu.VMEM((272, depth), bf16),
            pltpu.SemaphoreType.DMA((2,)),
            pltpu.SemaphoreType.DMA((2, count)),
        ],
        name="backward",
    )(core, small, magnitude, up, cot, merged_low)


def fold_kernel(bit_ref, keep_ref, low_ref, got_hbm, keep_out, low_out, send_hbm, got_ref, send_out, sem):
    bit = bit_ref[0]
    rows = keep_ref.shape[0]
    begin(got_hbm, got_ref, sem.at[0]).wait()
    for i in range(rows // 64):
        kept = pl.ds(pl.multiple_of((2 * i + bit) * 32, 32), 32)
        sent = pl.ds(pl.multiple_of((2 * i + 1 - bit) * 32, 32), 32)
        at = slice(32 * i, 32 * i + 32)
        keep_out[at, :] = keep_ref[kept, :] + got_ref[kept, :].astype(f32)
        send_out[at, :] = (keep_ref[sent, :] + got_ref[sent, :].astype(f32)).astype(bf16)
    low = low_ref[...] + unpack(got_ref[rows : rows + RANK, :])
    low_out[...] = pack(low, send_out.at[rows // 2 : rows // 2 + RANK, :])
    begin(send_out, send_hbm, sem.at[0]).wait()


def fold(bit, keep, low, got):
    rows, depth = keep.shape
    return call(
        fold_kernel,
        4 * rows * depth,
        12 * rows * depth,
        16,
        in_specs=[SMEM, VMEM, VMEM, ANY],
        out_specs=[VMEM, VMEM, ANY],
        out_shape=[
            jax.ShapeDtypeStruct((rows // 2, depth), f32),
            jax.ShapeDtypeStruct((RANK, CHUNK), f32),
            jax.ShapeDtypeStruct((rows // 2 + RANK, depth), bf16),
        ],
        scratch_shapes=[
            pltpu.VMEM((rows + RANK, depth), bf16),
            pltpu.VMEM((rows // 2 + RANK, depth), bf16),
            pltpu.SemaphoreType.DMA((1,)),
        ],
        name="fold",
    )(bit, keep, low, got)


def finish_kernel(
    keep_ref, low_ref, got_hbm, tokens_hbm, grad_hbm, down_hbm, got, tokens, grad, down, sem
):
    later = begin(tokens_hbm, tokens, sem.at[1])
    begin(got_hbm, got, sem.at[0]).wait()
    grad[...] = (keep_ref[...] + got[:32, :].astype(f32)).astype(bf16)
    first = begin(grad, grad_hbm, sem.at[0])
    low = low_ref[...] + unpack(got[32 : 32 + RANK, :])
    later.wait()
    down[...] = three(low * adapter_scale, tokens[...], 1, 0)
    begin(down, down_hbm, sem.at[1]).wait()
    first.wait()


def finish(keep, low, got, tokens):
    depth = tokens.shape[1]
    return call(
        finish_kernel,
        2 * 512 * 256 * depth,
        2 * MIB,
        16,
        in_specs=[VMEM, VMEM, ANY, ANY],
        out_specs=[ANY, ANY],
        out_shape=[
            jax.ShapeDtypeStruct((32, depth), bf16),
            jax.ShapeDtypeStruct((RANK, depth), f32),
        ],
        scratch_shapes=[
            pltpu.VMEM(got.shape, bf16),
            pltpu.VMEM(tokens.shape, bf16),
            pltpu.VMEM((32, depth), bf16),
            pltpu.VMEM((RANK, depth), f32),
            pltpu.SemaphoreType.DMA((2,)),
        ],
        name="finish",
    )(keep, low, got, tokens)


def up_kernel(small_hbm, magnitude_ref, cot_hbm, out_hbm, small, cot, out, sem, out_sem):
    width = cot.shape[1]
    chunks = chunks_of(width)
    first = begin(small_hbm, small, sem.at[len(chunks)])
    fetches, stores = [], []
    for j, (at, size) in enumerate(chunks):
        cols = slice(at, at + size)
        fetches.append(begin(cot_hbm.at[:, cols], cot.at[:, cols], sem.at[j]))
    first.wait()
    for j, (at, size) in enumerate(chunks):
        fetches[j].wait()
        cols = slice(at, at + size)
        norm = jnp.sqrt(small[RANK + j : RANK + j + 1, :size] + epsilon)
        grad = (cot[:, cols].astype(f32) * (magnitude_ref[:, cols] / norm)).astype(bf16)
        out[:, cols] = three(small[:RANK, :] * adapter_scale, grad, 1, 0)
        stores.append(begin(out.at[:, cols], out_hbm.at[:, cols], out_sem.at[j]))
    for copy in stores:
        copy.wait()


def up_gradient_of(small, magnitude, cot):
    tokens, width = cot.shape
    count = len(chunks_of(width)) + 1
    return call(
        up_kernel,
        2 * 512 * 256 * width,
        4 * MIB,
        16,
        in_specs=[ANY, VMEM, ANY],
        out_specs=ANY,
        out_shape=jax.ShapeDtypeStruct((RANK, width), f32),
        scratch_shapes=[
            pltpu.VMEM(small.shape, f32),
            pltpu.VMEM(cot.shape, bf16),
            pltpu.VMEM((RANK, width), f32),
            pltpu.SemaphoreType.DMA((count,)),
            pltpu.SemaphoreType.DMA((count,)),
        ],
        name="up_gradient",
    )(small, magnitude, cot)


def exchange(blocks, axis):
    return lax.all_to_all(blocks, axis, 0, 0, tiled=False)


def around(value, axis):
    one, two, other = [
        lax.ppermute(value, axis, [(i, (i + k) % 4) for i in range(4)]) for k in (1, 2, 3)
    ]
    return (value + two) + (one + other)


def add_row(value):
    return around(around(value, "x"), "y")


def on_device(tokens, weight, down_adapter, up_adapter, magnitude, out_cotangent):
    core = lax.axis_index("c").astype(jnp.int32).reshape(1)
    z = lax.axis_index("z").astype(jnp.int32)
    swap = [(0, 1), (1, 0)]
    down_t = down_adapter.T
    magnitude = magnitude.reshape(1, -1)
    cot_full = lax.all_gather(out_cotangent, ROW, axis=0, tiled=True)
    own_tokens = exchange(jnp.broadcast_to(tokens[None], (8,) + tokens.shape), "z")
    merged_low, sums = merge(down_t, up_adapter, weight)
    own_tokens, merged_low, sums = lax.optimization_barrier((own_tokens, merged_low, sums))
    other_tokens = lax.ppermute(own_tokens, "c", swap)
    part, tokens_full, small = forward(core, own_tokens, other_tokens, down_t, sums, merged_low)
    small = add_row(small)
    small, part, cot_full = lax.optimization_barrier((small, part, cot_full))
    part = add_magnitude(cot_full, part)
    out_parts = exchange(part, ROW)
    keep, send, low = backward(core, small, magnitude, up_adapter, cot_full, merged_low)
    got = lax.ppermute(send, "c", swap)
    for k in range(3):
        keep, low, send = fold(((z >> k) & 1).reshape(1), keep, low, got)
        got = lax.ppermute(send, "z", [(i, i ^ (1 << k)) for i in range(8)])
    grad_tokens, down_gradient = finish(keep, low, got, tokens_full.reshape(512, -1))
    up_gradient = up_gradient_of(small, magnitude, cot_full)
    output, grad_magnitude = output_of(small, magnitude, out_parts)
    return (output, grad_tokens, grad_magnitude.reshape(-1), up_gradient, down_gradient.T)


def solution(mesh):
    split = Mesh(mesh.devices.reshape(4, 4, 8, 2), ROW + COL)
    return jax.shard_map(
        on_device,
        mesh=split,
        in_specs=(P(COL, ROW), P(ROW, COL), P(ROW, None), P(None, COL), P(COL), P(ROW, COL)),
        out_specs=(P(ROW, COL), P(COL, ROW), P(COL), P(None, COL), P(ROW, None)),
        check_vma=False,
    )
```

time: 189 us -> 150 us (0.79)
  waiting for transfers between devices: 83.4 us -> 37.3 us
  local copies, waits for them, and re-layouts: 20.2 us -> 30.4 us
  Pallas kernels: 23.5 us -> 31.8 us
  starting transfers between devices: 40.9 us -> 34.2 us
  other arithmetic: 6.6 us -> 0.67 us
    ppermute x12 -> x6, waiting for transfers between devices: 60.2 us -> 7.67 us  [around(): lax.ppermute(value, axis, [(i, (i + k) % 4) for i in range(4)])]
    unnamed x30 -> x44, local copies, waits for them, and re-layouts: 18.5 us -> 28.7 us
    ppermute x12 -> x6, starting transfers between devices: 19 us -> 10.7 us  [around(): lax.ppermute(value, axis, [(i, (i + k) % 4) for i in range(4)])]
    pallas_call x4 -> x6, Pallas kernels: 15.2 us -> 20.4 us  [the longest x1 7.14 us: backward(): call(backward_kernel, 2 * 512 * depth * width, 12 * MIB, 28, in_specs=[SM...]
    ppermute x3, waiting for transfers between devices: 15.7 us -> 20.2 us  [on_device(): got = lax.ppermute(send, 'z', [(i, i ^ 1 << k) for i in range(8)])]
    reduce_sum x1 -> x0, other arithmetic: 3.4 us -> none  [on_device(): output = (jnp.sum(out_parts.astype(f32), axis=0) * factor).astype(bf16)]
    pallas_call x3, Pallas kernels: 1.33 us -> 4.57 us  [fold(): call(fold_kernel, 4 * rows * depth, 12 * rows * depth, 16, in_specs=[SMEM...]
    ppermute x1, waiting for transfers between devices: 0.01 us -> 2.3 us  [on_device(): got = lax.ppermute(send, 'c', swap)]
  transfers between devices with their start and end apart: 20 -> 14, of which waited for: 9 -> 11; matrix products, arithmetic and copies ran while one was open for 4% -> 1% of each run, Pallas kernels for 12% -> 19%
where the time goes in v3:
time: 150 us; the launch traced here: 149 us
  waiting for transfers between devices  37.3 us (25%)
  starting transfers between devices  34.2 us (23%)
  Pallas kernels  31.8 us (21%)
  local copies, waits for them, and re-layouts  30.4 us (20%)
  between operations  14.2 us (9%)
    unnamed x44, local copies, waits for them, and re-layouts  28.7 us
    ppermute x3, waiting for transfers between devices, on_device(): got = lax.ppermute(send, 'z', [(i, i ^ 1 << k) for i in range(8)])  20.2 us
    all_to_all x2, starting transfers between devices, exchange(): return lax.all_to_all(blocks, axis, 0, 0, tiled=False)  16.2 us
    ppermute x6, starting transfers between devices, around(): lax.ppermute(value, axis, [(i, (i + k) % 4) for i in range(4)])  10.7 us
    ppermute x6, waiting for transfers between devices, around(): lax.ppermute(value, axis, [(i, (i + k) % 4) for i in range(4)])  7.67 us
    ppermute x3, starting transfers between devices, on_device(): got = lax.ppermute(send, 'z', [(i, i ^ 1 << k) for i in range(8)])  7.32 us
    pallas_call x1, Pallas kernels, backward(): call(backward_kernel, 2 * 512 * depth * width, 12 * MIB, 28, in_specs=[SM...  7.14 us
    pallas_call x1, Pallas kernels, forward(): call(forward_kernel, 2 * 512 * depth * width, 12 * MIB, 24, in_specs=[SME...  6.79 us
  transfers between devices with their start and end apart: 14, of which 11 were waited for; matrix products, arithmetic and copies ran while one was open for 1% of the time, Pallas kernels for 19%

profile of v3, /device:TPU:8, one launch (start us, length us, event | category | flops | bytes accessed | tf_op | source)
XLA Modules:
  0.0 148.7 jit_solution(14362743791270130324)
XLA Ops:
  7.2 0.7 all-gather.2.cloned.1.call-update
  7.9 1.7 %broadcast_in_dim.2 = bf16[8,32,1024]{2,1,0:T(8,128)(2,1)} broadcast(bf16[32,1024]{1,0:T(8,128)(2,1)} %param.6), dimensions={1,2} | broadcast | bytes 589824 | tf_op jit(solution)/shard_map/broadcast_in_dim | solution.py:524
  9.6 8.5 %all-to-all-start = ((bf16[8,32,1024]{2,1,0:T(8,128)(2,1)}), bf16[8,32,1024]{2,1,0:T(8,128)(2,1)S(1)}, u32[]{:S(2)}, u32[]{:S(2)}) async-start(bf16[8,32,1024]{2,1,0:T(8,128)(2,1)} %broadcast_in_dim.2), calls=%async_computation | async-start | bytes 1048576 | tf_op jit(solution)/shard_map/all_to_all | solution.py:503
  18.1 2.9 %copy-done.5 = bf16[1024,3328]{1,0:T(8,128)(2,1)S(1)} copy-done((bf16[1024,3328]{1,0:T(8,128)(2,1)S(1)}, bf16[1024,3328]{1,0:T(8,128)(2,1)}, u32[]{:S(2)}) %copy-start.5) | copy-done | bytes 6815768
  21.0 0.9 copy-done.14
  21.9 0.8 copy-done.16
  22.8 5.4 %merge.1 = (bf16[1024,3328]{1,0:T(8,128)(2,1)S(1)}, f32[1,3328]{1,0:T(1,128)S(1)}) custom-call(f32[16,1024]{1,0:T(8,128)S(1)} %bitcast.8, f32[16,3328]{1,0:T(8,128)S(1)} %copy-done.14, bf16[1024,3328]{1,0:T(8,128)(2,1)S(1)} %copy-done.5), custom_call_target="tpu_custom_call" | custom-call | flops 40894464 | bytes 13631488 | tf_op jit(solution)/shard_map/merge/pallas_call | solution.py:96
  28.2 2.8 %copy-done.18 = bf16[1024,3328]{1,0:T(8,128)(2,1)} copy-done((bf16[1024,3328]{1,0:T(8,128)(2,1)}, bf16[1024,3328]{1,0:T(8,128)(2,1)S(1)}, u32[]{:S(2)}) %copy-start.18) | copy-done | bytes 6815768
  31.0 4.6 %all-to-all-done.own_hbm = bf16[8,32,1024]{2,1,0:T(8,128)(2,1)S(1)} async-done(((bf16[8,32,1024]{2,1,0:T(8,128)(2,1)}), bf16[8,32,1024]{2,1,0:T(8,128)(2,1)S(1)}, u32[]{:S(2)}, u32[]{:S(2)}) %all-to-all-start) | async-done | bytes 524320 | tf_op jit(solution)/shard_map/all_to_all | solution.py:503
  35.6 1.9 %collective-permute-done.other_hbm = bf16[8,32,1024]{2,1,0:T(8,128)(2,1)S(1)} collective-permute-done((bf16[8,32,1024]{2,1,0:T(8,128)(2,1)S(1)}, bf16[8,32,1024]{2,1,0:T(8,128)(2,1)S(1)}, u32[]{:S(2)}, u32[]{:S(2)}) %collective-permute-start) | collective-permute-done | bytes 524320 | tf_op jit(solution)/shard_map/ppermute | solution.py:527
  37.5 2.9 %copy-done.19 = bf16[1024,3328]{1,0:T(8,128)(2,1)S(1)} copy-done((bf16[1024,3328]{1,0:T(8,128)(2,1)S(1)}, bf16[1024,3328]{1,0:T(8,128)(2,1)}, u32[]{:S(2)}) %copy-start.19) | copy-done | bytes 6815768
  40.4 6.8 %forward.1 = (bf16[16,32,3584]{2,1,0:T(8,128)(2,1)S(1)}, bf16[8,2,32,1024]{3,2,1,0:T(8,128)(2,1)S(1)}, f32[24,512]{1,0:T(8,128)S(1)}) custom-call(s32[1]{0:T(128)} %bitcast.core_ref, bf16[8,32,1024]{2,1,0:T(8,128)(2,1)S(1)} %all-to-all-done.own_hbm, bf16[8,32,1024]{2,1,0:T(8,128)(2,1)S(1)} %collective-permute-done.other_hbm, f32[16,1024]{1,0:T(8,128)S(1)} %bitcast.9, ...), custom_call_target="tpu_custom_call" | custom-call | flops 3489660928 | bytes 12582912 | tf_op jit(solution)/shard_map/forward/pallas_call | solution.py:163
  47.2 1.9 %copy-done = bf16[16,32,3584]{2,1,0:T(8,128)(2,1)} copy-done((bf16[16,32,3584]{2,1,0:T(8,128)(2,1)}, bf16[16,32,3584]{2,1,0:T(8,128)(2,1)S(1)}, u32[]{:S(2)}) %copy-start) | copy-done | bytes 3670040
  49.1 1.0 copy-done.6
  50.1 2.8 %collective-permute-start.3 = (f32[24,512]{1,0:T(8,128)S(1)}, f32[24,512]{1,0:T(8,128)S(1)}, u32[]{:S(2)}, u32[]{:S(2)}) collective-permute-start(f32[24,512]{1,0:T(8,128)S(1)} %get-tuple-element.37), channel_id=1, source_target_pairs={{0,192},{64,0},{128,64},{192,128},{1,193},{65,1},{129,65},{193,129... | collective-permute-start | bytes 147464 | tf_op jit(solution)/shard_map/ppermute | solution.py:508
  52.8 2.3 %collective-permute-start.1 = (f32[24,512]{1,0:T(8,128)S(1)}, f32[24,512]{1,0:T(8,128)S(1)}, u32[]{:S(2)}, u32[]{:S(2)}) collective-permute-start(f32[24,512]{1,0:T(8,128)S(1)} %get-tuple-element.37), channel_id=1, source_target_pairs={{0,128},{64,192},{128,0},{192,64},{1,129},{65,193},{129,1},{193,65... | collective-permute-start | bytes 147464 | tf_op jit(solution)/shard_map/ppermute | solution.py:508
  55.4 4.8 %collective-permute-done.2 = f32[24,512]{1,0:T(8,128)S(1)} collective-permute-done((f32[24,512]{1,0:T(8,128)S(1)}, f32[24,512]{1,0:T(8,128)S(1)}, u32[]{:S(2)}, u32[]{:S(2)}) %collective-permute-start.2) | collective-permute-done | bytes 49184 | tf_op jit(solution)/shard_map/ppermute | solution.py:508
  61.0 1.6 %collective-permute-start.5 = (f32[24,512]{1,0:T(8,128)S(1)}, f32[24,512]{1,0:T(8,128)S(1)}, u32[]{:S(2)}, u32[]{:S(2)}) collective-permute-start(f32[24,512]{1,0:T(8,128)S(1)} %add_add_fusion.1), channel_id=1, source_target_pairs={{0,16},{16,32},{32,48},{48,0},{1,17},{17,33},{33,49},{49,1},{2,18}... | collective-permute-start | bytes 147464 | tf_op jit(solution)/shard_map/ppermute | solution.py:508
  62.6 3.5 %collective-permute-start.4 = (f32[24,512]{1,0:T(8,128)S(1)}, f32[24,512]{1,0:T(8,128)S(1)}, u32[]{:S(2)}, u32[]{:S(2)}) collective-permute-start(f32[24,512]{1,0:T(8,128)S(1)} %add_add_fusion.1), channel_id=1, source_target_pairs={{0,32},{16,48},{32,0},{48,16},{1,33},{17,49},{33,1},{49,17},{2,34}... | collective-permute-start | bytes 147464 | tf_op jit(solution)/shard_map/ppermute | solution.py:508
  66.1 0.9 collective-permute-done.5
  67.0 1.4 collective-permute-done.4
  68.5 2.0 %copy-done.1 = bf16[16,32,3584]{2,1,0:T(8,128)(2,1)S(1)} copy-done((bf16[16,32,3584]{2,1,0:T(8,128)(2,1)S(1)}, bf16[16,32,3584]{2,1,0:T(8,128)(2,1)}, u32[]{:S(2)}) %copy-start.1) | copy-done | bytes 3670040
  70.5 2.0 %copy-done.3 = bf16[512,3328]{1,0:T(8,128)(2,1)S(1)} copy-done((bf16[512,3328]{1,0:T(8,128)(2,1)S(1)}, bf16[512,3328]{1,0:T(8,128)(2,1)}, u32[]{:S(2)}) %copy-start.3) | copy-done | bytes 3407896
  72.5 1.2 magnitude.1
  73.7 1.9 %copy-done.2 = bf16[16,32,3584]{2,1,0:T(8,128)(2,1)} copy-done((bf16[16,32,3584]{2,1,0:T(8,128)(2,1)}, bf16[16,32,3584]{2,1,0:T(8,128)(2,1)S(1)}, u32[]{:S(2)}) %copy-start.2) | copy-done | bytes 3670040
  75.6 7.7 %all-to-all-start.1 = ((bf16[16,32,3584]{2,1,0:T(8,128)(2,1)}), bf16[16,32,3584]{2,1,0:T(8,128)(2,1)}, u32[]{:S(2)}, u32[]{:S(2)}) async-start(bf16[16,32,3584]{2,1,0:T(8,128)(2,1)} %copy-done.2), calls=%async_computation.1 | async-start | bytes 7340032 | tf_op jit(solution)/shard_map/all_to_all | solution.py:503
  83.3 0.9 copy-done.15
  84.3 2.9 %copy-done.20 = bf16[1024,3328]{1,0:T(8,128)(2,1)S(1)} copy-done((bf16[1024,3328]{1,0:T(8,128)(2,1)S(1)}, bf16[1024,3328]{1,0:T(8,128)(2,1)}, u32[]{:S(2)}) %copy-start.20) | copy-done | bytes 6815768
  87.2 7.1 %backward.1 = (f32[256,1024]{1,0:T(8,128)S(1)}, bf16[272,1024]{1,0:T(8,128)(2,1)}, f32[16,512]{1,0:T(8,128)S(1)}) custom-call(s32[1]{0:T(128)} %bitcast.core_ref, f32[24,512]{1,0:T(8,128)S(1)} %add_add_fusion.small_ref.small_hbm, f32[1,3328]{1,0:T(1,128)S(1)} %reshape.33.magnitude_ref, f32[16,3328]{1,0:T(8,128)S(1)} %copy-done.15, ...), custom_call_target="tpu_custom_call" | custom-call | flops 3489660928 | bytes 12582912 | tf_op jit(solution)/shard_map/backward/pallas_call | solution.py:358
  94.4 1.0 copy-done.8
  95.3 2.3 %collective-permute-done.7.got_hbm = bf16[272,1024]{1,0:T(8,128)(2,1)} collective-permute-done((bf16[272,1024]{1,0:T(8,128)(2,1)}, bf16[272,1024]{1,0:T(8,128)(2,1)}, u32[]{:S(2)}, u32[]{:S(2)}) %collective-permute-start.7) | collective-permute-done | bytes 557088 | tf_op jit(solution)/shard_map/ppermute | solution.py:534
  97.6 1.2 copy-done.9
  98.9 1.8 %fold.3 = (f32[128,1024]{1,0:T(8,128)S(1)}, f32[16,512]{1,0:T(8,128)S(1)}, bf16[144,1024]{1,0:T(8,128)(2,1)}) custom-call(s32[1]{0:T(128)} %bitcast.4.bit_ref, f32[256,1024]{1,0:T(8,128)S(1)} %copy-done.9, f32[16,512]{1,0:T(8,128)S(1)} %get-tuple-element.44.low_ref, bf16[272,1024]{1,0:T(8,128)(2,1)} %collective-permute-done.7.got_hbm), custom_call_target="tpu_custom_call" | custom-call | flops 1048576 | bytes 3145728 | tf_op jit(solution)/shard_map/fold/pallas_call | solution.py:401
  100.7 0.8 copy-done.10
  101.5 0.8 collective-permute-start.8
  102.2 8.6 %collective-permute-done.8.got_hbm = bf16[144,1024]{1,0:T(8,128)(2,1)} collective-permute-done((bf16[144,1024]{1,0:T(8,128)(2,1)}, bf16[144,1024]{1,0:T(8,128)(2,1)}, u32[]{:S(2)}, u32[]{:S(2)}) %collective-permute-start.8) | collective-permute-done | bytes 294944 | tf_op jit(solution)/shard_map/ppermute | solution.py:537
  110.8 1.0 copy-done.11
  111.9 1.7 %fold.4 = (f32[64,1024]{1,0:T(8,128)S(1)}, f32[16,512]{1,0:T(8,128)S(1)}, bf16[80,1024]{1,0:T(8,128)(2,1)}) custom-call(s32[1]{0:T(128)} %bitcast.3.bit_ref, f32[128,1024]{1,0:T(8,128)S(1)} %copy-done.11, f32[16,512]{1,0:T(8,128)S(1)} %get-tuple-element.47.low_ref, bf16[144,1024]{1,0:T(8,128)(2,1)} %collective-permute-done.8.got_hbm), custom_call_target="tpu_custom_call" | custom-call | flops 524288 | bytes 1572864 | tf_op jit(solution)/shard_map/fold/pallas_call | solution.py:401
  113.6 0.7 copy-done.12
  114.3 1.7 %collective-permute-start.9 = (bf16[80,1024]{1,0:T(8,128)(2,1)}, bf16[80,1024]{1,0:T(8,128)(2,1)}, u32[]{:S(2)}, u32[]{:S(2)}) collective-permute-start(bf16[80,1024]{1,0:T(8,128)(2,1)} %get-tuple-element.51), channel_id=1, source_target_pairs={{0,4},{2,6},{4,0},{6,2},{8,12},{10,14},{12,8},{14,10},{1,5},{3,7},... | collective-permute-start | bytes 491528 | tf_op jit(solution)/shard_map/ppermute | solution.py:537
  116.0 8.4 %collective-permute-done.9.got_hbm = bf16[80,1024]{1,0:T(8,128)(2,1)} collective-permute-done((bf16[80,1024]{1,0:T(8,128)(2,1)}, bf16[80,1024]{1,0:T(8,128)(2,1)}, u32[]{:S(2)}, u32[]{:S(2)}) %collective-permute-start.9) | collective-permute-done | bytes 163872 | tf_op jit(solution)/shard_map/ppermute | solution.py:537
  124.4 0.9 copy-done.13
  125.4 1.1 fold.5
  126.5 4.8 %collective-permute-start.10 = (bf16[48,1024]{1,0:T(8,128)(2,1)S(1)}, bf16[48,1024]{1,0:T(8,128)(2,1)S(1)}, u32[]{:S(2)}, u32[]{:S(2)}) collective-permute-start(bf16[48,1024]{1,0:T(8,128)(2,1)S(1)} %get-tuple-element.54), channel_id=1, source_target_pairs={{0,8},{2,10},{4,12},{6,14},{8,0},{10,2},{12,4},{14,6},{1,9},{3,11}... | collective-permute-start | bytes 294920 | tf_op jit(solution)/shard_map/ppermute | solution.py:537
  131.3 2.7 %up_gradient.1 = f32[16,3328]{1,0:T(8,128)} custom-call(f32[24,512]{1,0:T(8,128)S(1)} %add_add_fusion.small_ref.small_hbm, f32[1,3328]{1,0:T(1,128)S(1)} %reshape.33.magnitude_ref, bf16[512,3328]{1,0:T(8,128)(2,1)S(1)} %copy-done.4), custom_call_target="tpu_custom_call" | custom-call | flops 872415232 | bytes 4194304 | tf_op jit(solution)/shard_map/up_gradient/pallas_call | solution.py:483
  134.0 3.2 %collective-permute-done.10.got_hbm = bf16[48,1024]{1,0:T(8,128)(2,1)S(1)} collective-permute-done((bf16[48,1024]{1,0:T(8,128)(2,1)S(1)}, bf16[48,1024]{1,0:T(8,128)(2,1)S(1)}, u32[]{:S(2)}, u32[]{:S(2)}) %collective-permute-start.10) | collective-permute-done | bytes 98336 | tf_op jit(solution)/shard_map/ppermute | solution.py:537
  137.2 1.1 finish.1
  138.3 2.8 %output.1 = (bf16[32,3328]{1,0:T(8,128)(2,1)}, f32[1,3328]{1,0:T(1,128)S(1)}) custom-call(f32[24,512]{1,0:T(8,128)S(1)} %add_add_fusion.small_ref.small_hbm, f32[1,3328]{1,0:T(1,128)S(1)} %reshape.33.magnitude_ref, bf16[16,32,3584]{2,1,0:T(8,128)(2,1)} %all-to-all-done.1.parts_hbm), custom_call_target="tpu_custom_call" | custom-call | flops 1703936 | bytes 4194304 | tf_op jit(solution)/shard_map/output/pallas_call | solution.py:278
  (40 shorter events, 1.9 us)
Async XLA Ops:
  7.2 61.3 %all-gather.2.cloned.1.call-start = ((), (), s32[]{:S(2)}) async-start(), calls=%async_computation.2 | async-start | bytes 3620864 | tf_op jit(solution)/shard_map/all_gather | solution.py:523
  9.6 26.0 %all-to-all-start = ((bf16[8,32,1024]{2,1,0:T(8,128)(2,1)}), bf16[8,32,1024]{2,1,0:T(8,128)(2,1)S(1)}, u32[]{:S(2)}, u32[]{:S(2)}) async-start(bf16[8,32,1024]{2,1,0:T(8,128)(2,1)} %broadcast_in_dim.2), calls=%async_computation | async-start | bytes 1048576 | tf_op jit(solution)/shard_map/all_to_all | solution.py:503
  18.1 2.9 %copy-start.5 = (bf16[1024,3328]{1,0:T(8,128)(2,1)S(1)}, bf16[1024,3328]{1,0:T(8,128)(2,1)}, u32[]{:S(2)}) copy-start(bf16[1024,3328]{1,0:T(8,128)(2,1)} %weight_hbm.1) | copy-start | bytes 20447236
  21.0 0.9 copy-start.14
  21.9 0.8 copy-start.16
  22.8 14.7 %copy-start.17 = (f32[1024,16]{0,1:T(8,128)S(1)}, f32[1024,16]{0,1:T(8,128)}, u32[]{:S(2)}) copy-start(f32[1024,16]{0,1:T(8,128)} %param.8) | copy-start | bytes 196612
  28.2 2.8 %copy-start.18 = (bf16[1024,3328]{1,0:T(8,128)(2,1)}, bf16[1024,3328]{1,0:T(8,128)(2,1)S(1)}, u32[]{:S(2)}) copy-start(bf16[1024,3328]{1,0:T(8,128)(2,1)S(1)} %get-tuple-element.36.merged_hbm) | copy-start | bytes 20447236
  35.5 1.9 %collective-permute-start = (bf16[8,32,1024]{2,1,0:T(8,128)(2,1)S(1)}, bf16[8,32,1024]{2,1,0:T(8,128)(2,1)S(1)}, u32[]{:S(2)}, u32[]{:S(2)}) collective-permute-start(bf16[8,32,1024]{2,1,0:T(8,128)(2,1)S(1)} %all-to-all-done.own_hbm), channel_id=1, source_target_pairs={{0,1},{1,0},{2,3},{3,2},{4,5},{5,4},{6,7},{7,6},{8,9},{9,8},{10,11... | collective-permute-start | bytes 1572872 | tf_op jit(solution)/shard_map/ppermute | solution.py:527
  37.5 2.9 %copy-start.19 = (bf16[1024,3328]{1,0:T(8,128)(2,1)S(1)}, bf16[1024,3328]{1,0:T(8,128)(2,1)}, u32[]{:S(2)}) copy-start(bf16[1024,3328]{1,0:T(8,128)(2,1)} %copy-done.18) | copy-start | bytes 20447236
  47.2 1.9 %copy-start = (bf16[16,32,3584]{2,1,0:T(8,128)(2,1)}, bf16[16,32,3584]{2,1,0:T(8,128)(2,1)S(1)}, u32[]{:S(2)}) copy-start(bf16[16,32,3584]{2,1,0:T(8,128)(2,1)S(1)} %get-tuple-element.41.part_hbm) | copy-start | bytes 11010052
  49.1 1.0 copy-start.6
  50.1 5.3 %collective-permute-start.3 = (f32[24,512]{1,0:T(8,128)S(1)}, f32[24,512]{1,0:T(8,128)S(1)}, u32[]{:S(2)}, u32[]{:S(2)}) collective-permute-start(f32[24,512]{1,0:T(8,128)S(1)} %get-tuple-element.37), channel_id=1, source_target_pairs={{0,192},{64,0},{128,64},{192,128},{1,193},{65,1},{129,65},{193,129... | collective-permute-start | bytes 147464 | tf_op jit(solution)/shard_map/ppermute | solution.py:508
  52.8 7.4 %collective-permute-start.2 = (f32[24,512]{1,0:T(8,128)S(1)}, f32[24,512]{1,0:T(8,128)S(1)}, u32[]{:S(2)}, u32[]{:S(2)}) collective-permute-start(f32[24,512]{1,0:T(8,128)S(1)} %get-tuple-element.37), channel_id=1, source_target_pairs={{0,64},{64,128},{128,192},{192,0},{1,65},{65,129},{129,193},{193,1... | collective-permute-start | bytes 147464 | tf_op jit(solution)/shard_map/ppermute | solution.py:508
  52.8 7.6 %collective-permute-start.1 = (f32[24,512]{1,0:T(8,128)S(1)}, f32[24,512]{1,0:T(8,128)S(1)}, u32[]{:S(2)}, u32[]{:S(2)}) collective-permute-start(f32[24,512]{1,0:T(8,128)S(1)} %get-tuple-element.37), channel_id=1, source_target_pairs={{0,128},{64,192},{128,0},{192,64},{1,129},{65,193},{129,1},{193,65... | collective-permute-start | bytes 147464 | tf_op jit(solution)/shard_map/ppermute | solution.py:508
  60.5 5.6 %collective-permute-start.6 = (f32[24,512]{1,0:T(8,128)S(1)}, f32[24,512]{1,0:T(8,128)S(1)}, u32[]{:S(2)}, u32[]{:S(2)}) collective-permute-start(f32[24,512]{1,0:T(8,128)S(1)} %add_add_fusion.1), channel_id=1, source_target_pairs={{0,48},{16,0},{32,16},{48,32},{1,49},{17,1},{33,17},{49,33},{2,50}... | collective-permute-start | bytes 147464 | tf_op jit(solution)/shard_map/ppermute | solution.py:508
  61.0 6.0 %collective-permute-start.5 = (f32[24,512]{1,0:T(8,128)S(1)}, f32[24,512]{1,0:T(8,128)S(1)}, u32[]{:S(2)}, u32[]{:S(2)}) collective-permute-start(f32[24,512]{1,0:T(8,128)S(1)} %add_add_fusion.1), channel_id=1, source_target_pairs={{0,16},{16,32},{32,48},{48,0},{1,17},{17,33},{33,49},{49,1},{2,18}... | collective-permute-start | bytes 147464 | tf_op jit(solution)/shard_map/ppermute | solution.py:508
  62.6 5.8 %collective-permute-start.4 = (f32[24,512]{1,0:T(8,128)S(1)}, f32[24,512]{1,0:T(8,128)S(1)}, u32[]{:S(2)}, u32[]{:S(2)}) collective-permute-start(f32[24,512]{1,0:T(8,128)S(1)} %add_add_fusion.1), channel_id=1, source_target_pairs={{0,32},{16,48},{32,0},{48,16},{1,33},{17,49},{33,1},{49,17},{2,34}... | collective-permute-start | bytes 147464 | tf_op jit(solution)/shard_map/ppermute | solution.py:508
  68.5 2.0 %copy-start.1 = (bf16[16,32,3584]{2,1,0:T(8,128)(2,1)S(1)}, bf16[16,32,3584]{2,1,0:T(8,128)(2,1)}, u32[]{:S(2)}) copy-start(bf16[16,32,3584]{2,1,0:T(8,128)(2,1)} %copy-done) | copy-start | bytes 11010052
  70.5 2.0 %copy-start.3 = (bf16[512,3328]{1,0:T(8,128)(2,1)S(1)}, bf16[512,3328]{1,0:T(8,128)(2,1)}, u32[]{:S(2)}) copy-start(bf16[512,3328]{1,0:T(8,128)(2,1)} %all-gather.2.cloned.1.call-done.cot_hbm) | copy-start | bytes 10223620
  73.7 1.9 %copy-start.2 = (bf16[16,32,3584]{2,1,0:T(8,128)(2,1)}, bf16[16,32,3584]{2,1,0:T(8,128)(2,1)S(1)}, u32[]{:S(2)}) copy-start(bf16[16,32,3584]{2,1,0:T(8,128)(2,1)S(1)} %magnitude.1) | copy-start | bytes 11010052
  75.6 7.7 %copy-start.21 = (f32[3328]{0:T(1024)S(1)}, f32[3328]{0:T(1024)}, u32[]{:S(2)}) copy-start(f32[3328]{0:T(1024)} %param.10) | copy-start | bytes 39940
  75.6 7.7 %copy-start.4 = (bf16[512,3328]{1,0:T(8,128)(2,1)S(1)}, bf16[512,3328]{1,0:T(8,128)(2,1)}, u32[]{:S(2)}) copy-start(bf16[512,3328]{1,0:T(8,128)(2,1)} %all-gather.2.cloned.1.call-done.cot_hbm) | copy-start | bytes 10223620
  75.6 62.7 %all-to-all-start.1 = ((bf16[16,32,3584]{2,1,0:T(8,128)(2,1)}), bf16[16,32,3584]{2,1,0:T(8,128)(2,1)}, u32[]{:S(2)}, u32[]{:S(2)}) async-start(bf16[16,32,3584]{2,1,0:T(8,128)(2,1)} %copy-done.2), calls=%async_computation.1 | async-start | bytes 7340032 | tf_op jit(solution)/shard_map/all_to_all | solution.py:503
  83.3 0.9 copy-start.15
  84.3 2.9 %copy-start.20 = (bf16[1024,3328]{1,0:T(8,128)(2,1)S(1)}, bf16[1024,3328]{1,0:T(8,128)(2,1)}, u32[]{:S(2)}) copy-start(bf16[1024,3328]{1,0:T(8,128)(2,1)} %copy-done.18) | copy-start | bytes 20447236
  94.3 1.0 copy-start.8
  95.3 2.3 %collective-permute-start.7 = (bf16[272,1024]{1,0:T(8,128)(2,1)}, bf16[272,1024]{1,0:T(8,128)(2,1)}, u32[]{:S(2)}, u32[]{:S(2)}) collective-permute-start(bf16[272,1024]{1,0:T(8,128)(2,1)} %get-tuple-element.45), channel_id=1, source_target_pairs={{0,1},{1,0},{2,3},{3,2},{4,5},{5,4},{6,7},{7,6},{8,9},{9,8},{10,11... | collective-permute-start | bytes 1671176 | tf_op jit(solution)/shard_map/ppermute | solution.py:534
  97.6 1.2 copy-start.9
  100.7 0.8 copy-start.10
  101.5 9.4 %collective-permute-start.8 = (bf16[144,1024]{1,0:T(8,128)(2,1)}, bf16[144,1024]{1,0:T(8,128)(2,1)}, u32[]{:S(2)}, u32[]{:S(2)}) collective-permute-start(bf16[144,1024]{1,0:T(8,128)(2,1)} %get-tuple-element.48), channel_id=1, source_target_pairs={{0,2},{2,0},{4,6},{6,4},{8,10},{10,8},{12,14},{14,12},{1,3},{3,1},... | collective-permute-start | bytes 884744 | tf_op jit(solution)/shard_map/ppermute | solution.py:537
  110.8 1.0 copy-start.11
  113.6 0.7 copy-start.12
  114.3 10.1 %collective-permute-start.9 = (bf16[80,1024]{1,0:T(8,128)(2,1)}, bf16[80,1024]{1,0:T(8,128)(2,1)}, u32[]{:S(2)}, u32[]{:S(2)}) collective-permute-start(bf16[80,1024]{1,0:T(8,128)(2,1)} %get-tuple-element.51), channel_id=1, source_target_pairs={{0,4},{2,6},{4,0},{6,2},{8,12},{10,14},{12,8},{14,10},{1,5},{3,7},... | collective-permute-start | bytes 491528 | tf_op jit(solution)/shard_map/ppermute | solution.py:537
  116.0 21.2 %copy-start.7 = (bf16[8,2,32,1024]{3,2,1,0:T(8,128)(2,1)S(1)}, bf16[8,2,32,1024]{3,2,1,0:T(8,128)(2,1)}, u32[]{:S(2)}) copy-start(bf16[8,2,32,1024]{3,2,1,0:T(8,128)(2,1)} %copy-done.6) | copy-start | bytes 3145732
  124.4 1.0 copy-start.13
  126.5 10.7 %collective-permute-start.10 = (bf16[48,1024]{1,0:T(8,128)(2,1)S(1)}, bf16[48,1024]{1,0:T(8,128)(2,1)S(1)}, u32[]{:S(2)}, u32[]{:S(2)}) collective-permute-start(bf16[48,1024]{1,0:T(8,128)(2,1)S(1)} %get-tuple-element.54), channel_id=1, source_target_pairs={{0,8},{2,10},{4,12},{6,14},{8,0},{10,2},{12,4},{14,6},{1,9},{3,11}... | collective-permute-start | bytes 294920 | tf_op jit(solution)/shard_map/ppermute | solution.py:537
Sparse Core Ops, SparseCore 0:
  10.5 57.9 all-gather.1

commit v4 on v3

v4 whole, which is shorter than its diff:
```python
import jax
import jax.numpy as jnp
from jax import lax
from jax.experimental import pallas as pl
from jax.experimental.pallas import tpu as pltpu
from jax.sharding import Mesh
from jax.sharding import PartitionSpec as P

adapter_scale = 2.0
epsilon = 1e-06
bf16 = jnp.bfloat16
f32 = jnp.float32
ROW = ("x", "y")
COL = ("z", "c")
CHUNK = 512
RANK = 16
EXTRA = 256
MIB = 1024 * 1024
LIMIT = 62 * MIB
ANY = pl.BlockSpec(memory_space=pl.ANY)
SMEM = pl.BlockSpec(memory_space=pltpu.SMEM)


def pieces(value):
    high = value.astype(bf16)
    rest = value - high.astype(f32)
    mid = rest.astype(bf16)
    low = (rest - mid.astype(f32)).astype(bf16)
    return high, mid, low


def dot(left, right, left_dim, right_dim):
    return lax.dot_general(
        left, right, (((left_dim,), (right_dim,)), ((), ())), preferred_element_type=f32
    )


def three(left, right, left_dim, right_dim):
    out = dot(jnp.concatenate(pieces(left), axis=0), right, left_dim, right_dim)
    return out[:RANK] + out[RANK : 2 * RANK] + out[2 * RANK :]


def chunks_of(width):
    return [(at, min(CHUNK, width - at)) for at in range(0, width, CHUNK)]


def call(body, flops, moved, **options):
    return pl.pallas_call(
        body,
        compiler_params=pltpu.CompilerParams(vmem_limit_bytes=LIMIT),
        cost_estimate=pl.CostEstimate(flops=flops, bytes_accessed=moved, transcendentals=0),
        **options,
    )


def begin(source, target, sem):
    copy = pltpu.make_async_copy(source, target, sem)
    copy.start()
    return copy


def merge_kernel(
    shard_ref, tokens_hbm, down_hbm, up_hbm, weight_hbm, merged_hbm, small_hbm,
    tokens, down, up, weight, merged, small, up_cat, totals, small_sem, in_sem, out_sem,
):
    depth, width = weight.shape
    rows, tile = 256, 256
    chunks = chunks_of(width)
    steps = [slice(at, at + rows) for at in range(0, depth, rows)]
    first = begin(up_hbm, up, small_sem.at[0]), begin(down_hbm, down, small_sem.at[1])
    later = begin(tokens_hbm, tokens, small_sem.at[2])
    fetches = [begin(weight_hbm.at[p], weight.at[p], in_sem.at[j]) for j, p in enumerate(steps)]
    totals[...] = jnp.zeros_like(totals)
    for copy in first:
        copy.wait()
    for at in range(0, width, tile):
        cols = slice(at, at + tile)
        u1, u2, u3 = pieces(up[:, cols])
        up_cat[:, cols] = jnp.concatenate([u1, u2, u1, u3, u1, u2], axis=0)
    d1, d2, d3 = pieces(down[...] * adapter_scale)
    down_cat = jnp.concatenate([d1, d1, d2, d1, d3, d2], axis=0)
    stores = []
    for j, part in enumerate(steps):
        fetches[j].wait()
        for at in range(0, width, tile):
            cols = slice(at, at + tile)
            value = weight[part, cols].astype(f32) + dot(down_cat[:, part], up_cat[:, cols], 0, 0)
            merged[part, cols] = value.astype(bf16)
            totals[:, cols] += jnp.sum((value * value).reshape(rows // 8, 8, tile), axis=0)
        stores.append(begin(merged.at[part], merged_hbm.at[part], out_sem.at[j]))
    later.wait()
    proj = three(down[...], tokens[...], 1, 1)
    owner = lax.broadcasted_iota(jnp.int32, (RANK, CHUNK), 1) // 32
    small[:RANK, :] = jnp.where(owner == shard_ref[0], jnp.concatenate([proj] * 16, axis=1), 0.0)
    small[RANK:, :] = jnp.zeros((8, CHUNK), f32)
    for j, (at, size) in enumerate(chunks):
        sums = jnp.sum(totals[:, at : at + size], axis=0, keepdims=True)
        small[RANK + j : RANK + j + 1, :size] = sums
    stores.append(begin(small, small_hbm, small_sem.at[0]))
    for copy in stores:
        copy.wait()


def merge(shard, tokens, down_t, up, weight):
    depth, width = weight.shape
    return call(
        merge_kernel,
        12 * depth * width,
        4 * depth * width,
        in_specs=[SMEM, ANY, ANY, ANY, ANY],
        out_specs=[ANY, ANY],
        out_shape=[
            jax.ShapeDtypeStruct((depth, width), bf16),
            jax.ShapeDtypeStruct((RANK + 8, CHUNK), f32),
        ],
        scratch_shapes=[
            pltpu.VMEM(tokens.shape, bf16),
            pltpu.VMEM((RANK, depth), f32),
            pltpu.VMEM((RANK, width), f32),
            pltpu.VMEM((depth, width), bf16),
            pltpu.VMEM((depth, width), bf16),
            pltpu.VMEM((RANK + 8, CHUNK), f32),
            pltpu.VMEM((6 * RANK, width), bf16),
            pltpu.VMEM((8, width), f32),
            pltpu.SemaphoreType.DMA((3,)),
            pltpu.SemaphoreType.DMA((4,)),
            pltpu.SemaphoreType.DMA((4,)),
        ],
        name="merge",
    )(shard, tokens, down_t, up, weight)


def forward_kernel(*refs):
    place_ref, tokens_hbm, merged_hbm = refs[:3]
    halves = refs[3:7], refs[7:11]
    part_hbm, cot_hbm = refs[11:13]
    tokens, merged, cot, part, extra, cot_sem, in_sem, out_sem = refs[13:]
    x, y = place_ref[0], place_ref[1]
    depth, width = merged.shape
    chunks = chunks_of(width)
    first = begin(tokens_hbm, tokens, in_sem.at[len(chunks)])
    fetches, stores, arrived = [], [], []
    for j, (at, size) in enumerate(chunks):
        cols = slice(at, at + size)
        fetches.append(begin(merged_hbm.at[:, cols], merged.at[:, cols], in_sem.at[j]))
    for half, arrays in enumerate(halves):
        rows = slice(16 * half, 16 * half + 16)
        for j, array in enumerate(arrays):
            for k in range(4):
                near, far = (k, j) if half == 0 else (j, k)
                target = cot.at[lax.rem(x + 4 - near, 4), lax.rem(y + 4 - far, 4), rows]
                source = array.at[16 * k : 16 * k + 16]
                arrived.append(begin(source, target, cot_sem.at[16 * half + 4 * j + k]))
    first.wait()
    all_tokens = tokens[...].reshape(512, depth)
    rows = []
    for j, (at, size) in enumerate(chunks):
        fetches[j].wait()
        cols = slice(at, at + size)
        product = dot(all_tokens, merged[:, cols], 1, 0)
        part[:, :, cols] = product.astype(bf16).reshape(16, 32, size)
        stores.append(begin(part.at[:, :, cols], part_hbm.at[:, :, cols], out_sem.at[j]))
        if j == 0:
            for copy in arrived:
                copy.wait()
            stores.append(begin(cot, cot_hbm, cot_sem.at[0]))
        weighted = product * cot[:, :, :, cols].reshape(512, size).astype(f32)
        total = jnp.sum(weighted, axis=0, keepdims=True)
        rows += [total[:, k : k + EXTRA] for k in range(0, size, EXTRA)]
    rows += [jnp.zeros((1, EXTRA), f32)] * (16 - len(rows))
    value = jnp.concatenate(rows, axis=0)
    high = value.astype(bf16)
    rest = (value - high.astype(f32)).astype(bf16)
    extra[...] = jnp.broadcast_to(jnp.concatenate([high, rest], axis=0)[None], extra.shape)
    stores.append(begin(extra, part_hbm.at[:, :, width:], out_sem.at[len(chunks)]))
    for copy in stores:
        copy.wait()


def forward(place, tokens, merged_low, first_half, second_half):
    depth, width = merged_low.shape
    count = len(chunks_of(width)) + 1
    return call(
        forward_kernel,
        2 * 512 * depth * width,
        16 * MIB,
        in_specs=[SMEM] + [ANY] * 10,
        out_specs=[ANY, ANY],
        out_shape=[
            jax.ShapeDtypeStruct((16, 32, width + EXTRA), bf16),
            jax.ShapeDtypeStruct((4, 4, 32, width), bf16),
        ],
        scratch_shapes=[
            pltpu.VMEM((16, 32, depth), bf16),
            pltpu.VMEM((depth, width), bf16),
            pltpu.VMEM((4, 4, 32, width), bf16),
            pltpu.VMEM((16, 32, width), bf16),
            pltpu.VMEM((16, 32, EXTRA), bf16),
            pltpu.SemaphoreType.DMA((32,)),
            pltpu.SemaphoreType.DMA((count,)),
            pltpu.SemaphoreType.DMA((count,)),
        ],
        name="forward",
    )(place, tokens, merged_low, *first_half, *second_half)


def output_kernel(
    small_hbm, magnitude_hbm, parts_hbm, out_hbm, mag_hbm,
    small, magnitude, parts, out, mag, small_sem, sem, out_sem,
):
    width = out.shape[1]
    chunks = chunks_of(width)
    first = (
        begin(small_hbm, small, small_sem.at[0]),
        begin(magnitude_hbm, magnitude, small_sem.at[1]),
        begin(parts_hbm.at[:, :, width:], parts.at[:, :, width:], sem.at[len(chunks)]),
    )
    fetches, stores = [], []
    for j, (at, size) in enumerate(chunks):
        cols = slice(at, at + size)
        fetches.append(begin(parts_hbm.at[:, :, cols], parts.at[:, :, cols], sem.at[j]))

    def added(cols):
        total = parts[0, :, cols].astype(f32)
        for r in range(1, 16):
            total += parts[r, :, cols].astype(f32)
        return total

    for copy in first:
        copy.wait()
    extra = added(slice(width, width + EXTRA))
    extra = extra[:16] + extra[16:]
    for j, (at, size) in enumerate(chunks):
        fetches[j].wait()
        cols = slice(at, at + size)
        norm = jnp.sqrt(small[RANK + j : RANK + j + 1, :size] + epsilon)
        out[:, cols] = (added(cols) * (magnitude[:, cols] / norm)).astype(bf16)
        stores.append(begin(out.at[:, cols], out_hbm.at[:, cols], out_sem.at[j]))
        for k in range(0, size, EXTRA):
            row = (at + k) // EXTRA
            mag[:, at + k : at + k + EXTRA] = extra[row : row + 1] / norm[:, k : k + EXTRA]
    stores.append(begin(mag, mag_hbm, out_sem.at[len(chunks)]))
    for copy in stores:
        copy.wait()


def output_of(small, magnitude, parts):
    width = magnitude.shape[1]
    count = len(chunks_of(width)) + 1
    return call(
        output_kernel,
        16 * 32 * width,
        4 * MIB,
        in_specs=[ANY, ANY, ANY],
        out_specs=[ANY, ANY],
        out_shape=[
            jax.ShapeDtypeStruct((32, width), bf16),
            jax.ShapeDtypeStruct((1, width), f32),
        ],
        scratch_shapes=[
            pltpu.VMEM(small.shape, f32),
            pltpu.VMEM((1, width), f32),
            pltpu.VMEM(parts.shape, bf16),
            pltpu.VMEM((32, width), bf16),
            pltpu.VMEM((1, width), f32),
            pltpu.SemaphoreType.DMA((2,)),
            pltpu.SemaphoreType.DMA((count,)),
            pltpu.SemaphoreType.DMA((count,)),
        ],
        name="output",
    )(small, magnitude, parts)


def pack(low, out):
    high = low.astype(bf16)
    rest = (low - high.astype(f32)).astype(bf16)
    out[:, :CHUNK] = high
    out[:, CHUNK:] = rest
    return high.astype(f32) + rest.astype(f32)


def unpack(got):
    got = got.astype(f32)
    return got[:, :CHUNK] + got[:, CHUNK:]


def backward_kernel(
    core_ref, small_hbm, magnitude_hbm, up_hbm, cot_hbm, merged_hbm,
    own_hbm, send_hbm, small, magnitude, up, cot, merged, total, own, send, first_sem, sem,
):
    core = core_ref[0]
    width = merged.shape[1]
    chunks = chunks_of(width)
    first = (
        begin(small_hbm, small, first_sem.at[0]),
        begin(up_hbm, up, first_sem.at[1]),
        begin(magnitude_hbm, magnitude, first_sem.at[2]),
    )
    fetches = []
    for j, (at, size) in enumerate(chunks):
        cols = slice(at, at + size)
        fetches.append(
            (
                begin(cot_hbm.at[:, cols], cot.at[:, cols], sem.at[0, j]),
                begin(merged_hbm.at[:, cols], merged.at[:, cols], sem.at[1, j]),
            )
        )
    for copy in first:
        copy.wait()
    low = jnp.zeros((RANK, CHUNK), f32)
    for j, (at, size) in enumerate(chunks):
        for copy in fetches[j]:
            copy.wait()
        cols = slice(at, at + size)
        norm = jnp.sqrt(small[RANK + j : RANK + j + 1, :size] + epsilon)
        grad = (cot[:, cols].astype(f32) * (magnitude[:, cols] / norm)).astype(bf16)
        product = dot(grad, merged[:, cols], 1, 1)
        if j == 0:
            total[...] = product
        else:
            total[...] += product
        low += three(up[:, cols], grad, 1, 1)
    for z in range(8):
        theirs = pl.ds(pl.multiple_of((2 * z + 1 - core) * 32, 32), 32)
        send[32 * z : 32 * z + 32, :] = total[theirs, :].astype(bf16)
    pack(low, send.at[256:272, :])
    first = begin(send, send_hbm, first_sem.at[0])
    for z in range(8):
        mine = pl.ds(pl.multiple_of((2 * z + core) * 32, 32), 32)
        own[32 * z : 32 * z + 32, :] = total[mine, :].astype(bf16)
    own[256:272, :] = send[256:272, :]
    begin(own, own_hbm, first_sem.at[1]).wait()
    first.wait()


def backward(core, small, magnitude, up, cot, merged_low):
    depth, width = merged_low.shape
    count = len(chunks_of(width))
    return call(
        backward_kernel,
        2 * 512 * depth * width,
        12 * MIB,
        in_specs=[SMEM] + [ANY] * 5,
        out_specs=[ANY, ANY],
        out_shape=[jax.ShapeDtypeStruct((272, depth), bf16)] * 2,
        scratch_shapes=[
            pltpu.VMEM(small.shape, f32),
            pltpu.VMEM((1, width), f32),
            pltpu.VMEM((RANK, width), f32),
            pltpu.VMEM((512, width), bf16),
            pltpu.VMEM((depth, width), bf16),
            pltpu.VMEM((512, depth), f32),
            pltpu.VMEM((272, depth), bf16),
            pltpu.VMEM((272, depth), bf16),
            pltpu.SemaphoreType.DMA((3,)),
            pltpu.SemaphoreType.DMA((2, count)),
        ],
        name="backward",
    )(core, small, magnitude, up, cot, merged_low)


def pair_kernel(z_ref, own_hbm, got_hbm, *refs):
    out_hbm = refs[:8]
    own, got, send, sem, out_sem = refs[8:]
    z = z_ref[0]
    copies = begin(own_hbm, own, sem.at[0]), begin(got_hbm, got, sem.at[1])
    for copy in copies:
        copy.wait()
    low = unpack(own[256:272, :]) + unpack(got[256:272, :])
    pack(low, send.at[0, 32:48, :])
    stores = []
    for k in [1, 7, 2, 6, 3, 5, 4, 0]:
        block = pl.ds(pl.multiple_of(lax.rem(z + k, 8) * 32, 32), 32)
        send[k, :32, :] = (own[block, :].astype(f32) + got[block, :].astype(f32)).astype(bf16)
        if k:
            send[k, 32:48, :] = send[0, 32:48, :]
        stores.append(begin(send.at[k], out_hbm[k], out_sem.at[k]))
    for copy in stores:
        copy.wait()


def pair(z, own, got):
    rows, depth = own.shape
    return call(
        pair_kernel,
        4 * rows * depth,
        6 * rows * depth,
        in_specs=[SMEM, ANY, ANY],
        out_specs=[ANY] * 8,
        out_shape=[jax.ShapeDtypeStruct((48, depth), bf16)] * 8,
        scratch_shapes=[
            pltpu.VMEM((rows, depth), bf16),
            pltpu.VMEM((rows, depth), bf16),
            pltpu.VMEM((8, 48, depth), bf16),
            pltpu.SemaphoreType.DMA((2,)),
            pltpu.SemaphoreType.DMA((8,)),
        ],
        name="pair",
    )(z, own, got)


def finish_kernel(z_ref, tokens_hbm, *refs):
    parts_hbm = refs[:8]
    grad_hbm, down_hbm, parts, tokens, lows, grad, down, sem, out_sem = refs[8:]
    z = z_ref[0]
    later = begin(tokens_hbm, tokens, sem.at[8])
    copies = [begin(parts_hbm[k], parts.at[k], sem.at[k]) for k in range(8)]
    for copy in copies:
        copy.wait()
    total = parts[0, :32, :].astype(f32)
    for k in range(1, 8):
        total += parts[k, :32, :].astype(f32)
    grad[...] = total.astype(bf16)
    first = begin(grad, grad_hbm, out_sem.at[0])
    for k in range(8):
        lows[lax.rem(z + 8 - k, 8)] = unpack(parts[k, 32:48, :])
    low = lows[0]
    for k in range(1, 8):
        low += lows[k]
    later.wait()
    down[...] = three(low * adapter_scale, tokens[...], 1, 0)
    begin(down, down_hbm, out_sem.at[1]).wait()
    first.wait()


def finish(z, tokens, parts):
    depth = tokens.shape[1]
    return call(
        finish_kernel,
        2 * 512 * 256 * depth,
        2 * MIB,
        in_specs=[SMEM] + [ANY] * 9,
        out_specs=[ANY, ANY],
        out_shape=[
            jax.ShapeDtypeStruct((32, depth), bf16),
            jax.ShapeDtypeStruct((RANK, depth), f32),
        ],
        scratch_shapes=[
            pltpu.VMEM((8, 48, depth), bf16),
            pltpu.VMEM(tokens.shape, bf16),
            pltpu.VMEM((8, RANK, CHUNK), f32),
            pltpu.VMEM((32, depth), bf16),
            pltpu.VMEM((RANK, depth), f32),
            pltpu.SemaphoreType.DMA((9,)),
            pltpu.SemaphoreType.DMA((2,)),
        ],
        name="finish",
    )(z, tokens, *parts)


def up_kernel(
    proj_hbm, small_hbm, magnitude_hbm, cot_hbm, out_hbm,
    proj, small, magnitude, cot, out, first_sem, sem, out_sem,
):
    width = cot.shape[1]
    chunks = chunks_of(width)
    first = (
        begin(proj_hbm, proj, first_sem.at[0]),
        begin(small_hbm, small, first_sem.at[1]),
        begin(magnitude_hbm, magnitude, first_sem.at[2]),
    )
    fetches, stores = [], []
    for j, (at, size) in enumerate(chunks):
        cols = slice(at, at + size)
        fetches.append(begin(cot_hbm.at[:, cols], cot.at[:, cols], sem.at[j]))
    for copy in first:
        copy.wait()
    for j, (at, size) in enumerate(chunks):
        fetches[j].wait()
        cols = slice(at, at + size)
        norm = jnp.sqrt(small[RANK + j : RANK + j + 1, :size] + epsilon)
        grad = (cot[:, cols].astype(f32) * (magnitude[:, cols] / norm)).astype(bf16)
        out[:, cols] = three(proj[...] * adapter_scale, grad, 1, 0)
        stores.append(begin(out.at[:, cols], out_hbm.at[:, cols], out_sem.at[j]))
    for copy in stores:
        copy.wait()


def up_gradient_of(proj, small, magnitude, cot):
    tokens, width = cot.shape
    count = len(chunks_of(width))
    return call(
        up_kernel,
        2 * 512 * 256 * width,
        4 * MIB,
        in_specs=[ANY] * 4,
        out_specs=ANY,
        out_shape=jax.ShapeDtypeStruct((RANK, width), f32),
        scratch_shapes=[
            pltpu.VMEM(proj.shape, f32),
            pltpu.VMEM(small.shape, f32),
            pltpu.VMEM((1, width), f32),
            pltpu.VMEM(cot.shape, bf16),
            pltpu.VMEM((RANK, width), f32),
            pltpu.SemaphoreType.DMA((3,)),
            pltpu.SemaphoreType.DMA((count,)),
            pltpu.SemaphoreType.DMA((count,)),
        ],
        name="up_gradient",
    )(proj, small, magnitude, cot)


def shifted(value, axis, size):
    return [
        lax.ppermute(value, axis, [(i, (i + k) % size) for i in range(size)])
        for k in range(1, size)
    ]


def around(value, axis):
    one, two, other = shifted(value, axis, 4)
    return (value + two) + (one + other)


def add_col(value):
    value = value + lax.ppermute(value, "c", [(0, 1), (1, 0)])
    for k in (1, 2, 4):
        value = value + lax.ppermute(value, "z", [(i, i ^ k) for i in range(8)])
    return value


def on_device(tokens, weight, down_adapter, up_adapter, magnitude, out_cotangent):
    x, y, z, core = [lax.axis_index(name).astype(jnp.int32) for name in ROW + COL]
    shard = (2 * z + core).reshape(1)
    place = jnp.stack([x, y])
    down_t = down_adapter.T
    magnitude = magnitude.reshape(1, -1)
    tokens_full = lax.all_gather(tokens, COL, axis=0)
    first, second = out_cotangent[:16], out_cotangent[16:]
    first = [first] + shifted(first, "x", 4)
    second = [second] + shifted(second, "y", 4)
    merged_low, small = merge(shard, tokens, down_t, up_adapter, weight)
    small = around(small, "x")
    first = jnp.concatenate(first, axis=0)
    second = jnp.concatenate(second, axis=0)
    first, second, small = lax.optimization_barrier((first, second, small))
    first = [first] + shifted(first, "y", 4)
    second = [second] + shifted(second, "x", 4)
    small = around(small, "y")
    first, second, small = lax.optimization_barrier((first, second, small))
    part, cot_full = forward(place, tokens_full, merged_low, first, second)
    cot_full = cot_full.reshape(512, -1)
    parts = lax.all_to_all(part, ROW, 0, 0, tiled=False)
    own, send = backward(core.reshape(1), small, magnitude, up_adapter, cot_full, merged_low)
    got = lax.ppermute(send, "c", [(0, 1), (1, 0)])
    blocks = list(pair(z.reshape(1), own, got))
    for k in range(1, 8):
        blocks[k] = lax.ppermute(blocks[k], "z", [(i, (i + k) % 8) for i in range(8)])
    grad_tokens, down_gradient = finish(z.reshape(1), tokens_full.reshape(512, -1), blocks)
    proj = add_col(small[:RANK])
    up_gradient = up_gradient_of(proj, small, magnitude, cot_full)
    output, grad_magnitude = output_of(small, magnitude, parts)
    return (output, grad_tokens, grad_magnitude.reshape(-1), up_gradient, down_gradient.T)


def solution(mesh):
    split = Mesh(mesh.devices.reshape(4, 4, 8, 2), ROW + COL)
    return jax.shard_map(
        on_device,
        mesh=split,
        in_specs=(P(COL, ROW), P(ROW, COL), P(ROW, None), P(None, COL), P(COL), P(ROW, COL)),
        out_specs=(P(ROW, COL), P(COL, ROW), P(COL), P(None, COL), P(ROW, None)),
        check_vma=False,
    )
```

time: 150 us -> 155 us (1.033)
  starting transfers between devices: 34.2 us -> 63.9 us
  local copies, waits for them, and re-layouts: 30.4 us -> 2.62 us
  Pallas kernels: 31.8 us -> 38.9 us
  waiting for transfers between devices: 37.3 us -> 30.2 us
  other arithmetic: 0.67 us -> 4.13 us
    ppermute x11 -> x30, starting transfers between devices: 18 us -> 54.1 us  [the longest x18 27.4 us: shifted(): lax.ppermute(value, axis, [(i, (i + k) % size) for i in range(size)])]
    unnamed x44 -> x34, local copies, waits for them, and re-layouts: 28.7 us -> 1.99 us
    pallas_call x10 -> x7, Pallas kernels: 31.8 us -> 38.9 us  [the longest x1 10.7 us: forward(): call(forward_kernel, 2 * 512 * depth * width, 16 * MIB, in_specs=[SMEM] +...]
    all_to_all x2 -> x1, starting transfers between devices: 16.2 us -> 9.71 us  [on_device(): parts = lax.all_to_all(part, ROW, 0, 0, tiled=False)]
    all_to_all x2 -> x1, waiting for transfers between devices: 4.55 us -> 0.01 us  [on_device(): parts = lax.all_to_all(part, ROW, 0, 0, tiled=False)]
    ppermute x11 -> x30, waiting for transfers between devices: 32.1 us -> 30.2 us  [the longest x18 20.2 us: shifted(): lax.ppermute(value, axis, [(i, (i + k) % size) for i in range(size)])]
    broadcast_in_dim x1 -> x0, local copies, waits for them, and re-layouts: 1.69 us -> none  [on_device(): jnp.broadcast_to(tokens[None], (8,) + tokens.shape)]
  transfers between devices with their start and end apart: 14 -> 32, of which waited for: 11 -> 12; matrix products, arithmetic and copies ran while one was open for 1% -> 2% of each run, Pallas kernels for 19% -> 12%
where the time goes in v4:
time: 155 us; the launch traced here: 154 us
  starting transfers between devices  63.9 us (41%)
  Pallas kernels  38.9 us (25%)
  waiting for transfers between devices  30.2 us (19%)
  between operations  14.3 us (9%)
  other arithmetic  4.13 us (3%)
  local copies, waits for them, and re-layouts  2.62 us (2%)
    ppermute x18, starting transfers between devices, shifted(): lax.ppermute(value, axis, [(i, (i + k) % size) for i in range(size)])  27.4 us
    ppermute x18, waiting for transfers between devices, shifted(): lax.ppermute(value, axis, [(i, (i + k) % size) for i in range(size)])  20.2 us
    ppermute x7, starting transfers between devices, on_device(): lax.ppermute(blocks[k], 'z', [(i, (i + k) % 8) for i in range(8)])  16.4 us
    pallas_call x1, Pallas kernels, forward(): call(forward_kernel, 2 * 512 * depth * width, 16 * MIB, in_specs=[SMEM] +...  10.7 us
    pallas_call x1, Pallas kernels, backward(): call(backward_kernel, 2 * 512 * depth * width, 12 * MIB, in_specs=[SMEM]...  10.1 us
    ppermute x3, starting transfers between devices, add_col(): value = value + lax.ppermute(value, 'z', [(i, i ^ k) for i in range(8)])  9.8 us
    all_to_all x1, starting transfers between devices, on_device(): parts = lax.all_to_all(part, ROW, 0, 0, tiled=False)  9.71 us
    ppermute x7, waiting for transfers between devices, on_device(): lax.ppermute(blocks[k], 'z', [(i, (i + k) % 8) for i in range(8)])  6.26 us
  transfers between devices with their start and end apart: 32, of which 12 were waited for; matrix products, arithmetic and copies ran while one was open for 2% of the time, Pallas kernels for 12%

profile of v4, /device:TPU:8, one launch (start us, length us, event | category | flops | bytes accessed | tf_op | source)
XLA Modules:
  0.0 154.0 jit_solution(7713583777563813955)
XLA Ops:
  7.2 6.0 %merge.1 = (bf16[1024,3328]{1,0:T(8,128)(2,1)}, f32[24,512]{1,0:T(8,128)}) custom-call(s32[1]{0:T(128)} %bitcast.shard_ref, bf16[32,1024]{1,0:T(8,128)(2,1)} %tokens_hbm.1, f32[16,1024]{1,0:T(8,128)} %bitcast.12, f32[16,3328]{1,0:T(8,128)} %up_hbm.3, bf16[1024,3328]{1,0:T(8,128)(2,1)} %weight_hbm.1), custom_call_target="tpu_custom_call" | custom-call | flops 40894464 | bytes 13631488 | tf_op jit(solution)/shard_map/merge/pallas_call | solution.py:106
  13.3 3.1 %collective-permute-start.6 = (f32[24,512]{1,0:T(8,128)}, f32[24,512]{1,0:T(8,128)S(1)}, u32[]{:S(2)}, u32[]{:S(2)}) collective-permute-start(f32[24,512]{1,0:T(8,128)} %get-tuple-element.35), channel_id=1, source_target_pairs={{0,128},{64,192},{128,0},{192,64},{1,129},{65,193},{129,1},{193,65... | collective-permute-start | bytes 147464 | tf_op jit(solution)/shard_map/ppermute | solution.py:505
  16.4 0.6 collective-permute-start.7
  17.0 2.6 %collective-permute-start.8 = (f32[24,512]{1,0:T(8,128)}, f32[24,512]{1,0:T(8,128)S(1)}, u32[]{:S(2)}, u32[]{:S(2)}) collective-permute-start(f32[24,512]{1,0:T(8,128)} %get-tuple-element.35), channel_id=1, source_target_pairs={{0,192},{64,0},{128,64},{192,128},{1,193},{65,1},{129,65},{193,129... | collective-permute-start | bytes 147464 | tf_op jit(solution)/shard_map/ppermute | solution.py:505
  19.6 1.7 %collective-permute-start.3 = (bf16[16,3328]{1,0:T(8,128)(2,1)S(1)}, bf16[16,3328]{1,0:T(8,128)(2,1)S(1)}, u32[]{:S(2)}, u32[]{:S(2)}) collective-permute-start(bf16[16,3328]{1,0:T(8,128)(2,1)S(1)} %get-tuple-element.65), channel_id=1, source_target_pairs={{0,16},{16,32},{32,48},{48,0},{1,17},{17,33},{33,49},{49,1},{2,18}... | collective-permute-start | bytes 319496 | tf_op jit(solution)/shard_map/ppermute | solution.py:505
  21.3 0.9 collective-permute-start.4
  22.3 2.5 %collective-permute-start.5 = (bf16[16,3328]{1,0:T(8,128)(2,1)S(1)}, bf16[16,3328]{1,0:T(8,128)(2,1)S(1)}, u32[]{:S(2)}, u32[]{:S(2)}) collective-permute-start(bf16[16,3328]{1,0:T(8,128)(2,1)S(1)} %get-tuple-element.65), channel_id=1, source_target_pairs={{0,48},{16,0},{32,16},{48,32},{1,49},{17,1},{33,17},{49,33},{2,50}... | collective-permute-start | bytes 319496 | tf_op jit(solution)/shard_map/ppermute | solution.py:505
  24.8 1.5 collective-permute-start.1
  26.2 0.8 add_add_fusion.1
  27.1 1.9 %collective-permute-start.2 = (bf16[16,3328]{1,0:T(8,128)(2,1)S(1)}, bf16[16,3328]{1,0:T(8,128)(2,1)S(1)}, u32[]{:S(2)}, u32[]{:S(2)}) collective-permute-start(bf16[16,3328]{1,0:T(8,128)(2,1)S(1)} %get-tuple-element.66), channel_id=1, source_target_pairs={{0,192},{64,0},{128,64},{192,128},{1,193},{65,1},{129,65},{193,129... | collective-permute-start | bytes 319496 | tf_op jit(solution)/shard_map/ppermute | solution.py:505
  29.0 2.9 %collective-permute-done = bf16[16,3328]{1,0:T(8,128)(2,1)S(1)} collective-permute-done((bf16[16,3328]{1,0:T(8,128)(2,1)S(1)}, bf16[16,3328]{1,0:T(8,128)(2,1)S(1)}, u32[]{:S(2)}, u32[]{:S(2)}) %collective-permute-start) | collective-permute-done | bytes 106528 | tf_op jit(solution)/shard_map/ppermute | solution.py:505
  31.8 0.9 collective-permute-done.2
  33.1 3.3 %collective-permute-start.15 = (f32[24,512]{1,0:T(8,128)S(1)}, f32[24,512]{1,0:T(8,128)S(1)}, u32[]{:S(2)}, u32[]{:S(2)}) collective-permute-start(f32[24,512]{1,0:T(8,128)S(1)} %add_add_fusion.1), channel_id=1, source_target_pairs={{0,32},{16,48},{32,0},{48,16},{1,33},{17,49},{33,1},{49,17},{2,34}... | collective-permute-start | bytes 147464 | tf_op jit(solution)/shard_map/ppermute | solution.py:505
  36.3 2.0 %collective-permute-start.17 = (f32[24,512]{1,0:T(8,128)S(1)}, f32[24,512]{1,0:T(8,128)S(1)}, u32[]{:S(2)}, u32[]{:S(2)}) collective-permute-start(f32[24,512]{1,0:T(8,128)S(1)} %add_add_fusion.1), channel_id=1, source_target_pairs={{0,48},{16,0},{32,16},{48,32},{1,49},{17,1},{33,17},{49,33},{2,50}... | collective-permute-start | bytes 147464 | tf_op jit(solution)/shard_map/ppermute | solution.py:505
  38.4 2.6 %collective-permute-start.11 = (bf16[64,3328]{1,0:T(8,128)(2,1)S(1)}, bf16[64,3328]{1,0:T(8,128)(2,1)S(1)}, u32[]{:S(2)}, u32[]{:S(2)}) collective-permute-start(bf16[64,3328]{1,0:T(8,128)(2,1)S(1)} %pad_maximum_fusion.refs_3_), channel_id=1, source_target_pairs={{0,48},{16,0},{32,16},{48,32},{1,49},{17,1},{33,17},{49,33},{2,50}... | collective-permute-start | bytes 1277960 | tf_op jit(solution)/shard_map/ppermute | solution.py:505
  40.9 7.2 %collective-permute-done.15 = f32[24,512]{1,0:T(8,128)S(1)} collective-permute-done((f32[24,512]{1,0:T(8,128)S(1)}, f32[24,512]{1,0:T(8,128)S(1)}, u32[]{:S(2)}, u32[]{:S(2)}) %collective-permute-start.15) | collective-permute-done | bytes 49184 | tf_op jit(solution)/shard_map/ppermute | solution.py:505
  48.1 1.8 %collective-permute-start.12 = (bf16[64,3328]{1,0:T(8,128)(2,1)S(1)}, bf16[64,3328]{1,0:T(8,128)(2,1)S(1)}, u32[]{:S(2)}, u32[]{:S(2)}) collective-permute-start(bf16[64,3328]{1,0:T(8,128)(2,1)S(1)} %pad_maximum_fusion.1.refs_7_), channel_id=1, source_target_pairs={{0,64},{64,128},{128,192},{192,0},{1,65},{65,129},{129,193},{193,1... | collective-permute-start | bytes 1277960 | tf_op jit(solution)/shard_map/ppermute | solution.py:505
  49.9 2.3 %collective-permute-start.13 = (bf16[64,3328]{1,0:T(8,128)(2,1)S(1)}, bf16[64,3328]{1,0:T(8,128)(2,1)S(1)}, u32[]{:S(2)}, u32[]{:S(2)}) collective-permute-start(bf16[64,3328]{1,0:T(8,128)(2,1)S(1)} %pad_maximum_fusion.1.refs_7_), channel_id=1, source_target_pairs={{0,128},{64,192},{128,0},{192,64},{1,129},{65,193},{129,1},{193,65... | collective-permute-start | bytes 1277960 | tf_op jit(solution)/shard_map/ppermute | solution.py:505
  52.6 0.6 pad_add_fusion.refs_0_
  53.3 0.6 add_add_fusion.small_hbm
  54.3 3.8 %collective-permute-done.12.refs_8_ = bf16[64,3328]{1,0:T(8,128)(2,1)S(1)} collective-permute-done((bf16[64,3328]{1,0:T(8,128)(2,1)S(1)}, bf16[64,3328]{1,0:T(8,128)(2,1)S(1)}, u32[]{:S(2)}, u32[]{:S(2)}) %collective-permute-start.12) | collective-permute-done | bytes 426016 | tf_op jit(solution)/shard_map/ppermute | solution.py:505
  58.1 4.8 %collective-permute-done.13.refs_9_ = bf16[64,3328]{1,0:T(8,128)(2,1)S(1)} collective-permute-done((bf16[64,3328]{1,0:T(8,128)(2,1)S(1)}, bf16[64,3328]{1,0:T(8,128)(2,1)S(1)}, u32[]{:S(2)}, u32[]{:S(2)}) %collective-permute-start.13) | collective-permute-done | bytes 426016 | tf_op jit(solution)/shard_map/ppermute | solution.py:505
  63.7 10.7 %forward.1 = (bf16[16,32,3584]{2,1,0:T(8,128)(2,1)}, bf16[4,4,32,3328]{3,2,1,0:T(8,128)(2,1)}) custom-call(s32[2]{0:T(128)} %pad_add_fusion.refs_0_, bf16[16,32,1024]{2,1,0:T(8,128)(2,1)} %bitcast.11, bf16[1024,3328]{1,0:T(8,128)(2,1)} %get-tuple-element.40.refs_2_.merged_hbm, bf16[64,3328]{1,0:T(8,128)(2,1)} %copy-done.3, ...), custom_call_target="tpu_custom_call" | custom-call | flops 3489660928 | bytes 16777216 | tf_op jit(solution)/shard_map/forward/pallas_call | solution.py:183
  74.4 9.7 %all-to-all-start = ((bf16[16,32,3584]{2,1,0:T(8,128)(2,1)}), bf16[16,32,3584]{2,1,0:T(8,128)(2,1)}, u32[]{:S(2)}, u32[]{:S(2)}) async-start(bf16[16,32,3584]{2,1,0:T(8,128)(2,1)} %get-tuple-element.49), calls=%async_computation | async-start | bytes 7340032 | tf_op jit(solution)/shard_map/all_to_all | solution.py:543
  84.1 0.6 reshape.33.magnitude_hbm
  84.7 10.1 %backward.1 = (bf16[272,1024]{1,0:T(8,128)(2,1)}, bf16[272,1024]{1,0:T(8,128)(2,1)}) custom-call(s32[1]{0:T(128)} %bitcast.6.core_ref, f32[24,512]{1,0:T(8,128)} %add_add_fusion.small_hbm, f32[1,3328]{1,0:T(1,128)} %reshape.33.magnitude_hbm, f32[16,3328]{1,0:T(8,128)} %up_hbm.3, bf16[512,3328]{1,0:T(8,128)(2,1)} %bitcast.9, ...), custom_call_target="tpu_custom_call" | custom-call | flops 3489660928 | bytes 12582912 | tf_op jit(solution)/shard_map/backward/pallas_call | solution.py:339
  95.4 1.5 collective-permute-done.26
  96.9 1.9 %collective-permute-start.27 = (f32[16,512]{1,0:T(8,128)S(1)}, f32[16,512]{1,0:T(8,128)S(1)}, u32[]{:S(2)}, u32[]{:S(2)}) collective-permute-start(f32[16,512]{1,0:T(8,128)S(1)} %slice_add_fusion), channel_id=1, source_target_pairs={{0,2},{2,0},{4,6},{6,4},{8,10},{10,8},{12,14},{14,12},{1,3},{3,1},... | collective-permute-start | bytes 98312 | tf_op jit(solution)/shard_map/ppermute | solution.py:518
  98.8 0.8 copy-done.1
  99.6 2.2 %pair.1 = (bf16[48,1024]{1,0:T(8,128)(2,1)}, bf16[48,1024]{1,0:T(8,128)(2,1)}, bf16[48,1024]{1,0:T(8,128)(2,1)}, bf16[48,1024]{1,0:T(8,128)(2,1)}, bf16[48,1024]...) custom-call(s32[1]{0:T(128)} %bitcast.5.z_ref, ...), custom_call_target="tpu_custom_call" | custom-call | flops 1114112 | bytes 1671168 | tf_op jit(solution)/shard_map/pair/pallas_call | solution.py:384
  102.1 3.4 %collective-permute-start.20 = (bf16[48,1024]{1,0:T(8,128)(2,1)}, bf16[48,1024]{1,0:T(8,128)(2,1)S(1)}, u32[]{:S(2)}, u32[]{:S(2)}) collective-permute-start(bf16[48,1024]{1,0:T(8,128)(2,1)} %get-tuple-element.56), channel_id=1, source_target_pairs={{0,4},{2,6},{4,8},{6,10},{8,12},{10,14},{12,0},{14,2},{1,5},{3,7},... | collective-permute-start | bytes 294920 | tf_op jit(solution)/shard_map/ppermute | solution.py:548
  105.4 4.5 %collective-permute-start.28 = (f32[16,512]{1,0:T(8,128)S(1)}, f32[16,512]{1,0:T(8,128)S(1)}, u32[]{:S(2)}, u32[]{:S(2)}) collective-permute-start(f32[16,512]{1,0:T(8,128)S(1)} %add.41), channel_id=1, source_target_pairs={{0,4},{2,6},{4,0},{6,2},{8,12},{10,14},{12,8},{14,10},{1,5},{3,7},... | collective-permute-start | bytes 98312 | tf_op jit(solution)/shard_map/ppermute | solution.py:518
  109.9 2.2 %collective-permute-done.28 = f32[16,512]{1,0:T(8,128)S(1)} collective-permute-done((f32[16,512]{1,0:T(8,128)S(1)}, f32[16,512]{1,0:T(8,128)S(1)}, u32[]{:S(2)}, u32[]{:S(2)}) %collective-permute-start.28) | collective-permute-done | bytes 32800 | tf_op jit(solution)/shard_map/ppermute | solution.py:518
  112.2 3.5 %collective-permute-start.29 = (f32[16,512]{1,0:T(8,128)S(1)}, f32[16,512]{1,0:T(8,128)S(1)}, u32[]{:S(2)}, u32[]{:S(2)}) collective-permute-start(f32[16,512]{1,0:T(8,128)S(1)} %add.42), channel_id=1, source_target_pairs={{0,8},{2,10},{4,12},{6,14},{8,0},{10,2},{12,4},{14,6},{1,9},{3,11}... | collective-permute-start | bytes 98312 | tf_op jit(solution)/shard_map/ppermute | solution.py:518
  115.6 5.4 %collective-permute-start.21 = (bf16[48,1024]{1,0:T(8,128)(2,1)}, bf16[48,1024]{1,0:T(8,128)(2,1)S(1)}, u32[]{:S(2)}, u32[]{:S(2)}) collective-permute-start(bf16[48,1024]{1,0:T(8,128)(2,1)} %get-tuple-element.57), channel_id=1, source_target_pairs={{0,6},{2,8},{4,10},{6,12},{8,14},{10,0},{12,2},{14,4},{1,7},{3,9},... | collective-permute-start | bytes 294920 | tf_op jit(solution)/shard_map/ppermute | solution.py:548
  121.0 1.5 collective-permute-start.22
  122.5 2.0 %collective-permute-start.23 = (bf16[48,1024]{1,0:T(8,128)(2,1)}, bf16[48,1024]{1,0:T(8,128)(2,1)S(1)}, u32[]{:S(2)}, u32[]{:S(2)}) collective-permute-start(bf16[48,1024]{1,0:T(8,128)(2,1)} %get-tuple-element.59), channel_id=1, source_target_pairs={{0,10},{2,12},{4,14},{6,0},{8,2},{10,4},{12,6},{14,8},{1,11},{3,13... | collective-permute-start | bytes 294920 | tf_op jit(solution)/shard_map/ppermute | solution.py:548
  124.5 2.6 %collective-permute-start.24 = (bf16[48,1024]{1,0:T(8,128)(2,1)}, bf16[48,1024]{1,0:T(8,128)(2,1)S(1)}, u32[]{:S(2)}, u32[]{:S(2)}) collective-permute-start(bf16[48,1024]{1,0:T(8,128)(2,1)} %get-tuple-element.60), channel_id=1, source_target_pairs={{0,12},{2,14},{4,0},{6,2},{8,4},{10,6},{12,8},{14,10},{1,13},{3,15... | collective-permute-start | bytes 294920 | tf_op jit(solution)/shard_map/ppermute | solution.py:548
  127.2 1.2 collective-permute-start.25
  128.4 0.6 add.43.proj_hbm
  129.0 4.1 %up_gradient.1 = f32[16,3328]{1,0:T(8,128)} custom-call(f32[16,512]{1,0:T(8,128)} %add.43.proj_hbm, f32[24,512]{1,0:T(8,128)} %add_add_fusion.small_hbm, f32[1,3328]{1,0:T(1,128)} %reshape.33.magnitude_hbm, bf16[512,3328]{1,0:T(8,128)(2,1)} %bitcast.10), custom_call_target="tpu_custom_call" | custom-call | flops 872415232 | bytes 4194304 | tf_op jit(solution)/shard_map/up_gradient/pallas_call | solution.py:482
  133.2 1.7 %collective-permute-done.23.refs_5_ = bf16[48,1024]{1,0:T(8,128)(2,1)S(1)} collective-permute-done((bf16[48,1024]{1,0:T(8,128)(2,1)}, bf16[48,1024]{1,0:T(8,128)(2,1)S(1)}, u32[]{:S(2)}, u32[]{:S(2)}) %collective-permute-start.23) | collective-permute-done | bytes 98336 | tf_op jit(solution)/shard_map/ppermute | solution.py:548
  134.8 3.3 %collective-permute-done.24.refs_6_ = bf16[48,1024]{1,0:T(8,128)(2,1)S(1)} collective-permute-done((bf16[48,1024]{1,0:T(8,128)(2,1)}, bf16[48,1024]{1,0:T(8,128)(2,1)S(1)}, u32[]{:S(2)}, u32[]{:S(2)}) %collective-permute-start.24) | collective-permute-done | bytes 98336 | tf_op jit(solution)/shard_map/ppermute | solution.py:548
  138.2 1.3 collective-permute-done.25.refs_7_
  139.5 0.6 copy-done.11
  140.1 2.5 %finish.1 = (bf16[32,1024]{1,0:T(8,128)(2,1)}, f32[16,1024]{1,0:T(8,128)}) custom-call(s32[1]{0:T(128)} %bitcast.5.z_ref, bf16[512,1024]{1,0:T(8,128)(2,1)} %all-gather.3.cloned.1.call-done.tokens_hbm, bf16[48,1024]{1,0:T(8,128)(2,1)} %get-tuple-element.54.refs_0_, bf16[48,1024]{1,0:T(8,128)(2,1)} %copy-done.5, bf16[48,1024]{1,0:T(8,128)(2,1)} %copy-done.6, ...), custom_call_target="tpu_custom_call" | custom-call | flops 268435456 | bytes 2097152 | tf_op jit(solution)/shard_map/finish/pallas_call | solution.py:428
  142.6 3.2 %output.1 = (bf16[32,3328]{1,0:T(8,128)(2,1)}, f32[1,3328]{1,0:T(1,128)}) custom-call(f32[24,512]{1,0:T(8,128)} %add_add_fusion.small_hbm, f32[1,3328]{1,0:T(1,128)} %reshape.33.magnitude_hbm, bf16[16,32,3584]{2,1,0:T(8,128)(2,1)} %all-to-all-done.parts_hbm), custom_call_target="tpu_custom_call" | custom-call | flops 1703936 | bytes 4194304 | tf_op jit(solution)/shard_map/output/pallas_call | solution.py:250
  145.8 1.4 reduce
  (71 shorter events, 2.9 us)
Async XLA Ops:
  7.2 12.5 %copy-start.4 = (bf16[32,3328]{1,0:T(8,128)(2,1)S(1)}, bf16[32,3328]{1,0:T(8,128)(2,1)}, u32[]{:S(2)}) copy-start(bf16[32,3328]{1,0:T(8,128)(2,1)} %param.11) | copy-start | bytes 638980
  7.2 56.0 %all-gather.3.cloned.1.call-start = ((), (), s32[]{:S(2)}) async-start(), calls=%async_computation.1 | async-start | bytes 1114112 | tf_op jit(solution)/shard_map/all_gather | solution.py:528
  13.3 9.0 %collective-permute-start.6 = (f32[24,512]{1,0:T(8,128)}, f32[24,512]{1,0:T(8,128)S(1)}, u32[]{:S(2)}, u32[]{:S(2)}) collective-permute-start(f32[24,512]{1,0:T(8,128)} %get-tuple-element.35), channel_id=1, source_target_pairs={{0,128},{64,192},{128,0},{192,64},{1,129},{65,193},{129,1},{193,65... | collective-permute-start | bytes 147464 | tf_op jit(solution)/shard_map/ppermute | solution.py:505
  16.4 8.4 %collective-permute-start.7 = (f32[24,512]{1,0:T(8,128)}, f32[24,512]{1,0:T(8,128)S(1)}, u32[]{:S(2)}, u32[]{:S(2)}) collective-permute-start(f32[24,512]{1,0:T(8,128)} %get-tuple-element.35), channel_id=1, source_target_pairs={{0,64},{64,128},{128,192},{192,0},{1,65},{65,129},{129,193},{193,1... | collective-permute-start | bytes 147464 | tf_op jit(solution)/shard_map/ppermute | solution.py:505
  17.0 7.8 %collective-permute-start.8 = (f32[24,512]{1,0:T(8,128)}, f32[24,512]{1,0:T(8,128)S(1)}, u32[]{:S(2)}, u32[]{:S(2)}) collective-permute-start(f32[24,512]{1,0:T(8,128)} %get-tuple-element.35), channel_id=1, source_target_pairs={{0,192},{64,0},{128,64},{192,128},{1,193},{65,1},{129,65},{193,129... | collective-permute-start | bytes 147464 | tf_op jit(solution)/shard_map/ppermute | solution.py:505
  19.6 7.4 %collective-permute-start.3 = (bf16[16,3328]{1,0:T(8,128)(2,1)S(1)}, bf16[16,3328]{1,0:T(8,128)(2,1)S(1)}, u32[]{:S(2)}, u32[]{:S(2)}) collective-permute-start(bf16[16,3328]{1,0:T(8,128)(2,1)S(1)} %get-tuple-element.65), channel_id=1, source_target_pairs={{0,16},{16,32},{32,48},{48,0},{1,17},{17,33},{33,49},{49,1},{2,18}... | collective-permute-start | bytes 319496 | tf_op jit(solution)/shard_map/ppermute | solution.py:505
  21.3 7.6 %collective-permute-start.4 = (bf16[16,3328]{1,0:T(8,128)(2,1)S(1)}, bf16[16,3328]{1,0:T(8,128)(2,1)S(1)}, u32[]{:S(2)}, u32[]{:S(2)}) collective-permute-start(bf16[16,3328]{1,0:T(8,128)(2,1)S(1)} %get-tuple-element.65), channel_id=1, source_target_pairs={{0,32},{16,48},{32,0},{48,16},{1,33},{17,49},{33,1},{49,17},{2,34}... | collective-permute-start | bytes 319496 | tf_op jit(solution)/shard_map/ppermute | solution.py:505
  22.3 6.6 %collective-permute-start.5 = (bf16[16,3328]{1,0:T(8,128)(2,1)S(1)}, bf16[16,3328]{1,0:T(8,128)(2,1)S(1)}, u32[]{:S(2)}, u32[]{:S(2)}) collective-permute-start(bf16[16,3328]{1,0:T(8,128)(2,1)S(1)} %get-tuple-element.65), channel_id=1, source_target_pairs={{0,48},{16,0},{32,16},{48,32},{1,49},{17,1},{33,17},{49,33},{2,50}... | collective-permute-start | bytes 319496 | tf_op jit(solution)/shard_map/ppermute | solution.py:505
  24.8 7.1 %collective-permute-start = (bf16[16,3328]{1,0:T(8,128)(2,1)S(1)}, bf16[16,3328]{1,0:T(8,128)(2,1)S(1)}, u32[]{:S(2)}, u32[]{:S(2)}) collective-permute-start(bf16[16,3328]{1,0:T(8,128)(2,1)S(1)} %get-tuple-element.66), channel_id=1, source_target_pairs={{0,64},{64,128},{128,192},{192,0},{1,65},{65,129},{129,193},{193,1... | collective-permute-start | bytes 319496 | tf_op jit(solution)/shard_map/ppermute | solution.py:505
  24.8 7.1 %collective-permute-start.1 = (bf16[16,3328]{1,0:T(8,128)(2,1)S(1)}, bf16[16,3328]{1,0:T(8,128)(2,1)S(1)}, u32[]{:S(2)}, u32[]{:S(2)}) collective-permute-start(bf16[16,3328]{1,0:T(8,128)(2,1)S(1)} %get-tuple-element.66), channel_id=1, source_target_pairs={{0,128},{64,192},{128,0},{192,64},{1,129},{65,193},{129,1},{193,65... | collective-permute-start | bytes 319496 | tf_op jit(solution)/shard_map/ppermute | solution.py:505
  27.1 5.6 %collective-permute-start.2 = (bf16[16,3328]{1,0:T(8,128)(2,1)S(1)}, bf16[16,3328]{1,0:T(8,128)(2,1)S(1)}, u32[]{:S(2)}, u32[]{:S(2)}) collective-permute-start(bf16[16,3328]{1,0:T(8,128)(2,1)S(1)} %get-tuple-element.66), channel_id=1, source_target_pairs={{0,192},{64,0},{128,64},{192,128},{1,193},{65,1},{129,65},{193,129... | collective-permute-start | bytes 319496 | tf_op jit(solution)/shard_map/ppermute | solution.py:505
  29.0 34.7 %copy-start.2 = (bf16[64,3328]{1,0:T(8,128)(2,1)}, bf16[64,3328]{1,0:T(8,128)(2,1)S(1)}, u32[]{:S(2)}) copy-start(bf16[64,3328]{1,0:T(8,128)(2,1)S(1)} %pad_maximum_fusion.1.refs_7_) | copy-start | bytes 1277956
  32.7 31.0 %copy-start.3 = (bf16[64,3328]{1,0:T(8,128)(2,1)}, bf16[64,3328]{1,0:T(8,128)(2,1)S(1)}, u32[]{:S(2)}) copy-start(bf16[64,3328]{1,0:T(8,128)(2,1)S(1)} %pad_maximum_fusion.refs_3_) | copy-start | bytes 1277956
  32.7 19.9 %collective-permute-start.10 = (bf16[64,3328]{1,0:T(8,128)(2,1)S(1)}, bf16[64,3328]{1,0:T(8,128)(2,1)S(1)}, u32[]{:S(2)}, u32[]{:S(2)}) collective-permute-start(bf16[64,3328]{1,0:T(8,128)(2,1)S(1)} %pad_maximum_fusion.refs_3_), channel_id=1, source_target_pairs={{0,32},{16,48},{32,0},{48,16},{1,33},{17,49},{33,1},{49,17},{2,34}... | collective-permute-start | bytes 1277960 | tf_op jit(solution)/shard_map/ppermute | solution.py:505
  33.1 15.0 %collective-permute-start.15 = (f32[24,512]{1,0:T(8,128)S(1)}, f32[24,512]{1,0:T(8,128)S(1)}, u32[]{:S(2)}, u32[]{:S(2)}) collective-permute-start(f32[24,512]{1,0:T(8,128)S(1)} %add_add_fusion.1), channel_id=1, source_target_pairs={{0,32},{16,48},{32,0},{48,16},{1,33},{17,49},{33,1},{49,17},{2,34}... | collective-permute-start | bytes 147464 | tf_op jit(solution)/shard_map/ppermute | solution.py:505
  36.3 13.6 %collective-permute-start.16 = (f32[24,512]{1,0:T(8,128)S(1)}, f32[24,512]{1,0:T(8,128)S(1)}, u32[]{:S(2)}, u32[]{:S(2)}) collective-permute-start(f32[24,512]{1,0:T(8,128)S(1)} %add_add_fusion.1), channel_id=1, source_target_pairs={{0,16},{16,32},{32,48},{48,0},{1,17},{17,33},{33,49},{49,1},{2,18}... | collective-permute-start | bytes 147464 | tf_op jit(solution)/shard_map/ppermute | solution.py:505
  36.3 15.9 %collective-permute-start.17 = (f32[24,512]{1,0:T(8,128)S(1)}, f32[24,512]{1,0:T(8,128)S(1)}, u32[]{:S(2)}, u32[]{:S(2)}) collective-permute-start(f32[24,512]{1,0:T(8,128)S(1)} %add_add_fusion.1), channel_id=1, source_target_pairs={{0,48},{16,0},{32,16},{48,32},{1,49},{17,1},{33,17},{49,33},{2,50}... | collective-permute-start | bytes 147464 | tf_op jit(solution)/shard_map/ppermute | solution.py:505
  38.4 15.9 %collective-permute-start.11 = (bf16[64,3328]{1,0:T(8,128)(2,1)S(1)}, bf16[64,3328]{1,0:T(8,128)(2,1)S(1)}, u32[]{:S(2)}, u32[]{:S(2)}) collective-permute-start(bf16[64,3328]{1,0:T(8,128)(2,1)S(1)} %pad_maximum_fusion.refs_3_), channel_id=1, source_target_pairs={{0,48},{16,0},{32,16},{48,32},{1,49},{17,1},{33,17},{49,33},{2,50}... | collective-permute-start | bytes 1277960 | tf_op jit(solution)/shard_map/ppermute | solution.py:505
  48.1 10.0 %collective-permute-start.12 = (bf16[64,3328]{1,0:T(8,128)(2,1)S(1)}, bf16[64,3328]{1,0:T(8,128)(2,1)S(1)}, u32[]{:S(2)}, u32[]{:S(2)}) collective-permute-start(bf16[64,3328]{1,0:T(8,128)(2,1)S(1)} %pad_maximum_fusion.1.refs_7_), channel_id=1, source_target_pairs={{0,64},{64,128},{128,192},{192,0},{1,65},{65,129},{129,193},{193,1... | collective-permute-start | bytes 1277960 | tf_op jit(solution)/shard_map/ppermute | solution.py:505
  49.9 13.0 %collective-permute-start.13 = (bf16[64,3328]{1,0:T(8,128)(2,1)S(1)}, bf16[64,3328]{1,0:T(8,128)(2,1)S(1)}, u32[]{:S(2)}, u32[]{:S(2)}) collective-permute-start(bf16[64,3328]{1,0:T(8,128)(2,1)S(1)} %pad_maximum_fusion.1.refs_7_), channel_id=1, source_target_pairs={{0,128},{64,192},{128,0},{192,64},{1,129},{65,193},{129,1},{193,65... | collective-permute-start | bytes 1277960 | tf_op jit(solution)/shard_map/ppermute | solution.py:505
  52.3 10.9 %collective-permute-start.14 = (bf16[64,3328]{1,0:T(8,128)(2,1)S(1)}, bf16[64,3328]{1,0:T(8,128)(2,1)}, u32[]{:S(2)}, u32[]{:S(2)}) collective-permute-start(bf16[64,3328]{1,0:T(8,128)(2,1)S(1)} %pad_maximum_fusion.1.refs_7_), channel_id=1, source_target_pairs={{0,192},{64,0},{128,64},{192,128},{1,193},{65,1},{129,65},{193,129... | collective-permute-start | bytes 1277960 | tf_op jit(solution)/shard_map/ppermute | solution.py:505
  52.6 11.1 %copy-start.13 = (bf16[64,3328]{1,0:T(8,128)(2,1)}, bf16[64,3328]{1,0:T(8,128)(2,1)S(1)}, u32[]{:S(2)}) copy-start(bf16[64,3328]{1,0:T(8,128)(2,1)S(1)} %collective-permute-done.10.refs_5_) | copy-start | bytes 1277956
  52.6 10.5 %collective-permute-start.9 = (bf16[64,3328]{1,0:T(8,128)(2,1)S(1)}, bf16[64,3328]{1,0:T(8,128)(2,1)}, u32[]{:S(2)}, u32[]{:S(2)}) collective-permute-start(bf16[64,3328]{1,0:T(8,128)(2,1)S(1)} %pad_maximum_fusion.refs_3_), channel_id=1, source_target_pairs={{0,16},{16,32},{32,48},{48,0},{1,17},{17,33},{33,49},{49,1},{2,18}... | collective-permute-start | bytes 1277960 | tf_op jit(solution)/shard_map/ppermute | solution.py:505
  54.3 9.4 %copy-start.14 = (bf16[64,3328]{1,0:T(8,128)(2,1)}, bf16[64,3328]{1,0:T(8,128)(2,1)S(1)}, u32[]{:S(2)}) copy-start(bf16[64,3328]{1,0:T(8,128)(2,1)S(1)} %collective-permute-done.11.refs_6_) | copy-start | bytes 1277956
  58.1 5.0 %copy-start.15 = (bf16[64,3328]{1,0:T(8,128)(2,1)}, bf16[64,3328]{1,0:T(8,128)(2,1)S(1)}, u32[]{:S(2)}) copy-start(bf16[64,3328]{1,0:T(8,128)(2,1)S(1)} %collective-permute-done.12.refs_8_) | copy-start | bytes 1277956
  62.9 0.7 copy-start.16
  74.4 9.7 %copy-start.12 = (f32[3328]{0:T(1024)S(1)}, f32[3328]{0:T(1024)}, u32[]{:S(2)}) copy-start(f32[3328]{0:T(1024)} %param.10) | copy-start | bytes 39940
  74.4 68.2 %all-to-all-start = ((bf16[16,32,3584]{2,1,0:T(8,128)(2,1)}), bf16[16,32,3584]{2,1,0:T(8,128)(2,1)}, u32[]{:S(2)}, u32[]{:S(2)}) async-start(bf16[16,32,3584]{2,1,0:T(8,128)(2,1)} %get-tuple-element.49), calls=%async_computation | async-start | bytes 7340032 | tf_op jit(solution)/shard_map/all_to_all | solution.py:543
  84.7 10.2 %copy-start = (f32[24,512]{1,0:T(8,128)S(1)}, f32[24,512]{1,0:T(8,128)}, u32[]{:S(2)}) copy-start(f32[24,512]{1,0:T(8,128)} %add_add_fusion.small_hbm) | copy-start | bytes 147460
  94.8 4.0 %collective-permute-start.18 = (bf16[272,1024]{1,0:T(8,128)(2,1)}, bf16[272,1024]{1,0:T(8,128)(2,1)S(1)}, u32[]{:S(2)}, u32[]{:S(2)}) collective-permute-start(bf16[272,1024]{1,0:T(8,128)(2,1)} %get-tuple-element.53), channel_id=1, source_target_pairs={{0,1},{1,0},{2,3},{3,2},{4,5},{5,4},{6,7},{7,6},{8,9},{9,8},{10,11... | collective-permute-start | bytes 1671176 | tf_op jit(solution)/shard_map/ppermute | solution.py:545
  94.9 2.0 %collective-permute-start.26 = (f32[16,512]{1,0:T(8,128)S(1)}, f32[16,512]{1,0:T(8,128)S(1)}, u32[]{:S(2)}, u32[]{:S(2)}) collective-permute-start(f32[16,512]{1,0:T(8,128)S(1)} %slice.11), channel_id=1, source_target_pairs={{0,1},{1,0},{2,3},{3,2},{4,5},{5,4},{6,7},{7,6},{8,9},{9,8},{10,11... | collective-permute-start | bytes 98312 | tf_op jit(solution)/shard_map/ppermute | solution.py:516
  96.9 8.5 %collective-permute-start.27 = (f32[16,512]{1,0:T(8,128)S(1)}, f32[16,512]{1,0:T(8,128)S(1)}, u32[]{:S(2)}, u32[]{:S(2)}) collective-permute-start(f32[16,512]{1,0:T(8,128)S(1)} %slice_add_fusion), channel_id=1, source_target_pairs={{0,2},{2,0},{4,6},{6,4},{8,10},{10,8},{12,14},{14,12},{1,3},{3,1},... | collective-permute-start | bytes 98312 | tf_op jit(solution)/shard_map/ppermute | solution.py:518
  98.8 0.8 copy-start.1
  101.8 22.7 %collective-permute-start.19 = (bf16[48,1024]{1,0:T(8,128)(2,1)}, bf16[48,1024]{1,0:T(8,128)(2,1)S(1)}, u32[]{:S(2)}, u32[]{:S(2)}) collective-permute-start(bf16[48,1024]{1,0:T(8,128)(2,1)} %get-tuple-element.55), channel_id=1, source_target_pairs={{0,2},{2,4},{4,6},{6,8},{8,10},{10,12},{12,14},{14,0},{1,3},{3,5},... | collective-permute-start | bytes 294920 | tf_op jit(solution)/shard_map/ppermute | solution.py:548
  102.1 25.1 %collective-permute-start.20 = (bf16[48,1024]{1,0:T(8,128)(2,1)}, bf16[48,1024]{1,0:T(8,128)(2,1)S(1)}, u32[]{:S(2)}, u32[]{:S(2)}) collective-permute-start(bf16[48,1024]{1,0:T(8,128)(2,1)} %get-tuple-element.56), channel_id=1, source_target_pairs={{0,4},{2,6},{4,8},{6,10},{8,12},{10,14},{12,0},{14,2},{1,5},{3,7},... | collective-permute-start | bytes 294920 | tf_op jit(solution)/shard_map/ppermute | solution.py:548
  105.4 6.7 %collective-permute-start.28 = (f32[16,512]{1,0:T(8,128)S(1)}, f32[16,512]{1,0:T(8,128)S(1)}, u32[]{:S(2)}, u32[]{:S(2)}) collective-permute-start(f32[16,512]{1,0:T(8,128)S(1)} %add.41), channel_id=1, source_target_pairs={{0,4},{2,6},{4,0},{6,2},{8,12},{10,14},{12,8},{14,10},{1,5},{3,7},... | collective-permute-start | bytes 98312 | tf_op jit(solution)/shard_map/ppermute | solution.py:518
  112.2 10.4 %collective-permute-start.29 = (f32[16,512]{1,0:T(8,128)S(1)}, f32[16,512]{1,0:T(8,128)S(1)}, u32[]{:S(2)}, u32[]{:S(2)}) collective-permute-start(f32[16,512]{1,0:T(8,128)S(1)} %add.42), channel_id=1, source_target_pairs={{0,8},{2,10},{4,12},{6,14},{8,0},{10,2},{12,4},{14,6},{1,9},{3,11}... | collective-permute-start | bytes 98312 | tf_op jit(solution)/shard_map/ppermute | solution.py:518
  115.6 17.5 %collective-permute-start.21 = (bf16[48,1024]{1,0:T(8,128)(2,1)}, bf16[48,1024]{1,0:T(8,128)(2,1)S(1)}, u32[]{:S(2)}, u32[]{:S(2)}) collective-permute-start(bf16[48,1024]{1,0:T(8,128)(2,1)} %get-tuple-element.57), channel_id=1, source_target_pairs={{0,6},{2,8},{4,10},{6,12},{8,14},{10,0},{12,2},{14,4},{1,7},{3,9},... | collective-permute-start | bytes 294920 | tf_op jit(solution)/shard_map/ppermute | solution.py:548
  121.0 12.2 %collective-permute-start.22 = (bf16[48,1024]{1,0:T(8,128)(2,1)}, bf16[48,1024]{1,0:T(8,128)(2,1)S(1)}, u32[]{:S(2)}, u32[]{:S(2)}) collective-permute-start(bf16[48,1024]{1,0:T(8,128)(2,1)} %get-tuple-element.58), channel_id=1, source_target_pairs={{0,8},{2,10},{4,12},{6,14},{8,0},{10,2},{12,4},{14,6},{1,9},{3,11}... | collective-permute-start | bytes 294920 | tf_op jit(solution)/shard_map/ppermute | solution.py:548
  122.5 12.3 %collective-permute-start.23 = (bf16[48,1024]{1,0:T(8,128)(2,1)}, bf16[48,1024]{1,0:T(8,128)(2,1)S(1)}, u32[]{:S(2)}, u32[]{:S(2)}) collective-permute-start(bf16[48,1024]{1,0:T(8,128)(2,1)} %get-tuple-element.59), channel_id=1, source_target_pairs={{0,10},{2,12},{4,14},{6,0},{8,2},{10,4},{12,6},{14,8},{1,11},{3,13... | collective-permute-start | bytes 294920 | tf_op jit(solution)/shard_map/ppermute | solution.py:548
  124.5 14.9 %copy-start.5 = (bf16[48,1024]{1,0:T(8,128)(2,1)}, bf16[48,1024]{1,0:T(8,128)(2,1)S(1)}, u32[]{:S(2)}) copy-start(bf16[48,1024]{1,0:T(8,128)(2,1)S(1)} %collective-permute-done.19.refs_1_) | copy-start | bytes 294916
  124.5 13.6 %collective-permute-start.24 = (bf16[48,1024]{1,0:T(8,128)(2,1)}, bf16[48,1024]{1,0:T(8,128)(2,1)S(1)}, u32[]{:S(2)}, u32[]{:S(2)}) collective-permute-start(bf16[48,1024]{1,0:T(8,128)(2,1)} %get-tuple-element.60), channel_id=1, source_target_pairs={{0,12},{2,14},{4,0},{6,2},{8,4},{10,6},{12,8},{14,10},{1,13},{3,15... | collective-permute-start | bytes 294920 | tf_op jit(solution)/shard_map/ppermute | solution.py:548
  127.2 12.3 %copy-start.6 = (bf16[48,1024]{1,0:T(8,128)(2,1)}, bf16[48,1024]{1,0:T(8,128)(2,1)S(1)}, u32[]{:S(2)}) copy-start(bf16[48,1024]{1,0:T(8,128)(2,1)S(1)} %collective-permute-done.20.refs_2_) | copy-start | bytes 294916
  127.2 12.3 %collective-permute-start.25 = (bf16[48,1024]{1,0:T(8,128)(2,1)}, bf16[48,1024]{1,0:T(8,128)(2,1)S(1)}, u32[]{:S(2)}, u32[]{:S(2)}) collective-permute-start(bf16[48,1024]{1,0:T(8,128)(2,1)} %get-tuple-element.61), channel_id=1, source_target_pairs={{0,14},{2,0},{4,2},{6,4},{8,6},{10,8},{12,10},{14,12},{1,15},{3,1}... | collective-permute-start | bytes 294920 | tf_op jit(solution)/shard_map/ppermute | solution.py:548
  133.1 6.3 %copy-start.7 = (bf16[48,1024]{1,0:T(8,128)(2,1)}, bf16[48,1024]{1,0:T(8,128)(2,1)S(1)}, u32[]{:S(2)}) copy-start(bf16[48,1024]{1,0:T(8,128)(2,1)S(1)} %collective-permute-done.21.refs_3_) | copy-start | bytes 294916
  133.2 6.3 %copy-start.8 = (bf16[48,1024]{1,0:T(8,128)(2,1)}, bf16[48,1024]{1,0:T(8,128)(2,1)S(1)}, u32[]{:S(2)}) copy-start(bf16[48,1024]{1,0:T(8,128)(2,1)S(1)} %collective-permute-done.22.refs_4_) | copy-start | bytes 294916
  134.8 4.6 %copy-start.9 = (bf16[48,1024]{1,0:T(8,128)(2,1)}, bf16[48,1024]{1,0:T(8,128)(2,1)S(1)}, u32[]{:S(2)}) copy-start(bf16[48,1024]{1,0:T(8,128)(2,1)S(1)} %collective-permute-done.23.refs_5_) | copy-start | bytes 294916
  138.2 1.3 copy-start.10
  (1 other events, 0.6 us)
Sparse Core Ops, SparseCore 0:
  22.4 39.0 all-gather.2

commit v5 on v4

v5 whole, which is shorter than its diff:
```python
import jax
import jax.numpy as jnp
from jax import lax
from jax.experimental import pallas as pl
from jax.experimental.pallas import tpu as pltpu
from jax.sharding import Mesh
from jax.sharding import PartitionSpec as P

adapter_scale = 2.0
epsilon = 1e-06
bf16 = jnp.bfloat16
f32 = jnp.float32
ROW = ("x", "y")
COL = ("z", "c")
CHUNK = 512
RANK = 16
LANES = 128
MIB = 1024 * 1024
LIMIT = 62 * MIB
ANY = pl.BlockSpec(memory_space=pl.ANY)
SMEM = pl.BlockSpec(memory_space=pltpu.SMEM)


def pieces(value):
    high = value.astype(bf16)
    rest = value - high.astype(f32)
    mid = rest.astype(bf16)
    low = (rest - mid.astype(f32)).astype(bf16)
    return high, mid, low


def dot(left, right, left_dim, right_dim):
    return lax.dot_general(
        left, right, (((left_dim,), (right_dim,)), ((), ())), preferred_element_type=f32
    )


def three(left, right, left_dim, right_dim):
    out = dot(jnp.concatenate(pieces(left), axis=0), right, left_dim, right_dim)
    return out[:RANK] + out[RANK : 2 * RANK] + out[2 * RANK :]


def chunks_of(width):
    return [(at, min(CHUNK, width - at)) for at in range(0, width, CHUNK)]


def call(body, flops, moved, **options):
    return pl.pallas_call(
        body,
        compiler_params=pltpu.CompilerParams(vmem_limit_bytes=LIMIT),
        cost_estimate=pl.CostEstimate(flops=flops, bytes_accessed=moved, transcendentals=0),
        **options,
    )


def begin(source, target, sem):
    copy = pltpu.make_async_copy(source, target, sem)
    copy.start()
    return copy


def stream(pairs, sem, chunks):
    def copies(j):
        for i, (source, target) in enumerate(pairs):
            index = (slice(None),) * (len(target.shape) - 1) + (pl.ds(*chunks[j]),)
            yield pltpu.make_async_copy(source.at[index], target.at[index], sem.at[i, j])

    def start(j):
        if j < len(chunks):
            for copy in copies(j):
                copy.start()

    def ready(j):
        for copy in copies(j):
            copy.wait()
        start(j + 2)

    start(0)
    start(1)
    return ready


def in_rows(row):
    return [row[:, at : at + LANES] for at in range(0, row.shape[1], LANES)]


def in_line(rows, at, size):
    return jnp.concatenate(
        [rows[k : k + 1, :] for k in range(at // LANES, (at + size) // LANES)], axis=1
    )


def merge_kernel(
    down_hbm, up_hbm, weight_hbm, cot_hbm, merged_hbm, message_hbm,
    down, up, weight, cot, merged, extra, up_cat, totals, small_sem, in_sem, out_sem, copy_sem,
):
    depth, width = weight.shape
    rows, tile = 256, 256
    steps = [slice(at, at + rows) for at in range(0, depth, rows)]
    first = begin(up_hbm, up, small_sem.at[0]), begin(down_hbm, down, small_sem.at[1])
    fetches = [begin(weight_hbm.at[p], weight.at[p], in_sem.at[j]) for j, p in enumerate(steps)]
    later = begin(cot_hbm, cot, small_sem.at[2])
    totals[...] = jnp.zeros_like(totals)
    for copy in first:
        copy.wait()
    for at in range(0, width, tile):
        cols = slice(at, at + tile)
        u1, u2, u3 = pieces(up[:, cols])
        up_cat[:, cols] = jnp.concatenate([u1, u2, u1, u3, u1, u2], axis=0)
    d1, d2, d3 = pieces(down[...] * adapter_scale)
    down_cat = jnp.concatenate([d1, d1, d2, d1, d3, d2], axis=0)
    stores = []
    for j, part in enumerate(steps):
        fetches[j].wait()
        if j == len(steps) - 1:
            later.wait()
            for r in range(16):
                stores.append(begin(cot, message_hbm.at[r, :, :width], copy_sem.at[r]))
        for at in range(0, width, tile):
            cols = slice(at, at + tile)
            value = weight[part, cols].astype(f32) + dot(down_cat[:, part], up_cat[:, cols], 0, 0)
            merged[part, cols] = value.astype(bf16)
            totals[:, cols] += jnp.sum((value * value).reshape(rows // 8, 8, tile), axis=0)
        stores.append(begin(merged.at[part], merged_hbm.at[part], out_sem.at[j]))
    sums = in_rows(jnp.sum(totals[...], axis=0, keepdims=True))
    sums = jnp.concatenate(sums + [jnp.zeros((32 - len(sums), LANES), f32)], axis=0)
    high = sums.astype(bf16)
    rest = (sums - high.astype(f32)).astype(bf16)
    both = jnp.concatenate([high, rest], axis=1)
    extra[...] = jnp.broadcast_to(both[None], extra.shape)
    stores.append(begin(extra, message_hbm.at[:, :, width:], small_sem.at[0]))
    for copy in stores:
        copy.wait()


def merge(down_t, up, weight, cot):
    depth, width = weight.shape
    return call(
        merge_kernel,
        16 * 512 * depth * width,
        18 * MIB,
        in_specs=[ANY] * 4,
        out_specs=[ANY] * 2,
        out_shape=[
            jax.ShapeDtypeStruct((depth, width), bf16),
            jax.ShapeDtypeStruct((16, 32, width + 2 * LANES), bf16),
        ],
        scratch_shapes=[
            pltpu.VMEM((RANK, depth), f32),
            pltpu.VMEM((RANK, width), f32),
            pltpu.VMEM((depth, width), bf16),
            pltpu.VMEM((32, width), bf16),
            pltpu.VMEM((depth, width), bf16),
            pltpu.VMEM((16, 32, 2 * LANES), bf16),
            pltpu.VMEM((6 * RANK, width), bf16),
            pltpu.VMEM((8, width), f32),
            pltpu.SemaphoreType.DMA((3,)),
            pltpu.SemaphoreType.DMA((4,)),
            pltpu.SemaphoreType.DMA((4,)),
            pltpu.SemaphoreType.DMA((16,)),
        ],
        name="merge",
    )(down_t, up, weight, cot)


def forward_kernel(
    tokens_hbm, down_hbm, merged_hbm, part_hbm,
    tokens, down, merged, part, extra, first_sem, sem, out_sem,
):
    depth, width = merged.shape
    chunks = chunks_of(width)
    first = begin(tokens_hbm, tokens, first_sem.at[0]), begin(down_hbm, down, first_sem.at[1])
    ready = stream([(merged_hbm, merged)], sem, chunks)
    for copy in first:
        copy.wait()
    all_tokens = tokens[...].reshape(512, depth)
    proj = three(down[...], all_tokens, 1, 1).astype(bf16)
    proj = jnp.concatenate([proj[:, : 2 * LANES], proj[:, 2 * LANES :]], axis=0)
    extra[...] = jnp.broadcast_to(proj[None], extra.shape)
    beside = part_hbm.at[:, :, width : width + 2 * LANES]
    stores = [begin(extra, beside, first_sem.at[0])]
    for j, (at, size) in enumerate(chunks):
        ready(j)
        cols = slice(at, at + size)
        product = dot(all_tokens, merged[:, cols], 1, 0).astype(bf16)
        part[:, :, cols] = product.reshape(16, 32, size)
        stores.append(begin(part.at[:, :, cols], part_hbm.at[:, :, cols], out_sem.at[j]))
    for copy in stores:
        copy.wait()


def forward(tokens, down_t, merged_low):
    depth, width = merged_low.shape
    count = len(chunks_of(width))
    return call(
        forward_kernel,
        32 * 512 * depth * width,
        12 * MIB,
        in_specs=[ANY] * 3,
        out_specs=ANY,
        out_shape=jax.ShapeDtypeStruct((16, 32, width + 3 * LANES), bf16),
        scratch_shapes=[
            pltpu.VMEM((16, 32, depth), bf16),
            pltpu.VMEM((RANK, depth), f32),
            pltpu.VMEM((depth, width), bf16),
            pltpu.VMEM((16, 32, width), bf16),
            pltpu.VMEM((16, 32, 2 * LANES), bf16),
            pltpu.SemaphoreType.DMA((2,)),
            pltpu.SemaphoreType.DMA((1, count)),
            pltpu.SemaphoreType.DMA((count,)),
        ],
        name="forward",
    )(tokens, down_t, merged_low)


def magnitude_kernel(given_hbm, part_hbm, out_hbm, cot, part, extra, sem, out_sem):
    width = cot.shape[2]
    chunks = chunks_of(width)
    ready = stream([(given_hbm, cot), (part_hbm, part)], sem, chunks)
    rows = []
    for j, (at, size) in enumerate(chunks):
        ready(j)
        cols = slice(at, at + size)
        product = cot[:, :, cols].astype(f32) * part[:, :, cols].astype(f32)
        total = jnp.sum(product.reshape(64, 8, size), axis=0)
        rows += in_rows(jnp.sum(total, axis=0, keepdims=True))
    rows.append(jnp.zeros((32 - len(rows), LANES), f32))
    sums = jnp.concatenate(rows, axis=0).astype(bf16)
    extra[...] = jnp.broadcast_to(sums[None], extra.shape)
    begin(extra, out_hbm.at[:, :, width + 2 * LANES :], out_sem.at[0]).wait()


def add_magnitude(given, part):
    blocks, rows, width = given.shape
    width -= 2 * LANES
    return call(
        magnitude_kernel,
        4 * 512 * width,
        7 * MIB,
        in_specs=[ANY, ANY],
        out_specs=ANY,
        out_shape=jax.ShapeDtypeStruct(part.shape, bf16),
        scratch_shapes=[
            pltpu.VMEM((blocks, rows, width), bf16),
            pltpu.VMEM((blocks, rows, width), bf16),
            pltpu.VMEM((blocks, rows, LANES), bf16),
            pltpu.SemaphoreType.DMA((2, len(chunks_of(width)))),
            pltpu.SemaphoreType.DMA((1,)),
        ],
        input_output_aliases={1: 0},
        name="magnitude",
    )(given, part)


def pack(low, out):
    high = low.astype(bf16)
    rest = (low - high.astype(f32)).astype(bf16)
    out[:, :CHUNK] = high
    out[:, CHUNK:] = rest
    return high.astype(f32) + rest.astype(f32)


def unpack(got):
    got = got.astype(f32)
    return got[:, :CHUNK] + got[:, CHUNK:]


def backward_kernel(
    core_ref, magnitude_hbm, up_hbm, given_hbm, merged_hbm, own_hbm, send_hbm, scale_hbm,
    magnitude, squares, up, cot, merged, total, own, send, scale, first_sem, sem,
):
    core = core_ref[0]
    depth, width = merged.shape
    chunks = chunks_of(width)
    count = width // LANES
    first = (
        begin(given_hbm.at[:, :, width:], squares, first_sem.at[0]),
        begin(up_hbm, up, first_sem.at[1]),
        begin(magnitude_hbm, magnitude, first_sem.at[2]),
    )
    ready = stream([(given_hbm, cot), (merged_hbm, merged)], sem, chunks)
    for copy in first:
        copy.wait()
    sums = squares[0].astype(f32)
    for r in range(1, 16):
        sums += squares[r].astype(f32)
    norm = jnp.sqrt(sums[:, :LANES] + sums[:, LANES:] + epsilon)
    factors = magnitude[...] / norm[:count]
    scale[...] = jnp.zeros_like(scale)
    scale[:count, :] = factors
    scale[32:, :] = norm
    last = begin(scale, scale_hbm, first_sem.at[0])
    low = jnp.zeros((RANK, CHUNK), f32)
    for j, (at, size) in enumerate(chunks):
        ready(j)
        cols = slice(at, at + size)
        value = cot[:, :, cols].reshape(512, size).astype(f32)
        grad = (value * in_line(factors, at, size)).astype(bf16)
        product = dot(grad, merged[:, cols], 1, 1)
        if j == 0:
            total[...] = product
        else:
            total[...] += product
        low += three(up[:, cols], grad, 1, 1)
    for z in range(8):
        theirs = pl.ds(pl.multiple_of((2 * z + 1 - core) * 32, 32), 32)
        send[32 * z : 32 * z + 32, :] = total[theirs, :].astype(bf16)
    pack(low, send.at[256:272, :])
    first = begin(send, send_hbm, first_sem.at[1])
    for z in range(8):
        mine = pl.ds(pl.multiple_of((2 * z + core) * 32, 32), 32)
        own[32 * z : 32 * z + 32, :] = total[mine, :].astype(bf16)
    own[256:272, :] = send[256:272, :]
    begin(own, own_hbm, first_sem.at[2]).wait()
    first.wait()
    last.wait()


def backward(core, magnitude, up, given, merged_low):
    depth, width = merged_low.shape
    count = len(chunks_of(width))
    return call(
        backward_kernel,
        2 * 512 * depth * width,
        12 * MIB,
        in_specs=[SMEM] + [ANY] * 4,
        out_specs=[ANY] * 3,
        out_shape=[jax.ShapeDtypeStruct((272, depth), bf16)] * 2
        + [jax.ShapeDtypeStruct((64, LANES), f32)],
        scratch_shapes=[
            pltpu.VMEM(magnitude.shape, f32),
            pltpu.VMEM((16, 32, 2 * LANES), bf16),
            pltpu.VMEM((RANK, width), f32),
            pltpu.VMEM((16, 32, width), bf16),
            pltpu.VMEM((depth, width), bf16),
            pltpu.VMEM((512, depth), f32),
            pltpu.VMEM((272, depth), bf16),
            pltpu.VMEM((272, depth), bf16),
            pltpu.VMEM((64, LANES), f32),
            pltpu.SemaphoreType.DMA((3,)),
            pltpu.SemaphoreType.DMA((2, count)),
        ],
        name="backward",
    )(core, magnitude, up, given, merged_low)


def pair_kernel(z_ref, own_hbm, got_hbm, *refs):
    out_hbm = refs[:8]
    own, got, send, sem, out_sem = refs[8:]
    z = z_ref[0]
    copies = begin(own_hbm, own, sem.at[0]), begin(got_hbm, got, sem.at[1])
    for copy in copies:
        copy.wait()
    low = unpack(own[256:272, :]) + unpack(got[256:272, :])
    pack(low, send.at[0, 32:48, :])
    stores = []
    for k in [1, 7, 2, 6, 3, 5, 4, 0]:
        block = pl.ds(pl.multiple_of(lax.rem(z + k, 8) * 32, 32), 32)
        send[k, :32, :] = (own[block, :].astype(f32) + got[block, :].astype(f32)).astype(bf16)
        if k:
            send[k, 32:48, :] = send[0, 32:48, :]
        stores.append(begin(send.at[k], out_hbm[k], out_sem.at[k]))
    for copy in stores:
        copy.wait()


def pair(z, own, got):
    rows, depth = own.shape
    return call(
        pair_kernel,
        4 * rows * depth,
        6 * rows * depth,
        in_specs=[SMEM, ANY, ANY],
        out_specs=[ANY] * 8,
        out_shape=[jax.ShapeDtypeStruct((48, depth), bf16)] * 8,
        scratch_shapes=[
            pltpu.VMEM((rows, depth), bf16),
            pltpu.VMEM((rows, depth), bf16),
            pltpu.VMEM((8, 48, depth), bf16),
            pltpu.SemaphoreType.DMA((2,)),
            pltpu.SemaphoreType.DMA((8,)),
        ],
        name="pair",
    )(z, own, got)


def finish_kernel(z_ref, tokens_hbm, *refs):
    parts_hbm = refs[:8]
    grad_hbm, down_hbm, parts, tokens, lows, grad, down, sem, out_sem = refs[8:]
    z = z_ref[0]
    later = begin(tokens_hbm, tokens, sem.at[8])
    copies = [begin(parts_hbm[k], parts.at[k], sem.at[k]) for k in range(8)]
    for copy in copies:
        copy.wait()
    total = parts[0, :32, :].astype(f32)
    for k in range(1, 8):
        total += parts[k, :32, :].astype(f32)
    grad[...] = total.astype(bf16)
    first = begin(grad, grad_hbm, out_sem.at[0])
    for k in range(8):
        lows[lax.rem(z + 8 - k, 8)] = unpack(parts[k, 32:48, :])
    low = lows[0]
    for k in range(1, 8):
        low += lows[k]
    later.wait()
    down[...] = three(low * adapter_scale, tokens[...], 1, 0)
    begin(down, down_hbm, out_sem.at[1]).wait()
    first.wait()


def finish(z, tokens, parts):
    depth = tokens.shape[1]
    return call(
        finish_kernel,
        2 * 512 * 256 * depth,
        2 * MIB,
        in_specs=[SMEM] + [ANY] * 9,
        out_specs=[ANY, ANY],
        out_shape=[
            jax.ShapeDtypeStruct((32, depth), bf16),
            jax.ShapeDtypeStruct((RANK, depth), f32),
        ],
        scratch_shapes=[
            pltpu.VMEM((8, 48, depth), bf16),
            pltpu.VMEM(tokens.shape, bf16),
            pltpu.VMEM((8, RANK, CHUNK), f32),
            pltpu.VMEM((32, depth), bf16),
            pltpu.VMEM((RANK, depth), f32),
            pltpu.SemaphoreType.DMA((9,)),
            pltpu.SemaphoreType.DMA((2,)),
        ],
        name="finish",
    )(z, tokens, *parts)


def output_kernel(
    scale_hbm, given_hbm, parts_hbm, out_hbm, mag_hbm, up_hbm,
    scale, cot, parts, out, mag, up, first_sem, sem, out_sem,
):
    width = out.shape[1]
    chunks = chunks_of(width)
    count = width // LANES
    first = (
        begin(scale_hbm, scale, first_sem.at[0]),
        begin(parts_hbm.at[:, :, width:], parts.at[:, :, width:], first_sem.at[1]),
    )
    ready = stream([(given_hbm, cot), (parts_hbm, parts.at[:, :, :width])], sem, chunks)
    for copy in first:
        copy.wait()

    def added(cols):
        total = parts[0, :, cols].astype(f32)
        for r in range(1, 16):
            total += parts[r, :, cols].astype(f32)
        return total

    extra = added(slice(width, width + 3 * LANES))
    proj = jnp.concatenate([extra[:16, : 2 * LANES], extra[16:, : 2 * LANES]], axis=1)
    proj = proj * adapter_scale
    mag[...] = extra[:count, 2 * LANES :] / scale[32 : 32 + count, :]
    stores = [begin(mag, mag_hbm, first_sem.at[0])]
    factors = scale[:32, :]
    for j, (at, size) in enumerate(chunks):
        ready(j)
        cols = slice(at, at + size)
        factor = in_line(factors, at, size)
        out[:, cols] = (added(cols) * factor).astype(bf16)
        stores.append(begin(out.at[:, cols], out_hbm.at[:, cols], out_sem.at[0, j]))
        value = cot[:, :, cols].reshape(512, size).astype(f32)
        up[:, cols] = three(proj, (value * factor).astype(bf16), 1, 0)
        stores.append(begin(up.at[:, cols], up_hbm.at[:, cols], out_sem.at[1, j]))
    for copy in stores:
        copy.wait()


def output_of(scale, given, parts):
    width = given.shape[2] - 2 * LANES
    count = len(chunks_of(width))
    return call(
        output_kernel,
        2 * 512 * 256 * width,
        8 * MIB,
        in_specs=[ANY] * 3,
        out_specs=[ANY] * 3,
        out_shape=[
            jax.ShapeDtypeStruct((32, width), bf16),
            jax.ShapeDtypeStruct((width // LANES, LANES), f32),
            jax.ShapeDtypeStruct((RANK, width), f32),
        ],
        scratch_shapes=[
            pltpu.VMEM(scale.shape, f32),
            pltpu.VMEM((16, 32, width), bf16),
            pltpu.VMEM(parts.shape, bf16),
            pltpu.VMEM((32, width), bf16),
            pltpu.VMEM((width // LANES, LANES), f32),
            pltpu.VMEM((RANK, width), f32),
            pltpu.SemaphoreType.DMA((2,)),
            pltpu.SemaphoreType.DMA((2, count)),
            pltpu.SemaphoreType.DMA((2, count)),
        ],
        name="output",
    )(scale, given, parts)


def exchange(blocks):
    return lax.all_to_all(blocks, ROW, 0, 0, tiled=False)


def on_device(tokens, weight, down_adapter, up_adapter, magnitude, out_cotangent):
    z, core = [lax.axis_index(name).astype(jnp.int32).reshape(1) for name in COL]
    down_t = down_adapter.T
    magnitude = magnitude.reshape(-1, LANES)
    tokens_full = lax.all_gather(tokens, COL, axis=0)
    merged_low, message = merge(down_t, up_adapter, weight, out_cotangent)
    given = exchange(message)
    part = forward(tokens_full, down_t, merged_low)
    part = add_magnitude(given, part)
    parts = exchange(part)
    own, send, scale = backward(core, magnitude, up_adapter, given, merged_low)
    got = lax.ppermute(send, "c", [(0, 1), (1, 0)])
    blocks = list(pair(z, own, got))
    for k in range(1, 8):
        blocks[k] = lax.ppermute(blocks[k], "z", [(i, (i + k) % 8) for i in range(8)])
    grad_tokens, down_gradient = finish(z, tokens_full.reshape(512, -1), blocks)
    output, grad_magnitude, up_gradient = output_of(scale, given, parts)
    return (output, grad_tokens, grad_magnitude.reshape(-1), up_gradient, down_gradient.T)


def solution(mesh):
    split = Mesh(mesh.devices.reshape(4, 4, 8, 2), ROW + COL)
    return jax.shard_map(
        on_device,
        mesh=split,
        in_specs=(P(COL, ROW), P(ROW, COL), P(ROW, None), P(None, COL), P(COL), P(ROW, COL)),
        out_specs=(P(ROW, COL), P(COL, ROW), P(COL), P(None, COL), P(ROW, None)),
        check_vma=False,
    )
```

time: 155 us -> 154 us (level)
  waiting for transfers between devices: 30.2 us -> 55 us
  starting transfers between devices: 63.9 us -> 41.4 us
  other arithmetic: 4.13 us -> 0 us
    ppermute x22 -> x0, starting transfers between devices: 37.7 us -> none  [the longest x18 27.4 us: shifted(): lax.ppermute(value, axis, [(i, (i + k) % size) for i in range(size)])]
    all_gather x1, waiting for transfers between devices: 0.01 us -> 28.8 us  [on_device(): tokens_full = lax.all_gather(tokens, COL, axis=0)]
    ppermute x22 -> x0, waiting for transfers between devices: 23.9 us -> none  [the longest x18 20.2 us: shifted(): lax.ppermute(value, axis, [(i, (i + k) % size) for i in range(size)])]
    all_to_all x1 -> x2, waiting for transfers between devices: 0.01 us -> 12.7 us  [exchange(): return lax.all_to_all(blocks, ROW, 0, 0, tiled=False)]
    all_to_all x1 -> x2, starting transfers between devices: 9.71 us -> 22.2 us  [exchange(): return lax.all_to_all(blocks, ROW, 0, 0, tiled=False)]
    ppermute x7, waiting for transfers between devices: 6.26 us -> 10.7 us  [on_device(): lax.ppermute(blocks[k], 'z', [(i, (i + k) % 8) for i in range(8)])]
    pallas_call x4, Pallas kernels: 24.1 us -> 27.2 us  [the longest x1 8.13 us: forward(): call(forward_kernel, 32 * 512 * depth * width, 12 * MIB, in_specs=[ANY] *...]
    ppermute x7, starting transfers between devices: 16.4 us -> 19 us  [on_device(): lax.ppermute(blocks[k], 'z', [(i, (i + k) % 8) for i in range(8)])]
  transfers between devices with their start and end apart: 32 -> 11, of which waited for: 12 -> 8; matrix products, arithmetic and copies ran while one was open for 2% -> 0% of each run, Pallas kernels for 12% -> 18%
where the time goes in v5:
time: 154 us; the launch traced here: 152 us
  waiting for transfers between devices  55 us (36%)
  starting transfers between devices  41.4 us (27%)
  Pallas kernels  39.9 us (26%)
  between operations  14.1 us (9%)
    all_gather x1, waiting for transfers between devices, on_device(): tokens_full = lax.all_gather(tokens, COL, axis=0)  28.8 us
    all_to_all x2, starting transfers between devices, exchange(): return lax.all_to_all(blocks, ROW, 0, 0, tiled=False)  22.2 us
    ppermute x7, starting transfers between devices, on_device(): lax.ppermute(blocks[k], 'z', [(i, (i + k) % 8) for i in range(8)])  19 us
    all_to_all x2, waiting for transfers between devices, exchange(): return lax.all_to_all(blocks, ROW, 0, 0, tiled=False)  12.7 us
    ppermute x7, waiting for transfers between devices, on_device(): lax.ppermute(blocks[k], 'z', [(i, (i + k) % 8) for i in range(8)])  10.7 us
    pallas_call x1, Pallas kernels, forward(): call(forward_kernel, 32 * 512 * depth * width, 12 * MIB, in_specs=[ANY] *...  8.13 us
    pallas_call x1, Pallas kernels, backward(): call(backward_kernel, 2 * 512 * depth * width, 12 * MIB, in_specs=[SMEM]...  7.94 us
    pallas_call x1, Pallas kernels, merge(): call(merge_kernel, 16 * 512 * depth * width, 18 * MIB, in_specs=[ANY] * 4...  7.24 us
  transfers between devices with their start and end apart: 11, of which 8 were waited for; matrix products, arithmetic and copies ran while one was open for 0% of the time, Pallas kernels for 18%

profile of v5, /device:TPU:8, one launch (start us, length us, event | category | flops | bytes accessed | tf_op | source)
XLA Modules:
  0.0 151.9 jit_solution(6707888280815121370)
XLA Ops:
  7.2 0.0 all-gather.3.cloned.1.call-start
  7.2 0.7 all-gather.3.cloned.1.call-update
  7.9 7.2 %merge.1 = (bf16[1024,3328]{1,0:T(8,128)(2,1)}, bf16[16,32,3584]{2,1,0:T(8,128)(2,1)}) custom-call(f32[16,1024]{1,0:T(8,128)} %bitcast.8, f32[16,3328]{1,0:T(8,128)} %up_hbm.3, bf16[1024,3328]{1,0:T(8,128)(2,1)} %weight_hbm.1, bf16[32,3328]{1,0:T(8,128)(2,1)} %cot_hbm.1), custom_call_target="tpu_custom_call" | custom-call | flops 27917287424 | bytes 18874368 | tf_op jit(solution)/shard_map/merge/pallas_call | solution.py:138
  15.1 7.4 %all-to-all-start = ((bf16[16,32,3584]{2,1,0:T(8,128)(2,1)}), bf16[16,32,3584]{2,1,0:T(8,128)(2,1)}, u32[]{:S(2)}, u32[]{:S(2)}) async-start(bf16[16,32,3584]{2,1,0:T(8,128)(2,1)} %get-tuple-element.23), calls=%async_computation | async-start | bytes 7340032 | tf_op jit(solution)/shard_map/all_to_all | solution.py:506
  22.5 28.8 %all-gather.3.cloned.1.call-done.tokens_hbm = bf16[512,1024]{1,0:T(8,128)(2,1)} async-done(((bf16[32,1024]{1,0:T(8,128)(2,1)}), bf16[512,1024]{1,0:T(8,128)(2,1)}) %all-gather.3.cloned.1.call-update) | async-done | bytes 1048592 | tf_op jit(solution)/shard_map/all_gather | solution.py:513
  51.3 8.1 %forward.1.part_hbm = bf16[16,32,3712]{2,1,0:T(8,128)(2,1)} custom-call(bf16[16,32,1024]{2,1,0:T(8,128)(2,1)} %bitcast.7, f32[16,1024]{1,0:T(8,128)} %bitcast.9, bf16[1024,3328]{1,0:T(8,128)(2,1)} %get-tuple-element.24.merged_hbm), custom_call_target="tpu_custom_call" | custom-call | flops 55834574848 | bytes 12582912 | tf_op jit(solution)/shard_map/forward/pallas_call | solution.py:195
  59.5 10.4 %all-to-all-done.given_hbm = bf16[16,32,3584]{2,1,0:T(8,128)(2,1)} async-done(((bf16[16,32,3584]{2,1,0:T(8,128)(2,1)}), bf16[16,32,3584]{2,1,0:T(8,128)(2,1)}, u32[]{:S(2)}, u32[]{:S(2)}) %all-to-all-start) | async-done | bytes 3670048 | tf_op jit(solution)/shard_map/all_to_all | solution.py:506
  69.9 5.7 %magnitude.1 = bf16[16,32,3712]{2,1,0:T(8,128)(2,1)} custom-call(bf16[16,32,3584]{2,1,0:T(8,128)(2,1)} %all-to-all-done.given_hbm, bf16[16,32,3712]{2,1,0:T(8,128)(2,1)} %forward.1.part_hbm), custom_call_target="tpu_custom_call", output_to_operand_aliasing={{}: (1, {})} | custom-call | flops 6815744 | bytes 7340032 | tf_op jit(solution)/shard_map/magnitude/pallas_call | solution.py:236
  75.6 14.8 %all-to-all-start.1 = ((bf16[16,32,3712]{2,1,0:T(8,128)(2,1)}), bf16[16,32,3712]{2,1,0:T(8,128)(2,1)}, u32[]{:S(2)}, u32[]{:S(2)}) async-start(bf16[16,32,3712]{2,1,0:T(8,128)(2,1)} %magnitude.1), calls=%async_computation.1 | async-start | bytes 7602176 | tf_op jit(solution)/shard_map/all_to_all | solution.py:506
  90.5 7.9 %backward.1 = (bf16[272,1024]{1,0:T(8,128)(2,1)}, bf16[272,1024]{1,0:T(8,128)(2,1)}, f32[64,128]{1,0:T(8,128)}) custom-call(s32[1]{0:T(128)} %bitcast.core_ref, f32[26,128]{1,0:T(8,128)} %bitcast.11, f32[16,3328]{1,0:T(8,128)} %up_hbm.3, bf16[16,32,3584]{2,1,0:T(8,128)(2,1)} %all-to-all-done.given_hbm, bf16[1024,3328]{1,0:T(8,128)(2,1)} %get-tuple-element.24.merged_hbm), custom_call_target="tpu_custom_call" | custom-call | flops 3489660928 | bytes 12582912 | tf_op jit(solution)/shard_map/backward/pallas_call | solution.py:322
  98.4 0.1 collective-permute-start
  98.5 2.1 %collective-permute-done.got_hbm = bf16[272,1024]{1,0:T(8,128)(2,1)S(1)} collective-permute-done((bf16[272,1024]{1,0:T(8,128)(2,1)}, bf16[272,1024]{1,0:T(8,128)(2,1)S(1)}, u32[]{:S(2)}, u32[]{:S(2)}) %collective-permute-start) | collective-permute-done | bytes 557088 | tf_op jit(solution)/shard_map/ppermute | solution.py:520
  100.7 0.0 copy-start
  100.7 0.8 copy-done
  101.5 2.2 %pair.1 = (bf16[48,1024]{1,0:T(8,128)(2,1)}, bf16[48,1024]{1,0:T(8,128)(2,1)}, bf16[48,1024]{1,0:T(8,128)(2,1)}, bf16[48,1024]{1,0:T(8,128)(2,1)}, bf16[48,1024]...) custom-call(s32[1]{0:T(128)} %bitcast.4.z_ref, ...), custom_call_target="tpu_custom_call" | custom-call | flops 1114112 | bytes 1671168 | tf_op jit(solution)/shard_map/pair/pallas_call | solution.py:369
  103.7 2.1 %collective-permute-start.1 = (bf16[48,1024]{1,0:T(8,128)(2,1)}, bf16[48,1024]{1,0:T(8,128)(2,1)S(1)}, u32[]{:S(2)}, u32[]{:S(2)}) collective-permute-start(bf16[48,1024]{1,0:T(8,128)(2,1)} %get-tuple-element.30), channel_id=1, source_target_pairs={{0,2},{2,4},{4,6},{6,8},{8,10},{10,12},{12,14},{14,0},{1,3},{3,5},... | collective-permute-start | bytes 294920 | tf_op jit(solution)/shard_map/ppermute | solution.py:523
  105.8 3.3 %collective-permute-start.2 = (bf16[48,1024]{1,0:T(8,128)(2,1)}, bf16[48,1024]{1,0:T(8,128)(2,1)S(1)}, u32[]{:S(2)}, u32[]{:S(2)}) collective-permute-start(bf16[48,1024]{1,0:T(8,128)(2,1)} %get-tuple-element.31), channel_id=1, source_target_pairs={{0,4},{2,6},{4,8},{6,10},{8,12},{10,14},{12,0},{14,2},{1,5},{3,7},... | collective-permute-start | bytes 294920 | tf_op jit(solution)/shard_map/ppermute | solution.py:523
  109.1 3.8 %collective-permute-start.3 = (bf16[48,1024]{1,0:T(8,128)(2,1)}, bf16[48,1024]{1,0:T(8,128)(2,1)S(1)}, u32[]{:S(2)}, u32[]{:S(2)}) collective-permute-start(bf16[48,1024]{1,0:T(8,128)(2,1)} %get-tuple-element.32), channel_id=1, source_target_pairs={{0,6},{2,8},{4,10},{6,12},{8,14},{10,0},{12,2},{14,4},{1,7},{3,9},... | collective-permute-start | bytes 294920 | tf_op jit(solution)/shard_map/ppermute | solution.py:523
  112.9 0.8 collective-permute-start.4
  113.8 4.9 %collective-permute-start.5 = (bf16[48,1024]{1,0:T(8,128)(2,1)}, bf16[48,1024]{1,0:T(8,128)(2,1)S(1)}, u32[]{:S(2)}, u32[]{:S(2)}) collective-permute-start(bf16[48,1024]{1,0:T(8,128)(2,1)} %get-tuple-element.34), channel_id=1, source_target_pairs={{0,10},{2,12},{4,14},{6,0},{8,2},{10,4},{12,6},{14,8},{1,11},{3,13... | collective-permute-start | bytes 294920 | tf_op jit(solution)/shard_map/ppermute | solution.py:523
  118.6 0.0 collective-permute-done.1.refs_1_
  118.6 0.0 copy-start.1
  118.6 2.7 %collective-permute-start.6 = (bf16[48,1024]{1,0:T(8,128)(2,1)}, bf16[48,1024]{1,0:T(8,128)(2,1)S(1)}, u32[]{:S(2)}, u32[]{:S(2)}) collective-permute-start(bf16[48,1024]{1,0:T(8,128)(2,1)} %get-tuple-element.35), channel_id=1, source_target_pairs={{0,12},{2,14},{4,0},{6,2},{8,4},{10,6},{12,8},{14,10},{1,13},{3,15... | collective-permute-start | bytes 294920 | tf_op jit(solution)/shard_map/ppermute | solution.py:523
  121.3 0.0 collective-permute-done.2.refs_2_
  121.3 0.0 copy-start.2
  121.3 1.4 collective-permute-start.7
  122.7 4.0 %collective-permute-done.3.refs_3_ = bf16[48,1024]{1,0:T(8,128)(2,1)S(1)} collective-permute-done((bf16[48,1024]{1,0:T(8,128)(2,1)}, bf16[48,1024]{1,0:T(8,128)(2,1)S(1)}, u32[]{:S(2)}, u32[]{:S(2)}) %collective-permute-start.3) | collective-permute-done | bytes 98336 | tf_op jit(solution)/shard_map/ppermute | solution.py:523
  126.7 0.0 copy-start.3
  126.7 0.0 collective-permute-done.4.refs_4_
  126.7 0.0 copy-start.4
  126.7 4.7 %collective-permute-done.5.refs_5_ = bf16[48,1024]{1,0:T(8,128)(2,1)S(1)} collective-permute-done((bf16[48,1024]{1,0:T(8,128)(2,1)}, bf16[48,1024]{1,0:T(8,128)(2,1)S(1)}, u32[]{:S(2)}, u32[]{:S(2)}) %collective-permute-start.5) | collective-permute-done | bytes 98336 | tf_op jit(solution)/shard_map/ppermute | solution.py:523
  131.4 0.0 copy-start.5
  131.4 1.4 collective-permute-done.6.refs_6_
  132.8 0.0 copy-start.6
  132.8 0.7 collective-permute-done.7.refs_7_
  133.5 0.0 copy-start.7
  133.5 0.0 copy-done.1
  133.5 0.0 copy-done.2
  133.5 0.0 copy-done.3
  133.5 0.0 copy-done.4
  133.5 0.0 copy-done.5
  133.5 0.0 copy-done.6
  133.5 0.6 copy-done.7
  134.1 2.5 %finish.1 = (bf16[32,1024]{1,0:T(8,128)(2,1)}, f32[16,1024]{1,0:T(8,128)}) custom-call(s32[1]{0:T(128)} %bitcast.4.z_ref, bf16[512,1024]{1,0:T(8,128)(2,1)} %all-gather.3.cloned.1.call-done.tokens_hbm, bf16[48,1024]{1,0:T(8,128)(2,1)} %get-tuple-element.29.refs_0_, bf16[48,1024]{1,0:T(8,128)(2,1)} %copy-done.1, bf16[48,1024]{1,0:T(8,128)(2,1)} %copy-done.2, ...), custom_call_target="tpu_custom_call" | custom-call | flops 268435456 | bytes 2097152 | tf_op jit(solution)/shard_map/finish/pallas_call | solution.py:413
  136.7 2.2 %all-to-all-done.1.parts_hbm = bf16[16,32,3712]{2,1,0:T(8,128)(2,1)} async-done(((bf16[16,32,3712]{2,1,0:T(8,128)(2,1)}), bf16[16,32,3712]{2,1,0:T(8,128)(2,1)}, u32[]{:S(2)}, u32[]{:S(2)}) %all-to-all-start.1) | async-done | bytes 3801120 | tf_op jit(solution)/shard_map/all_to_all | solution.py:506
  138.9 6.1 %output.1 = (bf16[32,3328]{1,0:T(8,128)(2,1)}, f32[26,128]{1,0:T(8,128)}, f32[16,3328]{1,0:T(8,128)}) custom-call(f32[64,128]{1,0:T(8,128)} %get-tuple-element.25.scale_hbm, bf16[16,32,3584]{2,1,0:T(8,128)(2,1)} %all-to-all-done.given_hbm, bf16[16,32,3712]{2,1,0:T(8,128)(2,1)} %all-to-all-done.1.parts_hbm), custom_call_target="tpu_custom_call" | custom-call | flops 872415232 | bytes 8388608 | tf_op jit(solution)/shard_map/output/pallas_call | solution.py:479
Async XLA Ops:
  7.2 44.2 %all-gather.3.cloned.1.call-start = ((), (), s32[]{:S(2)}) async-start(), calls=%async_computation.2 | async-start | bytes 1114112 | tf_op jit(solution)/shard_map/all_gather | solution.py:513
  15.1 54.8 %all-to-all-start = ((bf16[16,32,3584]{2,1,0:T(8,128)(2,1)}), bf16[16,32,3584]{2,1,0:T(8,128)(2,1)}, u32[]{:S(2)}, u32[]{:S(2)}) async-start(bf16[16,32,3584]{2,1,0:T(8,128)(2,1)} %get-tuple-element.23), calls=%async_computation | async-start | bytes 7340032 | tf_op jit(solution)/shard_map/all_to_all | solution.py:506
  75.6 63.2 %all-to-all-start.1 = ((bf16[16,32,3712]{2,1,0:T(8,128)(2,1)}), bf16[16,32,3712]{2,1,0:T(8,128)(2,1)}, u32[]{:S(2)}, u32[]{:S(2)}) async-start(bf16[16,32,3712]{2,1,0:T(8,128)(2,1)} %magnitude.1), calls=%async_computation.1 | async-start | bytes 7602176 | tf_op jit(solution)/shard_map/all_to_all | solution.py:506
  98.4 2.3 %collective-permute-start = (bf16[272,1024]{1,0:T(8,128)(2,1)}, bf16[272,1024]{1,0:T(8,128)(2,1)S(1)}, u32[]{:S(2)}, u32[]{:S(2)}) collective-permute-start(bf16[272,1024]{1,0:T(8,128)(2,1)} %get-tuple-element.28), channel_id=1, source_target_pairs={{0,1},{1,0},{2,3},{3,2},{4,5},{5,4},{6,7},{7,6},{8,9},{9,8},{10,11... | collective-permute-start | bytes 1671176 | tf_op jit(solution)/shard_map/ppermute | solution.py:520
  100.7 0.8 copy-start
  103.7 14.9 %collective-permute-start.1 = (bf16[48,1024]{1,0:T(8,128)(2,1)}, bf16[48,1024]{1,0:T(8,128)(2,1)S(1)}, u32[]{:S(2)}, u32[]{:S(2)}) collective-permute-start(bf16[48,1024]{1,0:T(8,128)(2,1)} %get-tuple-element.30), channel_id=1, source_target_pairs={{0,2},{2,4},{4,6},{6,8},{8,10},{10,12},{12,14},{14,0},{1,3},{3,5},... | collective-permute-start | bytes 294920 | tf_op jit(solution)/shard_map/ppermute | solution.py:523
  105.8 15.5 %collective-permute-start.2 = (bf16[48,1024]{1,0:T(8,128)(2,1)}, bf16[48,1024]{1,0:T(8,128)(2,1)S(1)}, u32[]{:S(2)}, u32[]{:S(2)}) collective-permute-start(bf16[48,1024]{1,0:T(8,128)(2,1)} %get-tuple-element.31), channel_id=1, source_target_pairs={{0,4},{2,6},{4,8},{6,10},{8,12},{10,14},{12,0},{14,2},{1,5},{3,7},... | collective-permute-start | bytes 294920 | tf_op jit(solution)/shard_map/ppermute | solution.py:523
  109.1 17.6 %collective-permute-start.3 = (bf16[48,1024]{1,0:T(8,128)(2,1)}, bf16[48,1024]{1,0:T(8,128)(2,1)S(1)}, u32[]{:S(2)}, u32[]{:S(2)}) collective-permute-start(bf16[48,1024]{1,0:T(8,128)(2,1)} %get-tuple-element.32), channel_id=1, source_target_pairs={{0,6},{2,8},{4,10},{6,12},{8,14},{10,0},{12,2},{14,4},{1,7},{3,9},... | collective-permute-start | bytes 294920 | tf_op jit(solution)/shard_map/ppermute | solution.py:523
  112.9 13.8 %collective-permute-start.4 = (bf16[48,1024]{1,0:T(8,128)(2,1)}, bf16[48,1024]{1,0:T(8,128)(2,1)S(1)}, u32[]{:S(2)}, u32[]{:S(2)}) collective-permute-start(bf16[48,1024]{1,0:T(8,128)(2,1)} %get-tuple-element.33), channel_id=1, source_target_pairs={{0,8},{2,10},{4,12},{6,14},{8,0},{10,2},{12,4},{14,6},{1,9},{3,11}... | collective-permute-start | bytes 294920 | tf_op jit(solution)/shard_map/ppermute | solution.py:523
  113.8 17.6 %collective-permute-start.5 = (bf16[48,1024]{1,0:T(8,128)(2,1)}, bf16[48,1024]{1,0:T(8,128)(2,1)S(1)}, u32[]{:S(2)}, u32[]{:S(2)}) collective-permute-start(bf16[48,1024]{1,0:T(8,128)(2,1)} %get-tuple-element.34), channel_id=1, source_target_pairs={{0,10},{2,12},{4,14},{6,0},{8,2},{10,4},{12,6},{14,8},{1,11},{3,13... | collective-permute-start | bytes 294920 | tf_op jit(solution)/shard_map/ppermute | solution.py:523
  118.6 14.8 %copy-start.1 = (bf16[48,1024]{1,0:T(8,128)(2,1)}, bf16[48,1024]{1,0:T(8,128)(2,1)S(1)}, u32[]{:S(2)}) copy-start(bf16[48,1024]{1,0:T(8,128)(2,1)S(1)} %collective-permute-done.1.refs_1_) | copy-start | bytes 294916
  118.6 14.1 %collective-permute-start.6 = (bf16[48,1024]{1,0:T(8,128)(2,1)}, bf16[48,1024]{1,0:T(8,128)(2,1)S(1)}, u32[]{:S(2)}, u32[]{:S(2)}) collective-permute-start(bf16[48,1024]{1,0:T(8,128)(2,1)} %get-tuple-element.35), channel_id=1, source_target_pairs={{0,12},{2,14},{4,0},{6,2},{8,4},{10,6},{12,8},{14,10},{1,13},{3,15... | collective-permute-start | bytes 294920 | tf_op jit(solution)/shard_map/ppermute | solution.py:523
  121.3 12.1 %copy-start.2 = (bf16[48,1024]{1,0:T(8,128)(2,1)}, bf16[48,1024]{1,0:T(8,128)(2,1)S(1)}, u32[]{:S(2)}) copy-start(bf16[48,1024]{1,0:T(8,128)(2,1)S(1)} %collective-permute-done.2.refs_2_) | copy-start | bytes 294916
  121.3 12.1 %collective-permute-start.7 = (bf16[48,1024]{1,0:T(8,128)(2,1)}, bf16[48,1024]{1,0:T(8,128)(2,1)S(1)}, u32[]{:S(2)}, u32[]{:S(2)}) collective-permute-start(bf16[48,1024]{1,0:T(8,128)(2,1)} %get-tuple-element.36), channel_id=1, source_target_pairs={{0,14},{2,0},{4,2},{6,4},{8,6},{10,8},{12,10},{14,12},{1,15},{3,1}... | collective-permute-start | bytes 294920 | tf_op jit(solution)/shard_map/ppermute | solution.py:523
  126.7 6.8 %copy-start.3 = (bf16[48,1024]{1,0:T(8,128)(2,1)}, bf16[48,1024]{1,0:T(8,128)(2,1)S(1)}, u32[]{:S(2)}) copy-start(bf16[48,1024]{1,0:T(8,128)(2,1)S(1)} %collective-permute-done.3.refs_3_) | copy-start | bytes 294916
  126.7 6.8 %copy-start.4 = (bf16[48,1024]{1,0:T(8,128)(2,1)}, bf16[48,1024]{1,0:T(8,128)(2,1)S(1)}, u32[]{:S(2)}) copy-start(bf16[48,1024]{1,0:T(8,128)(2,1)S(1)} %collective-permute-done.4.refs_4_) | copy-start | bytes 294916
  131.4 2.1 %copy-start.5 = (bf16[48,1024]{1,0:T(8,128)(2,1)}, bf16[48,1024]{1,0:T(8,128)(2,1)S(1)}, u32[]{:S(2)}) copy-start(bf16[48,1024]{1,0:T(8,128)(2,1)S(1)} %collective-permute-done.5.refs_5_) | copy-start | bytes 294916
  132.8 0.7 copy-start.6
  133.5 0.7 copy-start.7
Sparse Core Ops, SparseCore 0:
  9.8 41.4 all-gather.2

commit v6 on v5

v6 whole, which is shorter than its diff:
```python
import jax
import jax.numpy as jnp
from jax import lax
from jax.experimental import pallas as pl
from jax.experimental.pallas import tpu as pltpu
from jax.sharding import Mesh
from jax.sharding import PartitionSpec as P

adapter_scale = 2.0
epsilon = 1e-06
bf16 = jnp.bfloat16
f32 = jnp.float32
ROW = ("x", "y")
COL = ("z", "c")
CHUNK = 512
RANK = 16
LANES = 128
MIB = 1024 * 1024
LIMIT = 62 * MIB
ANY = pl.BlockSpec(memory_space=pl.ANY)
SMEM = pl.BlockSpec(memory_space=pltpu.SMEM)


def pieces(value):
    high = value.astype(bf16)
    rest = value - high.astype(f32)
    mid = rest.astype(bf16)
    low = (rest - mid.astype(f32)).astype(bf16)
    return high, mid, low


def dot(left, right, left_dim, right_dim):
    return lax.dot_general(
        left, right, (((left_dim,), (right_dim,)), ((), ())), preferred_element_type=f32
    )


def three(left, right, left_dim, right_dim):
    out = dot(jnp.concatenate(pieces(left), axis=0), right, left_dim, right_dim)
    return out[:RANK] + out[RANK : 2 * RANK] + out[2 * RANK :]


def chunks_of(width):
    return [(at, min(CHUNK, width - at)) for at in range(0, width, CHUNK)]


def call(body, flops, moved, **options):
    return pl.pallas_call(
        body,
        compiler_params=pltpu.CompilerParams(vmem_limit_bytes=LIMIT),
        cost_estimate=pl.CostEstimate(flops=flops, bytes_accessed=moved, transcendentals=0),
        **options,
    )


def begin(source, target, sem):
    copy = pltpu.make_async_copy(source, target, sem)
    copy.start()
    return copy


def stream(pairs, sem, chunks, depth=2):
    def copies(j):
        for i, (source, target) in enumerate(pairs):
            index = (slice(None),) * (len(target.shape) - 1) + (pl.ds(*chunks[j]),)
            yield pltpu.make_async_copy(source.at[index], target.at[index], sem.at[i, j])

    def start(j):
        if j < len(chunks):
            for copy in copies(j):
                copy.start()

    def ready(j):
        for copy in copies(j):
            copy.wait()
        start(j + depth)

    for j in range(depth):
        start(j)
    return ready


def in_rows(row):
    return [row[:, at : at + LANES] for at in range(0, row.shape[1], LANES)]


def in_line(rows, at, size):
    return jnp.concatenate(
        [rows[k : k + 1, :] for k in range(at // LANES, (at + size) // LANES)], axis=1
    )


def merge_kernel(
    down_hbm, up_hbm, weight_hbm, merged_hbm, sums_hbm,
    down, up, weight, merged, sums, up_cat, totals, small_sem, in_sem, out_sem,
):
    depth, width = weight.shape
    rows, tile = 256, 256
    steps = [slice(at, at + rows) for at in range(0, depth, rows)]
    first = begin(up_hbm, up, small_sem.at[0]), begin(down_hbm, down, small_sem.at[1])
    fetches = [begin(weight_hbm.at[p], weight.at[p], in_sem.at[j]) for j, p in enumerate(steps)]
    totals[...] = jnp.zeros_like(totals)
    for copy in first:
        copy.wait()
    for at in range(0, width, tile):
        cols = slice(at, at + tile)
        u1, u2, u3 = pieces(up[:, cols])
        up_cat[:, cols] = jnp.concatenate([u1, u2, u1, u3, u1, u2], axis=0)
    d1, d2, d3 = pieces(down[...] * adapter_scale)
    down_cat = jnp.concatenate([d1, d1, d2, d1, d3, d2], axis=0)
    stores = []
    for j, part in enumerate(steps):
        fetches[j].wait()
        for at in range(0, width, tile):
            cols = slice(at, at + tile)
            value = weight[part, cols].astype(f32) + dot(down_cat[:, part], up_cat[:, cols], 0, 0)
            merged[part, cols] = value.astype(bf16)
            totals[:, cols] += jnp.sum((value * value).reshape(rows // 8, 8, tile), axis=0)
        stores.append(begin(merged.at[part], merged_hbm.at[part], out_sem.at[j]))
    lines = in_rows(jnp.sum(totals[...], axis=0, keepdims=True))
    sums[...] = jnp.concatenate(lines + [jnp.zeros((32 - len(lines), LANES), f32)], axis=0)
    stores.append(begin(sums, sums_hbm, small_sem.at[0]))
    for copy in stores:
        copy.wait()


def merge(down_t, up, weight):
    depth, width = weight.shape
    return call(
        merge_kernel,
        12 * depth * width,
        4 * depth * width,
        in_specs=[ANY] * 3,
        out_specs=[ANY] * 2,
        out_shape=[
            jax.ShapeDtypeStruct((depth, width), bf16),
            jax.ShapeDtypeStruct((32, LANES), f32),
        ],
        scratch_shapes=[
            pltpu.VMEM((RANK, depth), f32),
            pltpu.VMEM((RANK, width), f32),
            pltpu.VMEM((depth, width), bf16),
            pltpu.VMEM((depth, width), bf16),
            pltpu.VMEM((32, LANES), f32),
            pltpu.VMEM((6 * RANK, width), bf16),
            pltpu.VMEM((8, width), f32),
            pltpu.SemaphoreType.DMA((2,)),
            pltpu.SemaphoreType.DMA((4,)),
            pltpu.SemaphoreType.DMA((4,)),
        ],
        name="merge",
    )(down_t, up, weight)


def forward_kernel(
    core_ref, own_hbm, other_hbm, down_hbm, sums_hbm, merged_hbm, part_hbm, tokens_hbm, small_hbm,
    tokens, down, small, merged, part, first_sem, sem, out_sem,
):
    core = core_ref[0]
    depth, width = merged.shape
    chunks = chunks_of(width)
    first = (
        begin(own_hbm, tokens.at[:, core], first_sem.at[0]),
        begin(other_hbm, tokens.at[:, 1 - core], first_sem.at[1]),
        begin(down_hbm, down, first_sem.at[2]),
        begin(sums_hbm, small.at[64:], first_sem.at[3]),
    )
    ready = stream([(merged_hbm, merged)], sem, chunks)
    for copy in first:
        copy.wait()
    all_tokens = tokens[...].reshape(512, depth)
    proj = three(down[...], all_tokens, 1, 1)
    for k in range(4):
        small[RANK * k : RANK * k + RANK, :] = proj[:, LANES * k : LANES * k + LANES]
    stores = [
        begin(small, small_hbm, first_sem.at[0]),
        begin(tokens, tokens_hbm, first_sem.at[1]),
    ]
    for j, (at, size) in enumerate(chunks):
        ready(j)
        cols = slice(at, at + size)
        product = dot(all_tokens, merged[:, cols], 1, 0).astype(bf16)
        part[:, :, cols] = product.reshape(16, 32, size)
        stores.append(begin(part.at[:, :, cols], part_hbm.at[:, :, cols], out_sem.at[j]))
    for copy in stores:
        copy.wait()


def forward(core, own, other, down_t, sums, merged_low):
    depth, width = merged_low.shape
    count = len(chunks_of(width))
    return call(
        forward_kernel,
        2 * 512 * depth * width,
        12 * MIB,
        in_specs=[SMEM] + [ANY] * 5,
        out_specs=[ANY] * 3,
        out_shape=[
            jax.ShapeDtypeStruct((16, 32, width + LANES), bf16),
            jax.ShapeDtypeStruct((8, 2, 32, depth), bf16),
            jax.ShapeDtypeStruct((96, LANES), f32),
        ],
        scratch_shapes=[
            pltpu.VMEM((8, 2, 32, depth), bf16),
            pltpu.VMEM((RANK, depth), f32),
            pltpu.VMEM((96, LANES), f32),
            pltpu.VMEM((depth, width), bf16),
            pltpu.VMEM((16, 32, width), bf16),
            pltpu.SemaphoreType.DMA((4,)),
            pltpu.SemaphoreType.DMA((1, count)),
            pltpu.SemaphoreType.DMA((count,)),
        ],
        name="forward",
    )(core, own, other, down_t, sums, merged_low)


def magnitude_kernel(given_hbm, part_hbm, out_hbm, cot, part, extra, sem, out_sem):
    width = cot.shape[2]
    chunks = chunks_of(width)
    ready = stream([(given_hbm, cot), (part_hbm, part)], sem, chunks, len(chunks))
    rows = []
    for j, (at, size) in enumerate(chunks):
        ready(j)
        cols = slice(at, at + size)
        product = cot[:, :, cols].astype(f32) * part[:, :, cols].astype(f32)
        total = jnp.sum(product.reshape(64, 8, size), axis=0)
        rows += in_rows(jnp.sum(total, axis=0, keepdims=True))
    rows.append(jnp.zeros((32 - len(rows), LANES), f32))
    sums = jnp.concatenate(rows, axis=0).astype(bf16)
    extra[...] = jnp.broadcast_to(sums[None], extra.shape)
    begin(extra, out_hbm.at[:, :, width:], out_sem.at[0]).wait()


def add_magnitude(given, part):
    blocks, rows, width = given.shape
    return call(
        magnitude_kernel,
        4 * 512 * width,
        7 * MIB,
        in_specs=[ANY, ANY],
        out_specs=ANY,
        out_shape=jax.ShapeDtypeStruct(part.shape, bf16),
        scratch_shapes=[
            pltpu.VMEM((blocks, rows, width), bf16),
            pltpu.VMEM((blocks, rows, width), bf16),
            pltpu.VMEM((blocks, rows, LANES), bf16),
            pltpu.SemaphoreType.DMA((2, len(chunks_of(width)))),
            pltpu.SemaphoreType.DMA((1,)),
        ],
        input_output_aliases={1: 0},
        name="magnitude",
    )(given, part)


def pack(low, out):
    high = low.astype(bf16)
    rest = (low - high.astype(f32)).astype(bf16)
    out[:, :CHUNK] = high
    out[:, CHUNK:] = rest
    return high.astype(f32) + rest.astype(f32)


def unpack(got):
    got = got.astype(f32)
    return got[:, :CHUNK] + got[:, CHUNK:]


def backward_kernel(
    core_ref, small_hbm, magnitude_hbm, up_hbm, given_hbm, merged_hbm, own_hbm, send_hbm, scale_hbm,
    squares, magnitude, up, cot, merged, total, low_total, own, send, scale, first_sem, sem,
):
    core = core_ref[0]
    depth, width = merged.shape
    chunks = chunks_of(width)
    count = width // LANES
    first = (
        begin(small_hbm.at[64:], squares, first_sem.at[0]),
        begin(up_hbm, up, first_sem.at[1]),
        begin(magnitude_hbm, magnitude, first_sem.at[2]),
    )
    ready = stream([(given_hbm, cot), (merged_hbm, merged)], sem, chunks)
    for copy in first:
        copy.wait()
    norm = jnp.sqrt(squares[...] + epsilon)
    factors = magnitude[...] / norm[:count]
    scale[...] = jnp.zeros_like(scale)
    scale[:count, :] = factors
    scale[32:, :] = norm
    last = begin(scale, scale_hbm, first_sem.at[0])
    blank = jnp.zeros((LANES - 3 * RANK, CHUNK), bf16)
    for j, (at, size) in enumerate(chunks):
        ready(j)
        cols = slice(at, at + size)
        value = cot[:, :, cols].reshape(512, size).astype(f32)
        grad = (value * in_line(factors, at, size)).astype(bf16)
        product = dot(grad, merged[:, cols], 1, 1)
        up_cat = jnp.concatenate([*pieces(up[:, cols]), blank[:, :size]], axis=0)
        low = dot(grad, up_cat, 1, 1)
        if j == 0:
            total[...] = product
            low_total[...] = low
        else:
            total[...] += product
            low_total[...] += low
    for z in range(8):
        theirs = pl.ds(pl.multiple_of((2 * z + 1 - core) * 32, 32), 32)
        send[32 * z : 32 * z + 32, :] = total[theirs, :].astype(bf16)
    low = low_total[...].T
    low = low[:RANK] + low[RANK : 2 * RANK] + low[2 * RANK : 3 * RANK]
    pack(low, send.at[256:272, :])
    first = begin(send, send_hbm, first_sem.at[1])
    for z in range(8):
        mine = pl.ds(pl.multiple_of((2 * z + core) * 32, 32), 32)
        own[32 * z : 32 * z + 32, :] = total[mine, :].astype(bf16)
    own[256:272, :] = send[256:272, :]
    begin(own, own_hbm, first_sem.at[2]).wait()
    first.wait()
    last.wait()


def backward(core, small, magnitude, up, given, merged_low):
    depth, width = merged_low.shape
    count = len(chunks_of(width))
    return call(
        backward_kernel,
        2 * 512 * depth * width,
        12 * MIB,
        in_specs=[SMEM] + [ANY] * 5,
        out_specs=[ANY] * 3,
        out_shape=[jax.ShapeDtypeStruct((272, depth), bf16)] * 2
        + [jax.ShapeDtypeStruct((64, LANES), f32)],
        scratch_shapes=[
            pltpu.VMEM((32, LANES), f32),
            pltpu.VMEM(magnitude.shape, f32),
            pltpu.VMEM((RANK, width), f32),
            pltpu.VMEM((16, 32, width), bf16),
            pltpu.VMEM((depth, width), bf16),
            pltpu.VMEM((512, depth), f32),
            pltpu.VMEM((512, LANES), f32),
            pltpu.VMEM((272, depth), bf16),
            pltpu.VMEM((272, depth), bf16),
            pltpu.VMEM((64, LANES), f32),
            pltpu.SemaphoreType.DMA((3,)),
            pltpu.SemaphoreType.DMA((2, count)),
        ],
        name="backward",
    )(core, small, magnitude, up, given, merged_low)


def pair_kernel(z_ref, own_hbm, got_hbm, keep_hbm, send_hbm, own, got, keep, send, sem, out_sem):
    bit = lax.rem(z_ref[0], 2)
    copies = begin(own_hbm, own, sem.at[0]), begin(got_hbm, got, sem.at[1])
    for copy in copies:
        copy.wait()
    low = unpack(own[256:272, :]) + unpack(got[256:272, :])
    pack(low, send.at[128:144, :])
    keep[128:144, :] = send[128:144, :]
    stores = []
    for target, other, out in ((send, 1 - bit, send_hbm), (keep, bit, keep_hbm)):
        for i in range(4):
            block = pl.ds(pl.multiple_of((2 * i + other) * 32, 32), 32)
            value = own[block, :].astype(f32) + got[block, :].astype(f32)
            target[32 * i : 32 * i + 32, :] = value.astype(bf16)
        stores.append(begin(target, out, out_sem.at[len(stores)]))
    for copy in stores:
        copy.wait()


def pair(z, own, got):
    rows, depth = own.shape
    return call(
        pair_kernel,
        4 * rows * depth,
        6 * rows * depth,
        in_specs=[SMEM, ANY, ANY],
        out_specs=[ANY] * 2,
        out_shape=[jax.ShapeDtypeStruct((144, depth), bf16)] * 2,
        scratch_shapes=[pltpu.VMEM((rows, depth), bf16)] * 2
        + [pltpu.VMEM((144, depth), bf16)] * 2
        + [pltpu.SemaphoreType.DMA((2,))] * 2,
        name="pair",
    )(z, own, got)


def quad_kernel(z_ref, keep_hbm, got_hbm, *refs):
    out_hbm = refs[:4]
    keep, got, send, sem, out_sem = refs[4:]
    half = z_ref[0] // 2
    copies = begin(keep_hbm, keep, sem.at[0]), begin(got_hbm, got, sem.at[1])
    for copy in copies:
        copy.wait()
    low = unpack(keep[128:144, :]) + unpack(got[128:144, :])
    pack(low, send.at[0, 32:48, :])
    stores = []
    for k in [2, 1, 3, 0]:
        block = pl.ds(pl.multiple_of(lax.rem(half + k, 4) * 32, 32), 32)
        send[k, :32, :] = (keep[block, :].astype(f32) + got[block, :].astype(f32)).astype(bf16)
        if k:
            send[k, 32:48, :] = send[0, 32:48, :]
        stores.append(begin(send.at[k], out_hbm[k], out_sem.at[k]))
    for copy in stores:
        copy.wait()


def quad(z, keep, got):
    rows, depth = keep.shape
    return call(
        quad_kernel,
        4 * rows * depth,
        6 * rows * depth,
        in_specs=[SMEM, ANY, ANY],
        out_specs=[ANY] * 4,
        out_shape=[jax.ShapeDtypeStruct((48, depth), bf16)] * 4,
        scratch_shapes=[pltpu.VMEM((rows, depth), bf16)] * 2
        + [pltpu.VMEM((4, 48, depth), bf16)]
        + [pltpu.SemaphoreType.DMA((2,)), pltpu.SemaphoreType.DMA((4,))],
        name="quad",
    )(z, keep, got)


def finish_kernel(z_ref, tokens_hbm, *refs):
    parts_hbm = refs[:4]
    grad_hbm, down_hbm, parts, tokens, lows, grad, down, sem, out_sem = refs[4:]
    half = z_ref[0] // 2
    copies = [begin(parts_hbm[k], parts.at[k], sem.at[k]) for k in range(4)]
    later = begin(tokens_hbm, tokens, sem.at[4])
    for copy in copies:
        copy.wait()
    total = parts[0, :32, :].astype(f32)
    for k in range(1, 4):
        total += parts[k, :32, :].astype(f32)
    grad[...] = total.astype(bf16)
    first = begin(grad, grad_hbm, out_sem.at[0])
    for k in range(4):
        lows[lax.rem(half + 4 - k, 4)] = unpack(parts[k, 32:48, :])
    low = (lows[0] + lows[1]) + (lows[2] + lows[3])
    later.wait()
    down[...] = three(low * adapter_scale, tokens[...], 1, 0)
    begin(down, down_hbm, out_sem.at[1]).wait()
    first.wait()


def finish(z, tokens, parts):
    depth = tokens.shape[1]
    return call(
        finish_kernel,
        2 * 512 * 256 * depth,
        2 * MIB,
        in_specs=[SMEM] + [ANY] * 5,
        out_specs=[ANY, ANY],
        out_shape=[
            jax.ShapeDtypeStruct((32, depth), bf16),
            jax.ShapeDtypeStruct((RANK, depth), f32),
        ],
        scratch_shapes=[
            pltpu.VMEM((4, 48, depth), bf16),
            pltpu.VMEM(tokens.shape, bf16),
            pltpu.VMEM((4, RANK, CHUNK), f32),
            pltpu.VMEM((32, depth), bf16),
            pltpu.VMEM((RANK, depth), f32),
            pltpu.SemaphoreType.DMA((5,)),
            pltpu.SemaphoreType.DMA((2,)),
        ],
        name="finish",
    )(z, tokens, *parts)


def up_kernel(
    small_hbm, scale_hbm, given_hbm, out_hbm, small, scale, cot, out, first_sem, sem, out_sem
):
    width = cot.shape[2]
    chunks = chunks_of(width)
    first = begin(small_hbm, small, first_sem.at[0]), begin(scale_hbm, scale, first_sem.at[1])
    ready = stream([(given_hbm, cot)], sem, chunks, 3)
    for copy in first:
        copy.wait()
    proj = [small[RANK * k : RANK * k + RANK, :] for k in range(4)]
    proj = jnp.concatenate(proj, axis=1) * adapter_scale
    factors = scale[:32, :]
    stores = []
    for j, (at, size) in enumerate(chunks):
        ready(j)
        cols = slice(at, at + size)
        value = cot[:, :, cols].reshape(512, size).astype(f32)
        grad = (value * in_line(factors, at, size)).astype(bf16)
        out[:, cols] = three(proj, grad, 1, 0)
        stores.append(begin(out.at[:, cols], out_hbm.at[:, cols], out_sem.at[j]))
    for copy in stores:
        copy.wait()


def up_gradient_of(small, scale, given):
    width = given.shape[2]
    count = len(chunks_of(width))
    return call(
        up_kernel,
        2 * 512 * 256 * width,
        4 * MIB,
        in_specs=[ANY] * 3,
        out_specs=ANY,
        out_shape=jax.ShapeDtypeStruct((RANK, width), f32),
        scratch_shapes=[
            pltpu.VMEM(small.shape, f32),
            pltpu.VMEM(scale.shape, f32),
            pltpu.VMEM(given.shape, bf16),
            pltpu.VMEM((RANK, width), f32),
            pltpu.SemaphoreType.DMA((2,)),
            pltpu.SemaphoreType.DMA((1, count)),
            pltpu.SemaphoreType.DMA((count,)),
        ],
        name="up_gradient",
    )(small, scale, given)


def output_kernel(
    scale_hbm, parts_hbm, out_hbm, mag_hbm, scale, parts, out, mag, first_sem, sem, out_sem
):
    width = out.shape[1]
    chunks = chunks_of(width)
    count = width // LANES
    first = (
        begin(scale_hbm, scale, first_sem.at[0]),
        begin(parts_hbm.at[:, :, width:], parts.at[:, :, width:], first_sem.at[1]),
    )
    ready = stream([(parts_hbm, parts.at[:, :, :width])], sem, chunks, 4)
    for copy in first:
        copy.wait()

    def added(cols):
        total = parts[0, :, cols].astype(f32)
        for r in range(1, 16):
            total += parts[r, :, cols].astype(f32)
        return total

    mag[...] = added(slice(width, width + LANES))[:count] / scale[32 : 32 + count, :]
    stores = [begin(mag, mag_hbm, first_sem.at[0])]
    factors = scale[:32, :]
    for j, (at, size) in enumerate(chunks):
        ready(j)
        cols = slice(at, at + size)
        out[:, cols] = (added(cols) * in_line(factors, at, size)).astype(bf16)
        stores.append(begin(out.at[:, cols], out_hbm.at[:, cols], out_sem.at[j]))
    for copy in stores:
        copy.wait()


def output_of(scale, parts):
    width = parts.shape[2] - LANES
    count = len(chunks_of(width))
    return call(
        output_kernel,
        16 * 32 * width,
        4 * MIB,
        in_specs=[ANY] * 2,
        out_specs=[ANY] * 2,
        out_shape=[
            jax.ShapeDtypeStruct((32, width), bf16),
            jax.ShapeDtypeStruct((width // LANES, LANES), f32),
        ],
        scratch_shapes=[
            pltpu.VMEM(scale.shape, f32),
            pltpu.VMEM(parts.shape, bf16),
            pltpu.VMEM((32, width), bf16),
            pltpu.VMEM((width // LANES, LANES), f32),
            pltpu.SemaphoreType.DMA((2,)),
            pltpu.SemaphoreType.DMA((1, count)),
            pltpu.SemaphoreType.DMA((count,)),
        ],
        name="output",
    )(scale, parts)


def exchange(blocks, axis):
    return lax.all_to_all(blocks, axis, 0, 0, tiled=False)


def around(value, axis):
    one, two, other = [
        lax.ppermute(value, axis, [(i, (i + k) % 4) for i in range(4)]) for k in (1, 2, 3)
    ]
    return (value + two) + (one + other)


def on_device(tokens, weight, down_adapter, up_adapter, magnitude, out_cotangent):
    z, core = [lax.axis_index(name).astype(jnp.int32).reshape(1) for name in COL]
    swap = [(0, 1), (1, 0)]
    down_t = down_adapter.T
    magnitude = magnitude.reshape(-1, LANES)
    given = lax.all_gather(out_cotangent, ROW, axis=0)
    own_tokens = exchange(jnp.broadcast_to(tokens[None], (8,) + tokens.shape), "z")
    merged_low, sums = merge(down_t, up_adapter, weight)
    own_tokens, merged_low, sums = lax.optimization_barrier((own_tokens, merged_low, sums))
    other_tokens = lax.ppermute(own_tokens, "c", swap)
    part, tokens_full, small = forward(core, own_tokens, other_tokens, down_t, sums, merged_low)
    small = around(around(small, "x"), "y")
    small, part, given = lax.optimization_barrier((small, part, given))
    part = add_magnitude(given, part)
    parts = exchange(part, ROW)
    own, send, scale = backward(core, small, magnitude, up_adapter, given, merged_low)
    got = lax.ppermute(send, "c", swap)
    keep, send = pair(z, own, got)
    got = lax.ppermute(send, "z", [(i, i ^ 1) for i in range(8)])
    blocks = list(quad(z, keep, got))
    for k in range(1, 4):
        blocks[k] = lax.ppermute(blocks[k], "z", [(i, (i + 2 * k) % 8) for i in range(8)])
    up_gradient = up_gradient_of(small, scale, given)
    grad_tokens, down_gradient = finish(z, tokens_full.reshape(512, -1), blocks)
    output, grad_magnitude = output_of(scale, parts)
    return (output, grad_tokens, grad_magnitude.reshape(-1), up_gradient, down_gradient.T)


def solution(mesh):
    split = Mesh(mesh.devices.reshape(4, 4, 8, 2), ROW + COL)
    return jax.shard_map(
        on_device,
        mesh=split,
        in_specs=(P(COL, ROW), P(ROW, COL), P(ROW, None), P(None, COL), P(COL), P(ROW, COL)),
        out_specs=(P(ROW, COL), P(COL, ROW), P(COL), P(None, COL), P(ROW, None)),
        check_vma=False,
    )
```

time: 154 us -> 146 us (0.948)
  the two profiles are of different devices: /device:TPU:8 before, /device:TPU:60 now
where the time goes in v6:
time: 146 us; the launch traced here: 145 us
  waiting for transfers between devices  50.7 us (35%)
  Pallas kernels  41.7 us (29%)
  starting transfers between devices  32.3 us (22%)
  between operations  14.2 us (10%)
  local copies, waits for them, and re-layouts  4.67 us (3%)
    all_to_all x2, waiting for transfers between devices, exchange(): return lax.all_to_all(blocks, axis, 0, 0, tiled=False)  22.9 us
    all_to_all x2, starting transfers between devices, exchange(): return lax.all_to_all(blocks, axis, 0, 0, tiled=False)  16.4 us
    ppermute x6, waiting for transfers between devices, around(): lax.ppermute(value, axis, [(i, (i + k) % 4) for i in range(4)])  12.2 us
    pallas_call x1, Pallas kernels, backward(): call(backward_kernel, 2 * 512 * depth * width, 12 * MIB, in_specs=[SMEM]...  9.38 us
    ppermute x1, waiting for transfers between devices, on_device(): got = lax.ppermute(send, 'z', [(i, i ^ 1) for i in range(8)])  8.59 us
    ppermute x3, starting transfers between devices, on_device(): lax.ppermute(blocks[k], 'z', [(i, (i + 2 * k) % 8) for i in range(8)])  8.31 us
    pallas_call x1, Pallas kernels, forward(): call(forward_kernel, 2 * 512 * depth * width, 12 * MIB, in_specs=[SMEM] +...  8.02 us
    ppermute x6, starting transfers between devices, around(): lax.ppermute(value, axis, [(i, (i + k) % 4) for i in range(4)])  6.67 us
  transfers between devices with their start and end apart: 15, of which 13 were waited for; matrix products, arithmetic and copies ran while one was open for 2% of the time, Pallas kernels for 24%

profile of v6, /device:TPU:60, one launch (start us, length us, event | category | flops | bytes accessed | tf_op | source)
XLA Modules:
  0.0 144.9 jit_solution(5584991506830241456)
XLA Ops:
  7.2 0.0 all-gather.3.cloned.1.call-start
  7.2 0.7 all-gather.3.cloned.1.call-update
  7.9 1.7 %broadcast_in_dim.2 = bf16[8,32,1024]{2,1,0:T(8,128)(2,1)} broadcast(bf16[32,1024]{1,0:T(8,128)(2,1)} %param.6), dimensions={1,2} | broadcast | bytes 589824 | tf_op jit(solution)/shard_map/broadcast_in_dim | solution.py:590
  9.6 8.6 %all-to-all-start = ((bf16[8,32,1024]{2,1,0:T(8,128)(2,1)}), bf16[8,32,1024]{2,1,0:T(8,128)(2,1)S(1)}, u32[]{:S(2)}, u32[]{:S(2)}) async-start(bf16[8,32,1024]{2,1,0:T(8,128)(2,1)} %broadcast_in_dim.2), calls=%async_computation | async-start | bytes 1048576 | tf_op jit(solution)/shard_map/all_to_all | solution.py:574
  18.2 6.5 %merge.1 = (bf16[1024,3328]{1,0:T(8,128)(2,1)}, f32[32,128]{1,0:T(8,128)}) custom-call(f32[16,1024]{1,0:T(8,128)} %bitcast.12, f32[16,3328]{1,0:T(8,128)} %up_hbm.3, bf16[1024,3328]{1,0:T(8,128)(2,1)} %weight_hbm.1), custom_call_target="tpu_custom_call" | custom-call | flops 40894464 | bytes 13631488 | tf_op jit(solution)/shard_map/merge/pallas_call | solution.py:129
  24.7 9.5 %all-to-all-done.own_hbm = bf16[8,32,1024]{2,1,0:T(8,128)(2,1)S(1)} async-done(((bf16[8,32,1024]{2,1,0:T(8,128)(2,1)}), bf16[8,32,1024]{2,1,0:T(8,128)(2,1)S(1)}, u32[]{:S(2)}, u32[]{:S(2)}) %all-to-all-start) | async-done | bytes 524320 | tf_op jit(solution)/shard_map/all_to_all | solution.py:574
  34.2 0.0 collective-permute-start
  34.2 1.9 %collective-permute-done.other_hbm = bf16[8,32,1024]{2,1,0:T(8,128)(2,1)S(1)} collective-permute-done((bf16[8,32,1024]{2,1,0:T(8,128)(2,1)S(1)}, bf16[8,32,1024]{2,1,0:T(8,128)(2,1)S(1)}, u32[]{:S(2)}, u32[]{:S(2)}) %collective-permute-start) | collective-permute-done | bytes 524320 | tf_op jit(solution)/shard_map/ppermute | solution.py:593
  36.1 0.8 copy-done.6
  36.9 8.0 %forward.1 = (bf16[16,32,3456]{2,1,0:T(8,128)(2,1)}, bf16[8,2,32,1024]{3,2,1,0:T(8,128)(2,1)}, f32[96,128]{1,0:T(8,128)}) custom-call(s32[1]{0:T(128)} %bitcast.core_ref, bf16[8,32,1024]{2,1,0:T(8,128)(2,1)} %copy-done.1, bf16[8,32,1024]{2,1,0:T(8,128)(2,1)} %copy-done.6, f32[16,1024]{1,0:T(8,128)} %bitcast.13, f32[32,128]{1,0:T(8,128)} %get-tuple-element.32.sums_hbm, ...), custom_call_target="tpu_custom_call" | custom-call | flops 3489660928 | bytes 12582912 | tf_op jit(solution)/shard_map/forward/pallas_call | solution.py:192
  45.0 0.6 collective-permute-start.3
  45.6 1.5 %collective-permute-start.2 = (f32[96,128]{1,0:T(8,128)}, f32[96,128]{1,0:T(8,128)S(1)}, u32[]{:S(2)}, u32[]{:S(2)}) collective-permute-start(f32[96,128]{1,0:T(8,128)} %get-tuple-element.34), channel_id=1, source_target_pairs={{0,64},{64,128},{128,192},{192,0},{1,65},{65,129},{129,193},{193,1... | collective-permute-start | bytes 147464 | tf_op jit(solution)/shard_map/ppermute | solution.py:579
  47.1 1.2 collective-permute-start.1
  48.3 1.0 collective-permute-done.3
  49.3 1.4 collective-permute-done.2
  50.7 3.2 %collective-permute-done.1 = f32[96,128]{1,0:T(8,128)S(1)} collective-permute-done((f32[96,128]{1,0:T(8,128)}, f32[96,128]{1,0:T(8,128)S(1)}, u32[]{:S(2)}, u32[]{:S(2)}) %collective-permute-start.1) | collective-permute-done | bytes 49184 | tf_op jit(solution)/shard_map/ppermute | solution.py:579
  53.9 0.8 add_add_fusion.1
  54.8 0.8 collective-permute-start.6
  55.6 2.5 %collective-permute-start.5 = (f32[96,128]{1,0:T(8,128)S(1)}, f32[96,128]{1,0:T(8,128)S(1)}, u32[]{:S(2)}, u32[]{:S(2)}) collective-permute-start(f32[96,128]{1,0:T(8,128)S(1)} %add_add_fusion.1), channel_id=1, source_target_pairs={{0,16},{16,32},{32,48},{48,0},{1,17},{17,33},{33,49},{49,1},{2,18}... | collective-permute-start | bytes 147464 | tf_op jit(solution)/shard_map/ppermute | solution.py:579
  58.1 0.0 collective-permute-start.4
  58.1 3.4 %collective-permute-done.6 = f32[96,128]{1,0:T(8,128)S(1)} collective-permute-done((f32[96,128]{1,0:T(8,128)S(1)}, f32[96,128]{1,0:T(8,128)S(1)}, u32[]{:S(2)}, u32[]{:S(2)}) %collective-permute-start.6) | collective-permute-done | bytes 49184 | tf_op jit(solution)/shard_map/ppermute | solution.py:579
  61.5 0.0 collective-permute-done.5
  61.5 3.2 %collective-permute-done.4 = f32[96,128]{1,0:T(8,128)S(1)} collective-permute-done((f32[96,128]{1,0:T(8,128)S(1)}, f32[96,128]{1,0:T(8,128)S(1)}, u32[]{:S(2)}, u32[]{:S(2)}) %collective-permute-start.4) | collective-permute-done | bytes 49184 | tf_op jit(solution)/shard_map/ppermute | solution.py:579
  64.7 0.6 add_add_fusion.small_hbm
  65.3 1.2 all-gather.3.cloned.1.call-done
  66.5 3.8 %magnitude.1 = bf16[16,32,3456]{2,1,0:T(8,128)(2,1)} custom-call(bf16[16,32,3328]{2,1,0:T(8,128)(2,1)} %bitcast.8, bf16[16,32,3456]{2,1,0:T(8,128)(2,1)} %get-tuple-element.39.part_hbm), custom_call_target="tpu_custom_call", output_to_operand_aliasing={{}: (1, {})} | custom-call | flops 6815744 | bytes 7340032 | tf_op jit(solution)/shard_map/magnitude/pallas_call | solution.py:236
  70.3 7.8 %all-to-all-start.1 = ((bf16[16,32,3456]{2,1,0:T(8,128)(2,1)}), bf16[16,32,3456]{2,1,0:T(8,128)(2,1)}, u32[]{:S(2)}, u32[]{:S(2)}) async-start(bf16[16,32,3456]{2,1,0:T(8,128)(2,1)} %magnitude.1), calls=%async_computation.1 | async-start | bytes 7077888 | tf_op jit(solution)/shard_map/all_to_all | solution.py:574
  78.1 9.4 %backward.1 = (bf16[272,1024]{1,0:T(8,128)(2,1)}, bf16[272,1024]{1,0:T(8,128)(2,1)}, f32[64,128]{1,0:T(8,128)}) custom-call(s32[1]{0:T(128)} %bitcast.core_ref, f32[96,128]{1,0:T(8,128)} %add_add_fusion.small_hbm, f32[26,128]{1,0:T(8,128)} %bitcast.15, f32[16,3328]{1,0:T(8,128)} %up_hbm.3, bf16[16,32,3328]{2,1,0:T(8,128)(2,1)} %bitcast.9, ...), custom_call_target="tpu_custom_call" | custom-call | flops 3489660928 | bytes 12582912 | tf_op jit(solution)/shard_map/backward/pallas_call | solution.py:324
  87.5 0.1 collective-permute-start.7
  87.6 2.1 %collective-permute-done.7.got_hbm = bf16[272,1024]{1,0:T(8,128)(2,1)S(1)} collective-permute-done((bf16[272,1024]{1,0:T(8,128)(2,1)}, bf16[272,1024]{1,0:T(8,128)(2,1)S(1)}, u32[]{:S(2)}, u32[]{:S(2)}) %collective-permute-start.7) | collective-permute-done | bytes 557088 | tf_op jit(solution)/shard_map/ppermute | solution.py:600
  89.8 0.8 copy-done
  90.6 2.2 %pair.1 = (bf16[144,1024]{1,0:T(8,128)(2,1)}, bf16[144,1024]{1,0:T(8,128)(2,1)}) custom-call(s32[1]{0:T(128)} %bitcast.4.z_ref, bf16[272,1024]{1,0:T(8,128)(2,1)} %get-tuple-element.42.own_hbm, bf16[272,1024]{1,0:T(8,128)(2,1)} %copy-done), custom_call_target="tpu_custom_call" | custom-call | flops 1114112 | bytes 1671168 | tf_op jit(solution)/shard_map/pair/pallas_call | solution.py:371
  92.7 0.8 collective-permute-start.8
  93.5 8.6 %collective-permute-done.8.got_hbm = bf16[144,1024]{1,0:T(8,128)(2,1)S(1)} collective-permute-done((bf16[144,1024]{1,0:T(8,128)(2,1)}, bf16[144,1024]{1,0:T(8,128)(2,1)S(1)}, u32[]{:S(2)}, u32[]{:S(2)}) %collective-permute-start.8) | collective-permute-done | bytes 294944 | tf_op jit(solution)/shard_map/ppermute | solution.py:602
  102.1 0.7 copy-done.2
  102.8 1.9 %quad.1 = (bf16[48,1024]{1,0:T(8,128)(2,1)}, bf16[48,1024]{1,0:T(8,128)(2,1)}, bf16[48,1024]{1,0:T(8,128)(2,1)}, bf16[48,1024]{1,0:T(8,128)(2,1)}) custom-call(s32[1]{0:T(128)} %bitcast.4.z_ref, bf16[144,1024]{1,0:T(8,128)(2,1)} %get-tuple-element.44.keep_hbm, bf16[144,1024]{1,0:T(8,128)(2,1)} %copy-done.2), custom_call_target="tpu_custom_call" | custom-call | flops 589824 | bytes 884736 | tf_op jit(solution)/shard_map/quad/pallas_call | solution.py:407
  104.7 1.9 %collective-permute-start.9 = (bf16[48,1024]{1,0:T(8,128)(2,1)}, bf16[48,1024]{1,0:T(8,128)(2,1)S(1)}, u32[]{:S(2)}, u32[]{:S(2)}) collective-permute-start(bf16[48,1024]{1,0:T(8,128)(2,1)} %get-tuple-element.47), channel_id=1, source_target_pairs={{0,4},{2,6},{4,8},{6,10},{8,12},{10,14},{12,0},{14,2},{1,5},{3,7},... | collective-permute-start | bytes 294920 | tf_op jit(solution)/shard_map/ppermute | solution.py:605
  106.6 3.0 %collective-permute-start.10 = (bf16[48,1024]{1,0:T(8,128)(2,1)}, bf16[48,1024]{1,0:T(8,128)(2,1)S(1)}, u32[]{:S(2)}, u32[]{:S(2)}) collective-permute-start(bf16[48,1024]{1,0:T(8,128)(2,1)} %get-tuple-element.48), channel_id=1, source_target_pairs={{0,8},{2,10},{4,12},{6,14},{8,0},{10,2},{12,4},{14,6},{1,9},{3,11}... | collective-permute-start | bytes 294920 | tf_op jit(solution)/shard_map/ppermute | solution.py:605
  109.6 3.4 %collective-permute-start.11 = (bf16[48,1024]{1,0:T(8,128)(2,1)}, bf16[48,1024]{1,0:T(8,128)(2,1)S(1)}, u32[]{:S(2)}, u32[]{:S(2)}) collective-permute-start(bf16[48,1024]{1,0:T(8,128)(2,1)} %get-tuple-element.49), channel_id=1, source_target_pairs={{0,12},{2,14},{4,0},{6,2},{8,4},{10,6},{12,8},{14,10},{1,13},{3,15... | collective-permute-start | bytes 294920 | tf_op jit(solution)/shard_map/ppermute | solution.py:605
  113.0 4.2 %up_gradient.1 = f32[16,3328]{1,0:T(8,128)} custom-call(f32[96,128]{1,0:T(8,128)} %add_add_fusion.small_hbm, f32[64,128]{1,0:T(8,128)} %get-tuple-element.38.scale_hbm, bf16[16,32,3328]{2,1,0:T(8,128)(2,1)} %bitcast.10), custom_call_target="tpu_custom_call" | custom-call | flops 872415232 | bytes 4194304 | tf_op jit(solution)/shard_map/up_gradient/pallas_call | solution.py:495
  117.2 0.0 collective-permute-done.9.refs_1_
  117.2 0.4 collective-permute-done.10.refs_2_
  117.7 0.6 collective-permute-done.11.refs_3_
  118.3 0.0 copy-done.4
  118.3 0.6 copy-done.5
  118.9 2.4 %finish.1 = (bf16[32,1024]{1,0:T(8,128)(2,1)}, f32[16,1024]{1,0:T(8,128)}) custom-call(s32[1]{0:T(128)} %bitcast.4.z_ref, bf16[512,1024]{1,0:T(8,128)(2,1)} %bitcast.11, bf16[48,1024]{1,0:T(8,128)(2,1)} %get-tuple-element.46.refs_0_, bf16[48,1024]{1,0:T(8,128)(2,1)} %copy-done.3, bf16[48,1024]{1,0:T(8,128)(2,1)} %copy-done.4, bf16[48,1024]{1,0:T(8,128)(2,1)} %copy-done.5), custom_call_target="tpu_custom_call" | custom-call | flops 268435456 | bytes 2097152 | tf_op jit(solution)/shard_map/finish/pallas_call | solution.py:445
  121.3 13.4 %all-to-all-done.1.parts_hbm = bf16[16,32,3456]{2,1,0:T(8,128)(2,1)} async-done(((bf16[16,32,3456]{2,1,0:T(8,128)(2,1)}), bf16[16,32,3456]{2,1,0:T(8,128)(2,1)}, u32[]{:S(2)}, u32[]{:S(2)}) %all-to-all-start.1) | async-done | bytes 3538976 | tf_op jit(solution)/shard_map/all_to_all | solution.py:574
  134.7 3.3 %output.1 = (bf16[32,3328]{1,0:T(8,128)(2,1)}, f32[26,128]{1,0:T(8,128)}) custom-call(f32[64,128]{1,0:T(8,128)} %get-tuple-element.38.scale_hbm, bf16[16,32,3456]{2,1,0:T(8,128)(2,1)} %all-to-all-done.1.parts_hbm), custom_call_target="tpu_custom_call" | custom-call | flops 1703936 | bytes 4194304 | tf_op jit(solution)/shard_map/output/pallas_call | solution.py:550
  (9 shorter events, 0.0 us)
Async XLA Ops:
  7.2 59.4 %all-gather.3.cloned.1.call-start = ((), (), s32[]{:S(2)}) async-start(), calls=%async_computation.2 | async-start | bytes 3620864 | tf_op jit(solution)/shard_map/all_gather | solution.py:589
  9.6 24.6 %all-to-all-start = ((bf16[8,32,1024]{2,1,0:T(8,128)(2,1)}), bf16[8,32,1024]{2,1,0:T(8,128)(2,1)S(1)}, u32[]{:S(2)}, u32[]{:S(2)}) async-start(bf16[8,32,1024]{2,1,0:T(8,128)(2,1)} %broadcast_in_dim.2), calls=%async_computation | async-start | bytes 1048576 | tf_op jit(solution)/shard_map/all_to_all | solution.py:574
  34.2 1.9 %copy-start.1 = (bf16[8,32,1024]{2,1,0:T(8,128)(2,1)}, bf16[8,32,1024]{2,1,0:T(8,128)(2,1)S(1)}, u32[]{:S(2)}) copy-start(bf16[8,32,1024]{2,1,0:T(8,128)(2,1)S(1)} %all-to-all-done.own_hbm) | copy-start | bytes 1572868
  34.2 1.9 %collective-permute-start = (bf16[8,32,1024]{2,1,0:T(8,128)(2,1)S(1)}, bf16[8,32,1024]{2,1,0:T(8,128)(2,1)S(1)}, u32[]{:S(2)}, u32[]{:S(2)}) collective-permute-start(bf16[8,32,1024]{2,1,0:T(8,128)(2,1)S(1)} %all-to-all-done.own_hbm), channel_id=1, source_target_pairs={{0,1},{1,0},{2,3},{3,2},{4,5},{5,4},{6,7},{7,6},{8,9},{9,8},{10,11... | collective-permute-start | bytes 1572872 | tf_op jit(solution)/shard_map/ppermute | solution.py:593
  36.1 0.8 copy-start.6
  45.0 4.4 %collective-permute-start.3 = (f32[96,128]{1,0:T(8,128)}, f32[96,128]{1,0:T(8,128)S(1)}, u32[]{:S(2)}, u32[]{:S(2)}) collective-permute-start(f32[96,128]{1,0:T(8,128)} %get-tuple-element.34), channel_id=1, source_target_pairs={{0,192},{64,0},{128,64},{192,128},{1,193},{65,1},{129,65},{193,129... | collective-permute-start | bytes 147464 | tf_op jit(solution)/shard_map/ppermute | solution.py:579
  45.6 5.1 %collective-permute-start.2 = (f32[96,128]{1,0:T(8,128)}, f32[96,128]{1,0:T(8,128)S(1)}, u32[]{:S(2)}, u32[]{:S(2)}) collective-permute-start(f32[96,128]{1,0:T(8,128)} %get-tuple-element.34), channel_id=1, source_target_pairs={{0,64},{64,128},{128,192},{192,0},{1,65},{65,129},{129,193},{193,1... | collective-permute-start | bytes 147464 | tf_op jit(solution)/shard_map/ppermute | solution.py:579
  47.1 6.9 %collective-permute-start.1 = (f32[96,128]{1,0:T(8,128)}, f32[96,128]{1,0:T(8,128)S(1)}, u32[]{:S(2)}, u32[]{:S(2)}) collective-permute-start(f32[96,128]{1,0:T(8,128)} %get-tuple-element.34), channel_id=1, source_target_pairs={{0,128},{64,192},{128,0},{192,64},{1,129},{65,193},{129,1},{193,65... | collective-permute-start | bytes 147464 | tf_op jit(solution)/shard_map/ppermute | solution.py:579
  54.8 6.8 %collective-permute-start.6 = (f32[96,128]{1,0:T(8,128)S(1)}, f32[96,128]{1,0:T(8,128)S(1)}, u32[]{:S(2)}, u32[]{:S(2)}) collective-permute-start(f32[96,128]{1,0:T(8,128)S(1)} %add_add_fusion.1), channel_id=1, source_target_pairs={{0,48},{16,0},{32,16},{48,32},{1,49},{17,1},{33,17},{49,33},{2,50}... | collective-permute-start | bytes 147464 | tf_op jit(solution)/shard_map/ppermute | solution.py:579
  55.6 6.0 %collective-permute-start.5 = (f32[96,128]{1,0:T(8,128)S(1)}, f32[96,128]{1,0:T(8,128)S(1)}, u32[]{:S(2)}, u32[]{:S(2)}) collective-permute-start(f32[96,128]{1,0:T(8,128)S(1)} %add_add_fusion.1), channel_id=1, source_target_pairs={{0,16},{16,32},{32,48},{48,0},{1,17},{17,33},{33,49},{49,1},{2,18}... | collective-permute-start | bytes 147464 | tf_op jit(solution)/shard_map/ppermute | solution.py:579
  58.1 6.6 %collective-permute-start.4 = (f32[96,128]{1,0:T(8,128)S(1)}, f32[96,128]{1,0:T(8,128)S(1)}, u32[]{:S(2)}, u32[]{:S(2)}) collective-permute-start(f32[96,128]{1,0:T(8,128)S(1)} %add_add_fusion.1), channel_id=1, source_target_pairs={{0,32},{16,48},{32,0},{48,16},{1,33},{17,49},{33,1},{49,17},{2,34}... | collective-permute-start | bytes 147464 | tf_op jit(solution)/shard_map/ppermute | solution.py:579
  70.3 64.4 %all-to-all-start.1 = ((bf16[16,32,3456]{2,1,0:T(8,128)(2,1)}), bf16[16,32,3456]{2,1,0:T(8,128)(2,1)}, u32[]{:S(2)}, u32[]{:S(2)}) async-start(bf16[16,32,3456]{2,1,0:T(8,128)(2,1)} %magnitude.1), calls=%async_computation.1 | async-start | bytes 7077888 | tf_op jit(solution)/shard_map/all_to_all | solution.py:574
  87.5 2.3 %collective-permute-start.7 = (bf16[272,1024]{1,0:T(8,128)(2,1)}, bf16[272,1024]{1,0:T(8,128)(2,1)S(1)}, u32[]{:S(2)}, u32[]{:S(2)}) collective-permute-start(bf16[272,1024]{1,0:T(8,128)(2,1)} %get-tuple-element.43), channel_id=1, source_target_pairs={{0,1},{1,0},{2,3},{3,2},{4,5},{5,4},{6,7},{7,6},{8,9},{9,8},{10,11... | collective-permute-start | bytes 1671176 | tf_op jit(solution)/shard_map/ppermute | solution.py:600
  89.8 0.8 copy-start
  92.7 9.3 %collective-permute-start.8 = (bf16[144,1024]{1,0:T(8,128)(2,1)}, bf16[144,1024]{1,0:T(8,128)(2,1)S(1)}, u32[]{:S(2)}, u32[]{:S(2)}) collective-permute-start(bf16[144,1024]{1,0:T(8,128)(2,1)} %get-tuple-element.45), channel_id=1, source_target_pairs={{0,2},{2,0},{4,6},{6,4},{8,10},{10,8},{12,14},{14,12},{1,3},{3,1},... | collective-permute-start | bytes 884744 | tf_op jit(solution)/shard_map/ppermute | solution.py:602
  102.1 0.7 copy-start.2
  104.7 12.5 %collective-permute-start.9 = (bf16[48,1024]{1,0:T(8,128)(2,1)}, bf16[48,1024]{1,0:T(8,128)(2,1)S(1)}, u32[]{:S(2)}, u32[]{:S(2)}) collective-permute-start(bf16[48,1024]{1,0:T(8,128)(2,1)} %get-tuple-element.47), channel_id=1, source_target_pairs={{0,4},{2,6},{4,8},{6,10},{8,12},{10,14},{12,0},{14,2},{1,5},{3,7},... | collective-permute-start | bytes 294920 | tf_op jit(solution)/shard_map/ppermute | solution.py:605
  106.6 11.1 %collective-permute-start.10 = (bf16[48,1024]{1,0:T(8,128)(2,1)}, bf16[48,1024]{1,0:T(8,128)(2,1)S(1)}, u32[]{:S(2)}, u32[]{:S(2)}) collective-permute-start(bf16[48,1024]{1,0:T(8,128)(2,1)} %get-tuple-element.48), channel_id=1, source_target_pairs={{0,8},{2,10},{4,12},{6,14},{8,0},{10,2},{12,4},{14,6},{1,9},{3,11}... | collective-permute-start | bytes 294920 | tf_op jit(solution)/shard_map/ppermute | solution.py:605
  109.6 8.7 %collective-permute-start.11 = (bf16[48,1024]{1,0:T(8,128)(2,1)}, bf16[48,1024]{1,0:T(8,128)(2,1)S(1)}, u32[]{:S(2)}, u32[]{:S(2)}) collective-permute-start(bf16[48,1024]{1,0:T(8,128)(2,1)} %get-tuple-element.49), channel_id=1, source_target_pairs={{0,12},{2,14},{4,0},{6,2},{8,4},{10,6},{12,8},{14,10},{1,13},{3,15... | collective-permute-start | bytes 294920 | tf_op jit(solution)/shard_map/ppermute | solution.py:605
  117.2 1.1 copy-start.3
  117.7 0.6 copy-start.4
  118.3 0.6 copy-start.5
Sparse Core Ops, SparseCore 0:
  10.5 56.0 all-gather.2

commit v7 on v6

--- a/solution.py
+++ b/solution.py
@@ -91,7 +91,7 @@
 
 
 def merge_kernel(
-    down_hbm, up_hbm, weight_hbm, merged_hbm, sums_hbm,
+    after_hbm, down_hbm, up_hbm, weight_hbm, merged_hbm, sums_hbm,
     down, up, weight, merged, sums, up_cat, totals, small_sem, in_sem, out_sem,
 ):
     depth, width = weight.shape
@@ -124,13 +124,13 @@
         copy.wait()
 
 
-def merge(down_t, up, weight):
+def merge(after, down_t, up, weight):
     depth, width = weight.shape
     return call(
         merge_kernel,
         12 * depth * width,
         4 * depth * width,
-        in_specs=[ANY] * 3,
+        in_specs=[ANY] * 4,
         out_specs=[ANY] * 2,
         out_shape=[
             jax.ShapeDtypeStruct((depth, width), bf16),
@@ -149,69 +149,118 @@
             pltpu.SemaphoreType.DMA((4,)),
         ],
         name="merge",
-    )(down_t, up, weight)
-
-
-def forward_kernel(
-    core_ref, own_hbm, other_hbm, down_hbm, sums_hbm, merged_hbm, part_hbm, tokens_hbm, small_hbm,
-    tokens, down, small, merged, part, first_sem, sem, out_sem,
+    )(after, down_t, up, weight)
+
+
+def spread_kernel(cot_hbm, out_hbm, cot, in_sem, out_sem):
+    begin(cot_hbm, cot, in_sem.at[0]).wait()
+    copies = [begin(cot, out_hbm.at[r], out_sem.at[r]) for r in range(16)]
+    for copy in copies:
+        copy.wait()
+
+
+def spread(cot):
+    return call(
+        spread_kernel,
+        cot.size,
+        4 * MIB,
+        in_specs=[ANY],
+        out_specs=ANY,
+        out_shape=jax.ShapeDtypeStruct((16,) + cot.shape, bf16),
+        scratch_shapes=[
+            pltpu.VMEM(cot.shape, bf16),
+            pltpu.SemaphoreType.DMA((1,)),
+            pltpu.SemaphoreType.DMA((16,)),
+        ],
+        name="spread",
+    )(cot)
+
+
+def project_kernel(
+    place_ref, own_hbm, other_hbm, down_hbm, sums_hbm, small_hbm, tokens_hbm,
+    tokens, down, small, first_sem, sem,
 ):
-    core = core_ref[0]
+    z, core = place_ref[0], place_ref[1]
+    copies = [
+        begin(down_hbm, down, first_sem.at[0]),
+        begin(sums_hbm, small.at[64:], first_sem.at[1]),
+    ]
+    for k in range(8):
+        back = lax.rem(z + 8 - k, 8)
+        rows = slice(32 * k, 32 * k + 32)
+        copies.append(begin(own_hbm.at[rows], tokens.at[back, core], sem.at[0, k]))
+        copies.append(begin(other_hbm.at[rows], tokens.at[back, 1 - core], sem.at[1, k]))
+    for copy in copies:
+        copy.wait()
+    stores = [begin(tokens, tokens_hbm, first_sem.at[0])]
+    proj = three(down[...], tokens[...].reshape(512, down.shape[1]), 1, 1)
+    for k in range(4):
+        small[RANK * k : RANK * k + RANK, :] = proj[:, LANES * k : LANES * k + LANES]
+    stores.append(begin(small, small_hbm, first_sem.at[1]))
+    for copy in stores:
+        copy.wait()
+
+
+def project(place, own, other, down_t, sums):
+    depth = down_t.shape[1]
+    return call(
+        project_kernel,
+        2 * 512 * 256 * depth,
+        3 * MIB,
+        in_specs=[SMEM] + [ANY] * 4,
+        out_specs=[ANY] * 2,
+        out_shape=[
+            jax.ShapeDtypeStruct((96, LANES), f32),
+            jax.ShapeDtypeStruct((8, 2, 32, depth), bf16),
+        ],
+        scratch_shapes=[
+            pltpu.VMEM((8, 2, 32, depth), bf16),
+            pltpu.VMEM((RANK, depth), f32),
+            pltpu.VMEM((96, LANES), f32),
+            pltpu.SemaphoreType.DMA((2,)),
+            pltpu.SemaphoreType.DMA((2, 8)),
+        ],
+        name="project",
+    )(place, own, other, down_t, sums)
+
+
+def forward_kernel(tokens_hbm, merged_hbm, part_hbm, tokens, merged, part, first_sem, sem, out_sem):
     depth, width = merged.shape
     chunks = chunks_of(width)
-    first = (
-        begin(own_hbm, tokens.at[:, core], first_sem.at[0]),
-        begin(other_hbm, tokens.at[:, 1 - core], first_sem.at[1]),
-        begin(down_hbm, down, first_sem.at[2]),
-        begin(sums_hbm, small.at[64:], first_sem.at[3]),
-    )
+    first = begin(tokens_hbm, tokens, first_sem.at[0])
     ready = stream([(merged_hbm, merged)], sem, chunks)
-    for copy in first:
-        copy.wait()
-    all_tokens = tokens[...].reshape(512, depth)
-    proj = three(down[...], all_tokens, 1, 1)
-    for k in range(4):
-        small[RANK * k : RANK * k + RANK, :] = proj[:, LANES * k : LANES * k + LANES]
-    stores = [
-        begin(small, small_hbm, first_sem.at[0]),
-        begin(tokens, tokens_hbm, first_sem.at[1]),
-    ]
+    first.wait()
+    stores = []
     for j, (at, size) in enumerate(chunks):
         ready(j)
         cols = slice(at, at + size)
-        product = dot(all_tokens, merged[:, cols], 1, 0).astype(bf16)
+        product = dot(tokens[...], merged[:, cols], 1, 0).astype(bf16)
         part[:, :, cols] = product.reshape(16, 32, size)
         stores.append(begin(part.at[:, :, cols], part_hbm.at[:, :, cols], out_sem.at[j]))
     for copy in stores:
         copy.wait()
 
 
-def forward(core, own, other, down_t, sums, merged_low):
+def forward(tokens, merged_low):
     depth, width = merged_low.shape
     count = len(chunks_of(width))
     return call(
         forward_kernel,
         2 * 512 * depth * width,
         12 * MIB,
-        in_specs=[SMEM] + [ANY] * 5,
-        out_specs=[ANY] * 3,
-        out_shape=[
-            jax.ShapeDtypeStruct((16, 32, width + LANES), bf16),
-            jax.ShapeDtypeStruct((8, 2, 32, depth), bf16),
-            jax.ShapeDtypeStruct((96, LANES), f32),
-        ],
-        scratch_shapes=[
-            pltpu.VMEM((8, 2, 32, depth), bf16),
-            pltpu.VMEM((RANK, depth), f32),
-            pltpu.VMEM((96, LANES), f32),
+        in_specs=[ANY] * 2,
+        out_specs=ANY,
+        out_shape=jax.ShapeDtypeStruct((16, 32, width + LANES), bf16),
+        scratch_shapes=[
+            pltpu.VMEM((512, depth), bf16),
             pltpu.VMEM((depth, width), bf16),
             pltpu.VMEM((16, 32, width), bf16),
-            pltpu.SemaphoreType.DMA((4,)),
+            pltpu.SemaphoreType.DMA((1,)),
             pltpu.SemaphoreType.DMA((1, count)),
             pltpu.SemaphoreType.DMA((count,)),
         ],
         name="forward",
-    )(core, own, other, down_t, sums, merged_low)
+    )(tokens, merged_low)
 
 
 def magnitude_kernel(given_hbm, part_hbm, out_hbm, cot, part, extra, sem, out_sem):
@@ -267,7 +316,7 @@
 
 def backward_kernel(
     core_ref, small_hbm, magnitude_hbm, up_hbm, given_hbm, merged_hbm, own_hbm, send_hbm, scale_hbm,
-    squares, magnitude, up, cot, merged, total, low_total, own, send, scale, first_sem, sem,
+    squares, magnitude, up, cot, merged, total, own, send, scale, first_sem, sem,
 ):
     core = core_ref[0]
     depth, width = merged.shape
@@ -287,26 +336,21 @@
     scale[:count, :] = factors
     scale[32:, :] = norm
     last = begin(scale, scale_hbm, first_sem.at[0])
-    blank = jnp.zeros((LANES - 3 * RANK, CHUNK), bf16)
+    low = jnp.zeros((RANK, CHUNK), f32)
     for j, (at, size) in enumerate(chunks):
         ready(j)
         cols = slice(at, at + size)
         value = cot[:, :, cols].reshape(512, size).astype(f32)
         grad = (value * in_line(factors, at, size)).astype(bf16)
         product = dot(grad, merged[:, cols], 1, 1)
-        up_cat = jnp.concatenate([*pieces(up[:, cols]), blank[:, :size]], axis=0)
-        low = dot(grad, up_cat, 1, 1)
         if j == 0:
             total[...] = product
-            low_total[...] = low
         else:
             total[...] += product
-            low_total[...] += low
+        low += three(up[:, cols], grad, 1, 1)
     for z in range(8):
         theirs = pl.ds(pl.multiple_of((2 * z + 1 - core) * 32, 32), 32)
         send[32 * z : 32 * z + 32, :] = total[theirs, :].astype(bf16)
-    low = low_total[...].T
-    low = low[:RANK] + low[RANK : 2 * RANK] + low[2 * RANK : 3 * RANK]
     pack(low, send.at[256:272, :])
     first = begin(send, send_hbm, first_sem.at[1])
     for z in range(8):
@@ -336,7 +380,6 @@
             pltpu.VMEM((16, 32, width), bf16),
             pltpu.VMEM((depth, width), bf16),
             pltpu.VMEM((512, depth), f32),
-            pltpu.VMEM((512, LANES), f32),
             pltpu.VMEM((272, depth), bf16),
             pltpu.VMEM((272, depth), bf16),
             pltpu.VMEM((64, LANES), f32),
@@ -570,14 +613,20 @@
     )(scale, parts)
 
 
-def exchange(blocks, axis):
-    return lax.all_to_all(blocks, axis, 0, 0, tiled=False)
-
-
-def around(value, axis):
-    one, two, other = [
-        lax.ppermute(value, axis, [(i, (i + k) % 4) for i in range(4)]) for k in (1, 2, 3)
-    ]
+def exchange(blocks):
+    return lax.all_to_all(blocks, ROW, 0, 0, tiled=False)
+
+
+def further(value, axis, k, size):
+    return lax.ppermute(value, axis, [(i, (i + k) % size) for i in range(size)])
+
+
+def shifted(value, axis):
+    return [further(value, axis, k, 4) for k in (1, 2, 3)]
+
+
+def added(value, arrived):
+    one, two, other = arrived
     return (value + two) + (one + other)
 
 
@@ -586,25 +635,39 @@
     swap = [(0, 1), (1, 0)]
     down_t = down_adapter.T
     magnitude = magnitude.reshape(-1, LANES)
-    given = lax.all_gather(out_cotangent, ROW, axis=0)
-    own_tokens = exchange(jnp.broadcast_to(tokens[None], (8,) + tokens.shape), "z")
-    merged_low, sums = merge(down_t, up_adapter, weight)
-    own_tokens, merged_low, sums = lax.optimization_barrier((own_tokens, merged_low, sums))
-    other_tokens = lax.ppermute(own_tokens, "c", swap)
-    part, tokens_full, small = forward(core, own_tokens, other_tokens, down_t, sums, merged_low)
-    small = around(around(small, "x"), "y")
-    small, part, given = lax.optimization_barrier((small, part, given))
+    message = spread(out_cotangent)
+    given = exchange(message)
+    blocks = [tokens] * 8
+    for k in (4, 3, 5, 2):
+        blocks[k] = further(tokens, "z", k, 8)
+    merged_low, sums = merge(message, down_t, up_adapter, weight)
+    later, sums, merged_low = lax.optimization_barrier((tokens, sums, merged_low))
+    for k in (6, 1, 7):
+        blocks[k] = further(later, "z", k, 8)
+    own = jnp.concatenate(blocks, axis=0)
+    other = lax.ppermute(own, "c", swap)
+    place = jnp.concatenate([z, core])
+    small, tokens_full = project(place, own, other, down_t, sums)
+    tokens_full = tokens_full.reshape(512, -1)
+    part = forward(tokens_full, merged_low)
+    arrived = shifted(small, "x")
+    arrived, part = lax.optimization_barrier((arrived, part))
+    small = added(small, arrived)
     part = add_magnitude(given, part)
-    parts = exchange(part, ROW)
+    arrived = shifted(small, "y")
+    arrived, part = lax.optimization_barrier((arrived, part))
+    small = added(small, arrived)
+    small, part = lax.optimization_barrier((small, part))
+    parts = exchange(part)
     own, send, scale = backward(core, small, magnitude, up_adapter, given, merged_low)
     got = lax.ppermute(send, "c", swap)
     keep, send = pair(z, own, got)
     got = lax.ppermute(send, "z", [(i, i ^ 1) for i in range(8)])
     blocks = list(quad(z, keep, got))
     for k in range(1, 4):
-        blocks[k] = lax.ppermute(blocks[k], "z", [(i, (i + 2 * k) % 8) for i in range(8)])
+        blocks[k] = further(blocks[k], "z", 2 * k, 8)
     up_gradient = up_gradient_of(small, scale, given)
-    grad_tokens, down_gradient = finish(z, tokens_full.reshape(512, -1), blocks)
+    grad_tokens, down_gradient = finish(z, tokens_full, blocks)
     output, grad_magnitude = output_of(scale, parts)
     return (output, grad_tokens, grad_magnitude.reshape(-1), up_gradient, down_gradient.T)
 

time: 146 us -> 127 us (0.87)
  the two profiles are of different devices: /device:TPU:60 before, /device:TPU:8 now
where the time goes in v7:
time: 127 us; the launch traced here: 125 us
  starting transfers between devices  52.6 us (41%)
  Pallas kernels  45.9 us (36%)
  waiting for transfers between devices  21.4 us (17%)
  local copies, waits for them, and re-layouts  3.03 us (2%)
    ppermute x16, starting transfers between devices, further(): return lax.ppermute(value, axis, [(i, (i + k) % size) for i in range(size)])  36.9 us
    all_to_all x2, starting transfers between devices, exchange(): return lax.all_to_all(blocks, ROW, 0, 0, tiled=False)  13.5 us
    ppermute x16, waiting for transfers between devices, further(): return lax.ppermute(value, axis, [(i, (i + k) % size) for i in range(size)])  10.5 us
    pallas_call x1, Pallas kernels, backward(): call(backward_kernel, 2 * 512 * depth * width, 12 * MIB, in_specs=[SMEM]...  7.89 us
    pallas_call x1, Pallas kernels, forward(): call(forward_kernel, 2 * 512 * depth * width, 12 * MIB, in_specs=[ANY] *...  7.74 us
    ppermute x1, waiting for transfers between devices, on_device(): got = lax.ppermute(send, 'z', [(i, i ^ 1) for i in range(8)])  7.52 us
    pallas_call x1, Pallas kernels, merge(): call(merge_kernel, 12 * depth * width, 4 * depth * width, in_specs=[ANY]...  6.49 us
    pallas_call x1, Pallas kernels, up_gradient_of(): call(up_kernel, 2 * 512 * 256 * width, 4 * MIB, in_specs=[ANY] * 3, out_s...  4.18 us
  transfers between devices with their start and end apart: 21, of which 6 were waited for; matrix products, arithmetic and copies ran while one was open for 1% of the time, Pallas kernels for 32%

profile of v7, /device:TPU:8, one launch (start us, length us, event | category | flops | bytes accessed | tf_op | source)
XLA Modules:
  0.0 125.4 jit_solution(7614358434524737675)
XLA Ops:
  0.6 2.9 %spread.1.after_hbm = bf16[16,32,3328]{2,1,0:T(8,128)(2,1)} custom-call(bf16[32,3328]{1,0:T(8,128)(2,1)} %cot_hbm.1), custom_call_target="tpu_custom_call" | custom-call | flops 106496 | bytes 4194304 | tf_op jit(solution)/shard_map/spread/pallas_call | solution.py:163
  3.5 0.0 copy-start.7
  3.5 7.5 %all-to-all-start = ((bf16[16,32,3328]{2,1,0:T(8,128)(2,1)}), bf16[16,32,3328]{2,1,0:T(8,128)(2,1)}, u32[]{:S(2)}, u32[]{:S(2)}) async-start(bf16[16,32,3328]{2,1,0:T(8,128)(2,1)} %spread.1.after_hbm), calls=%async_computation | async-start | bytes 6815744 | tf_op jit(solution)/shard_map/all_to_all | solution.py:617
  11.1 7.3 %collective-permute-start.3 = (bf16[32,1024]{1,0:T(8,128)(2,1)S(1)}, bf16[32,1024]{1,0:T(8,128)(2,1)S(1)}, u32[]{:S(2)}, u32[]{:S(2)}) collective-permute-start(bf16[32,1024]{1,0:T(8,128)(2,1)S(1)} %copy-done.7), channel_id=1, source_target_pairs={{0,8},{2,10},{4,12},{6,14},{8,0},{10,2},{12,4},{14,6},{1,9},{3,11}... | collective-permute-start | bytes 196616 | tf_op jit(solution)/shard_map/ppermute | solution.py:621
  18.4 1.9 %collective-permute-start.2 = (bf16[32,1024]{1,0:T(8,128)(2,1)S(1)}, bf16[32,1024]{1,0:T(8,128)(2,1)S(1)}, u32[]{:S(2)}, u32[]{:S(2)}) collective-permute-start(bf16[32,1024]{1,0:T(8,128)(2,1)S(1)} %copy-done.7), channel_id=1, source_target_pairs={{0,6},{2,8},{4,10},{6,12},{8,14},{10,0},{12,2},{14,4},{1,7},{3,9},... | collective-permute-start | bytes 196616 | tf_op jit(solution)/shard_map/ppermute | solution.py:621
  20.3 4.6 %collective-permute-start.4 = (bf16[32,1024]{1,0:T(8,128)(2,1)S(1)}, bf16[32,1024]{1,0:T(8,128)(2,1)S(1)}, u32[]{:S(2)}, u32[]{:S(2)}) collective-permute-start(bf16[32,1024]{1,0:T(8,128)(2,1)S(1)} %copy-done.7), channel_id=1, source_target_pairs={{0,10},{2,12},{4,14},{6,0},{8,2},{10,4},{12,6},{14,8},{1,11},{3,13... | collective-permute-start | bytes 196616 | tf_op jit(solution)/shard_map/ppermute | solution.py:621
  24.9 6.5 %merge.1 = (bf16[1024,3328]{1,0:T(8,128)(2,1)}, f32[32,128]{1,0:T(8,128)}) custom-call(bf16[16,32,3328]{2,1,0:T(8,128)(2,1)} %spread.1.after_hbm, f32[16,1024]{1,0:T(8,128)} %bitcast.9, f32[16,3328]{1,0:T(8,128)} %up_hbm.3, bf16[1024,3328]{1,0:T(8,128)(2,1)} %weight_hbm.1), custom_call_target="tpu_custom_call" | custom-call | flops 40894464 | bytes 13631488 | tf_op jit(solution)/shard_map/merge/pallas_call | solution.py:129
  31.4 1.1 collective-permute-start
  32.5 4.4 %collective-permute-done = bf16[32,1024]{1,0:T(8,128)(2,1)S(1)} collective-permute-done((bf16[32,1024]{1,0:T(8,128)(2,1)S(1)}, bf16[32,1024]{1,0:T(8,128)(2,1)S(1)}, u32[]{:S(2)}, u32[]{:S(2)}) %collective-permute-start) | collective-permute-done | bytes 65568 | tf_op jit(solution)/shard_map/ppermute | solution.py:621
  36.9 0.0 collective-permute-start.6
  36.9 0.0 collective-permute-done.1
  37.0 1.5 %collective-permute-start.5 = (bf16[32,1024]{1,0:T(8,128)(2,1)S(1)}, bf16[32,1024]{1,0:T(8,128)(2,1)S(1)}, u32[]{:S(2)}, u32[]{:S(2)}) collective-permute-start(bf16[32,1024]{1,0:T(8,128)(2,1)S(1)} %copy-done.7), channel_id=1, source_target_pairs={{0,12},{2,14},{4,0},{6,2},{8,4},{10,6},{12,8},{14,10},{1,13},{3,15... | collective-permute-start | bytes 196616 | tf_op jit(solution)/shard_map/ppermute | solution.py:621
  38.5 0.0 collective-permute-done.3
  38.5 0.0 collective-permute-done.4
  38.6 3.6 %collective-permute-done.5 = bf16[32,1024]{1,0:T(8,128)(2,1)S(1)} collective-permute-done((bf16[32,1024]{1,0:T(8,128)(2,1)S(1)}, bf16[32,1024]{1,0:T(8,128)(2,1)S(1)}, u32[]{:S(2)}, u32[]{:S(2)}) %collective-permute-start.5) | collective-permute-done | bytes 65568 | tf_op jit(solution)/shard_map/ppermute | solution.py:621
  42.2 0.0 collective-permute-done.6
  42.2 0.1 collective-permute-start.7
  42.3 0.6 pad_add_fusion.place_ref
  42.9 1.3 %collective-permute-done.7.other_hbm = bf16[256,1024]{1,0:T(8,128)(2,1)S(1)} collective-permute-done((bf16[256,1024]{1,0:T(8,128)(2,1)S(1)}, bf16[256,1024]{1,0:T(8,128)(2,1)S(1)}, u32[]{:S(2)}, u32[]{:S(2)}) %collective-permute-start.7) | collective-permute-done | bytes 524320 | tf_op jit(solution)/shard_map/ppermute | solution.py:648
  44.2 0.8 copy-done.2
  45.0 3.1 %project.1 = (f32[96,128]{1,0:T(8,128)}, bf16[8,2,32,1024]{3,2,1,0:T(8,128)(2,1)}) custom-call(s32[2]{0:T(128)} %pad_add_fusion.place_ref, bf16[256,1024]{1,0:T(8,128)(2,1)} %copy-done, bf16[256,1024]{1,0:T(8,128)(2,1)} %copy-done.2, f32[16,1024]{1,0:T(8,128)} %bitcast.10, f32[32,128]{1,0:T(8,128)} %get-tuple-element.38.sums_hbm), custom_call_target="tpu_custom_call" | custom-call | flops 268435456 | bytes 3145728 | tf_op jit(solution)/shard_map/project/pallas_call | solution.py:206
  48.2 2.8 %collective-permute-start.10 = (f32[96,128]{1,0:T(8,128)}, f32[96,128]{1,0:T(8,128)S(1)}, u32[]{:S(2)}, u32[]{:S(2)}) collective-permute-start(f32[96,128]{1,0:T(8,128)} %get-tuple-element.39), channel_id=1, source_target_pairs={{0,192},{64,0},{128,64},{192,128},{1,193},{65,1},{129,65},{193,129... | collective-permute-start | bytes 147464 | tf_op jit(solution)/shard_map/ppermute | solution.py:621
  51.0 0.8 collective-permute-start.9
  51.8 0.9 collective-permute-start.8
  52.7 7.7 %forward.1.part_hbm = bf16[16,32,3456]{2,1,0:T(8,128)(2,1)} custom-call(bf16[512,1024]{1,0:T(8,128)(2,1)} %bitcast.7, bf16[1024,3328]{1,0:T(8,128)(2,1)} %get-tuple-element.41.merged_hbm), custom_call_target="tpu_custom_call" | custom-call | flops 3489660928 | bytes 12582912 | tf_op jit(solution)/shard_map/forward/pallas_call | solution.py:247
  60.5 0.6 collective-permute-start.13
  61.1 2.4 %collective-permute-start.12 = (f32[96,128]{1,0:T(8,128)S(1)}, f32[96,128]{1,0:T(8,128)S(1)}, u32[]{:S(2)}, u32[]{:S(2)}) collective-permute-start(f32[96,128]{1,0:T(8,128)S(1)} %add_add_fusion.1), channel_id=1, source_target_pairs={{0,32},{16,48},{32,0},{48,16},{1,33},{17,49},{33,1},{49,17},{2,34}... | collective-permute-start | bytes 147464 | tf_op jit(solution)/shard_map/ppermute | solution.py:621
  63.5 1.8 %collective-permute-start.11 = (f32[96,128]{1,0:T(8,128)S(1)}, f32[96,128]{1,0:T(8,128)S(1)}, u32[]{:S(2)}, u32[]{:S(2)}) collective-permute-start(f32[96,128]{1,0:T(8,128)S(1)} %add_add_fusion.1), channel_id=1, source_target_pairs={{0,16},{16,32},{32,48},{48,0},{1,17},{17,33},{33,49},{49,1},{2,18}... | collective-permute-start | bytes 147464 | tf_op jit(solution)/shard_map/ppermute | solution.py:621
  65.3 3.9 %magnitude.1 = bf16[16,32,3456]{2,1,0:T(8,128)(2,1)} custom-call(bf16[16,32,3328]{2,1,0:T(8,128)(2,1)} %all-to-all-done.given_hbm, bf16[16,32,3456]{2,1,0:T(8,128)(2,1)} %forward.1.part_hbm), custom_call_target="tpu_custom_call", output_to_operand_aliasing={{}: (1, {})} | custom-call | flops 6815744 | bytes 7340032 | tf_op jit(solution)/shard_map/magnitude/pallas_call | solution.py:285
  69.2 0.6 add_add_fusion.small_hbm
  69.8 6.0 %all-to-all-start.1 = ((bf16[16,32,3456]{2,1,0:T(8,128)(2,1)}), bf16[16,32,3456]{2,1,0:T(8,128)(2,1)}, u32[]{:S(2)}, u32[]{:S(2)}) async-start(bf16[16,32,3456]{2,1,0:T(8,128)(2,1)} %magnitude.1), calls=%async_computation.1 | async-start | bytes 7077888 | tf_op jit(solution)/shard_map/all_to_all | solution.py:617
  75.8 7.9 %backward.1 = (bf16[272,1024]{1,0:T(8,128)(2,1)}, bf16[272,1024]{1,0:T(8,128)(2,1)}, f32[64,128]{1,0:T(8,128)}) custom-call(s32[1]{0:T(128)} %bitcast.core_ref, f32[96,128]{1,0:T(8,128)} %add_add_fusion.small_hbm, f32[26,128]{1,0:T(8,128)} %bitcast.12, f32[16,3328]{1,0:T(8,128)} %up_hbm.3, bf16[16,32,3328]{2,1,0:T(8,128)(2,1)} %all-to-all-done.given_hbm, ...), custom_call_target="tpu_custom_call" | custom-call | flops 3489660928 | bytes 12582912 | tf_op jit(solution)/shard_map/backward/pallas_call | solution.py:368
  83.7 0.1 collective-permute-start.14
  83.8 2.2 %collective-permute-done.14.got_hbm = bf16[272,1024]{1,0:T(8,128)(2,1)S(1)} collective-permute-done((bf16[272,1024]{1,0:T(8,128)(2,1)}, bf16[272,1024]{1,0:T(8,128)(2,1)S(1)}, u32[]{:S(2)}, u32[]{:S(2)}) %collective-permute-start.14) | collective-permute-done | bytes 557088 | tf_op jit(solution)/shard_map/ppermute | solution.py:663
  85.9 0.8 copy-done.1
  86.7 2.2 %pair.1 = (bf16[144,1024]{1,0:T(8,128)(2,1)}, bf16[144,1024]{1,0:T(8,128)(2,1)}) custom-call(s32[1]{0:T(128)} %bitcast.1.z_ref, bf16[272,1024]{1,0:T(8,128)(2,1)} %get-tuple-element.54.own_hbm, bf16[272,1024]{1,0:T(8,128)(2,1)} %copy-done.1), custom_call_target="tpu_custom_call" | custom-call | flops 1114112 | bytes 1671168 | tf_op jit(solution)/shard_map/pair/pallas_call | solution.py:414
  88.9 2.0 %collective-permute-start.15 = (bf16[144,1024]{1,0:T(8,128)(2,1)}, bf16[144,1024]{1,0:T(8,128)(2,1)S(1)}, u32[]{:S(2)}, u32[]{:S(2)}) collective-permute-start(bf16[144,1024]{1,0:T(8,128)(2,1)} %get-tuple-element.57), channel_id=1, source_target_pairs={{0,2},{2,0},{4,6},{6,4},{8,10},{10,8},{12,14},{14,12},{1,3},{3,1},... | collective-permute-start | bytes 884744 | tf_op jit(solution)/shard_map/ppermute | solution.py:665
  90.9 7.5 %collective-permute-done.15.got_hbm = bf16[144,1024]{1,0:T(8,128)(2,1)S(1)} collective-permute-done((bf16[144,1024]{1,0:T(8,128)(2,1)}, bf16[144,1024]{1,0:T(8,128)(2,1)S(1)}, u32[]{:S(2)}, u32[]{:S(2)}) %collective-permute-start.15) | collective-permute-done | bytes 294944 | tf_op jit(solution)/shard_map/ppermute | solution.py:665
  98.4 0.7 copy-done.3
  99.1 1.9 %quad.1 = (bf16[48,1024]{1,0:T(8,128)(2,1)}, bf16[48,1024]{1,0:T(8,128)(2,1)}, bf16[48,1024]{1,0:T(8,128)(2,1)}, bf16[48,1024]{1,0:T(8,128)(2,1)}) custom-call(s32[1]{0:T(128)} %bitcast.1.z_ref, bf16[144,1024]{1,0:T(8,128)(2,1)} %get-tuple-element.56.keep_hbm, bf16[144,1024]{1,0:T(8,128)(2,1)} %copy-done.3), custom_call_target="tpu_custom_call" | custom-call | flops 589824 | bytes 884736 | tf_op jit(solution)/shard_map/quad/pallas_call | solution.py:450
  101.0 3.4 %collective-permute-start.16 = (bf16[48,1024]{1,0:T(8,128)(2,1)}, bf16[48,1024]{1,0:T(8,128)(2,1)S(1)}, u32[]{:S(2)}, u32[]{:S(2)}) collective-permute-start(bf16[48,1024]{1,0:T(8,128)(2,1)} %get-tuple-element.59), channel_id=1, source_target_pairs={{0,4},{2,6},{4,8},{6,10},{8,12},{10,14},{12,0},{14,2},{1,5},{3,7},... | collective-permute-start | bytes 294920 | tf_op jit(solution)/shard_map/ppermute | solution.py:621
  104.4 5.3 %collective-permute-start.17 = (bf16[48,1024]{1,0:T(8,128)(2,1)}, bf16[48,1024]{1,0:T(8,128)(2,1)S(1)}, u32[]{:S(2)}, u32[]{:S(2)}) collective-permute-start(bf16[48,1024]{1,0:T(8,128)(2,1)} %get-tuple-element.60), channel_id=1, source_target_pairs={{0,8},{2,10},{4,12},{6,14},{8,0},{10,2},{12,4},{14,6},{1,9},{3,11}... | collective-permute-start | bytes 294920 | tf_op jit(solution)/shard_map/ppermute | solution.py:621
  109.7 2.6 %collective-permute-start.18 = (bf16[48,1024]{1,0:T(8,128)(2,1)}, bf16[48,1024]{1,0:T(8,128)(2,1)S(1)}, u32[]{:S(2)}, u32[]{:S(2)}) collective-permute-start(bf16[48,1024]{1,0:T(8,128)(2,1)} %get-tuple-element.61), channel_id=1, source_target_pairs={{0,12},{2,14},{4,0},{6,2},{8,4},{10,6},{12,8},{14,10},{1,13},{3,15... | collective-permute-start | bytes 294920 | tf_op jit(solution)/shard_map/ppermute | solution.py:621
  112.2 4.2 %up_gradient.1 = f32[16,3328]{1,0:T(8,128)} custom-call(f32[96,128]{1,0:T(8,128)} %add_add_fusion.small_hbm, f32[64,128]{1,0:T(8,128)} %get-tuple-element.51.scale_hbm, bf16[16,32,3328]{2,1,0:T(8,128)(2,1)} %all-to-all-done.given_hbm), custom_call_target="tpu_custom_call" | custom-call | flops 872415232 | bytes 4194304 | tf_op jit(solution)/shard_map/up_gradient/pallas_call | solution.py:538
  116.5 2.3 %collective-permute-done.18.refs_3_ = bf16[48,1024]{1,0:T(8,128)(2,1)S(1)} collective-permute-done((bf16[48,1024]{1,0:T(8,128)(2,1)}, bf16[48,1024]{1,0:T(8,128)(2,1)S(1)}, u32[]{:S(2)}, u32[]{:S(2)}) %collective-permute-start.18) | collective-permute-done | bytes 98336 | tf_op jit(solution)/shard_map/ppermute | solution.py:621
  118.8 0.6 copy-done.6
  119.5 2.4 %finish.1 = (bf16[32,1024]{1,0:T(8,128)(2,1)}, f32[16,1024]{1,0:T(8,128)}) custom-call(s32[1]{0:T(128)} %bitcast.1.z_ref, bf16[512,1024]{1,0:T(8,128)(2,1)} %bitcast.8, bf16[48,1024]{1,0:T(8,128)(2,1)} %get-tuple-element.58.refs_0_, bf16[48,1024]{1,0:T(8,128)(2,1)} %copy-done.4, bf16[48,1024]{1,0:T(8,128)(2,1)} %copy-done.5, bf16[48,1024]{1,0:T(8,128)(2,1)} %copy-done.6), custom_call_target="tpu_custom_call" | custom-call | flops 268435456 | bytes 2097152 | tf_op jit(solution)/shard_map/finish/pallas_call | solution.py:488
  121.9 3.3 %output.1 = (bf16[32,3328]{1,0:T(8,128)(2,1)}, f32[26,128]{1,0:T(8,128)}) custom-call(f32[64,128]{1,0:T(8,128)} %get-tuple-element.51.scale_hbm, bf16[16,32,3456]{2,1,0:T(8,128)(2,1)} %all-to-all-done.1.parts_hbm), custom_call_target="tpu_custom_call" | custom-call | flops 1703936 | bytes 4194304 | tf_op jit(solution)/shard_map/output/pallas_call | solution.py:593
  (34 shorter events, 0.1 us)
Async XLA Ops:
  3.5 7.5 %copy-start.7 = (bf16[32,1024]{1,0:T(8,128)(2,1)S(1)}, bf16[32,1024]{1,0:T(8,128)(2,1)}, u32[]{:S(2)}) copy-start(bf16[32,1024]{1,0:T(8,128)(2,1)} %param.6) | copy-start | bytes 196612
  3.5 61.7 %all-to-all-start = ((bf16[16,32,3328]{2,1,0:T(8,128)(2,1)}), bf16[16,32,3328]{2,1,0:T(8,128)(2,1)}, u32[]{:S(2)}, u32[]{:S(2)}) async-start(bf16[16,32,3328]{2,1,0:T(8,128)(2,1)} %spread.1.after_hbm), calls=%async_computation | async-start | bytes 6815744 | tf_op jit(solution)/shard_map/all_to_all | solution.py:617
  11.1 27.4 %collective-permute-start.3 = (bf16[32,1024]{1,0:T(8,128)(2,1)S(1)}, bf16[32,1024]{1,0:T(8,128)(2,1)S(1)}, u32[]{:S(2)}, u32[]{:S(2)}) collective-permute-start(bf16[32,1024]{1,0:T(8,128)(2,1)S(1)} %copy-done.7), channel_id=1, source_target_pairs={{0,8},{2,10},{4,12},{6,14},{8,0},{10,2},{12,4},{14,6},{1,9},{3,11}... | collective-permute-start | bytes 196616 | tf_op jit(solution)/shard_map/ppermute | solution.py:621
  18.4 20.1 %collective-permute-start.2 = (bf16[32,1024]{1,0:T(8,128)(2,1)S(1)}, bf16[32,1024]{1,0:T(8,128)(2,1)S(1)}, u32[]{:S(2)}, u32[]{:S(2)}) collective-permute-start(bf16[32,1024]{1,0:T(8,128)(2,1)S(1)} %copy-done.7), channel_id=1, source_target_pairs={{0,6},{2,8},{4,10},{6,12},{8,14},{10,0},{12,2},{14,4},{1,7},{3,9},... | collective-permute-start | bytes 196616 | tf_op jit(solution)/shard_map/ppermute | solution.py:621
  20.3 16.6 %collective-permute-start.1 = (bf16[32,1024]{1,0:T(8,128)(2,1)S(1)}, bf16[32,1024]{1,0:T(8,128)(2,1)S(1)}, u32[]{:S(2)}, u32[]{:S(2)}) collective-permute-start(bf16[32,1024]{1,0:T(8,128)(2,1)S(1)} %copy-done.7), channel_id=1, source_target_pairs={{0,4},{2,6},{4,8},{6,10},{8,12},{10,14},{12,0},{14,2},{1,5},{3,7},... | collective-permute-start | bytes 196616 | tf_op jit(solution)/shard_map/ppermute | solution.py:621
  20.3 18.2 %collective-permute-start.4 = (bf16[32,1024]{1,0:T(8,128)(2,1)S(1)}, bf16[32,1024]{1,0:T(8,128)(2,1)S(1)}, u32[]{:S(2)}, u32[]{:S(2)}) collective-permute-start(bf16[32,1024]{1,0:T(8,128)(2,1)S(1)} %copy-done.7), channel_id=1, source_target_pairs={{0,10},{2,12},{4,14},{6,0},{8,2},{10,4},{12,6},{14,8},{1,11},{3,13... | collective-permute-start | bytes 196616 | tf_op jit(solution)/shard_map/ppermute | solution.py:621
  31.4 5.6 %collective-permute-start = (bf16[32,1024]{1,0:T(8,128)(2,1)S(1)}, bf16[32,1024]{1,0:T(8,128)(2,1)S(1)}, u32[]{:S(2)}, u32[]{:S(2)}) collective-permute-start(bf16[32,1024]{1,0:T(8,128)(2,1)S(1)} %copy-done.7), channel_id=1, source_target_pairs={{0,2},{2,4},{4,6},{6,8},{8,10},{10,12},{12,14},{14,0},{1,3},{3,5},... | collective-permute-start | bytes 196616 | tf_op jit(solution)/shard_map/ppermute | solution.py:621
  36.9 5.3 %collective-permute-start.6 = (bf16[32,1024]{1,0:T(8,128)(2,1)S(1)}, bf16[32,1024]{1,0:T(8,128)(2,1)S(1)}, u32[]{:S(2)}, u32[]{:S(2)}) collective-permute-start(bf16[32,1024]{1,0:T(8,128)(2,1)S(1)} %copy-done.7), channel_id=1, source_target_pairs={{0,14},{2,0},{4,2},{6,4},{8,6},{10,8},{12,10},{14,12},{1,15},{3,1}... | collective-permute-start | bytes 196616 | tf_op jit(solution)/shard_map/ppermute | solution.py:621
  37.0 5.3 %collective-permute-start.5 = (bf16[32,1024]{1,0:T(8,128)(2,1)S(1)}, bf16[32,1024]{1,0:T(8,128)(2,1)S(1)}, u32[]{:S(2)}, u32[]{:S(2)}) collective-permute-start(bf16[32,1024]{1,0:T(8,128)(2,1)S(1)} %copy-done.7), channel_id=1, source_target_pairs={{0,12},{2,14},{4,0},{6,2},{8,4},{10,6},{12,8},{14,10},{1,13},{3,15... | collective-permute-start | bytes 196616 | tf_op jit(solution)/shard_map/ppermute | solution.py:621
  42.2 2.0 %copy-start = (bf16[256,1024]{1,0:T(8,128)(2,1)}, bf16[256,1024]{1,0:T(8,128)(2,1)S(1)}, u32[]{:S(2)}) copy-start(bf16[256,1024]{1,0:T(8,128)(2,1)S(1)} %constant_dynamic-update-slice_fusion.own_hbm) | copy-start | bytes 1572868
  42.2 2.0 %collective-permute-start.7 = (bf16[256,1024]{1,0:T(8,128)(2,1)S(1)}, bf16[256,1024]{1,0:T(8,128)(2,1)S(1)}, u32[]{:S(2)}, u32[]{:S(2)}) collective-permute-start(bf16[256,1024]{1,0:T(8,128)(2,1)S(1)} %constant_dynamic-update-slice_fusion.own_hbm), channel_id=1, source_target_pairs={{0,1},{1,0},{2,3},{3,2},{4,5},{5,4},{6,7},{7,6},{8,9},{9,8},{10,11... | collective-permute-start | bytes 1572872 | tf_op jit(solution)/shard_map/ppermute | solution.py:648
  44.2 0.8 copy-start.2
  48.2 12.2 %collective-permute-start.10 = (f32[96,128]{1,0:T(8,128)}, f32[96,128]{1,0:T(8,128)S(1)}, u32[]{:S(2)}, u32[]{:S(2)}) collective-permute-start(f32[96,128]{1,0:T(8,128)} %get-tuple-element.39), channel_id=1, source_target_pairs={{0,192},{64,0},{128,64},{192,128},{1,193},{65,1},{129,65},{193,129... | collective-permute-start | bytes 147464 | tf_op jit(solution)/shard_map/ppermute | solution.py:621
  51.0 9.5 %collective-permute-start.9 = (f32[96,128]{1,0:T(8,128)}, f32[96,128]{1,0:T(8,128)S(1)}, u32[]{:S(2)}, u32[]{:S(2)}) collective-permute-start(f32[96,128]{1,0:T(8,128)} %get-tuple-element.39), channel_id=1, source_target_pairs={{0,128},{64,192},{128,0},{192,64},{1,129},{65,193},{129,1},{193,65... | collective-permute-start | bytes 147464 | tf_op jit(solution)/shard_map/ppermute | solution.py:621
  51.8 8.7 %collective-permute-start.8 = (f32[96,128]{1,0:T(8,128)}, f32[96,128]{1,0:T(8,128)S(1)}, u32[]{:S(2)}, u32[]{:S(2)}) collective-permute-start(f32[96,128]{1,0:T(8,128)} %get-tuple-element.39), channel_id=1, source_target_pairs={{0,64},{64,128},{128,192},{192,0},{1,65},{65,129},{129,193},{193,1... | collective-permute-start | bytes 147464 | tf_op jit(solution)/shard_map/ppermute | solution.py:621
  52.7 7.8 %copy-start.8 = (f32[96,128]{1,0:T(8,128)S(1)}, f32[96,128]{1,0:T(8,128)}, u32[]{:S(2)}) copy-start(f32[96,128]{1,0:T(8,128)} %get-tuple-element.39) | copy-start | bytes 147460
  60.5 8.6 %collective-permute-start.13 = (f32[96,128]{1,0:T(8,128)S(1)}, f32[96,128]{1,0:T(8,128)S(1)}, u32[]{:S(2)}, u32[]{:S(2)}) collective-permute-start(f32[96,128]{1,0:T(8,128)S(1)} %add_add_fusion.1), channel_id=1, source_target_pairs={{0,48},{16,0},{32,16},{48,32},{1,49},{17,1},{33,17},{49,33},{2,50}... | collective-permute-start | bytes 147464 | tf_op jit(solution)/shard_map/ppermute | solution.py:621
  61.1 8.0 %collective-permute-start.12 = (f32[96,128]{1,0:T(8,128)S(1)}, f32[96,128]{1,0:T(8,128)S(1)}, u32[]{:S(2)}, u32[]{:S(2)}) collective-permute-start(f32[96,128]{1,0:T(8,128)S(1)} %add_add_fusion.1), channel_id=1, source_target_pairs={{0,32},{16,48},{32,0},{48,16},{1,33},{17,49},{33,1},{49,17},{2,34}... | collective-permute-start | bytes 147464 | tf_op jit(solution)/shard_map/ppermute | solution.py:621
  63.5 5.7 %collective-permute-start.11 = (f32[96,128]{1,0:T(8,128)S(1)}, f32[96,128]{1,0:T(8,128)S(1)}, u32[]{:S(2)}, u32[]{:S(2)}) collective-permute-start(f32[96,128]{1,0:T(8,128)S(1)} %add_add_fusion.1), channel_id=1, source_target_pairs={{0,16},{16,32},{32,48},{48,0},{1,17},{17,33},{33,49},{49,1},{2,18}... | collective-permute-start | bytes 147464 | tf_op jit(solution)/shard_map/ppermute | solution.py:621
  69.8 52.1 %all-to-all-start.1 = ((bf16[16,32,3456]{2,1,0:T(8,128)(2,1)}), bf16[16,32,3456]{2,1,0:T(8,128)(2,1)}, u32[]{:S(2)}, u32[]{:S(2)}) async-start(bf16[16,32,3456]{2,1,0:T(8,128)(2,1)} %magnitude.1), calls=%async_computation.1 | async-start | bytes 7077888 | tf_op jit(solution)/shard_map/all_to_all | solution.py:617
  83.7 2.3 %collective-permute-start.14 = (bf16[272,1024]{1,0:T(8,128)(2,1)}, bf16[272,1024]{1,0:T(8,128)(2,1)S(1)}, u32[]{:S(2)}, u32[]{:S(2)}) collective-permute-start(bf16[272,1024]{1,0:T(8,128)(2,1)} %get-tuple-element.55), channel_id=1, source_target_pairs={{0,1},{1,0},{2,3},{3,2},{4,5},{5,4},{6,7},{7,6},{8,9},{9,8},{10,11... | collective-permute-start | bytes 1671176 | tf_op jit(solution)/shard_map/ppermute | solution.py:663
  85.9 0.8 copy-start.1
  88.9 9.5 %collective-permute-start.15 = (bf16[144,1024]{1,0:T(8,128)(2,1)}, bf16[144,1024]{1,0:T(8,128)(2,1)S(1)}, u32[]{:S(2)}, u32[]{:S(2)}) collective-permute-start(bf16[144,1024]{1,0:T(8,128)(2,1)} %get-tuple-element.57), channel_id=1, source_target_pairs={{0,2},{2,0},{4,6},{6,4},{8,10},{10,8},{12,14},{14,12},{1,3},{3,1},... | collective-permute-start | bytes 884744 | tf_op jit(solution)/shard_map/ppermute | solution.py:665
  98.4 0.7 copy-start.3
  101.0 15.4 %collective-permute-start.16 = (bf16[48,1024]{1,0:T(8,128)(2,1)}, bf16[48,1024]{1,0:T(8,128)(2,1)S(1)}, u32[]{:S(2)}, u32[]{:S(2)}) collective-permute-start(bf16[48,1024]{1,0:T(8,128)(2,1)} %get-tuple-element.59), channel_id=1, source_target_pairs={{0,4},{2,6},{4,8},{6,10},{8,12},{10,14},{12,0},{14,2},{1,5},{3,7},... | collective-permute-start | bytes 294920 | tf_op jit(solution)/shard_map/ppermute | solution.py:621
  104.4 12.0 %collective-permute-start.17 = (bf16[48,1024]{1,0:T(8,128)(2,1)}, bf16[48,1024]{1,0:T(8,128)(2,1)S(1)}, u32[]{:S(2)}, u32[]{:S(2)}) collective-permute-start(bf16[48,1024]{1,0:T(8,128)(2,1)} %get-tuple-element.60), channel_id=1, source_target_pairs={{0,8},{2,10},{4,12},{6,14},{8,0},{10,2},{12,4},{14,6},{1,9},{3,11}... | collective-permute-start | bytes 294920 | tf_op jit(solution)/shard_map/ppermute | solution.py:621
  109.7 9.1 %collective-permute-start.18 = (bf16[48,1024]{1,0:T(8,128)(2,1)}, bf16[48,1024]{1,0:T(8,128)(2,1)S(1)}, u32[]{:S(2)}, u32[]{:S(2)}) collective-permute-start(bf16[48,1024]{1,0:T(8,128)(2,1)} %get-tuple-element.61), channel_id=1, source_target_pairs={{0,12},{2,14},{4,0},{6,2},{8,4},{10,6},{12,8},{14,10},{1,13},{3,15... | collective-permute-start | bytes 294920 | tf_op jit(solution)/shard_map/ppermute | solution.py:621
  116.4 2.4 %copy-start.4 = (bf16[48,1024]{1,0:T(8,128)(2,1)}, bf16[48,1024]{1,0:T(8,128)(2,1)S(1)}, u32[]{:S(2)}) copy-start(bf16[48,1024]{1,0:T(8,128)(2,1)S(1)} %collective-permute-done.16.refs_1_) | copy-start | bytes 294916
  116.5 2.4 %copy-start.5 = (bf16[48,1024]{1,0:T(8,128)(2,1)}, bf16[48,1024]{1,0:T(8,128)(2,1)S(1)}, u32[]{:S(2)}) copy-start(bf16[48,1024]{1,0:T(8,128)(2,1)S(1)} %collective-permute-done.17.refs_2_) | copy-start | bytes 294916
  118.8 0.6 copy-start.6

commit v8 on v7

--- a/solution.py
+++ b/solution.py
@@ -16,7 +16,7 @@
 RANK = 16
 LANES = 128
 MIB = 1024 * 1024
-LIMIT = 62 * MIB
+LIMIT = 63 * MIB + 768 * 1024
 ANY = pl.BlockSpec(memory_space=pl.ANY)
 SMEM = pl.BlockSpec(memory_space=pltpu.SMEM)
 
@@ -186,7 +186,9 @@
         begin(sums_hbm, small.at[64:], first_sem.at[1]),
     ]
     for k in range(8):
-        back = lax.rem(z + 8 - k, 8)
+        back = lax.rem(z + 8 - (k - k % 2), 8)
+        if k % 2:
+            back = back + 1 - 2 * lax.rem(back, 2)
         rows = slice(32 * k, 32 * k + 32)
         copies.append(begin(own_hbm.at[rows], tokens.at[back, core], sem.at[0, k]))
         copies.append(begin(other_hbm.at[rows], tokens.at[back, 1 - core], sem.at[1, k]))
@@ -425,7 +427,7 @@
     )(z, own, got)
 
 
-def quad_kernel(z_ref, keep_hbm, got_hbm, *refs):
+def quad_kernel(z_ref, after_hbm, keep_hbm, got_hbm, *refs):
     out_hbm = refs[:4]
     keep, got, send, sem, out_sem = refs[4:]
     half = z_ref[0] // 2
@@ -445,67 +447,20 @@
         copy.wait()
 
 
-def quad(z, keep, got):
+def quad(z, after, keep, got):
     rows, depth = keep.shape
     return call(
         quad_kernel,
         4 * rows * depth,
         6 * rows * depth,
-        in_specs=[SMEM, ANY, ANY],
+        in_specs=[SMEM, ANY, ANY, ANY],
         out_specs=[ANY] * 4,
         out_shape=[jax.ShapeDtypeStruct((48, depth), bf16)] * 4,
         scratch_shapes=[pltpu.VMEM((rows, depth), bf16)] * 2
         + [pltpu.VMEM((4, 48, depth), bf16)]
         + [pltpu.SemaphoreType.DMA((2,)), pltpu.SemaphoreType.DMA((4,))],
         name="quad",
-    )(z, keep, got)
-
-
-def finish_kernel(z_ref, tokens_hbm, *refs):
-    parts_hbm = refs[:4]
-    grad_hbm, down_hbm, parts, tokens, lows, grad, down, sem, out_sem = refs[4:]
-    half = z_ref[0] // 2
-    copies = [begin(parts_hbm[k], parts.at[k], sem.at[k]) for k in range(4)]
-    later = begin(tokens_hbm, tokens, sem.at[4])
-    for copy in copies:
-        copy.wait()
-    total = parts[0, :32, :].astype(f32)
-    for k in range(1, 4):
-        total += parts[k, :32, :].astype(f32)
-    grad[...] = total.astype(bf16)
-    first = begin(grad, grad_hbm, out_sem.at[0])
-    for k in range(4):
-        lows[lax.rem(half + 4 - k, 4)] = unpack(parts[k, 32:48, :])
-    low = (lows[0] + lows[1]) + (lows[2] + lows[3])
-    later.wait()
-    down[...] = three(low * adapter_scale, tokens[...], 1, 0)
-    begin(down, down_hbm, out_sem.at[1]).wait()
-    first.wait()
-
-
-def finish(z, tokens, parts):
-    depth = tokens.shape[1]
-    return call(
-        finish_kernel,
-        2 * 512 * 256 * depth,
-        2 * MIB,
-        in_specs=[SMEM] + [ANY] * 5,
-        out_specs=[ANY, ANY],
-        out_shape=[
-            jax.ShapeDtypeStruct((32, depth), bf16),
-            jax.ShapeDtypeStruct((RANK, depth), f32),
-        ],
-        scratch_shapes=[
-            pltpu.VMEM((4, 48, depth), bf16),
-            pltpu.VMEM(tokens.shape, bf16),
-            pltpu.VMEM((4, RANK, CHUNK), f32),
-            pltpu.VMEM((32, depth), bf16),
-            pltpu.VMEM((RANK, depth), f32),
-            pltpu.SemaphoreType.DMA((5,)),
-            pltpu.SemaphoreType.DMA((2,)),
-        ],
-        name="finish",
-    )(z, tokens, *parts)
+    )(z, after, keep, got)
 
 
 def up_kernel(
@@ -555,62 +510,87 @@
     )(small, scale, given)
 
 
-def output_kernel(
-    scale_hbm, parts_hbm, out_hbm, mag_hbm, scale, parts, out, mag, first_sem, sem, out_sem
-):
+def finish_kernel(z_ref, tokens_hbm, scale_hbm, parts_hbm, *refs):
+    blocks_hbm, (grad_hbm, down_hbm, out_hbm, mag_hbm) = refs[:4], refs[4:8]
+    blocks, tokens, lows, grad, down, scale, parts, out, mag = refs[8:17]
+    block_sem, first_sem, sem, out_sem = refs[17:]
+    half = z_ref[0] // 2
     width = out.shape[1]
     chunks = chunks_of(width)
     count = width // LANES
-    first = (
-        begin(scale_hbm, scale, first_sem.at[0]),
-        begin(parts_hbm.at[:, :, width:], parts.at[:, :, width:], first_sem.at[1]),
+    copies = [begin(blocks_hbm[k], blocks.at[k], block_sem.at[k]) for k in range(4)]
+    later = (
+        begin(tokens_hbm, tokens, first_sem.at[0]),
+        begin(scale_hbm, scale, first_sem.at[1]),
+        begin(parts_hbm.at[:, :, width:], parts.at[:, :, width:], first_sem.at[2]),
     )
-    ready = stream([(parts_hbm, parts.at[:, :, :width])], sem, chunks, 4)
-    for copy in first:
-        copy.wait()
-
-    def added(cols):
+    ready = stream([(parts_hbm, parts.at[:, :, :width])], sem, chunks, len(chunks))
+    for copy in copies:
+        copy.wait()
+    total = blocks[0, :32, :].astype(f32)
+    for k in range(1, 4):
+        total += blocks[k, :32, :].astype(f32)
+    grad[...] = total.astype(bf16)
+    stores = [begin(grad, grad_hbm, block_sem.at[0])]
+    for k in range(4):
+        lows[lax.rem(half + 4 - k, 4)] = unpack(blocks[k, 32:48, :])
+    low = (lows[0] + lows[1]) + (lows[2] + lows[3])
+    for copy in later:
+        copy.wait()
+    down[...] = three(low * adapter_scale, tokens[...], 1, 0)
+    stores.append(begin(down, down_hbm, block_sem.at[1]))
+
+    def summed(cols):
         total = parts[0, :, cols].astype(f32)
         for r in range(1, 16):
             total += parts[r, :, cols].astype(f32)
         return total
 
-    mag[...] = added(slice(width, width + LANES))[:count] / scale[32 : 32 + count, :]
-    stores = [begin(mag, mag_hbm, first_sem.at[0])]
+    mag[...] = summed(slice(width, width + LANES))[:count] / scale[32 : 32 + count, :]
+    stores.append(begin(mag, mag_hbm, block_sem.at[2]))
     factors = scale[:32, :]
     for j, (at, size) in enumerate(chunks):
         ready(j)
         cols = slice(at, at + size)
-        out[:, cols] = (added(cols) * in_line(factors, at, size)).astype(bf16)
+        out[:, cols] = (summed(cols) * in_line(factors, at, size)).astype(bf16)
         stores.append(begin(out.at[:, cols], out_hbm.at[:, cols], out_sem.at[j]))
     for copy in stores:
         copy.wait()
 
 
-def output_of(scale, parts):
+def finish(z, tokens, scale, parts, blocks):
+    depth = tokens.shape[1]
     width = parts.shape[2] - LANES
     count = len(chunks_of(width))
     return call(
-        output_kernel,
-        16 * 32 * width,
-        4 * MIB,
-        in_specs=[ANY] * 2,
-        out_specs=[ANY] * 2,
+        finish_kernel,
+        2 * 512 * 256 * depth,
+        6 * MIB,
+        in_specs=[SMEM] + [ANY] * 7,
+        out_specs=[ANY] * 4,
         out_shape=[
+            jax.ShapeDtypeStruct((32, depth), bf16),
+            jax.ShapeDtypeStruct((RANK, depth), f32),
             jax.ShapeDtypeStruct((32, width), bf16),
             jax.ShapeDtypeStruct((width // LANES, LANES), f32),
         ],
         scratch_shapes=[
+            pltpu.VMEM((4, 48, depth), bf16),
+            pltpu.VMEM(tokens.shape, bf16),
+            pltpu.VMEM((4, RANK, CHUNK), f32),
+            pltpu.VMEM((32, depth), bf16),
+            pltpu.VMEM((RANK, depth), f32),
             pltpu.VMEM(scale.shape, f32),
             pltpu.VMEM(parts.shape, bf16),
             pltpu.VMEM((32, width), bf16),
             pltpu.VMEM((width // LANES, LANES), f32),
-            pltpu.SemaphoreType.DMA((2,)),
+            pltpu.SemaphoreType.DMA((4,)),
+            pltpu.SemaphoreType.DMA((3,)),
             pltpu.SemaphoreType.DMA((1, count)),
             pltpu.SemaphoreType.DMA((count,)),
         ],
-        name="output",
-    )(scale, parts)
+        name="finish",
+    )(z, tokens, scale, parts, *blocks)
 
 
 def exchange(blocks):
@@ -635,16 +615,12 @@
     swap = [(0, 1), (1, 0)]
     down_t = down_adapter.T
     magnitude = magnitude.reshape(-1, LANES)
-    message = spread(out_cotangent)
-    given = exchange(message)
-    blocks = [tokens] * 8
-    for k in (4, 3, 5, 2):
-        blocks[k] = further(tokens, "z", k, 8)
-    merged_low, sums = merge(message, down_t, up_adapter, weight)
-    later, sums, merged_low = lax.optimization_barrier((tokens, sums, merged_low))
-    for k in (6, 1, 7):
-        blocks[k] = further(later, "z", k, 8)
-    own = jnp.concatenate(blocks, axis=0)
+    given = exchange(spread(out_cotangent))
+    beside = [(i, i ^ 1) for i in range(8)]
+    two = jnp.concatenate([tokens, lax.ppermute(tokens, "z", beside)], axis=0)
+    own = [two] + [further(two, "z", 2 * k, 8) for k in (1, 2, 3)]
+    merged_low, sums = merge(two, down_t, up_adapter, weight)
+    own = jnp.concatenate(own, axis=0)
     other = lax.ppermute(own, "c", swap)
     place = jnp.concatenate([z, core])
     small, tokens_full = project(place, own, other, down_t, sums)
@@ -656,19 +632,19 @@
     part = add_magnitude(given, part)
     arrived = shifted(small, "y")
     arrived, part = lax.optimization_barrier((arrived, part))
+    parts = exchange(part)
     small = added(small, arrived)
-    small, part = lax.optimization_barrier((small, part))
-    parts = exchange(part)
     own, send, scale = backward(core, small, magnitude, up_adapter, given, merged_low)
     got = lax.ppermute(send, "c", swap)
     keep, send = pair(z, own, got)
-    got = lax.ppermute(send, "z", [(i, i ^ 1) for i in range(8)])
-    blocks = list(quad(z, keep, got))
+    got = lax.ppermute(send, "z", beside)
+    up_gradient = up_gradient_of(small, scale, given)
+    blocks = list(quad(z, up_gradient, keep, got))
     for k in range(1, 4):
         blocks[k] = further(blocks[k], "z", 2 * k, 8)
-    up_gradient = up_gradient_of(small, scale, given)
-    grad_tokens, down_gradient = finish(z, tokens_full, blocks)
-    output, grad_magnitude = output_of(scale, parts)
+    grad_tokens, down_gradient, output, grad_magnitude = finish(
+        z, tokens_full, scale, parts, blocks
+    )
     return (output, grad_tokens, grad_magnitude.reshape(-1), up_gradient, down_gradient.T)
 
 

time: 127 us -> 125 us (0.984)
  Pallas kernels: 45.9 us -> 44.1 us
    ppermute x16 -> x12, starting transfers between devices: 36.9 us -> 32 us  [further(): return lax.ppermute(value, axis, [(i, (i + k) % size) for i in range(size)])]
    ppermute x16 -> x12, waiting for transfers between devices: 10.5 us -> 13.4 us  [further(): return lax.ppermute(value, axis, [(i, (i + k) % size) for i in range(size)])]
    ppermute x1 -> x2, waiting for transfers between devices: 7.52 us -> 5.16 us  [the longest x1 3.43 us: on_device(): got = lax.ppermute(send, 'z', beside)]
    ppermute x1 -> x2, starting transfers between devices: 2.01 us -> 4.11 us  [the longest x1 2.1 us: on_device(): got = lax.ppermute(send, 'z', beside)]
    all_to_all x2, starting transfers between devices: 13.5 us -> 15.3 us  [exchange(): return lax.all_to_all(blocks, ROW, 0, 0, tiled=False)]
    pallas_call x2 -> x1, Pallas kernels: 5.72 us -> 3.99 us  [finish(): call(finish_kernel, 2 * 512 * 256 * depth, 6 * MIB, in_specs=[SMEM] + [AN...]
    ppermute x1, waiting for transfers between devices: 1.3 us -> 0.01 us  [on_device(): other = lax.ppermute(own, 'c', swap)]
    concatenate x1 -> x2, local copies, waits for them, and re-layouts: 0.01 us -> 1.28 us  [the longest x1 0.66 us: on_device(): own = jnp.concatenate(own, axis=0)]
  transfers between devices with their start and end apart: 21 -> 18, of which waited for: 6 -> 8; matrix products, arithmetic and copies ran while one was open for 1% -> 4% of each run, Pallas kernels for 32% -> 30%
where the time goes in v8:
time: 125 us; the launch traced here: 123 us
  starting transfers between devices  51.5 us (41%)
  Pallas kernels  44.1 us (35%)
  waiting for transfers between devices  21.2 us (17%)
  local copies, waits for them, and re-layouts  3.23 us (3%)
  other arithmetic  2.03 us (2%)
    ppermute x12, starting transfers between devices, further(): return lax.ppermute(value, axis, [(i, (i + k) % size) for i in range(size)])  32 us
    all_to_all x2, starting transfers between devices, exchange(): return lax.all_to_all(blocks, ROW, 0, 0, tiled=False)  15.3 us
    ppermute x12, waiting for transfers between devices, further(): return lax.ppermute(value, axis, [(i, (i + k) % size) for i in range(size)])  13.4 us
    pallas_call x1, Pallas kernels, backward(): call(backward_kernel, 2 * 512 * depth * width, 12 * MIB, in_specs=[SMEM]...  7.84 us
    pallas_call x1, Pallas kernels, forward(): call(forward_kernel, 2 * 512 * depth * width, 12 * MIB, in_specs=[ANY] *...  7.74 us
    pallas_call x1, Pallas kernels, merge(): call(merge_kernel, 12 * depth * width, 4 * depth * width, in_specs=[ANY]...  6.5 us
    pallas_call x1, Pallas kernels, up_gradient_of(): call(up_kernel, 2 * 512 * 256 * width, 4 * MIB, in_specs=[ANY] * 3, out_s...  4.18 us
    pallas_call x1, Pallas kernels, finish(): call(finish_kernel, 2 * 512 * 256 * depth, 6 * MIB, in_specs=[SMEM] + [AN...  3.99 us
  transfers between devices with their start and end apart: 18, of which 8 were waited for; matrix products, arithmetic and copies ran while one was open for 4% of the time, Pallas kernels for 30%

profile of v8, /device:TPU:8, one launch (start us, length us, event | category | flops | bytes accessed | tf_op | source)
XLA Modules:
  0.0 123.0 jit_solution(11197746866815365803)
XLA Ops:
  0.6 2.9 %spread.1 = bf16[16,32,3328]{2,1,0:T(8,128)(2,1)} custom-call(bf16[32,3328]{1,0:T(8,128)(2,1)} %cot_hbm.1), custom_call_target="tpu_custom_call" | custom-call | flops 106496 | bytes 4194304 | tf_op jit(solution)/shard_map/spread/pallas_call | solution.py:163
  3.5 0.0 copy-start.3
  3.5 7.5 %all-to-all-start = ((bf16[16,32,3328]{2,1,0:T(8,128)(2,1)}), bf16[16,32,3328]{2,1,0:T(8,128)(2,1)}, u32[]{:S(2)}, u32[]{:S(2)}) async-start(bf16[16,32,3328]{2,1,0:T(8,128)(2,1)} %spread.1), calls=%async_computation | async-start | bytes 6815744 | tf_op jit(solution)/shard_map/all_to_all | solution.py:597
  11.1 2.0 %collective-permute-start = (bf16[32,1024]{1,0:T(8,128)(2,1)S(1)}, bf16[32,1024]{1,0:T(8,128)(2,1)S(1)}, u32[]{:S(2)}, u32[]{:S(2)}) collective-permute-start(bf16[32,1024]{1,0:T(8,128)(2,1)S(1)} %copy-done.3), channel_id=1, source_target_pairs={{0,2},{2,0},{4,6},{6,4},{8,10},{10,8},{12,14},{14,12},{1,3},{3,1},... | collective-permute-start | bytes 196616 | tf_op jit(solution)/shard_map/ppermute | solution.py:620
  13.1 0.6 constant_dynamic-update-slice_fusion.1
  13.7 1.7 %collective-permute-done = bf16[32,1024]{1,0:T(8,128)(2,1)S(1)} collective-permute-done((bf16[32,1024]{1,0:T(8,128)(2,1)S(1)}, bf16[32,1024]{1,0:T(8,128)(2,1)S(1)}, u32[]{:S(2)}, u32[]{:S(2)}) %collective-permute-start) | collective-permute-done | bytes 65568 | tf_op jit(solution)/shard_map/ppermute | solution.py:620
  15.4 0.6 constant_dynamic-update-slice_fusion
  16.0 3.3 %collective-permute-start.1 = (bf16[64,1024]{1,0:T(8,128)(2,1)S(1)}, bf16[64,1024]{1,0:T(8,128)(2,1)S(1)}, u32[]{:S(2)}, u32[]{:S(2)}) collective-permute-start(bf16[64,1024]{1,0:T(8,128)(2,1)S(1)} %get-tuple-element.55.after_hbm), channel_id=1, source_target_pairs={{0,4},{2,6},{4,8},{6,10},{8,12},{10,14},{12,0},{14,2},{1,5},{3,7},... | collective-permute-start | bytes 393224 | tf_op jit(solution)/shard_map/ppermute | solution.py:601
  19.3 5.4 %collective-permute-start.2 = (bf16[64,1024]{1,0:T(8,128)(2,1)S(1)}, bf16[64,1024]{1,0:T(8,128)(2,1)S(1)}, u32[]{:S(2)}, u32[]{:S(2)}) collective-permute-start(bf16[64,1024]{1,0:T(8,128)(2,1)S(1)} %get-tuple-element.55.after_hbm), channel_id=1, source_target_pairs={{0,8},{2,10},{4,12},{6,14},{8,0},{10,2},{12,4},{14,6},{1,9},{3,11}... | collective-permute-start | bytes 393224 | tf_op jit(solution)/shard_map/ppermute | solution.py:601
  24.7 2.7 %collective-permute-start.3 = (bf16[64,1024]{1,0:T(8,128)(2,1)S(1)}, bf16[64,1024]{1,0:T(8,128)(2,1)S(1)}, u32[]{:S(2)}, u32[]{:S(2)}) collective-permute-start(bf16[64,1024]{1,0:T(8,128)(2,1)S(1)} %get-tuple-element.55.after_hbm), channel_id=1, source_target_pairs={{0,12},{2,14},{4,0},{6,2},{8,4},{10,6},{12,8},{14,10},{1,13},{3,15... | collective-permute-start | bytes 393224 | tf_op jit(solution)/shard_map/ppermute | solution.py:601
  27.4 0.7 constant_dynamic-update-slice_fusion.4
  28.0 5.0 %collective-permute-done.2 = bf16[64,1024]{1,0:T(8,128)(2,1)S(1)} collective-permute-done((bf16[64,1024]{1,0:T(8,128)(2,1)S(1)}, bf16[64,1024]{1,0:T(8,128)(2,1)S(1)}, u32[]{:S(2)}, u32[]{:S(2)}) %collective-permute-start.2) | collective-permute-done | bytes 131104 | tf_op jit(solution)/shard_map/ppermute | solution.py:601
  33.1 0.7 constant_dynamic-update-slice_fusion.3
  33.7 1.8 %collective-permute-done.3 = bf16[64,1024]{1,0:T(8,128)(2,1)S(1)} collective-permute-done((bf16[64,1024]{1,0:T(8,128)(2,1)S(1)}, bf16[64,1024]{1,0:T(8,128)(2,1)S(1)}, u32[]{:S(2)}, u32[]{:S(2)}) %collective-permute-start.3) | collective-permute-done | bytes 131104 | tf_op jit(solution)/shard_map/ppermute | solution.py:601
  35.5 0.7 constant_dynamic-update-slice_fusion.2.own_hbm
  36.2 0.6 pad_add_fusion.place_ref
  36.7 6.5 %merge.1 = (bf16[1024,3328]{1,0:T(8,128)(2,1)}, f32[32,128]{1,0:T(8,128)}) custom-call(bf16[64,1024]{1,0:T(8,128)(2,1)} %copy-done, f32[16,1024]{1,0:T(8,128)} %bitcast.9, f32[16,3328]{1,0:T(8,128)} %up_hbm.3, bf16[1024,3328]{1,0:T(8,128)(2,1)} %weight_hbm.1), custom_call_target="tpu_custom_call" | custom-call | flops 40894464 | bytes 13631488 | tf_op jit(solution)/shard_map/merge/pallas_call | solution.py:129
  43.3 3.1 %project.1 = (f32[96,128]{1,0:T(8,128)}, bf16[8,2,32,1024]{3,2,1,0:T(8,128)(2,1)}) custom-call(s32[2]{0:T(128)} %pad_add_fusion.place_ref, bf16[256,1024]{1,0:T(8,128)(2,1)} %constant_dynamic-update-slice_fusion.2.own_hbm, bf16[256,1024]{1,0:T(8,128)(2,1)} %collective-permute-done.4.other_hbm, f32[16,1024]{1,0:T(8,128)} %bitcast.10, ...), custom_call_target="tpu_custom_call" | custom-call | flops 268435456 | bytes 3145728 | tf_op jit(solution)/shard_map/project/pallas_call | solution.py:208
  46.4 2.8 %collective-permute-start.7 = (f32[96,128]{1,0:T(8,128)}, f32[96,128]{1,0:T(8,128)S(1)}, u32[]{:S(2)}, u32[]{:S(2)}) collective-permute-start(f32[96,128]{1,0:T(8,128)} %get-tuple-element.32), channel_id=1, source_target_pairs={{0,192},{64,0},{128,64},{192,128},{1,193},{65,1},{129,65},{193,129... | collective-permute-start | bytes 147464 | tf_op jit(solution)/shard_map/ppermute | solution.py:601
  49.2 0.8 collective-permute-start.6
  50.0 0.9 collective-permute-start.5
  50.9 7.7 %forward.1.part_hbm = bf16[16,32,3456]{2,1,0:T(8,128)(2,1)} custom-call(bf16[512,1024]{1,0:T(8,128)(2,1)} %bitcast.7, bf16[1024,3328]{1,0:T(8,128)(2,1)} %get-tuple-element.33.merged_hbm), custom_call_target="tpu_custom_call" | custom-call | flops 3489660928 | bytes 12582912 | tf_op jit(solution)/shard_map/forward/pallas_call | solution.py:249
  58.6 0.0 collective-permute-done.6
  58.7 0.0 collective-permute-done.5
  58.7 0.8 add_add_fusion.1
  59.5 0.8 collective-permute-start.10
  60.3 2.4 %collective-permute-start.9 = (f32[96,128]{1,0:T(8,128)S(1)}, f32[96,128]{1,0:T(8,128)S(1)}, u32[]{:S(2)}, u32[]{:S(2)}) collective-permute-start(f32[96,128]{1,0:T(8,128)S(1)} %add_add_fusion.1), channel_id=1, source_target_pairs={{0,32},{16,48},{32,0},{48,16},{1,33},{17,49},{33,1},{49,17},{2,34}... | collective-permute-start | bytes 147464 | tf_op jit(solution)/shard_map/ppermute | solution.py:601
  62.7 1.8 %collective-permute-start.8 = (f32[96,128]{1,0:T(8,128)S(1)}, f32[96,128]{1,0:T(8,128)S(1)}, u32[]{:S(2)}, u32[]{:S(2)}) collective-permute-start(f32[96,128]{1,0:T(8,128)S(1)} %add_add_fusion.1), channel_id=1, source_target_pairs={{0,16},{16,32},{32,48},{48,0},{1,17},{17,33},{33,49},{49,1},{2,18}... | collective-permute-start | bytes 147464 | tf_op jit(solution)/shard_map/ppermute | solution.py:601
  64.5 0.0 all-to-all-done.given_hbm
  64.5 3.8 %magnitude.1 = bf16[16,32,3456]{2,1,0:T(8,128)(2,1)} custom-call(bf16[16,32,3328]{2,1,0:T(8,128)(2,1)} %all-to-all-done.given_hbm, bf16[16,32,3456]{2,1,0:T(8,128)(2,1)} %forward.1.part_hbm), custom_call_target="tpu_custom_call", output_to_operand_aliasing={{}: (1, {})} | custom-call | flops 6815744 | bytes 7340032 | tf_op jit(solution)/shard_map/magnitude/pallas_call | solution.py:287
  68.3 0.0 collective-permute-done.10
  68.3 7.7 %all-to-all-start.1 = ((bf16[16,32,3456]{2,1,0:T(8,128)(2,1)}), bf16[16,32,3456]{2,1,0:T(8,128)(2,1)}, u32[]{:S(2)}, u32[]{:S(2)}) async-start(bf16[16,32,3456]{2,1,0:T(8,128)(2,1)} %magnitude.1), calls=%async_computation.1 | async-start | bytes 7077888 | tf_op jit(solution)/shard_map/all_to_all | solution.py:597
  76.0 0.6 add_add_fusion.small_hbm
  76.7 7.8 %backward.1 = (bf16[272,1024]{1,0:T(8,128)(2,1)}, bf16[272,1024]{1,0:T(8,128)(2,1)}, f32[64,128]{1,0:T(8,128)}) custom-call(s32[1]{0:T(128)} %bitcast.1.core_ref, f32[96,128]{1,0:T(8,128)} %add_add_fusion.small_hbm, f32[26,128]{1,0:T(8,128)} %bitcast.12, f32[16,3328]{1,0:T(8,128)} %up_hbm.3, bf16[16,32,3328]{2,1,0:T(8,128)(2,1)} %all-to-all-done.given_hbm, ...), custom_call_target="tpu_custom_call" | custom-call | flops 3489660928 | bytes 12582912 | tf_op jit(solution)/shard_map/backward/pallas_call | solution.py:370
  84.5 0.1 collective-permute-start.11
  84.6 2.3 %collective-permute-done.11.got_hbm = bf16[272,1024]{1,0:T(8,128)(2,1)} collective-permute-done((bf16[272,1024]{1,0:T(8,128)(2,1)}, bf16[272,1024]{1,0:T(8,128)(2,1)}, u32[]{:S(2)}, u32[]{:S(2)}) %collective-permute-start.11) | collective-permute-done | bytes 557088 | tf_op jit(solution)/shard_map/ppermute | solution.py:638
  86.9 2.2 %pair.1 = (bf16[144,1024]{1,0:T(8,128)(2,1)}, bf16[144,1024]{1,0:T(8,128)(2,1)}) custom-call(s32[1]{0:T(128)} %bitcast.z_ref, bf16[272,1024]{1,0:T(8,128)(2,1)} %get-tuple-element.43.own_hbm, bf16[272,1024]{1,0:T(8,128)(2,1)} %collective-permute-done.11.got_hbm), custom_call_target="tpu_custom_call" | custom-call | flops 1114112 | bytes 1671168 | tf_op jit(solution)/shard_map/pair/pallas_call | solution.py:416
  89.1 2.1 %collective-permute-start.12 = (bf16[144,1024]{1,0:T(8,128)(2,1)}, bf16[144,1024]{1,0:T(8,128)(2,1)}, u32[]{:S(2)}, u32[]{:S(2)}) collective-permute-start(bf16[144,1024]{1,0:T(8,128)(2,1)} %get-tuple-element.46), channel_id=1, source_target_pairs={{0,2},{2,0},{4,6},{6,4},{8,10},{10,8},{12,14},{14,12},{1,3},{3,1},... | collective-permute-start | bytes 884744 | tf_op jit(solution)/shard_map/ppermute | solution.py:640
  91.2 4.2 %up_gradient.1.after_hbm = f32[16,3328]{1,0:T(8,128)} custom-call(f32[96,128]{1,0:T(8,128)} %add_add_fusion.small_hbm, f32[64,128]{1,0:T(8,128)} %get-tuple-element.41.scale_hbm, bf16[16,32,3328]{2,1,0:T(8,128)(2,1)} %all-to-all-done.given_hbm), custom_call_target="tpu_custom_call" | custom-call | flops 872415232 | bytes 4194304 | tf_op jit(solution)/shard_map/up_gradient/pallas_call | solution.py:493
  95.4 3.4 %collective-permute-done.12.got_hbm = bf16[144,1024]{1,0:T(8,128)(2,1)} collective-permute-done((bf16[144,1024]{1,0:T(8,128)(2,1)}, bf16[144,1024]{1,0:T(8,128)(2,1)}, u32[]{:S(2)}, u32[]{:S(2)}) %collective-permute-start.12) | collective-permute-done | bytes 294944 | tf_op jit(solution)/shard_map/ppermute | solution.py:640
  98.8 1.9 %quad.1 = (bf16[48,1024]{1,0:T(8,128)(2,1)}, bf16[48,1024]{1,0:T(8,128)(2,1)}, bf16[48,1024]{1,0:T(8,128)(2,1)}, bf16[48,1024]{1,0:T(8,128)(2,1)}) custom-call(s32[1]{0:T(128)} %bitcast.z_ref, f32[16,3328]{1,0:T(8,128)} %up_gradient.1.after_hbm, bf16[144,1024]{1,0:T(8,128)(2,1)} %get-tuple-element.45.keep_hbm, bf16[144,1024]{1,0:T(8,128)(2,1)} %collective-permute-done.12.got_hbm), custom_call_target="tpu_custom_call" | custom-call | flops 589824 | bytes 884736 | tf_op jit(solution)/shard_map/quad/pallas_call | solution.py:452
  100.7 3.3 %collective-permute-start.13 = (bf16[48,1024]{1,0:T(8,128)(2,1)}, bf16[48,1024]{1,0:T(8,128)(2,1)S(1)}, u32[]{:S(2)}, u32[]{:S(2)}) collective-permute-start(bf16[48,1024]{1,0:T(8,128)(2,1)} %get-tuple-element.48), channel_id=1, source_target_pairs={{0,4},{2,6},{4,8},{6,10},{8,12},{10,14},{12,0},{14,2},{1,5},{3,7},... | collective-permute-start | bytes 294920 | tf_op jit(solution)/shard_map/ppermute | solution.py:601
  104.0 5.2 %collective-permute-start.14 = (bf16[48,1024]{1,0:T(8,128)(2,1)}, bf16[48,1024]{1,0:T(8,128)(2,1)S(1)}, u32[]{:S(2)}, u32[]{:S(2)}) collective-permute-start(bf16[48,1024]{1,0:T(8,128)(2,1)} %get-tuple-element.49), channel_id=1, source_target_pairs={{0,8},{2,10},{4,12},{6,14},{8,0},{10,2},{12,4},{14,6},{1,9},{3,11}... | collective-permute-start | bytes 294920 | tf_op jit(solution)/shard_map/ppermute | solution.py:601
  109.2 2.7 %collective-permute-start.15 = (bf16[48,1024]{1,0:T(8,128)(2,1)}, bf16[48,1024]{1,0:T(8,128)(2,1)}, u32[]{:S(2)}, u32[]{:S(2)}) collective-permute-start(bf16[48,1024]{1,0:T(8,128)(2,1)} %get-tuple-element.50), channel_id=1, source_target_pairs={{0,12},{2,14},{4,0},{6,2},{8,4},{10,6},{12,8},{14,10},{1,13},{3,15... | collective-permute-start | bytes 294920 | tf_op jit(solution)/shard_map/ppermute | solution.py:601
  111.9 4.0 %collective-permute-done.14.refs_2_ = bf16[48,1024]{1,0:T(8,128)(2,1)S(1)} collective-permute-done((bf16[48,1024]{1,0:T(8,128)(2,1)}, bf16[48,1024]{1,0:T(8,128)(2,1)S(1)}, u32[]{:S(2)}, u32[]{:S(2)}) %collective-permute-start.14) | collective-permute-done | bytes 98336 | tf_op jit(solution)/shard_map/ppermute | solution.py:601
  115.9 2.6 %collective-permute-done.15.refs_3_ = bf16[48,1024]{1,0:T(8,128)(2,1)} collective-permute-done((bf16[48,1024]{1,0:T(8,128)(2,1)}, bf16[48,1024]{1,0:T(8,128)(2,1)}, u32[]{:S(2)}, u32[]{:S(2)}) %collective-permute-start.15) | collective-permute-done | bytes 98336 | tf_op jit(solution)/shard_map/ppermute | solution.py:601
  118.4 0.4 all-to-all-done.1.parts_hbm
  118.9 4.0 %finish.1 = (bf16[32,1024]{1,0:T(8,128)(2,1)}, f32[16,1024]{1,0:T(8,128)}, bf16[32,3328]{1,0:T(8,128)(2,1)}, f32[26,128]{1,0:T(8,128)}) custom-call(s32[1]{0:T(128)} %bitcast.z_ref, bf16[512,1024]{1,0:T(8,128)(2,1)} %bitcast.8, f32[64,128]{1,0:T(8,128)} %get-tuple-element.41.scale_hbm, bf16[16,32,3456]{2,1,0:T(8,128)(2,1)} %all-to-all-done.1.parts_hbm, ...), custom_call_target="tpu_custom_call" | custom-call | flops 268435456 | bytes 6291456 | tf_op jit(solution)/shard_map/finish/pallas_call | solution.py:565
  (16 shorter events, 0.0 us)
Async XLA Ops:
  3.5 7.5 %copy-start.3 = (bf16[32,1024]{1,0:T(8,128)(2,1)S(1)}, bf16[32,1024]{1,0:T(8,128)(2,1)}, u32[]{:S(2)}) copy-start(bf16[32,1024]{1,0:T(8,128)(2,1)} %param.6) | copy-start | bytes 196612
  3.5 60.9 %all-to-all-start = ((bf16[16,32,3328]{2,1,0:T(8,128)(2,1)}), bf16[16,32,3328]{2,1,0:T(8,128)(2,1)}, u32[]{:S(2)}, u32[]{:S(2)}) async-start(bf16[16,32,3328]{2,1,0:T(8,128)(2,1)} %spread.1), calls=%async_computation | async-start | bytes 6815744 | tf_op jit(solution)/shard_map/all_to_all | solution.py:597
  11.1 4.4 %collective-permute-start = (bf16[32,1024]{1,0:T(8,128)(2,1)S(1)}, bf16[32,1024]{1,0:T(8,128)(2,1)S(1)}, u32[]{:S(2)}, u32[]{:S(2)}) collective-permute-start(bf16[32,1024]{1,0:T(8,128)(2,1)S(1)} %copy-done.3), channel_id=1, source_target_pairs={{0,2},{2,0},{4,6},{6,4},{8,10},{10,8},{12,14},{14,12},{1,3},{3,1},... | collective-permute-start | bytes 196616 | tf_op jit(solution)/shard_map/ppermute | solution.py:620
  16.0 20.7 %copy-start = (bf16[64,1024]{1,0:T(8,128)(2,1)}, bf16[64,1024]{1,0:T(8,128)(2,1)S(1)}, u32[]{:S(2)}) copy-start(bf16[64,1024]{1,0:T(8,128)(2,1)S(1)} %get-tuple-element.55.after_hbm) | copy-start | bytes 393220
  16.0 11.3 %collective-permute-start.1 = (bf16[64,1024]{1,0:T(8,128)(2,1)S(1)}, bf16[64,1024]{1,0:T(8,128)(2,1)S(1)}, u32[]{:S(2)}, u32[]{:S(2)}) collective-permute-start(bf16[64,1024]{1,0:T(8,128)(2,1)S(1)} %get-tuple-element.55.after_hbm), channel_id=1, source_target_pairs={{0,4},{2,6},{4,8},{6,10},{8,12},{10,14},{12,0},{14,2},{1,5},{3,7},... | collective-permute-start | bytes 393224 | tf_op jit(solution)/shard_map/ppermute | solution.py:601
  19.3 13.7 %collective-permute-start.2 = (bf16[64,1024]{1,0:T(8,128)(2,1)S(1)}, bf16[64,1024]{1,0:T(8,128)(2,1)S(1)}, u32[]{:S(2)}, u32[]{:S(2)}) collective-permute-start(bf16[64,1024]{1,0:T(8,128)(2,1)S(1)} %get-tuple-element.55.after_hbm), channel_id=1, source_target_pairs={{0,8},{2,10},{4,12},{6,14},{8,0},{10,2},{12,4},{14,6},{1,9},{3,11}... | collective-permute-start | bytes 393224 | tf_op jit(solution)/shard_map/ppermute | solution.py:601
  24.7 10.8 %collective-permute-start.3 = (bf16[64,1024]{1,0:T(8,128)(2,1)S(1)}, bf16[64,1024]{1,0:T(8,128)(2,1)S(1)}, u32[]{:S(2)}, u32[]{:S(2)}) collective-permute-start(bf16[64,1024]{1,0:T(8,128)(2,1)S(1)} %get-tuple-element.55.after_hbm), channel_id=1, source_target_pairs={{0,12},{2,14},{4,0},{6,2},{8,4},{10,6},{12,8},{14,10},{1,13},{3,15... | collective-permute-start | bytes 393224 | tf_op jit(solution)/shard_map/ppermute | solution.py:601
  36.2 7.1 %collective-permute-start.4 = (bf16[256,1024]{1,0:T(8,128)(2,1)}, bf16[256,1024]{1,0:T(8,128)(2,1)}, u32[]{:S(2)}, u32[]{:S(2)}) collective-permute-start(bf16[256,1024]{1,0:T(8,128)(2,1)} %constant_dynamic-update-slice_fusion.2.own_hbm), channel_id=1, source_target_pairs={{0,1},{1,0},{2,3},{3,2},{4,5},{5,4},{6,7},{7,6},{8,9},{9,8},{10,11... | collective-permute-start | bytes 1572872 | tf_op jit(solution)/shard_map/ppermute | solution.py:624
  46.4 12.2 %collective-permute-start.7 = (f32[96,128]{1,0:T(8,128)}, f32[96,128]{1,0:T(8,128)S(1)}, u32[]{:S(2)}, u32[]{:S(2)}) collective-permute-start(f32[96,128]{1,0:T(8,128)} %get-tuple-element.32), channel_id=1, source_target_pairs={{0,192},{64,0},{128,64},{192,128},{1,193},{65,1},{129,65},{193,129... | collective-permute-start | bytes 147464 | tf_op jit(solution)/shard_map/ppermute | solution.py:601
  49.2 9.5 %collective-permute-start.6 = (f32[96,128]{1,0:T(8,128)}, f32[96,128]{1,0:T(8,128)S(1)}, u32[]{:S(2)}, u32[]{:S(2)}) collective-permute-start(f32[96,128]{1,0:T(8,128)} %get-tuple-element.32), channel_id=1, source_target_pairs={{0,128},{64,192},{128,0},{192,64},{1,129},{65,193},{129,1},{193,65... | collective-permute-start | bytes 147464 | tf_op jit(solution)/shard_map/ppermute | solution.py:601
  50.0 8.7 %collective-permute-start.5 = (f32[96,128]{1,0:T(8,128)}, f32[96,128]{1,0:T(8,128)}, u32[]{:S(2)}, u32[]{:S(2)}) collective-permute-start(f32[96,128]{1,0:T(8,128)} %get-tuple-element.32), channel_id=1, source_target_pairs={{0,64},{64,128},{128,192},{192,0},{1,65},{65,129},{129,193},{193,1... | collective-permute-start | bytes 147464 | tf_op jit(solution)/shard_map/ppermute | solution.py:601
  50.9 7.8 %copy-start.4 = (f32[96,128]{1,0:T(8,128)S(1)}, f32[96,128]{1,0:T(8,128)}, u32[]{:S(2)}) copy-start(f32[96,128]{1,0:T(8,128)} %get-tuple-element.32) | copy-start | bytes 147460
  59.5 8.8 %collective-permute-start.10 = (f32[96,128]{1,0:T(8,128)S(1)}, f32[96,128]{1,0:T(8,128)S(1)}, u32[]{:S(2)}, u32[]{:S(2)}) collective-permute-start(f32[96,128]{1,0:T(8,128)S(1)} %add_add_fusion.1), channel_id=1, source_target_pairs={{0,48},{16,0},{32,16},{48,32},{1,49},{17,1},{33,17},{49,33},{2,50}... | collective-permute-start | bytes 147464 | tf_op jit(solution)/shard_map/ppermute | solution.py:601
  60.3 8.0 %collective-permute-start.9 = (f32[96,128]{1,0:T(8,128)S(1)}, f32[96,128]{1,0:T(8,128)S(1)}, u32[]{:S(2)}, u32[]{:S(2)}) collective-permute-start(f32[96,128]{1,0:T(8,128)S(1)} %add_add_fusion.1), channel_id=1, source_target_pairs={{0,32},{16,48},{32,0},{48,16},{1,33},{17,49},{33,1},{49,17},{2,34}... | collective-permute-start | bytes 147464 | tf_op jit(solution)/shard_map/ppermute | solution.py:601
  62.7 5.6 %collective-permute-start.8 = (f32[96,128]{1,0:T(8,128)S(1)}, f32[96,128]{1,0:T(8,128)S(1)}, u32[]{:S(2)}, u32[]{:S(2)}) collective-permute-start(f32[96,128]{1,0:T(8,128)S(1)} %add_add_fusion.1), channel_id=1, source_target_pairs={{0,16},{16,32},{32,48},{48,0},{1,17},{17,33},{33,49},{49,1},{2,18}... | collective-permute-start | bytes 147464 | tf_op jit(solution)/shard_map/ppermute | solution.py:601
  68.3 50.6 %all-to-all-start.1 = ((bf16[16,32,3456]{2,1,0:T(8,128)(2,1)}), bf16[16,32,3456]{2,1,0:T(8,128)(2,1)}, u32[]{:S(2)}, u32[]{:S(2)}) async-start(bf16[16,32,3456]{2,1,0:T(8,128)(2,1)} %magnitude.1), calls=%async_computation.1 | async-start | bytes 7077888 | tf_op jit(solution)/shard_map/all_to_all | solution.py:597
  84.5 2.4 %collective-permute-start.11 = (bf16[272,1024]{1,0:T(8,128)(2,1)}, bf16[272,1024]{1,0:T(8,128)(2,1)}, u32[]{:S(2)}, u32[]{:S(2)}) collective-permute-start(bf16[272,1024]{1,0:T(8,128)(2,1)} %get-tuple-element.44), channel_id=1, source_target_pairs={{0,1},{1,0},{2,3},{3,2},{4,5},{5,4},{6,7},{7,6},{8,9},{9,8},{10,11... | collective-permute-start | bytes 1671176 | tf_op jit(solution)/shard_map/ppermute | solution.py:638
  89.1 9.7 %collective-permute-start.12 = (bf16[144,1024]{1,0:T(8,128)(2,1)}, bf16[144,1024]{1,0:T(8,128)(2,1)}, u32[]{:S(2)}, u32[]{:S(2)}) collective-permute-start(bf16[144,1024]{1,0:T(8,128)(2,1)} %get-tuple-element.46), channel_id=1, source_target_pairs={{0,2},{2,0},{4,6},{6,4},{8,10},{10,8},{12,14},{14,12},{1,3},{3,1},... | collective-permute-start | bytes 884744 | tf_op jit(solution)/shard_map/ppermute | solution.py:640
  100.7 11.2 %collective-permute-start.13 = (bf16[48,1024]{1,0:T(8,128)(2,1)}, bf16[48,1024]{1,0:T(8,128)(2,1)S(1)}, u32[]{:S(2)}, u32[]{:S(2)}) collective-permute-start(bf16[48,1024]{1,0:T(8,128)(2,1)} %get-tuple-element.48), channel_id=1, source_target_pairs={{0,4},{2,6},{4,8},{6,10},{8,12},{10,14},{12,0},{14,2},{1,5},{3,7},... | collective-permute-start | bytes 294920 | tf_op jit(solution)/shard_map/ppermute | solution.py:601
  104.0 11.8 %collective-permute-start.14 = (bf16[48,1024]{1,0:T(8,128)(2,1)}, bf16[48,1024]{1,0:T(8,128)(2,1)S(1)}, u32[]{:S(2)}, u32[]{:S(2)}) collective-permute-start(bf16[48,1024]{1,0:T(8,128)(2,1)} %get-tuple-element.49), channel_id=1, source_target_pairs={{0,8},{2,10},{4,12},{6,14},{8,0},{10,2},{12,4},{14,6},{1,9},{3,11}... | collective-permute-start | bytes 294920 | tf_op jit(solution)/shard_map/ppermute | solution.py:601
  109.2 9.2 %collective-permute-start.15 = (bf16[48,1024]{1,0:T(8,128)(2,1)}, bf16[48,1024]{1,0:T(8,128)(2,1)}, u32[]{:S(2)}, u32[]{:S(2)}) collective-permute-start(bf16[48,1024]{1,0:T(8,128)(2,1)} %get-tuple-element.50), channel_id=1, source_target_pairs={{0,12},{2,14},{4,0},{6,2},{8,4},{10,6},{12,8},{14,10},{1,13},{3,15... | collective-permute-start | bytes 294920 | tf_op jit(solution)/shard_map/ppermute | solution.py:601
  111.9 6.9 %copy-start.1 = (bf16[48,1024]{1,0:T(8,128)(2,1)}, bf16[48,1024]{1,0:T(8,128)(2,1)S(1)}, u32[]{:S(2)}) copy-start(bf16[48,1024]{1,0:T(8,128)(2,1)S(1)} %collective-permute-done.13.refs_1_) | copy-start | bytes 294916
  115.9 3.0 %copy-start.2 = (bf16[48,1024]{1,0:T(8,128)(2,1)}, bf16[48,1024]{1,0:T(8,128)(2,1)S(1)}, u32[]{:S(2)}) copy-start(bf16[48,1024]{1,0:T(8,128)(2,1)S(1)} %collective-permute-done.14.refs_2_) | copy-start | bytes 294916

commit v9 on v7

--- a/solution.py
+++ b/solution.py
@@ -16,7 +16,7 @@
 RANK = 16
 LANES = 128
 MIB = 1024 * 1024
-LIMIT = 62 * MIB
+LIMIT = 63 * MIB + 768 * 1024
 ANY = pl.BlockSpec(memory_space=pl.ANY)
 SMEM = pl.BlockSpec(memory_space=pltpu.SMEM)
 
@@ -186,7 +186,9 @@
         begin(sums_hbm, small.at[64:], first_sem.at[1]),
     ]
     for k in range(8):
-        back = lax.rem(z + 8 - k, 8)
+        back = lax.rem(z + 8 - (k - k % 2), 8)
+        if k % 2:
+            back = back + 1 - 2 * lax.rem(back, 2)
         rows = slice(32 * k, 32 * k + 32)
         copies.append(begin(own_hbm.at[rows], tokens.at[back, core], sem.at[0, k]))
         copies.append(begin(other_hbm.at[rows], tokens.at[back, 1 - core], sem.at[1, k]))
@@ -425,7 +427,7 @@
     )(z, own, got)
 
 
-def quad_kernel(z_ref, keep_hbm, got_hbm, *refs):
+def quad_kernel(z_ref, after_hbm, keep_hbm, got_hbm, *refs):
     out_hbm = refs[:4]
     keep, got, send, sem, out_sem = refs[4:]
     half = z_ref[0] // 2
@@ -445,20 +447,20 @@
         copy.wait()
 
 
-def quad(z, keep, got):
+def quad(z, after, keep, got):
     rows, depth = keep.shape
     return call(
         quad_kernel,
         4 * rows * depth,
         6 * rows * depth,
-        in_specs=[SMEM, ANY, ANY],
+        in_specs=[SMEM, ANY, ANY, ANY],
         out_specs=[ANY] * 4,
         out_shape=[jax.ShapeDtypeStruct((48, depth), bf16)] * 4,
         scratch_shapes=[pltpu.VMEM((rows, depth), bf16)] * 2
         + [pltpu.VMEM((4, 48, depth), bf16)]
         + [pltpu.SemaphoreType.DMA((2,)), pltpu.SemaphoreType.DMA((4,))],
         name="quad",
-    )(z, keep, got)
+    )(z, after, keep, got)
 
 
 def finish_kernel(z_ref, tokens_hbm, *refs):
@@ -556,7 +558,7 @@
 
 
 def output_kernel(
-    scale_hbm, parts_hbm, out_hbm, mag_hbm, scale, parts, out, mag, first_sem, sem, out_sem
+    after_hbm, scale_hbm, parts_hbm, out_hbm, mag_hbm, scale, parts, out, mag, first_sem, sem, out_sem
 ):
     width = out.shape[1]
     chunks = chunks_of(width)
@@ -565,7 +567,7 @@
         begin(scale_hbm, scale, first_sem.at[0]),
         begin(parts_hbm.at[:, :, width:], parts.at[:, :, width:], first_sem.at[1]),
     )
-    ready = stream([(parts_hbm, parts.at[:, :, :width])], sem, chunks, 4)
+    ready = stream([(parts_hbm, parts.at[:, :, :width])], sem, chunks, len(chunks))
     for copy in first:
         copy.wait()
 
@@ -587,14 +589,14 @@
         copy.wait()
 
 
-def output_of(scale, parts):
+def output_of(after, scale, parts):
     width = parts.shape[2] - LANES
     count = len(chunks_of(width))
     return call(
         output_kernel,
         16 * 32 * width,
         4 * MIB,
-        in_specs=[ANY] * 2,
+        in_specs=[ANY] * 3,
         out_specs=[ANY] * 2,
         out_shape=[
             jax.ShapeDtypeStruct((32, width), bf16),
@@ -610,7 +612,7 @@
             pltpu.SemaphoreType.DMA((count,)),
         ],
         name="output",
-    )(scale, parts)
+    )(after, scale, parts)
 
 
 def exchange(blocks):
@@ -635,16 +637,12 @@
     swap = [(0, 1), (1, 0)]
     down_t = down_adapter.T
     magnitude = magnitude.reshape(-1, LANES)
-    message = spread(out_cotangent)
-    given = exchange(message)
-    blocks = [tokens] * 8
-    for k in (4, 3, 5, 2):
-        blocks[k] = further(tokens, "z", k, 8)
-    merged_low, sums = merge(message, down_t, up_adapter, weight)
-    later, sums, merged_low = lax.optimization_barrier((tokens, sums, merged_low))
-    for k in (6, 1, 7):
-        blocks[k] = further(later, "z", k, 8)
-    own = jnp.concatenate(blocks, axis=0)
+    given = exchange(spread(out_cotangent))
+    beside = [(i, i ^ 1) for i in range(8)]
+    two = jnp.concatenate([tokens, lax.ppermute(tokens, "z", beside)], axis=0)
+    own = [two] + [further(two, "z", 2 * k, 8) for k in (1, 2, 3)]
+    merged_low, sums = merge(two, down_t, up_adapter, weight)
+    own = jnp.concatenate(own, axis=0)
     other = lax.ppermute(own, "c", swap)
     place = jnp.concatenate([z, core])
     small, tokens_full = project(place, own, other, down_t, sums)
@@ -656,19 +654,18 @@
     part = add_magnitude(given, part)
     arrived = shifted(small, "y")
     arrived, part = lax.optimization_barrier((arrived, part))
+    parts = exchange(part)
     small = added(small, arrived)
-    small, part = lax.optimization_barrier((small, part))
-    parts = exchange(part)
     own, send, scale = backward(core, small, magnitude, up_adapter, given, merged_low)
     got = lax.ppermute(send, "c", swap)
     keep, send = pair(z, own, got)
-    got = lax.ppermute(send, "z", [(i, i ^ 1) for i in range(8)])
-    blocks = list(quad(z, keep, got))
+    got = lax.ppermute(send, "z", beside)
+    up_gradient = up_gradient_of(small, scale, given)
+    blocks = list(quad(z, up_gradient, keep, got))
     for k in range(1, 4):
         blocks[k] = further(blocks[k], "z", 2 * k, 8)
-    up_gradient = up_gradient_of(small, scale, given)
     grad_tokens, down_gradient = finish(z, tokens_full, blocks)
-    output, grad_magnitude = output_of(scale, parts)
+    output, grad_magnitude = output_of(grad_tokens, scale, parts)
     return (output, grad_tokens, grad_magnitude.reshape(-1), up_gradient, down_gradient.T)
 
 

time: 127 us -> 125 us (0.984)
    ppermute x16 -> x12, starting transfers between devices: 36.9 us -> 31.9 us  [further(): return lax.ppermute(value, axis, [(i, (i + k) % size) for i in range(size)])]
    ppermute x16 -> x12, waiting for transfers between devices: 10.5 us -> 13.4 us  [further(): return lax.ppermute(value, axis, [(i, (i + k) % size) for i in range(size)])]
    ppermute x1 -> x2, waiting for transfers between devices: 7.52 us -> 5.16 us  [the longest x1 3.43 us: on_device(): got = lax.ppermute(send, 'z', beside)]
    ppermute x1 -> x2, starting transfers between devices: 2.01 us -> 4.11 us  [the longest x1 2.1 us: on_device(): got = lax.ppermute(send, 'z', beside)]
    all_to_all x2, starting transfers between devices: 13.5 us -> 15.3 us  [exchange(): return lax.all_to_all(blocks, ROW, 0, 0, tiled=False)]
    ppermute x1, waiting for transfers between devices: 1.3 us -> 0.01 us  [on_device(): other = lax.ppermute(own, 'c', swap)]
    concatenate x1 -> x2, local copies, waits for them, and re-layouts: 0.01 us -> 1.28 us  [the longest x1 0.66 us: on_device(): own = jnp.concatenate(own, axis=0)]
    unnamed x25 -> x13, local copies, waits for them, and re-layouts: 3.02 us -> 1.94 us
  transfers between devices with their start and end apart: 21 -> 18, of which waited for: 6 -> 8; matrix products, arithmetic and copies ran while one was open for 1% -> 4% of each run, Pallas kernels for 32% -> 32%
where the time goes in v9:
time: 125 us; the launch traced here: 124 us
  starting transfers between devices  51.4 us (41%)
  Pallas kernels  45.3 us (36%)
  waiting for transfers between devices  20.9 us (17%)
  local copies, waits for them, and re-layouts  3.22 us (3%)
  other arithmetic  2.03 us (2%)
    ppermute x12, starting transfers between devices, further(): return lax.ppermute(value, axis, [(i, (i + k) % size) for i in range(size)])  31.9 us
    all_to_all x2, starting transfers between devices, exchange(): return lax.all_to_all(blocks, ROW, 0, 0, tiled=False)  15.3 us
    ppermute x12, waiting for transfers between devices, further(): return lax.ppermute(value, axis, [(i, (i + k) % size) for i in range(size)])  13.4 us
    pallas_call x1, Pallas kernels, backward(): call(backward_kernel, 2 * 512 * depth * width, 12 * MIB, in_specs=[SMEM]...  7.83 us
    pallas_call x1, Pallas kernels, forward(): call(forward_kernel, 2 * 512 * depth * width, 12 * MIB, in_specs=[ANY] *...  7.72 us
    pallas_call x1, Pallas kernels, merge(): call(merge_kernel, 12 * depth * width, 4 * depth * width, in_specs=[ANY]...  6.51 us
    pallas_call x1, Pallas kernels, up_gradient_of(): call(up_kernel, 2 * 512 * 256 * width, 4 * MIB, in_specs=[ANY] * 3, out_s...  4.19 us
    pallas_call x1, Pallas kernels, add_magnitude(): call(magnitude_kernel, 4 * 512 * width, 7 * MIB, in_specs=[ANY, ANY], out...  3.81 us
  transfers between devices with their start and end apart: 18, of which 8 were waited for; matrix products, arithmetic and copies ran while one was open for 4% of the time, Pallas kernels for 32%

profile of v9, /device:TPU:8, one launch (start us, length us, event | category | flops | bytes accessed | tf_op | source)
XLA Modules:
  0.0 123.8 jit_solution(3259460826240041860)
XLA Ops:
  0.6 2.9 %spread.1 = bf16[16,32,3328]{2,1,0:T(8,128)(2,1)} custom-call(bf16[32,3328]{1,0:T(8,128)(2,1)} %cot_hbm.1), custom_call_target="tpu_custom_call" | custom-call | flops 106496 | bytes 4194304 | tf_op jit(solution)/shard_map/spread/pallas_call | solution.py:163
  3.5 0.0 copy-start.3
  3.5 7.5 %all-to-all-start = ((bf16[16,32,3328]{2,1,0:T(8,128)(2,1)}), bf16[16,32,3328]{2,1,0:T(8,128)(2,1)}, u32[]{:S(2)}, u32[]{:S(2)}) async-start(bf16[16,32,3328]{2,1,0:T(8,128)(2,1)} %spread.1), calls=%async_computation | async-start | bytes 6815744 | tf_op jit(solution)/shard_map/all_to_all | solution.py:619
  11.1 2.0 %collective-permute-start = (bf16[32,1024]{1,0:T(8,128)(2,1)S(1)}, bf16[32,1024]{1,0:T(8,128)(2,1)S(1)}, u32[]{:S(2)}, u32[]{:S(2)}) collective-permute-start(bf16[32,1024]{1,0:T(8,128)(2,1)S(1)} %copy-done.3), channel_id=1, source_target_pairs={{0,2},{2,0},{4,6},{6,4},{8,10},{10,8},{12,14},{14,12},{1,3},{3,1},... | collective-permute-start | bytes 196616 | tf_op jit(solution)/shard_map/ppermute | solution.py:642
  13.1 0.6 constant_dynamic-update-slice_fusion.1
  13.7 1.7 %collective-permute-done = bf16[32,1024]{1,0:T(8,128)(2,1)S(1)} collective-permute-done((bf16[32,1024]{1,0:T(8,128)(2,1)S(1)}, bf16[32,1024]{1,0:T(8,128)(2,1)S(1)}, u32[]{:S(2)}, u32[]{:S(2)}) %collective-permute-start) | collective-permute-done | bytes 65568 | tf_op jit(solution)/shard_map/ppermute | solution.py:642
  15.4 0.6 constant_dynamic-update-slice_fusion
  16.1 3.3 %collective-permute-start.1 = (bf16[64,1024]{1,0:T(8,128)(2,1)S(1)}, bf16[64,1024]{1,0:T(8,128)(2,1)S(1)}, u32[]{:S(2)}, u32[]{:S(2)}) collective-permute-start(bf16[64,1024]{1,0:T(8,128)(2,1)S(1)} %get-tuple-element.55.after_hbm), channel_id=1, source_target_pairs={{0,4},{2,6},{4,8},{6,10},{8,12},{10,14},{12,0},{14,2},{1,5},{3,7},... | collective-permute-start | bytes 393224 | tf_op jit(solution)/shard_map/ppermute | solution.py:623
  19.3 5.4 %collective-permute-start.2 = (bf16[64,1024]{1,0:T(8,128)(2,1)S(1)}, bf16[64,1024]{1,0:T(8,128)(2,1)S(1)}, u32[]{:S(2)}, u32[]{:S(2)}) collective-permute-start(bf16[64,1024]{1,0:T(8,128)(2,1)S(1)} %get-tuple-element.55.after_hbm), channel_id=1, source_target_pairs={{0,8},{2,10},{4,12},{6,14},{8,0},{10,2},{12,4},{14,6},{1,9},{3,11}... | collective-permute-start | bytes 393224 | tf_op jit(solution)/shard_map/ppermute | solution.py:623
  24.7 2.7 %collective-permute-start.3 = (bf16[64,1024]{1,0:T(8,128)(2,1)S(1)}, bf16[64,1024]{1,0:T(8,128)(2,1)S(1)}, u32[]{:S(2)}, u32[]{:S(2)}) collective-permute-start(bf16[64,1024]{1,0:T(8,128)(2,1)S(1)} %get-tuple-element.55.after_hbm), channel_id=1, source_target_pairs={{0,12},{2,14},{4,0},{6,2},{8,4},{10,6},{12,8},{14,10},{1,13},{3,15... | collective-permute-start | bytes 393224 | tf_op jit(solution)/shard_map/ppermute | solution.py:623
  27.4 0.0 collective-permute-done.1
  27.4 0.7 constant_dynamic-update-slice_fusion.4
  28.0 5.0 %collective-permute-done.2 = bf16[64,1024]{1,0:T(8,128)(2,1)S(1)} collective-permute-done((bf16[64,1024]{1,0:T(8,128)(2,1)S(1)}, bf16[64,1024]{1,0:T(8,128)(2,1)S(1)}, u32[]{:S(2)}, u32[]{:S(2)}) %collective-permute-start.2) | collective-permute-done | bytes 131104 | tf_op jit(solution)/shard_map/ppermute | solution.py:623
  33.1 0.7 constant_dynamic-update-slice_fusion.3
  33.7 1.8 %collective-permute-done.3 = bf16[64,1024]{1,0:T(8,128)(2,1)S(1)} collective-permute-done((bf16[64,1024]{1,0:T(8,128)(2,1)S(1)}, bf16[64,1024]{1,0:T(8,128)(2,1)S(1)}, u32[]{:S(2)}, u32[]{:S(2)}) %collective-permute-start.3) | collective-permute-done | bytes 131104 | tf_op jit(solution)/shard_map/ppermute | solution.py:623
  35.5 0.7 constant_dynamic-update-slice_fusion.2.own_hbm
  36.2 0.6 pad_add_fusion.place_ref
  36.8 6.5 %merge.1 = (bf16[1024,3328]{1,0:T(8,128)(2,1)}, f32[32,128]{1,0:T(8,128)}) custom-call(bf16[64,1024]{1,0:T(8,128)(2,1)} %copy-done, f32[16,1024]{1,0:T(8,128)} %bitcast.9, f32[16,3328]{1,0:T(8,128)} %up_hbm.3, bf16[1024,3328]{1,0:T(8,128)(2,1)} %weight_hbm.1), custom_call_target="tpu_custom_call" | custom-call | flops 40894464 | bytes 13631488 | tf_op jit(solution)/shard_map/merge/pallas_call | solution.py:129
  43.3 3.1 %project.1 = (f32[96,128]{1,0:T(8,128)}, bf16[8,2,32,1024]{3,2,1,0:T(8,128)(2,1)}) custom-call(s32[2]{0:T(128)} %pad_add_fusion.place_ref, bf16[256,1024]{1,0:T(8,128)(2,1)} %constant_dynamic-update-slice_fusion.2.own_hbm, bf16[256,1024]{1,0:T(8,128)(2,1)} %collective-permute-done.4.other_hbm, f32[16,1024]{1,0:T(8,128)} %bitcast.10, ...), custom_call_target="tpu_custom_call" | custom-call | flops 268435456 | bytes 3145728 | tf_op jit(solution)/shard_map/project/pallas_call | solution.py:208
  46.4 2.7 %collective-permute-start.7 = (f32[96,128]{1,0:T(8,128)}, f32[96,128]{1,0:T(8,128)S(1)}, u32[]{:S(2)}, u32[]{:S(2)}) collective-permute-start(f32[96,128]{1,0:T(8,128)} %get-tuple-element.32), channel_id=1, source_target_pairs={{0,192},{64,0},{128,64},{192,128},{1,193},{65,1},{129,65},{193,129... | collective-permute-start | bytes 147464 | tf_op jit(solution)/shard_map/ppermute | solution.py:623
  49.2 0.9 collective-permute-start.6
  50.0 0.9 collective-permute-start.5
  50.9 7.7 %forward.1.part_hbm = bf16[16,32,3456]{2,1,0:T(8,128)(2,1)} custom-call(bf16[512,1024]{1,0:T(8,128)(2,1)} %bitcast.7, bf16[1024,3328]{1,0:T(8,128)(2,1)} %get-tuple-element.33.merged_hbm), custom_call_target="tpu_custom_call" | custom-call | flops 3489660928 | bytes 12582912 | tf_op jit(solution)/shard_map/forward/pallas_call | solution.py:249
  58.6 0.0 collective-permute-done.7
  58.6 0.1 collective-permute-done.5
  58.7 0.8 add_add_fusion.1
  59.5 0.8 collective-permute-start.10
  60.3 2.4 %collective-permute-start.9 = (f32[96,128]{1,0:T(8,128)S(1)}, f32[96,128]{1,0:T(8,128)S(1)}, u32[]{:S(2)}, u32[]{:S(2)}) collective-permute-start(f32[96,128]{1,0:T(8,128)S(1)} %add_add_fusion.1), channel_id=1, source_target_pairs={{0,32},{16,48},{32,0},{48,16},{1,33},{17,49},{33,1},{49,17},{2,34}... | collective-permute-start | bytes 147464 | tf_op jit(solution)/shard_map/ppermute | solution.py:623
  62.7 1.8 %collective-permute-start.8 = (f32[96,128]{1,0:T(8,128)S(1)}, f32[96,128]{1,0:T(8,128)S(1)}, u32[]{:S(2)}, u32[]{:S(2)}) collective-permute-start(f32[96,128]{1,0:T(8,128)S(1)} %add_add_fusion.1), channel_id=1, source_target_pairs={{0,16},{16,32},{32,48},{48,0},{1,17},{17,33},{33,49},{49,1},{2,18}... | collective-permute-start | bytes 147464 | tf_op jit(solution)/shard_map/ppermute | solution.py:623
  64.4 3.8 %magnitude.1 = bf16[16,32,3456]{2,1,0:T(8,128)(2,1)} custom-call(bf16[16,32,3328]{2,1,0:T(8,128)(2,1)} %all-to-all-done.given_hbm, bf16[16,32,3456]{2,1,0:T(8,128)(2,1)} %forward.1.part_hbm), custom_call_target="tpu_custom_call", output_to_operand_aliasing={{}: (1, {})} | custom-call | flops 6815744 | bytes 7340032 | tf_op jit(solution)/shard_map/magnitude/pallas_call | solution.py:287
  68.3 0.0 collective-permute-done.9
  68.3 7.8 %all-to-all-start.1 = ((bf16[16,32,3456]{2,1,0:T(8,128)(2,1)}), bf16[16,32,3456]{2,1,0:T(8,128)(2,1)}, u32[]{:S(2)}, u32[]{:S(2)}) async-start(bf16[16,32,3456]{2,1,0:T(8,128)(2,1)} %magnitude.1), calls=%async_computation.1 | async-start | bytes 7077888 | tf_op jit(solution)/shard_map/all_to_all | solution.py:619
  76.1 0.6 add_add_fusion.small_hbm
  76.7 7.8 %backward.1 = (bf16[272,1024]{1,0:T(8,128)(2,1)}, bf16[272,1024]{1,0:T(8,128)(2,1)}, f32[64,128]{1,0:T(8,128)}) custom-call(s32[1]{0:T(128)} %bitcast.1.core_ref, f32[96,128]{1,0:T(8,128)} %add_add_fusion.small_hbm, f32[26,128]{1,0:T(8,128)} %bitcast.12, f32[16,3328]{1,0:T(8,128)} %up_hbm.3, bf16[16,32,3328]{2,1,0:T(8,128)(2,1)} %all-to-all-done.given_hbm, ...), custom_call_target="tpu_custom_call" | custom-call | flops 3489660928 | bytes 12582912 | tf_op jit(solution)/shard_map/backward/pallas_call | solution.py:370
  84.5 0.1 collective-permute-start.11
  84.6 2.3 %collective-permute-done.11.got_hbm = bf16[272,1024]{1,0:T(8,128)(2,1)} collective-permute-done((bf16[272,1024]{1,0:T(8,128)(2,1)}, bf16[272,1024]{1,0:T(8,128)(2,1)}, u32[]{:S(2)}, u32[]{:S(2)}) %collective-permute-start.11) | collective-permute-done | bytes 557088 | tf_op jit(solution)/shard_map/ppermute | solution.py:660
  86.9 2.1 %pair.1 = (bf16[144,1024]{1,0:T(8,128)(2,1)}, bf16[144,1024]{1,0:T(8,128)(2,1)}) custom-call(s32[1]{0:T(128)} %bitcast.z_ref, bf16[272,1024]{1,0:T(8,128)(2,1)} %get-tuple-element.42.own_hbm, bf16[272,1024]{1,0:T(8,128)(2,1)} %collective-permute-done.11.got_hbm), custom_call_target="tpu_custom_call" | custom-call | flops 1114112 | bytes 1671168 | tf_op jit(solution)/shard_map/pair/pallas_call | solution.py:416
  89.1 2.1 %collective-permute-start.12 = (bf16[144,1024]{1,0:T(8,128)(2,1)}, bf16[144,1024]{1,0:T(8,128)(2,1)}, u32[]{:S(2)}, u32[]{:S(2)}) collective-permute-start(bf16[144,1024]{1,0:T(8,128)(2,1)} %get-tuple-element.45), channel_id=1, source_target_pairs={{0,2},{2,0},{4,6},{6,4},{8,10},{10,8},{12,14},{14,12},{1,3},{3,1},... | collective-permute-start | bytes 884744 | tf_op jit(solution)/shard_map/ppermute | solution.py:662
  91.2 4.2 %up_gradient.1.after_hbm = f32[16,3328]{1,0:T(8,128)} custom-call(f32[96,128]{1,0:T(8,128)} %add_add_fusion.small_hbm, f32[64,128]{1,0:T(8,128)} %get-tuple-element.41.scale_hbm, bf16[16,32,3328]{2,1,0:T(8,128)(2,1)} %all-to-all-done.given_hbm), custom_call_target="tpu_custom_call" | custom-call | flops 872415232 | bytes 4194304 | tf_op jit(solution)/shard_map/up_gradient/pallas_call | solution.py:540
  95.4 3.4 %collective-permute-done.12.got_hbm = bf16[144,1024]{1,0:T(8,128)(2,1)} collective-permute-done((bf16[144,1024]{1,0:T(8,128)(2,1)}, bf16[144,1024]{1,0:T(8,128)(2,1)}, u32[]{:S(2)}, u32[]{:S(2)}) %collective-permute-start.12) | collective-permute-done | bytes 294944 | tf_op jit(solution)/shard_map/ppermute | solution.py:662
  98.8 1.9 %quad.1 = (bf16[48,1024]{1,0:T(8,128)(2,1)}, bf16[48,1024]{1,0:T(8,128)(2,1)}, bf16[48,1024]{1,0:T(8,128)(2,1)}, bf16[48,1024]{1,0:T(8,128)(2,1)}) custom-call(s32[1]{0:T(128)} %bitcast.z_ref, f32[16,3328]{1,0:T(8,128)} %up_gradient.1.after_hbm, bf16[144,1024]{1,0:T(8,128)(2,1)} %get-tuple-element.44.keep_hbm, bf16[144,1024]{1,0:T(8,128)(2,1)} %collective-permute-done.12.got_hbm), custom_call_target="tpu_custom_call" | custom-call | flops 589824 | bytes 884736 | tf_op jit(solution)/shard_map/quad/pallas_call | solution.py:452
  100.7 3.3 %collective-permute-start.13 = (bf16[48,1024]{1,0:T(8,128)(2,1)}, bf16[48,1024]{1,0:T(8,128)(2,1)S(1)}, u32[]{:S(2)}, u32[]{:S(2)}) collective-permute-start(bf16[48,1024]{1,0:T(8,128)(2,1)} %get-tuple-element.47), channel_id=1, source_target_pairs={{0,4},{2,6},{4,8},{6,10},{8,12},{10,14},{12,0},{14,2},{1,5},{3,7},... | collective-permute-start | bytes 294920 | tf_op jit(solution)/shard_map/ppermute | solution.py:623
  104.0 5.2 %collective-permute-start.14 = (bf16[48,1024]{1,0:T(8,128)(2,1)}, bf16[48,1024]{1,0:T(8,128)(2,1)S(1)}, u32[]{:S(2)}, u32[]{:S(2)}) collective-permute-start(bf16[48,1024]{1,0:T(8,128)(2,1)} %get-tuple-element.48), channel_id=1, source_target_pairs={{0,8},{2,10},{4,12},{6,14},{8,0},{10,2},{12,4},{14,6},{1,9},{3,11}... | collective-permute-start | bytes 294920 | tf_op jit(solution)/shard_map/ppermute | solution.py:623
  109.2 2.7 %collective-permute-start.15 = (bf16[48,1024]{1,0:T(8,128)(2,1)}, bf16[48,1024]{1,0:T(8,128)(2,1)}, u32[]{:S(2)}, u32[]{:S(2)}) collective-permute-start(bf16[48,1024]{1,0:T(8,128)(2,1)} %get-tuple-element.49), channel_id=1, source_target_pairs={{0,12},{2,14},{4,0},{6,2},{8,4},{10,6},{12,8},{14,10},{1,13},{3,15... | collective-permute-start | bytes 294920 | tf_op jit(solution)/shard_map/ppermute | solution.py:623
  111.9 3.9 %collective-permute-done.14.refs_2_ = bf16[48,1024]{1,0:T(8,128)(2,1)S(1)} collective-permute-done((bf16[48,1024]{1,0:T(8,128)(2,1)}, bf16[48,1024]{1,0:T(8,128)(2,1)S(1)}, u32[]{:S(2)}, u32[]{:S(2)}) %collective-permute-start.14) | collective-permute-done | bytes 98336 | tf_op jit(solution)/shard_map/ppermute | solution.py:623
  115.8 2.6 %collective-permute-done.15.refs_3_ = bf16[48,1024]{1,0:T(8,128)(2,1)} collective-permute-done((bf16[48,1024]{1,0:T(8,128)(2,1)}, bf16[48,1024]{1,0:T(8,128)(2,1)}, u32[]{:S(2)}, u32[]{:S(2)}) %collective-permute-start.15) | collective-permute-done | bytes 98336 | tf_op jit(solution)/shard_map/ppermute | solution.py:623
  118.4 2.4 %finish.1 = (bf16[32,1024]{1,0:T(8,128)(2,1)}, f32[16,1024]{1,0:T(8,128)}) custom-call(s32[1]{0:T(128)} %bitcast.z_ref, bf16[512,1024]{1,0:T(8,128)(2,1)} %bitcast.8, bf16[48,1024]{1,0:T(8,128)(2,1)} %get-tuple-element.46.refs_0_, bf16[48,1024]{1,0:T(8,128)(2,1)} %copy-done.1, bf16[48,1024]{1,0:T(8,128)(2,1)} %copy-done.2, ...), custom_call_target="tpu_custom_call" | custom-call | flops 268435456 | bytes 2097152 | tf_op jit(solution)/shard_map/finish/pallas_call | solution.py:490
  120.8 2.8 %output.1 = (bf16[32,3328]{1,0:T(8,128)(2,1)}, f32[26,128]{1,0:T(8,128)}) custom-call(bf16[32,1024]{1,0:T(8,128)(2,1)} %get-tuple-element.26.after_hbm, f32[64,128]{1,0:T(8,128)} %get-tuple-element.41.scale_hbm, bf16[16,32,3456]{2,1,0:T(8,128)(2,1)} %all-to-all-done.1.parts_hbm), custom_call_target="tpu_custom_call" | custom-call | flops 1703936 | bytes 4194304 | tf_op jit(solution)/shard_map/output/pallas_call | solution.py:595
  (17 shorter events, 0.0 us)
Async XLA Ops:
  3.5 7.5 %copy-start.3 = (bf16[32,1024]{1,0:T(8,128)(2,1)S(1)}, bf16[32,1024]{1,0:T(8,128)(2,1)}, u32[]{:S(2)}) copy-start(bf16[32,1024]{1,0:T(8,128)(2,1)} %param.6) | copy-start | bytes 196612
  3.5 60.9 %all-to-all-start = ((bf16[16,32,3328]{2,1,0:T(8,128)(2,1)}), bf16[16,32,3328]{2,1,0:T(8,128)(2,1)}, u32[]{:S(2)}, u32[]{:S(2)}) async-start(bf16[16,32,3328]{2,1,0:T(8,128)(2,1)} %spread.1), calls=%async_computation | async-start | bytes 6815744 | tf_op jit(solution)/shard_map/all_to_all | solution.py:619
  11.1 4.4 %collective-permute-start = (bf16[32,1024]{1,0:T(8,128)(2,1)S(1)}, bf16[32,1024]{1,0:T(8,128)(2,1)S(1)}, u32[]{:S(2)}, u32[]{:S(2)}) collective-permute-start(bf16[32,1024]{1,0:T(8,128)(2,1)S(1)} %copy-done.3), channel_id=1, source_target_pairs={{0,2},{2,0},{4,6},{6,4},{8,10},{10,8},{12,14},{14,12},{1,3},{3,1},... | collective-permute-start | bytes 196616 | tf_op jit(solution)/shard_map/ppermute | solution.py:642
  16.1 20.7 %copy-start = (bf16[64,1024]{1,0:T(8,128)(2,1)}, bf16[64,1024]{1,0:T(8,128)(2,1)S(1)}, u32[]{:S(2)}) copy-start(bf16[64,1024]{1,0:T(8,128)(2,1)S(1)} %get-tuple-element.55.after_hbm) | copy-start | bytes 393220
  16.1 11.3 %collective-permute-start.1 = (bf16[64,1024]{1,0:T(8,128)(2,1)S(1)}, bf16[64,1024]{1,0:T(8,128)(2,1)S(1)}, u32[]{:S(2)}, u32[]{:S(2)}) collective-permute-start(bf16[64,1024]{1,0:T(8,128)(2,1)S(1)} %get-tuple-element.55.after_hbm), channel_id=1, source_target_pairs={{0,4},{2,6},{4,8},{6,10},{8,12},{10,14},{12,0},{14,2},{1,5},{3,7},... | collective-permute-start | bytes 393224 | tf_op jit(solution)/shard_map/ppermute | solution.py:623
  19.3 13.7 %collective-permute-start.2 = (bf16[64,1024]{1,0:T(8,128)(2,1)S(1)}, bf16[64,1024]{1,0:T(8,128)(2,1)S(1)}, u32[]{:S(2)}, u32[]{:S(2)}) collective-permute-start(bf16[64,1024]{1,0:T(8,128)(2,1)S(1)} %get-tuple-element.55.after_hbm), channel_id=1, source_target_pairs={{0,8},{2,10},{4,12},{6,14},{8,0},{10,2},{12,4},{14,6},{1,9},{3,11}... | collective-permute-start | bytes 393224 | tf_op jit(solution)/shard_map/ppermute | solution.py:623
  24.7 10.8 %collective-permute-start.3 = (bf16[64,1024]{1,0:T(8,128)(2,1)S(1)}, bf16[64,1024]{1,0:T(8,128)(2,1)S(1)}, u32[]{:S(2)}, u32[]{:S(2)}) collective-permute-start(bf16[64,1024]{1,0:T(8,128)(2,1)S(1)} %get-tuple-element.55.after_hbm), channel_id=1, source_target_pairs={{0,12},{2,14},{4,0},{6,2},{8,4},{10,6},{12,8},{14,10},{1,13},{3,15... | collective-permute-start | bytes 393224 | tf_op jit(solution)/shard_map/ppermute | solution.py:623
  36.2 7.1 %collective-permute-start.4 = (bf16[256,1024]{1,0:T(8,128)(2,1)}, bf16[256,1024]{1,0:T(8,128)(2,1)}, u32[]{:S(2)}, u32[]{:S(2)}) collective-permute-start(bf16[256,1024]{1,0:T(8,128)(2,1)} %constant_dynamic-update-slice_fusion.2.own_hbm), channel_id=1, source_target_pairs={{0,1},{1,0},{2,3},{3,2},{4,5},{5,4},{6,7},{7,6},{8,9},{9,8},{10,11... | collective-permute-start | bytes 1572872 | tf_op jit(solution)/shard_map/ppermute | solution.py:646
  46.4 12.2 %collective-permute-start.7 = (f32[96,128]{1,0:T(8,128)}, f32[96,128]{1,0:T(8,128)S(1)}, u32[]{:S(2)}, u32[]{:S(2)}) collective-permute-start(f32[96,128]{1,0:T(8,128)} %get-tuple-element.32), channel_id=1, source_target_pairs={{0,192},{64,0},{128,64},{192,128},{1,193},{65,1},{129,65},{193,129... | collective-permute-start | bytes 147464 | tf_op jit(solution)/shard_map/ppermute | solution.py:623
  49.2 9.5 %collective-permute-start.6 = (f32[96,128]{1,0:T(8,128)}, f32[96,128]{1,0:T(8,128)S(1)}, u32[]{:S(2)}, u32[]{:S(2)}) collective-permute-start(f32[96,128]{1,0:T(8,128)} %get-tuple-element.32), channel_id=1, source_target_pairs={{0,128},{64,192},{128,0},{192,64},{1,129},{65,193},{129,1},{193,65... | collective-permute-start | bytes 147464 | tf_op jit(solution)/shard_map/ppermute | solution.py:623
  50.0 8.7 %collective-permute-start.5 = (f32[96,128]{1,0:T(8,128)}, f32[96,128]{1,0:T(8,128)}, u32[]{:S(2)}, u32[]{:S(2)}) collective-permute-start(f32[96,128]{1,0:T(8,128)} %get-tuple-element.32), channel_id=1, source_target_pairs={{0,64},{64,128},{128,192},{192,0},{1,65},{65,129},{129,193},{193,1... | collective-permute-start | bytes 147464 | tf_op jit(solution)/shard_map/ppermute | solution.py:623
  50.9 7.8 %copy-start.4 = (f32[96,128]{1,0:T(8,128)S(1)}, f32[96,128]{1,0:T(8,128)}, u32[]{:S(2)}) copy-start(f32[96,128]{1,0:T(8,128)} %get-tuple-element.32) | copy-start | bytes 147460
  59.5 8.7 %collective-permute-start.10 = (f32[96,128]{1,0:T(8,128)S(1)}, f32[96,128]{1,0:T(8,128)S(1)}, u32[]{:S(2)}, u32[]{:S(2)}) collective-permute-start(f32[96,128]{1,0:T(8,128)S(1)} %add_add_fusion.1), channel_id=1, source_target_pairs={{0,48},{16,0},{32,16},{48,32},{1,49},{17,1},{33,17},{49,33},{2,50}... | collective-permute-start | bytes 147464 | tf_op jit(solution)/shard_map/ppermute | solution.py:623
  60.3 8.0 %collective-permute-start.9 = (f32[96,128]{1,0:T(8,128)S(1)}, f32[96,128]{1,0:T(8,128)S(1)}, u32[]{:S(2)}, u32[]{:S(2)}) collective-permute-start(f32[96,128]{1,0:T(8,128)S(1)} %add_add_fusion.1), channel_id=1, source_target_pairs={{0,32},{16,48},{32,0},{48,16},{1,33},{17,49},{33,1},{49,17},{2,34}... | collective-permute-start | bytes 147464 | tf_op jit(solution)/shard_map/ppermute | solution.py:623
  62.7 5.6 %collective-permute-start.8 = (f32[96,128]{1,0:T(8,128)S(1)}, f32[96,128]{1,0:T(8,128)S(1)}, u32[]{:S(2)}, u32[]{:S(2)}) collective-permute-start(f32[96,128]{1,0:T(8,128)S(1)} %add_add_fusion.1), channel_id=1, source_target_pairs={{0,16},{16,32},{32,48},{48,0},{1,17},{17,33},{33,49},{49,1},{2,18}... | collective-permute-start | bytes 147464 | tf_op jit(solution)/shard_map/ppermute | solution.py:623
  68.3 52.6 %all-to-all-start.1 = ((bf16[16,32,3456]{2,1,0:T(8,128)(2,1)}), bf16[16,32,3456]{2,1,0:T(8,128)(2,1)}, u32[]{:S(2)}, u32[]{:S(2)}) async-start(bf16[16,32,3456]{2,1,0:T(8,128)(2,1)} %magnitude.1), calls=%async_computation.1 | async-start | bytes 7077888 | tf_op jit(solution)/shard_map/all_to_all | solution.py:619
  84.5 2.4 %collective-permute-start.11 = (bf16[272,1024]{1,0:T(8,128)(2,1)}, bf16[272,1024]{1,0:T(8,128)(2,1)}, u32[]{:S(2)}, u32[]{:S(2)}) collective-permute-start(bf16[272,1024]{1,0:T(8,128)(2,1)} %get-tuple-element.43), channel_id=1, source_target_pairs={{0,1},{1,0},{2,3},{3,2},{4,5},{5,4},{6,7},{7,6},{8,9},{9,8},{10,11... | collective-permute-start | bytes 1671176 | tf_op jit(solution)/shard_map/ppermute | solution.py:660
  89.1 9.7 %collective-permute-start.12 = (bf16[144,1024]{1,0:T(8,128)(2,1)}, bf16[144,1024]{1,0:T(8,128)(2,1)}, u32[]{:S(2)}, u32[]{:S(2)}) collective-permute-start(bf16[144,1024]{1,0:T(8,128)(2,1)} %get-tuple-element.45), channel_id=1, source_target_pairs={{0,2},{2,0},{4,6},{6,4},{8,10},{10,8},{12,14},{14,12},{1,3},{3,1},... | collective-permute-start | bytes 884744 | tf_op jit(solution)/shard_map/ppermute | solution.py:662
  100.7 11.2 %collective-permute-start.13 = (bf16[48,1024]{1,0:T(8,128)(2,1)}, bf16[48,1024]{1,0:T(8,128)(2,1)S(1)}, u32[]{:S(2)}, u32[]{:S(2)}) collective-permute-start(bf16[48,1024]{1,0:T(8,128)(2,1)} %get-tuple-element.47), channel_id=1, source_target_pairs={{0,4},{2,6},{4,8},{6,10},{8,12},{10,14},{12,0},{14,2},{1,5},{3,7},... | collective-permute-start | bytes 294920 | tf_op jit(solution)/shard_map/ppermute | solution.py:623
  104.0 11.8 %collective-permute-start.14 = (bf16[48,1024]{1,0:T(8,128)(2,1)}, bf16[48,1024]{1,0:T(8,128)(2,1)S(1)}, u32[]{:S(2)}, u32[]{:S(2)}) collective-permute-start(bf16[48,1024]{1,0:T(8,128)(2,1)} %get-tuple-element.48), channel_id=1, source_target_pairs={{0,8},{2,10},{4,12},{6,14},{8,0},{10,2},{12,4},{14,6},{1,9},{3,11}... | collective-permute-start | bytes 294920 | tf_op jit(solution)/shard_map/ppermute | solution.py:623
  109.2 9.2 %collective-permute-start.15 = (bf16[48,1024]{1,0:T(8,128)(2,1)}, bf16[48,1024]{1,0:T(8,128)(2,1)}, u32[]{:S(2)}, u32[]{:S(2)}) collective-permute-start(bf16[48,1024]{1,0:T(8,128)(2,1)} %get-tuple-element.49), channel_id=1, source_target_pairs={{0,12},{2,14},{4,0},{6,2},{8,4},{10,6},{12,8},{14,10},{1,13},{3,15... | collective-permute-start | bytes 294920 | tf_op jit(solution)/shard_map/ppermute | solution.py:623
  111.9 6.5 %copy-start.1 = (bf16[48,1024]{1,0:T(8,128)(2,1)}, bf16[48,1024]{1,0:T(8,128)(2,1)S(1)}, u32[]{:S(2)}) copy-start(bf16[48,1024]{1,0:T(8,128)(2,1)S(1)} %collective-permute-done.13.refs_1_) | copy-start | bytes 294916
  115.8 2.6 %copy-start.2 = (bf16[48,1024]{1,0:T(8,128)(2,1)}, bf16[48,1024]{1,0:T(8,128)(2,1)S(1)}, u32[]{:S(2)}) copy-start(bf16[48,1024]{1,0:T(8,128)(2,1)S(1)} %collective-permute-done.14.refs_2_) | copy-start | bytes 294916

commit v10 on v8

--- a/solution.py
+++ b/solution.py
@@ -640,7 +640,7 @@
     got = lax.ppermute(send, "z", beside)
     up_gradient = up_gradient_of(small, scale, given)
     blocks = list(quad(z, up_gradient, keep, got))
-    for k in range(1, 4):
+    for k in (2, 1, 3):
         blocks[k] = further(blocks[k], "z", 2 * k, 8)
     grad_tokens, down_gradient, output, grad_magnitude = finish(
         z, tokens_full, scale, parts, blocks

time: 125 us -> 125 us (level)
  no operation moved by 1% of the time
where the time goes in v10:
time: 125 us; the launch traced here: 123 us
  starting transfers between devices  51.5 us (41%)
  Pallas kernels  44.1 us (35%)
  waiting for transfers between devices  21.2 us (17%)
  local copies, waits for them, and re-layouts  3.23 us (3%)
  other arithmetic  2.03 us (2%)
    ppermute x12, starting transfers between devices, further(): return lax.ppermute(value, axis, [(i, (i + k) % size) for i in range(size)])  32 us
    all_to_all x2, starting transfers between devices, exchange(): return lax.all_to_all(blocks, ROW, 0, 0, tiled=False)  15.3 us
    ppermute x12, waiting for transfers between devices, further(): return lax.ppermute(value, axis, [(i, (i + k) % size) for i in range(size)])  13.4 us
    pallas_call x1, Pallas kernels, backward(): call(backward_kernel, 2 * 512 * depth * width, 12 * MIB, in_specs=[SMEM]...  7.84 us
    pallas_call x1, Pallas kernels, forward(): call(forward_kernel, 2 * 512 * depth * width, 12 * MIB, in_specs=[ANY] *...  7.74 us
    pallas_call x1, Pallas kernels, merge(): call(merge_kernel, 12 * depth * width, 4 * depth * width, in_specs=[ANY]...  6.5 us
    pallas_call x1, Pallas kernels, up_gradient_of(): call(up_kernel, 2 * 512 * 256 * width, 4 * MIB, in_specs=[ANY] * 3, out_s...  4.18 us
    pallas_call x1, Pallas kernels, finish(): call(finish_kernel, 2 * 512 * 256 * depth, 6 * MIB, in_specs=[SMEM] + [AN...  3.99 us
  transfers between devices with their start and end apart: 18, of which 8 were waited for; matrix products, arithmetic and copies ran while one was open for 4% of the time, Pallas kernels for 30%

profile of v10, /device:TPU:8, one launch (start us, length us, event | category | flops | bytes accessed | tf_op | source)
XLA Modules:
  0.0 123.0 jit_solution(11197746866815365803)
XLA Ops:
  0.6 2.9 %spread.1 = bf16[16,32,3328]{2,1,0:T(8,128)(2,1)} custom-call(bf16[32,3328]{1,0:T(8,128)(2,1)} %cot_hbm.1), custom_call_target="tpu_custom_call" | custom-call | flops 106496 | bytes 4194304 | tf_op jit(solution)/shard_map/spread/pallas_call | solution.py:163
  3.5 0.0 copy-start.3
  3.5 7.5 %all-to-all-start = ((bf16[16,32,3328]{2,1,0:T(8,128)(2,1)}), bf16[16,32,3328]{2,1,0:T(8,128)(2,1)}, u32[]{:S(2)}, u32[]{:S(2)}) async-start(bf16[16,32,3328]{2,1,0:T(8,128)(2,1)} %spread.1), calls=%async_computation | async-start | bytes 6815744 | tf_op jit(solution)/shard_map/all_to_all | solution.py:597
  11.1 2.0 %collective-permute-start = (bf16[32,1024]{1,0:T(8,128)(2,1)S(1)}, bf16[32,1024]{1,0:T(8,128)(2,1)S(1)}, u32[]{:S(2)}, u32[]{:S(2)}) collective-permute-start(bf16[32,1024]{1,0:T(8,128)(2,1)S(1)} %copy-done.3), channel_id=1, source_target_pairs={{0,2},{2,0},{4,6},{6,4},{8,10},{10,8},{12,14},{14,12},{1,3},{3,1},... | collective-permute-start | bytes 196616 | tf_op jit(solution)/shard_map/ppermute | solution.py:620
  13.1 0.6 constant_dynamic-update-slice_fusion.1
  13.7 1.7 %collective-permute-done = bf16[32,1024]{1,0:T(8,128)(2,1)S(1)} collective-permute-done((bf16[32,1024]{1,0:T(8,128)(2,1)S(1)}, bf16[32,1024]{1,0:T(8,128)(2,1)S(1)}, u32[]{:S(2)}, u32[]{:S(2)}) %collective-permute-start) | collective-permute-done | bytes 65568 | tf_op jit(solution)/shard_map/ppermute | solution.py:620
  15.4 0.6 constant_dynamic-update-slice_fusion
  16.0 3.3 %collective-permute-start.1 = (bf16[64,1024]{1,0:T(8,128)(2,1)S(1)}, bf16[64,1024]{1,0:T(8,128)(2,1)S(1)}, u32[]{:S(2)}, u32[]{:S(2)}) collective-permute-start(bf16[64,1024]{1,0:T(8,128)(2,1)S(1)} %get-tuple-element.55.after_hbm), channel_id=1, source_target_pairs={{0,4},{2,6},{4,8},{6,10},{8,12},{10,14},{12,0},{14,2},{1,5},{3,7},... | collective-permute-start | bytes 393224 | tf_op jit(solution)/shard_map/ppermute | solution.py:601
  19.3 5.4 %collective-permute-start.2 = (bf16[64,1024]{1,0:T(8,128)(2,1)S(1)}, bf16[64,1024]{1,0:T(8,128)(2,1)S(1)}, u32[]{:S(2)}, u32[]{:S(2)}) collective-permute-start(bf16[64,1024]{1,0:T(8,128)(2,1)S(1)} %get-tuple-element.55.after_hbm), channel_id=1, source_target_pairs={{0,8},{2,10},{4,12},{6,14},{8,0},{10,2},{12,4},{14,6},{1,9},{3,11}... | collective-permute-start | bytes 393224 | tf_op jit(solution)/shard_map/ppermute | solution.py:601
  24.7 2.7 %collective-permute-start.3 = (bf16[64,1024]{1,0:T(8,128)(2,1)S(1)}, bf16[64,1024]{1,0:T(8,128)(2,1)S(1)}, u32[]{:S(2)}, u32[]{:S(2)}) collective-permute-start(bf16[64,1024]{1,0:T(8,128)(2,1)S(1)} %get-tuple-element.55.after_hbm), channel_id=1, source_target_pairs={{0,12},{2,14},{4,0},{6,2},{8,4},{10,6},{12,8},{14,10},{1,13},{3,15... | collective-permute-start | bytes 393224 | tf_op jit(solution)/shard_map/ppermute | solution.py:601
  27.4 0.7 constant_dynamic-update-slice_fusion.4
  28.0 5.0 %collective-permute-done.2 = bf16[64,1024]{1,0:T(8,128)(2,1)S(1)} collective-permute-done((bf16[64,1024]{1,0:T(8,128)(2,1)S(1)}, bf16[64,1024]{1,0:T(8,128)(2,1)S(1)}, u32[]{:S(2)}, u32[]{:S(2)}) %collective-permute-start.2) | collective-permute-done | bytes 131104 | tf_op jit(solution)/shard_map/ppermute | solution.py:601
  33.1 0.7 constant_dynamic-update-slice_fusion.3
  33.7 1.8 %collective-permute-done.3 = bf16[64,1024]{1,0:T(8,128)(2,1)S(1)} collective-permute-done((bf16[64,1024]{1,0:T(8,128)(2,1)S(1)}, bf16[64,1024]{1,0:T(8,128)(2,1)S(1)}, u32[]{:S(2)}, u32[]{:S(2)}) %collective-permute-start.3) | collective-permute-done | bytes 131104 | tf_op jit(solution)/shard_map/ppermute | solution.py:601
  35.5 0.7 constant_dynamic-update-slice_fusion.2.own_hbm
  36.2 0.6 pad_add_fusion.place_ref
  36.7 6.5 %merge.1 = (bf16[1024,3328]{1,0:T(8,128)(2,1)}, f32[32,128]{1,0:T(8,128)}) custom-call(bf16[64,1024]{1,0:T(8,128)(2,1)} %copy-done, f32[16,1024]{1,0:T(8,128)} %bitcast.9, f32[16,3328]{1,0:T(8,128)} %up_hbm.3, bf16[1024,3328]{1,0:T(8,128)(2,1)} %weight_hbm.1), custom_call_target="tpu_custom_call" | custom-call | flops 40894464 | bytes 13631488 | tf_op jit(solution)/shard_map/merge/pallas_call | solution.py:129
  43.3 3.1 %project.1 = (f32[96,128]{1,0:T(8,128)}, bf16[8,2,32,1024]{3,2,1,0:T(8,128)(2,1)}) custom-call(s32[2]{0:T(128)} %pad_add_fusion.place_ref, bf16[256,1024]{1,0:T(8,128)(2,1)} %constant_dynamic-update-slice_fusion.2.own_hbm, bf16[256,1024]{1,0:T(8,128)(2,1)} %collective-permute-done.4.other_hbm, f32[16,1024]{1,0:T(8,128)} %bitcast.10, ...), custom_call_target="tpu_custom_call" | custom-call | flops 268435456 | bytes 3145728 | tf_op jit(solution)/shard_map/project/pallas_call | solution.py:208
  46.4 2.8 %collective-permute-start.7 = (f32[96,128]{1,0:T(8,128)}, f32[96,128]{1,0:T(8,128)S(1)}, u32[]{:S(2)}, u32[]{:S(2)}) collective-permute-start(f32[96,128]{1,0:T(8,128)} %get-tuple-element.32), channel_id=1, source_target_pairs={{0,192},{64,0},{128,64},{192,128},{1,193},{65,1},{129,65},{193,129... | collective-permute-start | bytes 147464 | tf_op jit(solution)/shard_map/ppermute | solution.py:601
  49.2 0.8 collective-permute-start.6
  50.0 0.9 collective-permute-start.5
  50.9 7.7 %forward.1.part_hbm = bf16[16,32,3456]{2,1,0:T(8,128)(2,1)} custom-call(bf16[512,1024]{1,0:T(8,128)(2,1)} %bitcast.7, bf16[1024,3328]{1,0:T(8,128)(2,1)} %get-tuple-element.33.merged_hbm), custom_call_target="tpu_custom_call" | custom-call | flops 3489660928 | bytes 12582912 | tf_op jit(solution)/shard_map/forward/pallas_call | solution.py:249
  58.6 0.0 collective-permute-done.6
  58.7 0.0 collective-permute-done.5
  58.7 0.8 add_add_fusion.1
  59.5 0.8 collective-permute-start.10
  60.3 2.4 %collective-permute-start.9 = (f32[96,128]{1,0:T(8,128)S(1)}, f32[96,128]{1,0:T(8,128)S(1)}, u32[]{:S(2)}, u32[]{:S(2)}) collective-permute-start(f32[96,128]{1,0:T(8,128)S(1)} %add_add_fusion.1), channel_id=1, source_target_pairs={{0,32},{16,48},{32,0},{48,16},{1,33},{17,49},{33,1},{49,17},{2,34}... | collective-permute-start | bytes 147464 | tf_op jit(solution)/shard_map/ppermute | solution.py:601
  62.7 1.8 %collective-permute-start.8 = (f32[96,128]{1,0:T(8,128)S(1)}, f32[96,128]{1,0:T(8,128)S(1)}, u32[]{:S(2)}, u32[]{:S(2)}) collective-permute-start(f32[96,128]{1,0:T(8,128)S(1)} %add_add_fusion.1), channel_id=1, source_target_pairs={{0,16},{16,32},{32,48},{48,0},{1,17},{17,33},{33,49},{49,1},{2,18}... | collective-permute-start | bytes 147464 | tf_op jit(solution)/shard_map/ppermute | solution.py:601
  64.5 0.0 all-to-all-done.given_hbm
  64.5 3.8 %magnitude.1 = bf16[16,32,3456]{2,1,0:T(8,128)(2,1)} custom-call(bf16[16,32,3328]{2,1,0:T(8,128)(2,1)} %all-to-all-done.given_hbm, bf16[16,32,3456]{2,1,0:T(8,128)(2,1)} %forward.1.part_hbm), custom_call_target="tpu_custom_call", output_to_operand_aliasing={{}: (1, {})} | custom-call | flops 6815744 | bytes 7340032 | tf_op jit(solution)/shard_map/magnitude/pallas_call | solution.py:287
  68.3 0.0 collective-permute-done.10
  68.3 7.7 %all-to-all-start.1 = ((bf16[16,32,3456]{2,1,0:T(8,128)(2,1)}), bf16[16,32,3456]{2,1,0:T(8,128)(2,1)}, u32[]{:S(2)}, u32[]{:S(2)}) async-start(bf16[16,32,3456]{2,1,0:T(8,128)(2,1)} %magnitude.1), calls=%async_computation.1 | async-start | bytes 7077888 | tf_op jit(solution)/shard_map/all_to_all | solution.py:597
  76.0 0.6 add_add_fusion.small_hbm
  76.7 7.8 %backward.1 = (bf16[272,1024]{1,0:T(8,128)(2,1)}, bf16[272,1024]{1,0:T(8,128)(2,1)}, f32[64,128]{1,0:T(8,128)}) custom-call(s32[1]{0:T(128)} %bitcast.1.core_ref, f32[96,128]{1,0:T(8,128)} %add_add_fusion.small_hbm, f32[26,128]{1,0:T(8,128)} %bitcast.12, f32[16,3328]{1,0:T(8,128)} %up_hbm.3, bf16[16,32,3328]{2,1,0:T(8,128)(2,1)} %all-to-all-done.given_hbm, ...), custom_call_target="tpu_custom_call" | custom-call | flops 3489660928 | bytes 12582912 | tf_op jit(solution)/shard_map/backward/pallas_call | solution.py:370
  84.5 0.1 collective-permute-start.11
  84.6 2.3 %collective-permute-done.11.got_hbm = bf16[272,1024]{1,0:T(8,128)(2,1)} collective-permute-done((bf16[272,1024]{1,0:T(8,128)(2,1)}, bf16[272,1024]{1,0:T(8,128)(2,1)}, u32[]{:S(2)}, u32[]{:S(2)}) %collective-permute-start.11) | collective-permute-done | bytes 557088 | tf_op jit(solution)/shard_map/ppermute | solution.py:638
  86.9 2.2 %pair.1 = (bf16[144,1024]{1,0:T(8,128)(2,1)}, bf16[144,1024]{1,0:T(8,128)(2,1)}) custom-call(s32[1]{0:T(128)} %bitcast.z_ref, bf16[272,1024]{1,0:T(8,128)(2,1)} %get-tuple-element.43.own_hbm, bf16[272,1024]{1,0:T(8,128)(2,1)} %collective-permute-done.11.got_hbm), custom_call_target="tpu_custom_call" | custom-call | flops 1114112 | bytes 1671168 | tf_op jit(solution)/shard_map/pair/pallas_call | solution.py:416
  89.1 2.1 %collective-permute-start.12 = (bf16[144,1024]{1,0:T(8,128)(2,1)}, bf16[144,1024]{1,0:T(8,128)(2,1)}, u32[]{:S(2)}, u32[]{:S(2)}) collective-permute-start(bf16[144,1024]{1,0:T(8,128)(2,1)} %get-tuple-element.46), channel_id=1, source_target_pairs={{0,2},{2,0},{4,6},{6,4},{8,10},{10,8},{12,14},{14,12},{1,3},{3,1},... | collective-permute-start | bytes 884744 | tf_op jit(solution)/shard_map/ppermute | solution.py:640
  91.2 4.2 %up_gradient.1.after_hbm = f32[16,3328]{1,0:T(8,128)} custom-call(f32[96,128]{1,0:T(8,128)} %add_add_fusion.small_hbm, f32[64,128]{1,0:T(8,128)} %get-tuple-element.41.scale_hbm, bf16[16,32,3328]{2,1,0:T(8,128)(2,1)} %all-to-all-done.given_hbm), custom_call_target="tpu_custom_call" | custom-call | flops 872415232 | bytes 4194304 | tf_op jit(solution)/shard_map/up_gradient/pallas_call | solution.py:493
  95.4 3.4 %collective-permute-done.12.got_hbm = bf16[144,1024]{1,0:T(8,128)(2,1)} collective-permute-done((bf16[144,1024]{1,0:T(8,128)(2,1)}, bf16[144,1024]{1,0:T(8,128)(2,1)}, u32[]{:S(2)}, u32[]{:S(2)}) %collective-permute-start.12) | collective-permute-done | bytes 294944 | tf_op jit(solution)/shard_map/ppermute | solution.py:640
  98.8 1.9 %quad.1 = (bf16[48,1024]{1,0:T(8,128)(2,1)}, bf16[48,1024]{1,0:T(8,128)(2,1)}, bf16[48,1024]{1,0:T(8,128)(2,1)}, bf16[48,1024]{1,0:T(8,128)(2,1)}) custom-call(s32[1]{0:T(128)} %bitcast.z_ref, f32[16,3328]{1,0:T(8,128)} %up_gradient.1.after_hbm, bf16[144,1024]{1,0:T(8,128)(2,1)} %get-tuple-element.45.keep_hbm, bf16[144,1024]{1,0:T(8,128)(2,1)} %collective-permute-done.12.got_hbm), custom_call_target="tpu_custom_call" | custom-call | flops 589824 | bytes 884736 | tf_op jit(solution)/shard_map/quad/pallas_call | solution.py:452
  100.7 3.3 %collective-permute-start.13 = (bf16[48,1024]{1,0:T(8,128)(2,1)}, bf16[48,1024]{1,0:T(8,128)(2,1)S(1)}, u32[]{:S(2)}, u32[]{:S(2)}) collective-permute-start(bf16[48,1024]{1,0:T(8,128)(2,1)} %get-tuple-element.48), channel_id=1, source_target_pairs={{0,4},{2,6},{4,8},{6,10},{8,12},{10,14},{12,0},{14,2},{1,5},{3,7},... | collective-permute-start | bytes 294920 | tf_op jit(solution)/shard_map/ppermute | solution.py:601
  104.0 5.2 %collective-permute-start.14 = (bf16[48,1024]{1,0:T(8,128)(2,1)}, bf16[48,1024]{1,0:T(8,128)(2,1)S(1)}, u32[]{:S(2)}, u32[]{:S(2)}) collective-permute-start(bf16[48,1024]{1,0:T(8,128)(2,1)} %get-tuple-element.49), channel_id=1, source_target_pairs={{0,8},{2,10},{4,12},{6,14},{8,0},{10,2},{12,4},{14,6},{1,9},{3,11}... | collective-permute-start | bytes 294920 | tf_op jit(solution)/shard_map/ppermute | solution.py:601
  109.2 2.7 %collective-permute-start.15 = (bf16[48,1024]{1,0:T(8,128)(2,1)}, bf16[48,1024]{1,0:T(8,128)(2,1)}, u32[]{:S(2)}, u32[]{:S(2)}) collective-permute-start(bf16[48,1024]{1,0:T(8,128)(2,1)} %get-tuple-element.50), channel_id=1, source_target_pairs={{0,12},{2,14},{4,0},{6,2},{8,4},{10,6},{12,8},{14,10},{1,13},{3,15... | collective-permute-start | bytes 294920 | tf_op jit(solution)/shard_map/ppermute | solution.py:601
  111.9 4.0 %collective-permute-done.14.refs_2_ = bf16[48,1024]{1,0:T(8,128)(2,1)S(1)} collective-permute-done((bf16[48,1024]{1,0:T(8,128)(2,1)}, bf16[48,1024]{1,0:T(8,128)(2,1)S(1)}, u32[]{:S(2)}, u32[]{:S(2)}) %collective-permute-start.14) | collective-permute-done | bytes 98336 | tf_op jit(solution)/shard_map/ppermute | solution.py:601
  115.9 2.6 %collective-permute-done.15.refs_3_ = bf16[48,1024]{1,0:T(8,128)(2,1)} collective-permute-done((bf16[48,1024]{1,0:T(8,128)(2,1)}, bf16[48,1024]{1,0:T(8,128)(2,1)}, u32[]{:S(2)}, u32[]{:S(2)}) %collective-permute-start.15) | collective-permute-done | bytes 98336 | tf_op jit(solution)/shard_map/ppermute | solution.py:601
  118.4 0.4 all-to-all-done.1.parts_hbm
  118.9 4.0 %finish.1 = (bf16[32,1024]{1,0:T(8,128)(2,1)}, f32[16,1024]{1,0:T(8,128)}, bf16[32,3328]{1,0:T(8,128)(2,1)}, f32[26,128]{1,0:T(8,128)}) custom-call(s32[1]{0:T(128)} %bitcast.z_ref, bf16[512,1024]{1,0:T(8,128)(2,1)} %bitcast.8, f32[64,128]{1,0:T(8,128)} %get-tuple-element.41.scale_hbm, bf16[16,32,3456]{2,1,0:T(8,128)(2,1)} %all-to-all-done.1.parts_hbm, ...), custom_call_target="tpu_custom_call" | custom-call | flops 268435456 | bytes 6291456 | tf_op jit(solution)/shard_map/finish/pallas_call | solution.py:565
  (16 shorter events, 0.0 us)
Async XLA Ops:
  3.5 7.5 %copy-start.3 = (bf16[32,1024]{1,0:T(8,128)(2,1)S(1)}, bf16[32,1024]{1,0:T(8,128)(2,1)}, u32[]{:S(2)}) copy-start(bf16[32,1024]{1,0:T(8,128)(2,1)} %param.6) | copy-start | bytes 196612
  3.5 60.9 %all-to-all-start = ((bf16[16,32,3328]{2,1,0:T(8,128)(2,1)}), bf16[16,32,3328]{2,1,0:T(8,128)(2,1)}, u32[]{:S(2)}, u32[]{:S(2)}) async-start(bf16[16,32,3328]{2,1,0:T(8,128)(2,1)} %spread.1), calls=%async_computation | async-start | bytes 6815744 | tf_op jit(solution)/shard_map/all_to_all | solution.py:597
  11.1 4.4 %collective-permute-start = (bf16[32,1024]{1,0:T(8,128)(2,1)S(1)}, bf16[32,1024]{1,0:T(8,128)(2,1)S(1)}, u32[]{:S(2)}, u32[]{:S(2)}) collective-permute-start(bf16[32,1024]{1,0:T(8,128)(2,1)S(1)} %copy-done.3), channel_id=1, source_target_pairs={{0,2},{2,0},{4,6},{6,4},{8,10},{10,8},{12,14},{14,12},{1,3},{3,1},... | collective-permute-start | bytes 196616 | tf_op jit(solution)/shard_map/ppermute | solution.py:620
  16.0 20.7 %copy-start = (bf16[64,1024]{1,0:T(8,128)(2,1)}, bf16[64,1024]{1,0:T(8,128)(2,1)S(1)}, u32[]{:S(2)}) copy-start(bf16[64,1024]{1,0:T(8,128)(2,1)S(1)} %get-tuple-element.55.after_hbm) | copy-start | bytes 393220
  16.0 11.3 %collective-permute-start.1 = (bf16[64,1024]{1,0:T(8,128)(2,1)S(1)}, bf16[64,1024]{1,0:T(8,128)(2,1)S(1)}, u32[]{:S(2)}, u32[]{:S(2)}) collective-permute-start(bf16[64,1024]{1,0:T(8,128)(2,1)S(1)} %get-tuple-element.55.after_hbm), channel_id=1, source_target_pairs={{0,4},{2,6},{4,8},{6,10},{8,12},{10,14},{12,0},{14,2},{1,5},{3,7},... | collective-permute-start | bytes 393224 | tf_op jit(solution)/shard_map/ppermute | solution.py:601
  19.3 13.7 %collective-permute-start.2 = (bf16[64,1024]{1,0:T(8,128)(2,1)S(1)}, bf16[64,1024]{1,0:T(8,128)(2,1)S(1)}, u32[]{:S(2)}, u32[]{:S(2)}) collective-permute-start(bf16[64,1024]{1,0:T(8,128)(2,1)S(1)} %get-tuple-element.55.after_hbm), channel_id=1, source_target_pairs={{0,8},{2,10},{4,12},{6,14},{8,0},{10,2},{12,4},{14,6},{1,9},{3,11}... | collective-permute-start | bytes 393224 | tf_op jit(solution)/shard_map/ppermute | solution.py:601
  24.7 10.8 %collective-permute-start.3 = (bf16[64,1024]{1,0:T(8,128)(2,1)S(1)}, bf16[64,1024]{1,0:T(8,128)(2,1)S(1)}, u32[]{:S(2)}, u32[]{:S(2)}) collective-permute-start(bf16[64,1024]{1,0:T(8,128)(2,1)S(1)} %get-tuple-element.55.after_hbm), channel_id=1, source_target_pairs={{0,12},{2,14},{4,0},{6,2},{8,4},{10,6},{12,8},{14,10},{1,13},{3,15... | collective-permute-start | bytes 393224 | tf_op jit(solution)/shard_map/ppermute | solution.py:601
  36.2 7.1 %collective-permute-start.4 = (bf16[256,1024]{1,0:T(8,128)(2,1)}, bf16[256,1024]{1,0:T(8,128)(2,1)}, u32[]{:S(2)}, u32[]{:S(2)}) collective-permute-start(bf16[256,1024]{1,0:T(8,128)(2,1)} %constant_dynamic-update-slice_fusion.2.own_hbm), channel_id=1, source_target_pairs={{0,1},{1,0},{2,3},{3,2},{4,5},{5,4},{6,7},{7,6},{8,9},{9,8},{10,11... | collective-permute-start | bytes 1572872 | tf_op jit(solution)/shard_map/ppermute | solution.py:624
  46.4 12.2 %collective-permute-start.7 = (f32[96,128]{1,0:T(8,128)}, f32[96,128]{1,0:T(8,128)S(1)}, u32[]{:S(2)}, u32[]{:S(2)}) collective-permute-start(f32[96,128]{1,0:T(8,128)} %get-tuple-element.32), channel_id=1, source_target_pairs={{0,192},{64,0},{128,64},{192,128},{1,193},{65,1},{129,65},{193,129... | collective-permute-start | bytes 147464 | tf_op jit(solution)/shard_map/ppermute | solution.py:601
  49.2 9.5 %collective-permute-start.6 = (f32[96,128]{1,0:T(8,128)}, f32[96,128]{1,0:T(8,128)S(1)}, u32[]{:S(2)}, u32[]{:S(2)}) collective-permute-start(f32[96,128]{1,0:T(8,128)} %get-tuple-element.32), channel_id=1, source_target_pairs={{0,128},{64,192},{128,0},{192,64},{1,129},{65,193},{129,1},{193,65... | collective-permute-start | bytes 147464 | tf_op jit(solution)/shard_map/ppermute | solution.py:601
  50.0 8.7 %collective-permute-start.5 = (f32[96,128]{1,0:T(8,128)}, f32[96,128]{1,0:T(8,128)}, u32[]{:S(2)}, u32[]{:S(2)}) collective-permute-start(f32[96,128]{1,0:T(8,128)} %get-tuple-element.32), channel_id=1, source_target_pairs={{0,64},{64,128},{128,192},{192,0},{1,65},{65,129},{129,193},{193,1... | collective-permute-start | bytes 147464 | tf_op jit(solution)/shard_map/ppermute | solution.py:601
  50.9 7.8 %copy-start.4 = (f32[96,128]{1,0:T(8,128)S(1)}, f32[96,128]{1,0:T(8,128)}, u32[]{:S(2)}) copy-start(f32[96,128]{1,0:T(8,128)} %get-tuple-element.32) | copy-start | bytes 147460
  59.5 8.8 %collective-permute-start.10 = (f32[96,128]{1,0:T(8,128)S(1)}, f32[96,128]{1,0:T(8,128)S(1)}, u32[]{:S(2)}, u32[]{:S(2)}) collective-permute-start(f32[96,128]{1,0:T(8,128)S(1)} %add_add_fusion.1), channel_id=1, source_target_pairs={{0,48},{16,0},{32,16},{48,32},{1,49},{17,1},{33,17},{49,33},{2,50}... | collective-permute-start | bytes 147464 | tf_op jit(solution)/shard_map/ppermute | solution.py:601
  60.3 8.0 %collective-permute-start.9 = (f32[96,128]{1,0:T(8,128)S(1)}, f32[96,128]{1,0:T(8,128)S(1)}, u32[]{:S(2)}, u32[]{:S(2)}) collective-permute-start(f32[96,128]{1,0:T(8,128)S(1)} %add_add_fusion.1), channel_id=1, source_target_pairs={{0,32},{16,48},{32,0},{48,16},{1,33},{17,49},{33,1},{49,17},{2,34}... | collective-permute-start | bytes 147464 | tf_op jit(solution)/shard_map/ppermute | solution.py:601
  62.7 5.6 %collective-permute-start.8 = (f32[96,128]{1,0:T(8,128)S(1)}, f32[96,128]{1,0:T(8,128)S(1)}, u32[]{:S(2)}, u32[]{:S(2)}) collective-permute-start(f32[96,128]{1,0:T(8,128)S(1)} %add_add_fusion.1), channel_id=1, source_target_pairs={{0,16},{16,32},{32,48},{48,0},{1,17},{17,33},{33,49},{49,1},{2,18}... | collective-permute-start | bytes 147464 | tf_op jit(solution)/shard_map/ppermute | solution.py:601
  68.3 50.6 %all-to-all-start.1 = ((bf16[16,32,3456]{2,1,0:T(8,128)(2,1)}), bf16[16,32,3456]{2,1,0:T(8,128)(2,1)}, u32[]{:S(2)}, u32[]{:S(2)}) async-start(bf16[16,32,3456]{2,1,0:T(8,128)(2,1)} %magnitude.1), calls=%async_computation.1 | async-start | bytes 7077888 | tf_op jit(solution)/shard_map/all_to_all | solution.py:597
  84.5 2.4 %collective-permute-start.11 = (bf16[272,1024]{1,0:T(8,128)(2,1)}, bf16[272,1024]{1,0:T(8,128)(2,1)}, u32[]{:S(2)}, u32[]{:S(2)}) collective-permute-start(bf16[272,1024]{1,0:T(8,128)(2,1)} %get-tuple-element.44), channel_id=1, source_target_pairs={{0,1},{1,0},{2,3},{3,2},{4,5},{5,4},{6,7},{7,6},{8,9},{9,8},{10,11... | collective-permute-start | bytes 1671176 | tf_op jit(solution)/shard_map/ppermute | solution.py:638
  89.1 9.7 %collective-permute-start.12 = (bf16[144,1024]{1,0:T(8,128)(2,1)}, bf16[144,1024]{1,0:T(8,128)(2,1)}, u32[]{:S(2)}, u32[]{:S(2)}) collective-permute-start(bf16[144,1024]{1,0:T(8,128)(2,1)} %get-tuple-element.46), channel_id=1, source_target_pairs={{0,2},{2,0},{4,6},{6,4},{8,10},{10,8},{12,14},{14,12},{1,3},{3,1},... | collective-permute-start | bytes 884744 | tf_op jit(solution)/shard_map/ppermute | solution.py:640
  100.7 11.2 %collective-permute-start.13 = (bf16[48,1024]{1,0:T(8,128)(2,1)}, bf16[48,1024]{1,0:T(8,128)(2,1)S(1)}, u32[]{:S(2)}, u32[]{:S(2)}) collective-permute-start(bf16[48,1024]{1,0:T(8,128)(2,1)} %get-tuple-element.48), channel_id=1, source_target_pairs={{0,4},{2,6},{4,8},{6,10},{8,12},{10,14},{12,0},{14,2},{1,5},{3,7},... | collective-permute-start | bytes 294920 | tf_op jit(solution)/shard_map/ppermute | solution.py:601
  104.0 11.8 %collective-permute-start.14 = (bf16[48,1024]{1,0:T(8,128)(2,1)}, bf16[48,1024]{1,0:T(8,128)(2,1)S(1)}, u32[]{:S(2)}, u32[]{:S(2)}) collective-permute-start(bf16[48,1024]{1,0:T(8,128)(2,1)} %get-tuple-element.49), channel_id=1, source_target_pairs={{0,8},{2,10},{4,12},{6,14},{8,0},{10,2},{12,4},{14,6},{1,9},{3,11}... | collective-permute-start | bytes 294920 | tf_op jit(solution)/shard_map/ppermute | solution.py:601
  109.2 9.2 %collective-permute-start.15 = (bf16[48,1024]{1,0:T(8,128)(2,1)}, bf16[48,1024]{1,0:T(8,128)(2,1)}, u32[]{:S(2)}, u32[]{:S(2)}) collective-permute-start(bf16[48,1024]{1,0:T(8,128)(2,1)} %get-tuple-element.50), channel_id=1, source_target_pairs={{0,12},{2,14},{4,0},{6,2},{8,4},{10,6},{12,8},{14,10},{1,13},{3,15... | collective-permute-start | bytes 294920 | tf_op jit(solution)/shard_map/ppermute | solution.py:601
  111.9 6.9 %copy-start.1 = (bf16[48,1024]{1,0:T(8,128)(2,1)}, bf16[48,1024]{1,0:T(8,128)(2,1)S(1)}, u32[]{:S(2)}) copy-start(bf16[48,1024]{1,0:T(8,128)(2,1)S(1)} %collective-permute-done.13.refs_1_) | copy-start | bytes 294916
  115.9 3.0 %copy-start.2 = (bf16[48,1024]{1,0:T(8,128)(2,1)}, bf16[48,1024]{1,0:T(8,128)(2,1)S(1)}, u32[]{:S(2)}) copy-start(bf16[48,1024]{1,0:T(8,128)(2,1)S(1)} %collective-permute-done.14.refs_2_) | copy-start | bytes 294916
